TPU v7x, 512 devices: a whole 4x8x8 slice. The times are simulated.
512 devices in a mesh: dp: 8 (over y), seq: 64 (over x, z, core).
Axes of the slice: x: 4, y: 8, z: 8, core: 2. Of those that a mesh axis runs over, the one named last changes fastest.
Arguments:
- tokens: bfloat16 [8, 16384, 512], P('dp', 'seq'), may hold values from -6 to 6
- cotangent: bfloat16 [8, 16384, 512], P('dp', 'seq'), may hold values from -1.25 to 1.25
- up_weight: bfloat16 [512, 2048], P('seq'), may hold values from -0.25 to 0.25
- down_weight: bfloat16 [2048, 512], P('seq'), may hold values from -0.125 to 0.125
- kernel: float32 [31, 512], replicated, may hold values from -1 to 1
- norm_gain: float32 [512], replicated, may hold values from 0.1 to 1.9
- frame_mask: int32 [8, 16384], P('dp', 'seq'), may hold values 0 or 1
- error_memory: float32 [8, 512, 2048], P('dp', 'seq'), may hold values from -6 to 6
- seed_matrix: int32 [2048, 32], replicated, may hold values from -128 to 127
Outputs:
- mixed: bfloat16 [8, 16384, 512], P('dp', 'seq')
- new_memory: float32 [8, 512, 2048], P('dp', 'seq')
- compressed: float32 [512, 2048], P('seq')
All inputs are finite; a program needn't handle non-finite values. No bound on the sum of `frame_mask` on one device may be relied on, other than what follows from the above.
Results may differ from a plain program's by a relative error of at most 0.0071.
Values may be sent and summed in bfloat16 or wider, within the bound.
No kernel may reach another device: no remote copies, remote signals or barrier semaphores. Data moves between devices by JAX's collectives and lax.ppermute only.
A program may use at most 64 MiB of HBM per device.

v0:
```python
import jax
import jax.numpy as jnp
from jax import lax
from jax.sharding import PartitionSpec as P


def padded(block, sides, width):
    for axis, dim in sides:
        count = lax.axis_size(axis)
        forward = [(i, i + 1) for i in range(count - 1)]
        backward = [(target, source) for source, target in forward]
        low = lax.ppermute(
            lax.slice_in_dim(block, block.shape[dim] - width, None, axis=dim), axis, forward
        )
        high = lax.ppermute(lax.slice_in_dim(block, 0, width, axis=dim), axis, backward)
        block = jnp.concatenate([low, block, high], axis=dim)
    return block


def layer_norm(stream, norm_gain):
    values = stream.astype(jnp.float32)
    center = jnp.mean(values, axis=1, keepdims=True)
    spread = jnp.mean((values - center) ** 2, axis=1, keepdims=True)
    return ((values - center) * lax.rsqrt(spread + 1e-05) * norm_gain).astype(jnp.bfloat16)


def orthonormal(rows_part, gram_matrix):
    cholesky_factor = jnp.linalg.cholesky(gram_matrix)
    return jax.scipy.linalg.solve_triangular(cholesky_factor, rows_part.T, lower=True).T


def per_device(
    tokens,
    cotangent,
    up_weight,
    down_weight,
    kernel,
    norm_gain,
    frame_mask,
    error_memory,
    seed_matrix,
):
    highest = lax.Precision.HIGHEST
    half_width = kernel.shape[0] // 2
    frames = tokens.shape[1]
    widened = padded(tokens, (("seq", 1),), half_width)[0].astype(jnp.float32)
    filtered = kernel[0] * widened[0:frames]
    for offset in range(1, kernel.shape[0]):
        filtered = filtered + kernel[offset] * widened[offset : offset + frames]
    stream = (tokens[0].astype(jnp.float32) + filtered * jax.nn.sigmoid(filtered)).astype(
        jnp.bfloat16
    )
    normed = layer_norm(stream, norm_gain)
    columns = normed
    projected = jnp.dot(
        columns,
        lax.all_gather(up_weight, "seq", axis=0, tiled=True),
        preferred_element_type=jnp.float32,
    )
    squashed = jax.nn.sigmoid(projected)
    hidden = (projected * squashed).astype(jnp.bfloat16)
    down_whole = lax.all_gather(down_weight, "seq", axis=0, tiled=True)
    mixed = (
        stream.astype(jnp.float32)
        + 0.5 * jnp.dot(hidden, down_whole, preferred_element_type=jnp.float32)
    ).astype(jnp.bfloat16)
    masked = cotangent[0] * frame_mask[0][:, None].astype(jnp.bfloat16)
    upstream = lax.dot_general(
        masked, down_whole, (((1,), (1,)), ((), ())), preferred_element_type=jnp.float32
    )
    delta_hidden = (0.5 * upstream * squashed * (1.0 + projected * (1.0 - squashed))).astype(
        jnp.bfloat16
    )
    columns = normed
    grad_rows = lax.psum_scatter(
        lax.dot_general(
            columns, delta_hidden, (((0,), (0,)), ((), ())), preferred_element_type=jnp.float32
        ),
        "seq",
        scatter_dimension=0,
        tiled=True,
    )
    memory_rows = grad_rows + error_memory[0]
    replicas = lax.axis_size("dp")
    start_matrix = seed_matrix.astype(jnp.float32) / 128.0
    left_term = jnp.dot(memory_rows, start_matrix, precision=highest)
    left_rows = lax.psum(left_term, "dp") / replicas
    gram_matrix = lax.psum(jnp.dot(left_rows.T, left_rows, precision=highest), "seq")
    basis_rows = orthonormal(left_rows, gram_matrix)
    right_factor = (
        lax.psum(jnp.dot(memory_rows.T, basis_rows, precision=highest), ("dp", "seq")) / replicas
    )
    compressed = jnp.dot(basis_rows, right_factor.T, precision=highest)
    new_memory = memory_rows - compressed
    return (mixed[None], new_memory[None], compressed)


def solution(mesh):
    in_specs = (
        P("dp", "seq", None),
        P("dp", "seq", None),
        P("seq", None),
        P("seq", None),
        P(),
        P(),
        P("dp", "seq"),
        P("dp", "seq", None),
        P(),
    )
    out_specs = (P("dp", "seq", None), P("dp", "seq", None), P("seq", None))
    return jax.shard_map(
        per_device, mesh=mesh, in_specs=in_specs, out_specs=out_specs, check_vma=False
    )
```

profile of v0, /device:TPU:1, one launch (start us, length us, event | category | flops | bytes accessed | tf_op | source)
XLA Modules:
  0.0 888.1 jit_solution(13995495428252953654)
XLA Ops:
  7.2 0.0 all-gather.3.cloned.1.call-start
  7.2 0.7 all-gather.3.cloned.1.call-update
  7.9 0.0 all-gather.5.cloned.1.call-start
  7.9 0.7 all-gather.5.cloned.1.call-update
  8.6 0.0 reduce-scatter.2.cloned.1.call-start
  8.7 0.7 fusion.106
  9.4 5.4 collective-permute-start
  14.8 4.7 collective-permute-start.1
  19.5 1.0 fusion.108
  20.5 1.1 fusion.107
  21.7 0.7 convert_reduce_fusion.1
  22.4 0.0 collective-permute-done
  22.4 0.0 collective-permute-done.1
  22.4 1.0 maximum_convert_fusion
  23.4 0.0 copy-start.4
  23.4 3.7 convert_reduce_fusion
  27.1 0.2 fusion.13
  27.4 0.0 copy-start.5
  27.4 73.3 %all-gather.3.cloned.1.call-done = bf16[512,2048]{1,0:T(8,128)(2,1)} async-done(((bf16[8,2048]{1,0:T(8,128)(2,1)}), bf16[512,2048]{1,0:T(8,128)(2,1)}) %all-gather.3.cloned.1.call-update) | async-done | bytes 2097168 | tf_op jit(solution)/shard_map/all_gather | solution.py:57
  100.7 0.0 copy-done.4
  100.7 2.4 fusion.103
  103.1 81.6 %all-gather.5.cloned.1.call-done = bf16[2048,512]{1,0:T(8,128)(2,1)} async-done(((bf16[32,512]{1,0:T(8,128)(2,1)}), bf16[2048,512]{1,0:T(8,128)(2,1)}) %all-gather.5.cloned.1.call-update) | async-done | bytes 2097168 | tf_op jit(solution)/shard_map/all_gather | solution.py:62
  184.7 0.0 copy-done.5
  184.7 5.1 fusion.3
  189.8 0.0 copy-start
  189.8 0.0 copy-start.2
  189.8 0.0 reduce-scatter.2.cloned.1.call-update
  189.9 0.0 all-reduce.2.cloned.1.call-start
  189.9 144.6 %reduce-scatter.2.cloned.1.call-done = f32[8,2048]{1,0:T(8,128)} async-done(((f32[512,2048]{1,0:T(8,128)}), f32[8,2048]{1,0:T(8,128)}) %reduce-scatter.2.cloned.1.call-update) | async-done | bytes 65552 | tf_op jit(solution)/shard_map/reduce_scatter | solution.py:75
  334.5 0.0 copy-done
  334.5 0.0 copy-done.2
  334.5 1.1 fusion.79
  335.6 13.1 %psum.21 = f32[8,32]{1,0:T(8,128)S(1)} all-reduce(f32[8,32]{1,0:T(8,128)S(1)} %fusion.79), channel_id=1, replica_groups=mesh['dp'=8,'seq'=64] {'dp'}, use_global_device_ids=true, to_apply=%region_3.0 | all-reduce | flops 256 | bytes 2048 | tf_op jit(solution)/shard_map/psum | solution.py:87
  348.7 0.2 fusion.90
  348.9 250.2 %psum.22 = f32[32,32]{0,1:T(8,128)S(1)} all-reduce(f32[32,32]{0,1:T(8,128)S(1)} %fusion.90), channel_id=1, replica_groups=mesh['dp'=8,'seq'=64] {'seq'}, use_global_device_ids=true, to_apply=%region_4.0 | all-reduce | flops 1024 | bytes 8192 | tf_op jit(solution)/shard_map/psum | solution.py:88
  599.1 0.1 copy.13
  599.2 2.9 cholesky.16
  602.2 0.6 compare_reduce_fusion
  602.8 0.7 fusion.85
  603.5 2.4 custom-call.7
  605.9 0.2 fusion.86
  606.1 3.7 fusion.101
  609.8 0.0 all-reduce.2.cloned.1.call-update
  609.8 0.0 copy-start.1
  609.8 3.1 fusion.6
  612.9 265.8 %all-reduce.2.cloned.1.call-done = f32[2048,32]{1,0:T(8,128)} async-done(((f32[2048,32]{1,0:T(8,128)}), f32[2048,32]{1,0:T(8,128)}) %all-reduce.2.cloned.1.call-update) | async-done | bytes 262160 | tf_op jit(solution)/shard_map/psum | solution.py:91
  878.7 2.1 fusion.7
  880.8 0.0 copy-done.1
  880.8 0.0 copy-start.3
  880.8 0.7 subtract_bitcast_fusion
  881.5 0.0 copy-done.3
  (4 shorter events, 0.1 us)
Async XLA Ops:
  7.2 93.5 %all-gather.3.cloned.1.call-start = ((), (), s32[]{:S(2)}) async-start(), calls=%async_computation.1 | async-start | bytes 2129920 | tf_op jit(solution)/shard_map/all_gather | solution.py:57
  7.9 176.8 %all-gather.5.cloned.1.call-start = ((), (), s32[]{:S(2)}) async-start(), calls=%async_computation.2 | async-start | bytes 2129920 | tf_op jit(solution)/shard_map/all_gather | solution.py:62
  8.6 325.8 %reduce-scatter.2.cloned.1.call-start = ((), (), s32[]{:S(2)}) async-start(), calls=%async_computation.3 | async-start | bytes 4259840 | tf_op jit(solution)/shard_map/reduce_scatter | solution.py:75
  9.4 12.9 %collective-permute-start = (bf16[1,15,512]{2,1,0:T(8,128)(2,1)S(1)}, bf16[1,15,512]{2,1,0:T(8,128)(2,1)S(1)}, u32[]{:S(2)}, u32[]{:S(2)}) collective-permute-start(bf16[1,15,512]{2,1,0:T(8,128)(2,1)S(1)} %get-tuple-element.5), channel_id=1, source_target_pairs={{0,1},{1,2},{2,3},{3,4},{4,5},{5,6},{6,7},{7,8},{8,9},{9,10},{10,1... | collective-permute-start | bytes 46088 | tf_op jit(solution)/shard_map/ppermute | solution.py:12
  14.8 7.6 collective-permute-start.1
  23.4 77.3 %copy-start.4 = (f32[512]{0:T(512)S(1)}, f32[512]{0:T(512)}, u32[]{:S(2)}) copy-start(f32[512]{0:T(512)} %param.14) | copy-start | bytes 6148
  27.4 157.3 %copy-start.5 = (bf16[1,256,512]{2,1,0:T(8,128)(2,1)S(1)}, bf16[1,256,512]{2,1,0:T(8,128)(2,1)}, u32[]{:S(2)}) copy-start(bf16[1,256,512]{2,1,0:T(8,128)(2,1)} %param.10) | copy-start | bytes 786436
  189.8 144.7 %copy-start = (f32[1,8,2048]{2,1,0:T(8,128)S(1)}, f32[1,8,2048]{2,1,0:T(8,128)}, u32[]{:S(2)}) copy-start(f32[1,8,2048]{2,1,0:T(8,128)} %param.16) | copy-start | bytes 196612
  189.8 144.7 %copy-start.2 = (s32[2048,32]{0,1:T(8,128)S(1)}, s32[2048,32]{0,1:T(8,128)}, u32[]{:S(2)}) copy-start(s32[2048,32]{0,1:T(8,128)} %param.17) | copy-start | bytes 786436
  189.9 688.8 %all-reduce.2.cloned.1.call-start = ((), (), s32[]{:S(2)}) async-start(), calls=%async_computation.4 | async-start | bytes 2097152 | tf_op jit(solution)/shard_map/psum | solution.py:91
  609.8 271.1 %copy-start.1 = (f32[8,2048]{1,0:T(8,128)S(1)}, f32[8,2048]{1,0:T(8,128)}, u32[]{:S(2)}) copy-start(f32[8,2048]{1,0:T(8,128)} %reduce-scatter.2.cloned.1.call-done) | copy-start | bytes 196612
  880.8 0.7 copy-start.3
Sparse Core Ops, SparseCore 0:
  11.4 89.2 all-gather.2
  104.1 80.5 all-gather.4
  190.0 144.4 reduce-scatter.1
  609.9 268.7 all-reduce.1
where the time goes:
time: 889 us; the launch traced here: 888 us
  waiting for transfers between devices  567 us (64%)
  blocking collectives  263 us (30%)
  matrix products  17.9 us (2%)
  between operations  13.9 us (2%)
  other arithmetic  13 us (1%)
  starting transfers between devices  10.2 us (1%)
    psum x1, waiting for transfers between devices, per_device(): lax.psum(jnp.dot(memory_rows.T, basis_rows, precision=highest), ('dp', 's...  266 us
    psum x1, blocking collectives, per_device(): lax.psum(jnp.dot(left_rows.T, left_rows, precision=highest), 'seq')  250 us
    reduce_scatter x1, waiting for transfers between devices, per_device(): lax.psum_scatter(lax.dot_general(columns, delta_hidden, (((0,), (0,)), ((...  145 us
    all_gather x1, waiting for transfers between devices, per_device(): down_whole = lax.all_gather(down_weight, 'seq', axis=0, tiled=True)  81.6 us
    all_gather x1, waiting for transfers between devices, per_device(): lax.all_gather(up_weight, 'seq', axis=0, tiled=True)  73.3 us
  transfers between devices with their start and end apart: 6, of which 4 were waited for; matrix products, arithmetic and copies ran while one was open for 2% of the time, Pallas kernels for 0%

commit v1 on v0

v1 whole, which is shorter than its diff:
```python
import jax
import jax.numpy as jnp
from jax import lax
from jax.sharding import Mesh
from jax.sharding import PartitionSpec as P

Y, X, Z, C = 8, 4, 8, 2
CHIPS = X * Z
SEQ = ("x", "z", "c")
HIGHEST = lax.Precision.HIGHEST


def halo(block, width):
    count = CHIPS * C
    forward = [(i, i + 1) for i in range(count - 1)]
    backward = [(target, source) for source, target in forward]
    low = lax.ppermute(block[block.shape[0] - width :], SEQ, forward)
    high = lax.ppermute(block[:width], SEQ, backward)
    return low, high


def swap_cores(block):
    return lax.ppermute(block, "c", [(0, 1), (1, 0)])


def layer_norm(stream, norm_gain):
    values = stream.astype(jnp.float32)
    center = jnp.mean(values, axis=1, keepdims=True)
    spread = jnp.mean((values - center) ** 2, axis=1, keepdims=True)
    return ((values - center) * lax.rsqrt(spread + 1e-05) * norm_gain).astype(jnp.bfloat16)


def gather_by_exchange(block, axis):
    copies = jnp.broadcast_to(block[None], (lax.axis_size(axis), *block.shape))
    return lax.all_to_all(copies, axis, 0, 0, tiled=True)


def half_weights(up_weight, down_weight):
    rows, hidden = up_weight.shape
    half = hidden // C
    down_rows, features = down_weight.shape
    moves = []
    for x in range(X):
        for z in range(Z):
            for c in range(C):
                source = (x * Z + z) * C + c
                target = ((2 * (x % 2) + c) * Z + z) * C + x // 2
                moves.append((source, target))
    down_block = lax.ppermute(down_weight, SEQ, moves)
    up_split = up_weight.reshape(rows, C, half).transpose(1, 0, 2)
    up_block = lax.all_to_all(up_split, "c", 0, 0, tiled=True).reshape(C * rows, half)
    packed = jnp.concatenate([up_block[:, :features], up_block[:, features:], down_block], axis=0)
    line = gather_by_exchange(packed, "z")
    whole = gather_by_exchange(line, "x")
    chip_rows = C * rows
    left_part = whole[:, :, :chip_rows].reshape(CHIPS * chip_rows, features)
    right_part = whole[:, :, chip_rows : 2 * chip_rows].reshape(CHIPS * chip_rows, features)
    up_half = jnp.concatenate([left_part, right_part], axis=1)
    down_half = whole[:, :, 2 * chip_rows :].reshape(X // 2, 2, Z, down_rows, features)
    down_half = down_half.transpose(0, 2, 1, 3, 4).reshape(half, features)
    return up_half, down_half


def per_device(
    tokens,
    cotangent,
    up_weight,
    down_weight,
    kernel,
    norm_gain,
    frame_mask,
    error_memory,
    seed_matrix,
):
    half_width = kernel.shape[0] // 2
    frames, features = tokens.shape[1:]
    low, high = halo(tokens[0], half_width)
    masked = cotangent[0] * frame_mask[0][:, None].astype(jnp.bfloat16)
    masked_other = swap_cores(masked)
    up_half, down_half = half_weights(up_weight, down_weight)

    widened = jnp.concatenate([low, tokens[0], high], axis=0).astype(jnp.float32)
    filtered = kernel[0] * widened[0:frames]
    for offset in range(1, kernel.shape[0]):
        filtered = filtered + kernel[offset] * widened[offset : offset + frames]
    stream = (tokens[0].astype(jnp.float32) + filtered * jax.nn.sigmoid(filtered)).astype(
        jnp.bfloat16
    )
    normed = layer_norm(stream, norm_gain)
    normed_other = swap_cores(normed)
    normed_all = jnp.concatenate([normed, normed_other], axis=0)
    masked_all = jnp.concatenate([masked, masked_other], axis=0)
    projected = jnp.dot(normed_all, up_half, preferred_element_type=jnp.float32)
    squashed = jax.nn.sigmoid(projected)
    hidden = (projected * squashed).astype(jnp.bfloat16)
    upstream = lax.dot_general(
        masked_all, down_half, (((1,), (1,)), ((), ())), preferred_element_type=jnp.float32
    )
    delta_hidden = (0.5 * upstream * squashed * (1.0 + projected * (1.0 - squashed))).astype(
        jnp.bfloat16
    )
    grad_part = lax.dot_general(
        normed_all, delta_hidden, (((0,), (0,)), ((), ())), preferred_element_type=jnp.float32
    ).astype(jnp.bfloat16)

    chip_rows = features // CHIPS
    half = grad_part.shape[1]
    pieces = lax.all_to_all(grad_part.reshape(CHIPS, chip_rows, half), ("x", "z"), 0, 0, tiled=True)
    summed = jnp.sum(pieces.astype(jnp.float32), axis=0)

    mixed_part = jnp.dot(hidden, down_half, preferred_element_type=jnp.float32)
    mixed_other = swap_cores(mixed_part[frames:])
    mixed = (stream.astype(jnp.float32) + 0.5 * (mixed_part[:frames] + mixed_other)).astype(
        jnp.bfloat16
    )

    rows = chip_rows // C
    halves = lax.all_to_all(summed.reshape(C, rows, half), "c", 0, 0, tiled=True)
    grad_rows = halves.transpose(1, 0, 2).reshape(rows, C * half)
    memory_rows = grad_rows + error_memory[0]

    chunks = Y * C
    width = memory_rows.shape[1] // chunks
    start_matrix = seed_matrix.astype(jnp.float32) / 128.0
    left_term = jnp.dot(memory_rows, start_matrix, precision=HIGHEST)
    rank = left_term.shape[1]
    by_chunk = memory_rows.reshape(rows, chunks, width).transpose(1, 0, 2)
    message = jnp.concatenate(
        [by_chunk, jnp.broadcast_to(left_term[None], (chunks, rows, rank))], axis=2
    )
    arrived = lax.all_to_all(message, ("y", "c"), 0, 0, tiled=True)
    mean_rows = jnp.sum(arrived.reshape(Y, chip_rows, width + rank), axis=0) / Y
    columns = gather_by_exchange(mean_rows, ("x", "z")).reshape(features, width + rank)
    mean_columns, left_factor = columns[:, :width], columns[:, width:]

    gram_matrix = jnp.dot(left_factor.T, left_factor, precision=HIGHEST)
    cholesky_factor = jnp.linalg.cholesky(gram_matrix)
    basis = jax.scipy.linalg.solve_triangular(cholesky_factor, left_factor.T, lower=True).T
    right_chunk = jnp.dot(mean_columns.T, basis, precision=HIGHEST)
    chip = lax.axis_index(("x", "z"))
    basis_rows = lax.dynamic_slice_in_dim(basis, chip * chip_rows, chip_rows, axis=0)
    piece = jnp.dot(basis_rows, right_chunk.T, precision=HIGHEST)

    piece = jnp.broadcast_to(piece.reshape(1, C, rows, width), (Y, C, rows, width))
    compressed = lax.all_to_all(piece.reshape(chunks, rows, width), ("y", "c"), 0, 0, tiled=True)
    compressed = compressed.transpose(1, 0, 2).reshape(rows, chunks * width)
    new_memory = memory_rows - compressed
    return (mixed[None], new_memory[None], compressed)


def solution(mesh):
    fine = Mesh(mesh.devices.reshape(Y, X, Z, C), ("y", "x", "z", "c"))
    in_specs = (
        P("y", SEQ, None),
        P("y", SEQ, None),
        P(SEQ, None),
        P(SEQ, None),
        P(),
        P(),
        P("y", SEQ),
        P("y", SEQ, None),
        P(),
    )
    out_specs = (P("y", SEQ, None), P("y", SEQ, None), P(SEQ, None))
    return jax.shard_map(
        per_device, mesh=fine, in_specs=in_specs, out_specs=out_specs, check_vma=False
    )
```

time: 889 us -> 181 us (0.20)
  waiting for transfers between devices: 567 us -> 49.4 us
  blocking collectives: 263 us -> 53.7 us
  starting transfers between devices: 10.2 us -> 47 us
  between operations: 13.9 us -> 0.96 us
    psum x1 -> x0, waiting for transfers between devices: 266 us -> none  [per_device(): lax.psum(jnp.dot(memory_rows.T, basis_rows, precision=highest), ('dp', 's...]
    psum x2 -> x0, blocking collectives: 263 us -> none  [the longest x1 250 us: per_device(): lax.psum(jnp.dot(left_rows.T, left_rows, precision=highest), 'seq')]
    all_gather x2 -> x0, waiting for transfers between devices: 155 us -> none  [the longest x1 81.6 us: per_device(): down_whole = lax.all_gather(down_weight, 'seq', axis=0, tiled=True)]
    reduce_scatter x1 -> x0, waiting for transfers between devices: 145 us -> none  [per_device(): lax.psum_scatter(lax.dot_general(columns, delta_hidden, (((0,), (0,)), ((...]
    all_to_all x0 -> x3, blocking collectives: none -> 53.7 us  [the longest x1 28.5 us: per_device(): lax.all_to_all(grad_part.reshape(CHIPS, chip_rows, half), ('x', 'z'), 0,...]
    all_to_all x0 -> x5, waiting for transfers between devices: none -> 46.1 us  [the longest x3 39.1 us: gather_by_exchange(): return lax.all_to_all(copies, axis, 0, 0, tiled=True)]
    all_to_all x0 -> x5, starting transfers between devices: none -> 28.8 us  [the longest x3 14.1 us: gather_by_exchange(): return lax.all_to_all(copies, axis, 0, 0, tiled=True)]
    ppermute x2 -> x6, starting transfers between devices: 10.1 us -> 18.2 us  [the longest x3 7.61 us: swap_cores(): return lax.ppermute(block, 'c', [(0, 1), (1, 0)])]
  transfers between devices with their start and end apart: 6 -> 11, of which waited for: 4 -> 5; matrix products, arithmetic and copies ran while one was open for 2% -> 13% of each run, Pallas kernels for 0% -> 0%
where the time goes in v1:
time: 181 us; the launch traced here: 180 us
  blocking collectives  53.7 us (30%)
  waiting for transfers between devices  49.4 us (27%)
  starting transfers between devices  47 us (26%)
  other arithmetic  13.1 us (7%)
  matrix products  9.42 us (5%)
  local copies, waits for them, and re-layouts  6.48 us (4%)
    all_to_all x3, waiting for transfers between devices, gather_by_exchange(): return lax.all_to_all(copies, axis, 0, 0, tiled=True)  39.1 us
    all_to_all x1, blocking collectives, per_device(): lax.all_to_all(grad_part.reshape(CHIPS, chip_rows, half), ('x', 'z'), 0,...  28.5 us
    all_to_all x1, blocking collectives, per_device(): arrived = lax.all_to_all(message, ('y', 'c'), 0, 0, tiled=True)  16.4 us
    all_to_all x3, starting transfers between devices, gather_by_exchange(): return lax.all_to_all(copies, axis, 0, 0, tiled=True)  14.1 us
    all_to_all x1, starting transfers between devices, half_weights(): lax.all_to_all(up_split, 'c', 0, 0, tiled=True).reshape(C * rows, half)  10.3 us
    all_to_all x1, blocking collectives, per_device(): lax.all_to_all(summed.reshape(C, rows, half), 'c', 0, 0, tiled=True)  8.78 us
    ppermute x3, starting transfers between devices, swap_cores(): return lax.ppermute(block, 'c', [(0, 1), (1, 0)])  7.61 us
    all_to_all x1, waiting for transfers between devices, per_device(): lax.all_to_all(piece.reshape(chunks, rows, width), ('y', 'c'), 0, 0, tile...  6.99 us
  transfers between devices with their start and end apart: 11, of which 5 were waited for; matrix products, arithmetic and copies ran while one was open for 13% of the time, Pallas kernels for 0%

profile of v1, /device:TPU:1, one launch (start us, length us, event | category | flops | bytes accessed | tf_op | source)
XLA Modules:
  0.0 180.0 jit_solution(10586587638373052754)
XLA Ops:
  0.6 0.0 copy-start
  0.6 0.0 copy-start.2
  0.7 0.0 copy-start.4
  0.7 10.3 %all-to-all-start = ((bf16[2,8,1024]{2,1,0:T(8,128)(2,1)}), bf16[2,8,1024]{2,1,0:T(8,128)(2,1)S(1)}, u32[]{:S(2)}, u32[]{:S(2)}) async-start(bf16[2,8,1024]{2,1,0:T(8,128)(2,1)} %bitcast.113), calls=%async_computation | async-start | bytes 65536 | tf_op jit(solution)/shard_map/all_to_all | solution.py:51
  10.9 0.7 slice_bitcast_fusion.1
  11.7 1.9 %collective-permute-start = (bf16[15,512]{1,0:T(8,128)(2,1)S(1)}, bf16[15,512]{1,0:T(8,128)(2,1)S(1)}, u32[]{:S(2)}, u32[]{:S(2)}) collective-permute-start(bf16[15,512]{1,0:T(8,128)(2,1)S(1)} %get-tuple-element.7), channel_id=1, source_target_pairs={{0,1},{1,2},{2,3},{3,4},{4,5},{5,6},{6,7},{7,8},{8,9},{9,10},{10,1... | collective-permute-start | bytes 46088 | tf_op jit(solution)/shard_map/ppermute | solution.py:17
  13.6 2.4 %collective-permute-start.1 = (bf16[15,512]{1,0:T(8,128)(2,1)S(1)}, bf16[15,512]{1,0:T(8,128)(2,1)S(1)}, u32[]{:S(2)}, u32[]{:S(2)}) collective-permute-start(bf16[15,512]{1,0:T(8,128)(2,1)S(1)} %get-tuple-element.8), channel_id=1, source_target_pairs={{1,0},{2,1},{3,2},{4,3},{5,4},{6,5},{7,6},{8,7},{9,8},{10,9},{11,1... | collective-permute-start | bytes 46088 | tf_op jit(solution)/shard_map/ppermute | solution.py:18
  16.0 6.3 %collective-permute-start.3 = (bf16[32,512]{1,0:T(8,128)(2,1)}, bf16[32,512]{1,0:T(8,128)(2,1)S(1)}, u32[]{:S(2)}, u32[]{:S(2)}) collective-permute-start(bf16[32,512]{1,0:T(8,128)(2,1)} %param.12), channel_id=1, source_target_pairs={{0,0},{1,16},{2,2},{3,18},{4,4},{5,20},{6,6},{7,22},{8,8},{9,24},{... | collective-permute-start | bytes 98312 | tf_op jit(solution)/shard_map/ppermute | solution.py:49
  22.3 0.0 all-to-all-done
  22.3 3.3 %collective-permute-done.3 = bf16[32,512]{1,0:T(8,128)(2,1)S(1)} collective-permute-done((bf16[32,512]{1,0:T(8,128)(2,1)}, bf16[32,512]{1,0:T(8,128)(2,1)S(1)}, u32[]{:S(2)}, u32[]{:S(2)}) %collective-permute-start.3) | collective-permute-done | bytes 32800 | tf_op jit(solution)/shard_map/ppermute | solution.py:49
  25.6 0.8 broadcast_in_dim.15
  26.4 3.8 %all-to-all-start.1 = ((bf16[8,64,512]{2,1,0:T(8,128)(2,1)}), bf16[8,64,512]{2,1,0:T(8,128)(2,1)S(1)}, u32[]{:S(2)}, u32[]{:S(2)}) async-start(bf16[8,64,512]{2,1,0:T(8,128)(2,1)} %broadcast_in_dim.15), calls=%async_computation.1 | async-start | bytes 1048576 | tf_op jit(solution)/shard_map/all_to_all | solution.py:35
  30.3 0.7 convert_reduce_fusion.2
  31.0 0.0 copy-done.2
  31.0 0.1 bitcast_multiply_fusion
  31.1 1.9 %collective-permute-start.5 = (bf16[256,512]{1,0:T(8,128)(2,1)S(1)}, bf16[256,512]{1,0:T(8,128)(2,1)}, u32[]{:S(2)}, u32[]{:S(2)}) collective-permute-start(bf16[256,512]{1,0:T(8,128)(2,1)S(1)} %bitcast_multiply_fusion), channel_id=1, source_target_pairs={{0,1},{1,0},{2,3},{3,2},{4,5},{5,4},{6,7},{7,6},{8,9},{9,8},{10,11... | collective-permute-start | bytes 786440 | tf_op jit(solution)/shard_map/ppermute | solution.py:23
  33.1 0.6 fusion.76
  33.7 0.0 collective-permute-done
  33.7 0.0 collective-permute-done.1
  33.7 0.1 maximum_convert_fusion
  33.8 10.1 %all-to-all-done.1 = bf16[8,64,512]{2,1,0:T(8,128)(2,1)S(1)} async-done(((bf16[8,64,512]{2,1,0:T(8,128)(2,1)}), bf16[8,64,512]{2,1,0:T(8,128)(2,1)S(1)}, u32[]{:S(2)}, u32[]{:S(2)}) %all-to-all-start.1) | async-done | bytes 524320 | tf_op jit(solution)/shard_map/all_to_all | solution.py:35
  43.9 1.6 broadcast_in_dim.16
  45.5 5.5 %all-to-all-start.2 = ((bf16[4,8,64,512]{3,2,1,0:T(8,128)(2,1)}), bf16[4,8,64,512]{3,2,1,0:T(8,128)(2,1)S(1)}, u32[]{:S(2)}, u32[]{:S(2)}) async-start(bf16[4,8,64,512]{3,2,1,0:T(8,128)(2,1)} %broadcast_in_dim.16), calls=%async_computation.2 | async-start | bytes 4194304 | tf_op jit(solution)/shard_map/all_to_all | solution.py:35
  50.9 3.5 %convert_reduce_fusion.1 = (f32[256]{0:T(256)S(1)}, bf16[256,512]{1,0:T(8,128)(2,1)S(1)}) fusion(f32[286,512]{1,0:T(8,128)S(1)} %maximum_convert_fusion, f32[512]{0:T(512)} %bitcast.143, f32[512]{0:T(512)} %bitcast.144, f32[512]{0:T(512)S(1)} %bitcast.115, f32[512]{0:T(512)S(1)} %bitcast.116, f32[512]{0:T(512)S(1)} %bitcast.117, f32[512]{0:T(512)S(1)} %bitcast.118, ...), kind=kLoop, calls=%fused_computation.15 | loop fusion | flops 9174784 | bytes 16841728 | tf_op jit(solution)/shard_map/reduce_sum | solution.py:28
  54.4 0.2 fusion.9
  54.7 0.1 fusion.11
  54.8 3.8 %collective-permute-start.2 = (bf16[256,512]{1,0:T(8,128)(2,1)S(1)}, bf16[256,512]{1,0:T(8,128)(2,1)S(1)}, u32[]{:S(2)}, u32[]{:S(2)}) collective-permute-start(bf16[256,512]{1,0:T(8,128)(2,1)S(1)} %fusion.11), channel_id=1, source_target_pairs={{0,1},{1,0},{2,3},{3,2},{4,5},{5,4},{6,7},{7,6},{8,9},{9,8},{10,11... | collective-permute-start | bytes 786440 | tf_op jit(solution)/shard_map/ppermute | solution.py:23
  58.6 16.9 %all-to-all-done.2 = bf16[4,8,64,512]{3,2,1,0:T(8,128)(2,1)S(1)} async-done(((bf16[4,8,64,512]{3,2,1,0:T(8,128)(2,1)}), bf16[4,8,64,512]{3,2,1,0:T(8,128)(2,1)S(1)}, u32[]{:S(2)}, u32[]{:S(2)}) %all-to-all-start.2) | async-done | bytes 2097184 | tf_op jit(solution)/shard_map/all_to_all | solution.py:35
  75.4 0.1 fusion.74
  75.5 0.1 slice.347
  75.6 0.1 copy.14
  75.8 0.0 collective-permute-done.2
  75.8 2.1 %fusion = f32[512,1024]{1,0:T(8,128)} fusion(bf16[512,512]{1,0:T(8,128)(2,1)S(1)} %bitcast.110, bf16[512,512]{1,0:T(8,128)(2,1)S(1)} %bitcast.109, bf16[256,512]{1,0:T(8,128)(2,1)S(1)} %collective-permute-done.2, bf16[256,512]{1,0:T(8,128)(2,1)S(1)} %fusion.11), kind=kOutput, calls=%fused_computation.6 | convolution fusion | flops 540016640 | bytes 3670016 | tf_op jit(solution)/shard_map/dot_general | solution.py:93
  77.8 0.0 collective-permute-done.5
  77.8 3.3 %convolution_convert_fusion = bf16[512,1024]{1,0:T(8,128)(2,1)S(1)} fusion(f32[512,1024]{1,0:T(8,128)} %fusion, bf16[1024,512]{1,0:T(8,128)(2,1)S(1)} %bitcast.104, bf16[256,512]{1,0:T(8,128)(2,1)} %collective-permute-done.5, bf16[256,512]{1,0:T(8,128)(2,1)S(1)} %bitcast_multiply_fusion, bf16[256,512]{1,0:T(8,128)(2,1)S(1)} %collective-permute-done.2, ...), kind=kOutput, calls=%fused_computation.4 | convolution fusion | flops 1081606144 | bytes 5242880 | tf_op jit(solution)/shard_map/dot_general | solution.py:102
  81.1 0.0 copy-start.1
  81.1 0.0 copy-start.3
  81.1 28.5 %all_to_all.40 = bf16[32,16,1024]{2,1,0:T(8,128)(2,1)S(1)} all-to-all(bf16[32,16,1024]{2,1,0:T(8,128)(2,1)S(1)} %bitcast.106), channel_id=1, replica_groups=mesh['y'=8,'x'=4,'z'=8,'c'=2] {'x','z'}, dimensions={0} | all-to-all | bytes 2097152 | tf_op jit(solution)/shard_map/all_to_all | solution.py:108
  109.6 0.2 convert_reduce_fusion
  109.8 8.8 %all_to_all.41 = f32[2,8,1024]{2,1,0:T(8,128)S(1)} all-to-all(f32[2,8,1024]{2,1,0:T(8,128)S(1)} %bitcast.111), channel_id=1, replica_groups=mesh['y'=8,'x'=4,'z'=8,'c'=2] {'c'}, dimensions={0} | all-to-all | bytes 131072 | tf_op jit(solution)/shard_map/all_to_all | solution.py:118
  118.6 0.3 fusion.53
  118.8 0.1 broadcast_in_dim.18
  118.9 16.4 %all_to_all.42 = f32[16,8,160]{2,1,0:T(8,128)S(1)} all-to-all(f32[16,8,160]{2,1,0:T(8,128)S(1)} %pad_maximum_fusion.3), channel_id=1, replica_groups=mesh['y'=8,'x'=4,'z'=8,'c'=2] {'y','c'}, dimensions={0} | all-to-all | bytes 163840 | tf_op jit(solution)/shard_map/all_to_all | solution.py:131
  135.4 0.9 broadcast_in_dim.19
  136.2 4.8 %all-to-all-start.6 = ((f32[32,16,160]{2,1,0:T(8,128)}), f32[32,16,160]{2,1,0:T(8,128)S(1)}, u32[]{:S(2)}, u32[]{:S(2)}) async-start(f32[32,16,160]{2,1,0:T(8,128)} %broadcast_in_dim.19), calls=%async_computation.6 | async-start | bytes 1048576 | tf_op jit(solution)/shard_map/all_to_all | solution.py:35
  141.0 2.3 %fusion.6 = f32[512,512]{1,0:T(8,128)S(1)} fusion(bf16[1024,512]{1,0:T(8,128)(2,1)S(1)} %bitcast.105, f32[512,1024]{1,0:T(8,128)} %fusion), kind=kOutput, calls=%fused_computation.12 | convolution fusion | flops 539492352 | bytes 4194304 | tf_op jit(solution)/shard_map/dot_general | solution.py:111
  143.4 1.9 %collective-permute-start.4 = (f32[256,512]{1,0:T(8,128)S(1)}, f32[256,512]{1,0:T(8,128)S(1)}, u32[]{:S(2)}, u32[]{:S(2)}) collective-permute-start(f32[256,512]{1,0:T(8,128)S(1)} %slice.349), channel_id=1, source_target_pairs={{0,1},{1,0},{2,3},{3,2},{4,5},{5,4},{6,7},{7,6},{8,9},{9,8},{10,11... | collective-permute-start | bytes 1572872 | tf_op jit(solution)/shard_map/ppermute | solution.py:23
  145.3 12.2 %all-to-all-done.6 = f32[32,16,160]{2,1,0:T(8,128)S(1)} async-done(((f32[32,16,160]{2,1,0:T(8,128)}), f32[32,16,160]{2,1,0:T(8,128)S(1)}, u32[]{:S(2)}, u32[]{:S(2)}) %all-to-all-start.6) | async-done | bytes 327712 | tf_op jit(solution)/shard_map/all_to_all | solution.py:35
  157.5 0.6 fusion.58
  158.0 0.1 copy.15
  158.1 2.9 %cholesky.16 = f32[32,32]{1,0:T(8,128)S(1)} custom-call(f32[32,32]{1,0:T(8,128)S(1)} %fusion.64), custom_call_target="Cholesky" | custom-call | tf_op jit(solution)/shard_map/jit(cholesky)/cholesky | solution.py:137
  161.1 0.6 compare_reduce_fusion
  161.7 0.7 fusion.62
  162.4 2.4 %custom-call.7 = f32[1,32,32]{1,2,0:T(8,128)S(1)} custom-call(f32[1,32,32]{2,1,0:T(8,128)S(1)} %fusion.62), custom_call_target="InvertDiagBlocksLowerTriangular" | custom-call | tf_op jit(solution)/shard_map/jit(_solve_triangular)/triangular_solve | solution.py:138
  164.8 0.4 fusion.56
  165.2 0.3 fusion.51
  165.5 0.3 convolution_bitcast_fusion
  165.8 0.7 broadcast_in_dim.22
  166.4 4.4 %all-to-all-start.7 = ((f32[16,8,128]{2,1,0:T(8,128)}), f32[16,8,128]{2,1,0:T(8,128)S(1)}, u32[]{:S(2)}, u32[]{:S(2)}) async-start(f32[16,8,128]{2,1,0:T(8,128)} %bitcast.59), calls=%async_computation.7 | async-start | bytes 131072 | tf_op jit(solution)/shard_map/all_to_all | solution.py:145
  170.9 0.0 collective-permute-done.4
  170.9 0.8 fusion.50
  171.7 7.0 %all-to-all-done.7 = f32[16,8,128]{2,1,0:T(8,128)S(1)} async-done(((f32[16,8,128]{2,1,0:T(8,128)}), f32[16,8,128]{2,1,0:T(8,128)S(1)}, u32[]{:S(2)}, u32[]{:S(2)}) %all-to-all-start.7) | async-done | bytes 65568 | tf_op jit(solution)/shard_map/all_to_all | solution.py:145
  178.7 0.6 bitcast_subtract_fusion
  179.4 0.6 copy.17
  (18 shorter events, 0.2 us)
Async XLA Ops:
  0.6 33.1 %copy-start = (bf16[1,256,512]{2,1,0:T(8,128)(2,1)S(1)}, bf16[1,256,512]{2,1,0:T(8,128)(2,1)}, u32[]{:S(2)}) copy-start(bf16[1,256,512]{2,1,0:T(8,128)(2,1)} %param.9) | copy-start | bytes 786436
  0.6 30.3 %copy-start.2 = (bf16[1,256,512]{2,1,0:T(8,128)(2,1)S(1)}, bf16[1,256,512]{2,1,0:T(8,128)(2,1)}, u32[]{:S(2)}) copy-start(bf16[1,256,512]{2,1,0:T(8,128)(2,1)} %param.10) | copy-start | bytes 786436
  0.7 32.4 %copy-start.4 = (f32[31,512]{1,0:T(8,128)S(1)}, f32[31,512]{1,0:T(8,128)}, u32[]{:S(2)}) copy-start(f32[31,512]{1,0:T(8,128)} %param.13) | copy-start | bytes 190468
  0.7 21.6 %all-to-all-start = ((bf16[2,8,1024]{2,1,0:T(8,128)(2,1)}), bf16[2,8,1024]{2,1,0:T(8,128)(2,1)S(1)}, u32[]{:S(2)}, u32[]{:S(2)}) async-start(bf16[2,8,1024]{2,1,0:T(8,128)(2,1)} %bitcast.113), calls=%async_computation | async-start | bytes 65536 | tf_op jit(solution)/shard_map/all_to_all | solution.py:51
  11.7 22.0 %collective-permute-start = (bf16[15,512]{1,0:T(8,128)(2,1)S(1)}, bf16[15,512]{1,0:T(8,128)(2,1)S(1)}, u32[]{:S(2)}, u32[]{:S(2)}) collective-permute-start(bf16[15,512]{1,0:T(8,128)(2,1)S(1)} %get-tuple-element.7), channel_id=1, source_target_pairs={{0,1},{1,2},{2,3},{3,4},{4,5},{5,6},{6,7},{7,8},{8,9},{9,10},{10,1... | collective-permute-start | bytes 46088 | tf_op jit(solution)/shard_map/ppermute | solution.py:17
  13.6 20.1 %collective-permute-start.1 = (bf16[15,512]{1,0:T(8,128)(2,1)S(1)}, bf16[15,512]{1,0:T(8,128)(2,1)S(1)}, u32[]{:S(2)}, u32[]{:S(2)}) collective-permute-start(bf16[15,512]{1,0:T(8,128)(2,1)S(1)} %get-tuple-element.8), channel_id=1, source_target_pairs={{1,0},{2,1},{3,2},{4,3},{5,4},{6,5},{7,6},{8,7},{9,8},{10,9},{11,1... | collective-permute-start | bytes 46088 | tf_op jit(solution)/shard_map/ppermute | solution.py:18
  16.0 9.6 %collective-permute-start.3 = (bf16[32,512]{1,0:T(8,128)(2,1)}, bf16[32,512]{1,0:T(8,128)(2,1)S(1)}, u32[]{:S(2)}, u32[]{:S(2)}) collective-permute-start(bf16[32,512]{1,0:T(8,128)(2,1)} %param.12), channel_id=1, source_target_pairs={{0,0},{1,16},{2,2},{3,18},{4,4},{5,20},{6,6},{7,22},{8,8},{9,24},{... | collective-permute-start | bytes 98312 | tf_op jit(solution)/shard_map/ppermute | solution.py:49
  26.4 17.4 %all-to-all-start.1 = ((bf16[8,64,512]{2,1,0:T(8,128)(2,1)}), bf16[8,64,512]{2,1,0:T(8,128)(2,1)S(1)}, u32[]{:S(2)}, u32[]{:S(2)}) async-start(bf16[8,64,512]{2,1,0:T(8,128)(2,1)} %broadcast_in_dim.15), calls=%async_computation.1 | async-start | bytes 1048576 | tf_op jit(solution)/shard_map/all_to_all | solution.py:35
  31.1 46.7 %collective-permute-start.5 = (bf16[256,512]{1,0:T(8,128)(2,1)S(1)}, bf16[256,512]{1,0:T(8,128)(2,1)}, u32[]{:S(2)}, u32[]{:S(2)}) collective-permute-start(bf16[256,512]{1,0:T(8,128)(2,1)S(1)} %bitcast_multiply_fusion), channel_id=1, source_target_pairs={{0,1},{1,0},{2,3},{3,2},{4,5},{5,4},{6,7},{7,6},{8,9},{9,8},{10,11... | collective-permute-start | bytes 786440 | tf_op jit(solution)/shard_map/ppermute | solution.py:23
  45.5 30.0 %all-to-all-start.2 = ((bf16[4,8,64,512]{3,2,1,0:T(8,128)(2,1)}), bf16[4,8,64,512]{3,2,1,0:T(8,128)(2,1)S(1)}, u32[]{:S(2)}, u32[]{:S(2)}) async-start(bf16[4,8,64,512]{3,2,1,0:T(8,128)(2,1)} %broadcast_in_dim.16), calls=%async_computation.2 | async-start | bytes 4194304 | tf_op jit(solution)/shard_map/all_to_all | solution.py:35
  50.9 3.7 %copy-start.5 = (f32[512]{0:T(512)S(1)}, f32[512]{0:T(512)}, u32[]{:S(2)}) copy-start(f32[512]{0:T(512)} %param.14) | copy-start | bytes 6148
  54.8 20.9 %collective-permute-start.2 = (bf16[256,512]{1,0:T(8,128)(2,1)S(1)}, bf16[256,512]{1,0:T(8,128)(2,1)S(1)}, u32[]{:S(2)}, u32[]{:S(2)}) collective-permute-start(bf16[256,512]{1,0:T(8,128)(2,1)S(1)} %fusion.11), channel_id=1, source_target_pairs={{0,1},{1,0},{2,3},{3,2},{4,5},{5,4},{6,7},{7,6},{8,9},{9,8},{10,11... | collective-permute-start | bytes 786440 | tf_op jit(solution)/shard_map/ppermute | solution.py:23
  81.1 37.4 %copy-start.1 = (f32[1,8,2048]{2,1,0:T(8,128)S(1)}, f32[1,8,2048]{2,1,0:T(8,128)}, u32[]{:S(2)}) copy-start(f32[1,8,2048]{2,1,0:T(8,128)} %param.16) | copy-start | bytes 196612
  81.1 37.4 %copy-start.3 = (s32[2048,32]{0,1:T(8,128)S(1)}, s32[2048,32]{0,1:T(8,128)}, u32[]{:S(2)}) copy-start(s32[2048,32]{0,1:T(8,128)} %param.17) | copy-start | bytes 786436
  136.2 21.3 %all-to-all-start.6 = ((f32[32,16,160]{2,1,0:T(8,128)}), f32[32,16,160]{2,1,0:T(8,128)S(1)}, u32[]{:S(2)}, u32[]{:S(2)}) async-start(f32[32,16,160]{2,1,0:T(8,128)} %broadcast_in_dim.19), calls=%async_computation.6 | async-start | bytes 1048576 | tf_op jit(solution)/shard_map/all_to_all | solution.py:35
  143.4 27.5 %collective-permute-start.4 = (f32[256,512]{1,0:T(8,128)S(1)}, f32[256,512]{1,0:T(8,128)S(1)}, u32[]{:S(2)}, u32[]{:S(2)}) collective-permute-start(f32[256,512]{1,0:T(8,128)S(1)} %slice.349), channel_id=1, source_target_pairs={{0,1},{1,0},{2,3},{3,2},{4,5},{5,4},{6,7},{7,6},{8,9},{9,8},{10,11... | collective-permute-start | bytes 1572872 | tf_op jit(solution)/shard_map/ppermute | solution.py:23
  166.4 12.3 %all-to-all-start.7 = ((f32[16,8,128]{2,1,0:T(8,128)}), f32[16,8,128]{2,1,0:T(8,128)S(1)}, u32[]{:S(2)}, u32[]{:S(2)}) async-start(f32[16,8,128]{2,1,0:T(8,128)} %bitcast.59), calls=%async_computation.7 | async-start | bytes 131072 | tf_op jit(solution)/shard_map/all_to_all | solution.py:145

commit v2 on v1

--- a/solution.py
+++ b/solution.py
@@ -1,11 +1,14 @@
 import jax
 import jax.numpy as jnp
 from jax import lax
+from jax.experimental import pallas as pl
+from jax.experimental.pallas import tpu as pltpu
 from jax.sharding import Mesh
 from jax.sharding import PartitionSpec as P
 
 Y, X, Z, C = 8, 4, 8, 2
 CHIPS = X * Z
+RANK = 32
 SEQ = ("x", "z", "c")
 HIGHEST = lax.Precision.HIGHEST
 
@@ -38,27 +41,73 @@
 def half_weights(up_weight, down_weight):
     rows, hidden = up_weight.shape
     half = hidden // C
+    up_split = up_weight.reshape(rows, C, half).transpose(1, 0, 2)
+    up_split = jnp.broadcast_to(up_split[None], (Z, C, rows, half)).reshape(Z * C, rows, half)
+    up_line = lax.all_to_all(up_split, ("z", "c"), 0, 0, tiled=True).reshape(Z * C * rows, half)
+    up_half = gather_by_exchange(up_line, "x").reshape(X * Z * C * rows, half)
+
     down_rows, features = down_weight.shape
-    moves = []
-    for x in range(X):
-        for z in range(Z):
-            for c in range(C):
-                source = (x * Z + z) * C + c
-                target = ((2 * (x % 2) + c) * Z + z) * C + x // 2
-                moves.append((source, target))
-    down_block = lax.ppermute(down_weight, SEQ, moves)
-    up_split = up_weight.reshape(rows, C, half).transpose(1, 0, 2)
-    up_block = lax.all_to_all(up_split, "c", 0, 0, tiled=True).reshape(C * rows, half)
-    packed = jnp.concatenate([up_block[:, :features], up_block[:, features:], down_block], axis=0)
-    line = gather_by_exchange(packed, "z")
-    whole = gather_by_exchange(line, "x")
-    chip_rows = C * rows
-    left_part = whole[:, :, :chip_rows].reshape(CHIPS * chip_rows, features)
-    right_part = whole[:, :, chip_rows : 2 * chip_rows].reshape(CHIPS * chip_rows, features)
-    up_half = jnp.concatenate([left_part, right_part], axis=1)
-    down_half = whole[:, :, 2 * chip_rows :].reshape(X // 2, 2, Z, down_rows, features)
-    down_half = down_half.transpose(0, 2, 1, 3, 4).reshape(half, features)
+    down_line = gather_by_exchange(down_weight, ("x", "c")).reshape(X, C * down_rows, features)
+    pair = lax.dynamic_slice_in_dim(down_line, lax.axis_index("c") * (X // C), X // C, axis=0)
+    down_half = gather_by_exchange(pair, "z").transpose(1, 0, 2, 3).reshape(half, features)
     return up_half, down_half
+
+
+def top_bits(values):
+    return lax.reduce_precision(values, exponent_bits=8, mantissa_bits=7)
+
+
+def terms(values, count):
+    parts = []
+    for _ in range(count):
+        part = top_bits(values)
+        parts.append(part.astype(jnp.bfloat16))
+        values = values - part
+    return parts
+
+
+def tail_kernel(chip_ref, columns_ref, piece_ref, rows_scratch):
+    width = piece_ref.shape[1]
+    rank = RANK
+    columns = columns_ref[...].astype(jnp.float32)
+    mean_columns = columns[:, :width] + columns[:, width : 2 * width]
+    first, second, third = (
+        columns[:, 2 * width + rank * i : 2 * width + rank * (i + 1)] for i in range(3)
+    )
+    left = first + second + third
+    left_t = left.T
+    gram = jnp.dot(left_t, left, precision=HIGHEST, preferred_element_type=jnp.float32)
+    row_index = lax.broadcasted_iota(jnp.int32, (rank, 1), 0)
+    solved = left_t
+    for k in range(rank):
+        scale = lax.rsqrt(gram[k : k + 1, k : k + 1])
+        factor = jnp.where(row_index > k, gram[:, k : k + 1] * scale, 0.0)
+        gram_row = gram[k : k + 1, :] * scale
+        solved_row = solved[k : k + 1, :] * scale
+        gram = gram - factor * gram_row
+        solved = jnp.where(row_index == k, solved_row, solved - factor * solved_row)
+    right_t = jnp.dot(solved, mean_columns, precision=HIGHEST, preferred_element_type=jnp.float32)
+    rows_scratch[...] = solved.T
+    chip_rows = piece_ref.shape[0]
+    basis_rows = rows_scratch[pl.ds(pl.multiple_of(chip_ref[0] * chip_rows, chip_rows), chip_rows), :]
+    piece_ref[...] = jnp.dot(
+        basis_rows, right_t, precision=HIGHEST, preferred_element_type=jnp.float32
+    )
+
+
+def tail(chip, columns, chip_rows, width):
+    features = columns.shape[0]
+    return pl.pallas_call(
+        tail_kernel,
+        out_shape=jax.ShapeDtypeStruct((chip_rows, width), jnp.float32),
+        in_specs=[
+            pl.BlockSpec(memory_space=pltpu.SMEM),
+            pl.BlockSpec(memory_space=pltpu.VMEM),
+        ],
+        out_specs=pl.BlockSpec(memory_space=pltpu.VMEM),
+        scratch_shapes=[pltpu.VMEM((features, RANK), jnp.float32)],
+        name="tail",
+    )(chip, columns)
 
 
 def per_device(
@@ -103,10 +152,15 @@
         normed_all, delta_hidden, (((0,), (0,)), ((), ())), preferred_element_type=jnp.float32
     ).astype(jnp.bfloat16)
 
-    chip_rows = features // CHIPS
     half = grad_part.shape[1]
-    pieces = lax.all_to_all(grad_part.reshape(CHIPS, chip_rows, half), ("x", "z"), 0, 0, tiled=True)
-    summed = jnp.sum(pieces.astype(jnp.float32), axis=0)
+    line_rows = features // X
+    rows = line_rows // (Z * C)
+    lines = lax.all_to_all(grad_part.reshape(X, line_rows, half), "x", 0, 0, tiled=True)
+    line_sum = jnp.sum(lines.astype(jnp.float32), axis=0).reshape(Z * C, rows, half)
+    pieces = lax.all_to_all(line_sum, ("z", "c"), 0, 0, tiled=True)
+    grad_rows = jnp.sum(pieces.reshape(Z, C, rows, half), axis=0)
+    grad_rows = grad_rows.transpose(1, 0, 2).reshape(rows, C * half)
+    memory_rows = grad_rows + error_memory[0]
 
     mixed_part = jnp.dot(hidden, down_half, preferred_element_type=jnp.float32)
     mixed_other = swap_cores(mixed_part[frames:])
@@ -114,13 +168,9 @@
         jnp.bfloat16
     )
 
-    rows = chip_rows // C
-    halves = lax.all_to_all(summed.reshape(C, rows, half), "c", 0, 0, tiled=True)
-    grad_rows = halves.transpose(1, 0, 2).reshape(rows, C * half)
-    memory_rows = grad_rows + error_memory[0]
-
     chunks = Y * C
     width = memory_rows.shape[1] // chunks
+    chip_rows = C * rows
     start_matrix = seed_matrix.astype(jnp.float32) / 128.0
     left_term = jnp.dot(memory_rows, start_matrix, precision=HIGHEST)
     rank = left_term.shape[1]
@@ -130,16 +180,17 @@
     )
     arrived = lax.all_to_all(message, ("y", "c"), 0, 0, tiled=True)
     mean_rows = jnp.sum(arrived.reshape(Y, chip_rows, width + rank), axis=0) / Y
-    columns = gather_by_exchange(mean_rows, ("x", "z")).reshape(features, width + rank)
-    mean_columns, left_factor = columns[:, :width], columns[:, width:]
-
-    gram_matrix = jnp.dot(left_factor.T, left_factor, precision=HIGHEST)
-    cholesky_factor = jnp.linalg.cholesky(gram_matrix)
-    basis = jax.scipy.linalg.solve_triangular(cholesky_factor, left_factor.T, lower=True).T
-    right_chunk = jnp.dot(mean_columns.T, basis, precision=HIGHEST)
-    chip = lax.axis_index(("x", "z"))
-    basis_rows = lax.dynamic_slice_in_dim(basis, chip * chip_rows, chip_rows, axis=0)
-    piece = jnp.dot(basis_rows, right_chunk.T, precision=HIGHEST)
+    packed = jnp.concatenate(
+        [
+            *terms(mean_rows[:, :width], 2),
+            *terms(mean_rows[:, width:], 3),
+            jnp.zeros((chip_rows, width - 3 * rank), jnp.bfloat16),
+        ],
+        axis=1,
+    )
+    columns = gather_by_exchange(packed, ("x", "z")).reshape(features, packed.shape[1])
+    chip = lax.axis_index(("x", "z")).astype(jnp.int32).reshape(1)
+    piece = tail(chip, columns, chip_rows, width)
 
     piece = jnp.broadcast_to(piece.reshape(1, C, rows, width), (Y, C, rows, width))
     compressed = lax.all_to_all(piece.reshape(chunks, rows, width), ("y", "c"), 0, 0, tiled=True)

time: 181 us -> 192 us (1.061)
  blocking collectives: 53.7 us -> 89.5 us
  starting transfers between devices: 47 us -> 25.7 us
  other arithmetic: 13.1 us -> 6.14 us
  Pallas kernels: 0 us -> 5.02 us
  waiting for transfers between devices: 49.4 us -> 45.1 us
  local copies, waits for them, and re-layouts: 6.48 us -> 8.74 us
    all_to_all x2 -> x4, blocking collectives: 37.3 us -> 73.4 us  [the longest x1 21.2 us: per_device(): pieces = lax.all_to_all(line_sum, ('z', 'c'), 0, 0, tiled=True)]
    all_to_all x1 -> x0, starting transfers between devices: 10.3 us -> none  [half_weights(): lax.all_to_all(up_split, 'c', 0, 0, tiled=True).reshape(C * rows, half)]
    another operation x5 -> x0, other arithmetic: 6.69 us -> none  [the longest x3 3.6 us: per_device(): cholesky_factor = jnp.linalg.cholesky(gram_matrix)]
    ppermute x1 -> x0, starting transfers between devices: 6.26 us -> none  [half_weights(): down_block = lax.ppermute(down_weight, SEQ, moves)]
    pallas_call x0 -> x1, Pallas kernels: none -> 5.02 us  [tail(): pl.pallas_call(tail_kernel, out_shape=jax.ShapeDtypeStruct((chip_rows, wi...]
    ppermute x1 -> x0, waiting for transfers between devices: 3.3 us -> none  [half_weights(): down_block = lax.ppermute(down_weight, SEQ, moves)]
    all_to_all x3, starting transfers between devices: 14.1 us -> 10.9 us  [gather_by_exchange(): return lax.all_to_all(copies, axis, 0, 0, tiled=True)]
    all_to_all x3, waiting for transfers between devices: 39.1 us -> 36.2 us  [gather_by_exchange(): return lax.all_to_all(copies, axis, 0, 0, tiled=True)]
  transfers between devices with their start and end apart: 11 -> 9, of which waited for: 5 -> 5; matrix products, arithmetic and copies ran while one was open for 13% -> 7% of each run, Pallas kernels for 0% -> 3%
where the time goes in v2:
time: 192 us; the launch traced here: 191 us
  blocking collectives  89.5 us (47%)
  waiting for transfers between devices  45.1 us (23%)
  starting transfers between devices  25.7 us (13%)
  matrix products  9.71 us (5%)
  local copies, waits for them, and re-layouts  8.74 us (5%)
  other arithmetic  6.14 us (3%)
  Pallas kernels  5.02 us (3%)
    all_to_all x3, waiting for transfers between devices, gather_by_exchange(): return lax.all_to_all(copies, axis, 0, 0, tiled=True)  36.2 us
    all_to_all x1, blocking collectives, per_device(): pieces = lax.all_to_all(line_sum, ('z', 'c'), 0, 0, tiled=True)  21.2 us
    all_to_all x1, blocking collectives, half_weights(): lax.all_to_all(up_split, ('z', 'c'), 0, 0, tiled=True)  19.2 us
    all_to_all x1, blocking collectives, per_device(): lax.all_to_all(grad_part.reshape(X, line_rows, half), 'x', 0, 0, tiled=True)  17.1 us
    all_to_all x1, blocking collectives, per_device(): arrived = lax.all_to_all(message, ('y', 'c'), 0, 0, tiled=True)  16.2 us
    all_to_all x1, blocking collectives, gather_by_exchange(): return lax.all_to_all(copies, axis, 0, 0, tiled=True)  15.8 us
    all_to_all x3, starting transfers between devices, gather_by_exchange(): return lax.all_to_all(copies, axis, 0, 0, tiled=True)  10.9 us
    ppermute x3, starting transfers between devices, swap_cores(): return lax.ppermute(block, 'c', [(0, 1), (1, 0)])  6.25 us
  transfers between devices with their start and end apart: 9, of which 5 were waited for; matrix products, arithmetic and copies ran while one was open for 7% of the time, Pallas kernels for 3%

profile of v2, /device:TPU:1, one launch (start us, length us, event | category | flops | bytes accessed | tf_op | source)
XLA Modules:
  0.0 191.0 jit_solution(15663720470422762587)
XLA Ops:
  0.6 0.8 broadcast_in_dim.25
  1.4 15.8 %all_to_all.45 = bf16[8,32,512]{2,1,0:T(8,128)(2,1)S(1)} all-to-all(bf16[8,32,512]{2,1,0:T(8,128)(2,1)S(1)} %broadcast_in_dim.25), channel_id=1, replica_groups=mesh['y'=8,'x'=4,'z'=8,'c'=2] {'x','c'}, dimensions={0} | all-to-all | bytes 524288 | tf_op jit(solution)/shard_map/all_to_all | solution.py:38
  17.2 0.0 copy-start.2
  17.2 0.0 copy-start.6
  17.2 0.8 broadcast_in_dim.22
  18.0 19.2 %all_to_all.46 = bf16[16,8,1024]{2,1,0:T(8,128)(2,1)S(1)} all-to-all(bf16[16,8,1024]{2,1,0:T(8,128)(2,1)S(1)} %bitcast.96), channel_id=1, replica_groups=mesh['y'=8,'x'=4,'z'=8,'c'=2] {'z','c'}, dimensions={0} | all-to-all | bytes 524288 | tf_op jit(solution)/shard_map/all_to_all | solution.py:46
  37.2 1.1 broadcast_in_dim.24
  38.3 3.5 %all-to-all-start.1 = ((bf16[4,128,1024]{2,1,0:T(8,128)(2,1)}), bf16[4,128,1024]{2,1,0:T(8,128)(2,1)S(1)}, u32[]{:S(2)}, u32[]{:S(2)}) async-start(bf16[4,128,1024]{2,1,0:T(8,128)(2,1)} %broadcast_in_dim.24), calls=%async_computation.1 | async-start | bytes 2097152 | tf_op jit(solution)/shard_map/all_to_all | solution.py:38
  41.8 0.0 copy-done.2
  41.9 1.9 %collective-permute-start = (bf16[15,512]{1,0:T(8,128)(2,1)S(1)}, bf16[15,512]{1,0:T(8,128)(2,1)S(1)}, u32[]{:S(2)}, u32[]{:S(2)}) collective-permute-start(bf16[15,512]{1,0:T(8,128)(2,1)S(1)} %get-tuple-element.5), channel_id=1, source_target_pairs={{0,1},{1,2},{2,3},{3,4},{4,5},{5,6},{6,7},{7,8},{8,9},{9,10},{10,1... | collective-permute-start | bytes 46088 | tf_op jit(solution)/shard_map/ppermute | solution.py:20
  43.8 2.4 %collective-permute-start.1 = (bf16[15,512]{1,0:T(8,128)(2,1)S(1)}, bf16[15,512]{1,0:T(8,128)(2,1)S(1)}, u32[]{:S(2)}, u32[]{:S(2)}) collective-permute-start(bf16[15,512]{1,0:T(8,128)(2,1)S(1)} %get-tuple-element.6), channel_id=1, source_target_pairs={{1,0},{2,1},{3,2},{4,3},{5,4},{6,5},{7,6},{8,7},{9,8},{10,9},{11,1... | collective-permute-start | bytes 46088 | tf_op jit(solution)/shard_map/ppermute | solution.py:21
  46.2 0.0 copy-done.6
  46.3 0.0 collective-permute-done
  46.3 2.8 %collective-permute-done.1 = bf16[15,512]{1,0:T(8,128)(2,1)S(1)} collective-permute-done((bf16[15,512]{1,0:T(8,128)(2,1)S(1)}, bf16[15,512]{1,0:T(8,128)(2,1)S(1)}, u32[]{:S(2)}, u32[]{:S(2)}) %collective-permute-start.1) | collective-permute-done | bytes 15392 | tf_op jit(solution)/shard_map/ppermute | solution.py:21
  49.2 0.1 maximum_convert_fusion
  49.3 8.3 %all-to-all-done.1 = bf16[4,128,1024]{2,1,0:T(8,128)(2,1)S(1)} async-done(((bf16[4,128,1024]{2,1,0:T(8,128)(2,1)}), bf16[4,128,1024]{2,1,0:T(8,128)(2,1)S(1)}, u32[]{:S(2)}, u32[]{:S(2)}) %all-to-all-start.1) | async-done | bytes 1048608 | tf_op jit(solution)/shard_map/all_to_all | solution.py:38
  57.6 1.1 broadcast_in_dim.26
  58.7 3.6 %all-to-all-start.3 = ((bf16[8,2,64,512]{3,2,1,0:T(8,128)(2,1)}), bf16[8,2,64,512]{3,2,1,0:T(8,128)(2,1)S(1)}, u32[]{:S(2)}, u32[]{:S(2)}) async-start(bf16[8,2,64,512]{3,2,1,0:T(8,128)(2,1)} %broadcast_in_dim.26), calls=%async_computation.3 | async-start | bytes 2097152 | tf_op jit(solution)/shard_map/all_to_all | solution.py:38
  62.3 0.0 copy-start.7
  62.3 0.0 copy-start.8
  62.3 0.0 copy-start.5
  62.3 2.8 %convert_reduce_fusion.1 = (f32[256]{0:T(256)S(1)}, bf16[256,512]{1,0:T(8,128)(2,1)S(1)}) fusion(f32[286,512]{1,0:T(8,128)S(1)} %maximum_convert_fusion, f32[512]{0:T(512)S(1)} %bitcast.134, f32[512]{0:T(512)S(1)} %bitcast.135, f32[512]{0:T(512)S(1)} %bitcast.106, f32[512]{0:T(512)S(1)} %bitcast.107, f32[512]{0:T(512)S(1)} %bitcast.108, ...), kind=kLoop, calls=%fused_computation.10 | loop fusion | flops 9174784 | bytes 16841728 | tf_op jit(solution)/shard_map/reduce_sum | solution.py:31
  65.1 0.2 fusion.5
  65.3 0.0 copy-done.7
  65.3 0.1 fusion.7
  65.5 2.3 %collective-permute-start.2 = (bf16[256,512]{1,0:T(8,128)(2,1)S(1)}, bf16[256,512]{1,0:T(8,128)(2,1)S(1)}, u32[]{:S(2)}, u32[]{:S(2)}) collective-permute-start(bf16[256,512]{1,0:T(8,128)(2,1)S(1)} %fusion.7), channel_id=1, source_target_pairs={{0,1},{1,0},{2,3},{3,2},{4,5},{5,4},{6,7},{7,6},{8,9},{9,8},{10,11... | collective-permute-start | bytes 786440 | tf_op jit(solution)/shard_map/ppermute | solution.py:26
  67.8 0.0 copy-done.8
  67.9 0.0 copy-done.5
  67.9 0.1 bitcast_multiply_fusion
  68.0 2.0 %collective-permute-start.4 = (bf16[256,512]{1,0:T(8,128)(2,1)S(1)}, bf16[256,512]{1,0:T(8,128)(2,1)S(1)}, u32[]{:S(2)}, u32[]{:S(2)}) collective-permute-start(bf16[256,512]{1,0:T(8,128)(2,1)S(1)} %bitcast_multiply_fusion), channel_id=1, source_target_pairs={{0,1},{1,0},{2,3},{3,2},{4,5},{5,4},{6,7},{7,6},{8,9},{9,8},{10,11... | collective-permute-start | bytes 786440 | tf_op jit(solution)/shard_map/ppermute | solution.py:26
  70.0 0.0 collective-permute-done.2
  70.0 2.0 %fusion.46 = f32[512,1024]{1,0:T(8,128)} fusion(bf16[512,1024]{1,0:T(8,128)(2,1)S(1)} %bitcast.87, bf16[256,512]{1,0:T(8,128)(2,1)S(1)} %collective-permute-done.2, bf16[256,512]{1,0:T(8,128)(2,1)S(1)} %fusion.7), kind=kOutput, calls=%fused_computation.85 | convolution fusion | flops 537919488 | bytes 3670016 | tf_op jit(solution)/shard_map/dot_general | solution.py:142
  72.0 19.4 %all-to-all-done.3 = bf16[8,2,64,512]{3,2,1,0:T(8,128)(2,1)S(1)} async-done(((bf16[8,2,64,512]{3,2,1,0:T(8,128)(2,1)}), bf16[8,2,64,512]{3,2,1,0:T(8,128)(2,1)S(1)}, u32[]{:S(2)}, u32[]{:S(2)}) %all-to-all-start.3) | async-done | bytes 1048608 | tf_op jit(solution)/shard_map/all_to_all | solution.py:38
  91.5 0.1 copy.13
  91.6 0.0 copy-start.3
  91.6 0.0 collective-permute-done.4
  91.6 3.5 %convolution_convert_fusion = bf16[512,1024]{1,0:T(8,128)(2,1)S(1)} fusion(f32[512,1024]{1,0:T(8,128)} %fusion.46, bf16[1024,512]{1,0:T(8,128)(2,1)S(1)} %bitcast.93, bf16[256,512]{1,0:T(8,128)(2,1)S(1)} %collective-permute-done.4, bf16[256,512]{1,0:T(8,128)(2,1)S(1)} %bitcast_multiply_fusion, bf16[256,512]{1,0:T(8,128)(2,1)S(1)} %collective-permute-done.2, ...), kind=kOutput, calls=%fused_computation.4 | convolution fusion | flops 1081606144 | bytes 5242880 | tf_op jit(solution)/shard_map/dot_general | solution.py:151
  95.1 0.0 copy-done.3
  95.1 17.1 %all_to_all.47 = bf16[4,128,1024]{2,1,0:T(8,128)(2,1)S(1)} all-to-all(bf16[4,128,1024]{2,1,0:T(8,128)(2,1)S(1)} %bitcast.95), channel_id=1, replica_groups=mesh['y'=8,'x'=4,'z'=8,'c'=2] {'x'}, dimensions={0} | all-to-all | bytes 2097152 | tf_op jit(solution)/shard_map/all_to_all | solution.py:158
  112.3 0.0 copy-start.4
  112.3 0.2 convert_reduce_fusion
  112.5 0.0 copy-start
  112.5 21.2 %all_to_all.48 = f32[16,8,1024]{2,1,0:T(8,128)S(1)} all-to-all(f32[16,8,1024]{2,1,0:T(8,128)S(1)} %bitcast.88), channel_id=1, replica_groups=mesh['y'=8,'x'=4,'z'=8,'c'=2] {'z','c'}, dimensions={0} | all-to-all | bytes 1048576 | tf_op jit(solution)/shard_map/all_to_all | solution.py:160
  133.7 0.0 copy-done.4
  133.8 1.2 fusion.48
  135.0 0.1 broadcast_in_dim.28
  135.1 16.2 %all_to_all.49 = f32[16,8,160]{2,1,0:T(8,128)S(1)} all-to-all(f32[16,8,160]{2,1,0:T(8,128)S(1)} %pad_maximum_fusion.3), channel_id=1, replica_groups=mesh['y'=8,'x'=4,'z'=8,'c'=2] {'y','c'}, dimensions={0} | all-to-all | bytes 163840 | tf_op jit(solution)/shard_map/all_to_all | solution.py:181
  151.3 0.1 concatenate.19
  151.4 0.8 broadcast_in_dim.30
  152.2 3.9 %all-to-all-start.7 = ((bf16[32,16,384]{2,1,0:T(8,128)(2,1)}), bf16[32,16,384]{2,1,0:T(8,128)(2,1)S(1)}, u32[]{:S(2)}, u32[]{:S(2)}) async-start(bf16[32,16,384]{2,1,0:T(8,128)(2,1)} %broadcast_in_dim.30), calls=%async_computation.7 | async-start | bytes 786432 | tf_op jit(solution)/shard_map/all_to_all | solution.py:38
  156.1 0.0 copy-done
  156.1 2.9 %fusion.2 = f32[512,512]{1,0:T(8,128)} fusion(bf16[1024,512]{1,0:T(8,128)(2,1)} %bitcast.94, f32[512,1024]{1,0:T(8,128)S(1)} %copy-done), kind=kOutput, calls=%fused_computation.7 | convolution fusion | flops 539492352 | bytes 4194304 | tf_op jit(solution)/shard_map/dot_general | solution.py:165
  159.0 1.1 slice.312
  160.1 1.9 %collective-permute-start.3 = (f32[256,512]{1,0:T(8,128)S(1)}, f32[256,512]{1,0:T(8,128)S(1)}, u32[]{:S(2)}, u32[]{:S(2)}) collective-permute-start(f32[256,512]{1,0:T(8,128)S(1)} %slice.312), channel_id=1, source_target_pairs={{0,1},{1,0},{2,3},{3,2},{4,5},{5,4},{6,7},{7,6},{8,9},{9,8},{10,11... | collective-permute-start | bytes 1572872 | tf_op jit(solution)/shard_map/ppermute | solution.py:26
  162.0 8.5 %all-to-all-done.7 = bf16[32,16,384]{2,1,0:T(8,128)(2,1)S(1)} async-done(((bf16[32,16,384]{2,1,0:T(8,128)(2,1)}), bf16[32,16,384]{2,1,0:T(8,128)(2,1)S(1)}, u32[]{:S(2)}, u32[]{:S(2)}) %all-to-all-start.7) | async-done | bytes 393248 | tf_op jit(solution)/shard_map/all_to_all | solution.py:38
  170.5 0.8 copy-done.1
  171.3 5.0 %tail.1 = f32[16,128]{1,0:T(8,128)} custom-call(s32[1]{0:T(128)} %bitcast.50.chip_ref, bf16[512,384]{1,0:T(8,128)(2,1)} %bitcast.90), custom_call_target="tpu_custom_call" | custom-call | tf_op jit(solution)/shard_map/tail/pallas_call | solution.py:100
  176.3 1.3 broadcast_in_dim.64
  177.6 4.2 %all-to-all-start.8 = ((f32[16,8,128]{2,1,0:T(8,128)}), f32[16,8,128]{2,1,0:T(8,128)S(1)}, u32[]{:S(2)}, u32[]{:S(2)}) async-start(f32[16,8,128]{2,1,0:T(8,128)} %bitcast.59), calls=%async_computation.8 | async-start | bytes 131072 | tf_op jit(solution)/shard_map/all_to_all | solution.py:196
  181.9 0.0 collective-permute-done.3
  181.9 1.9 fusion.47
  183.7 5.9 %all-to-all-done.8 = f32[16,8,128]{2,1,0:T(8,128)S(1)} async-done(((f32[16,8,128]{2,1,0:T(8,128)}), f32[16,8,128]{2,1,0:T(8,128)S(1)}, u32[]{:S(2)}, u32[]{:S(2)}) %all-to-all-start.8) | async-done | bytes 65568 | tf_op jit(solution)/shard_map/all_to_all | solution.py:196
  189.7 0.6 bitcast_subtract_fusion
  190.3 0.6 copy.15
  (16 shorter events, 0.2 us)
Async XLA Ops:
  17.2 24.7 %copy-start.2 = (bf16[1,256,512]{2,1,0:T(8,128)(2,1)S(1)}, bf16[1,256,512]{2,1,0:T(8,128)(2,1)}, u32[]{:S(2)}) copy-start(bf16[1,256,512]{2,1,0:T(8,128)(2,1)} %param.9) | copy-start | bytes 786436
  17.2 29.0 %copy-start.6 = (f32[31,512]{1,0:T(8,128)S(1)}, f32[31,512]{1,0:T(8,128)}, u32[]{:S(2)}) copy-start(f32[31,512]{1,0:T(8,128)} %param.13) | copy-start | bytes 190468
  38.3 19.3 %all-to-all-start.1 = ((bf16[4,128,1024]{2,1,0:T(8,128)(2,1)}), bf16[4,128,1024]{2,1,0:T(8,128)(2,1)S(1)}, u32[]{:S(2)}, u32[]{:S(2)}) async-start(bf16[4,128,1024]{2,1,0:T(8,128)(2,1)} %broadcast_in_dim.24), calls=%async_computation.1 | async-start | bytes 2097152 | tf_op jit(solution)/shard_map/all_to_all | solution.py:38
  41.9 4.4 %collective-permute-start = (bf16[15,512]{1,0:T(8,128)(2,1)S(1)}, bf16[15,512]{1,0:T(8,128)(2,1)S(1)}, u32[]{:S(2)}, u32[]{:S(2)}) collective-permute-start(bf16[15,512]{1,0:T(8,128)(2,1)S(1)} %get-tuple-element.5), channel_id=1, source_target_pairs={{0,1},{1,2},{2,3},{3,4},{4,5},{5,6},{6,7},{7,8},{8,9},{9,10},{10,1... | collective-permute-start | bytes 46088 | tf_op jit(solution)/shard_map/ppermute | solution.py:20
  43.8 5.4 %collective-permute-start.1 = (bf16[15,512]{1,0:T(8,128)(2,1)S(1)}, bf16[15,512]{1,0:T(8,128)(2,1)S(1)}, u32[]{:S(2)}, u32[]{:S(2)}) collective-permute-start(bf16[15,512]{1,0:T(8,128)(2,1)S(1)} %get-tuple-element.6), channel_id=1, source_target_pairs={{1,0},{2,1},{3,2},{4,3},{5,4},{6,5},{7,6},{8,7},{9,8},{10,9},{11,1... | collective-permute-start | bytes 46088 | tf_op jit(solution)/shard_map/ppermute | solution.py:21
  58.7 32.8 %all-to-all-start.3 = ((bf16[8,2,64,512]{3,2,1,0:T(8,128)(2,1)}), bf16[8,2,64,512]{3,2,1,0:T(8,128)(2,1)S(1)}, u32[]{:S(2)}, u32[]{:S(2)}) async-start(bf16[8,2,64,512]{3,2,1,0:T(8,128)(2,1)} %broadcast_in_dim.26), calls=%async_computation.3 | async-start | bytes 2097152 | tf_op jit(solution)/shard_map/all_to_all | solution.py:38
  62.3 3.1 %copy-start.7 = (f32[512]{0:T(512)S(1)}, f32[512]{0:T(512)}, u32[]{:S(2)}) copy-start(f32[512]{0:T(512)} %param.14) | copy-start | bytes 6148
  62.3 5.6 %copy-start.8 = (s32[1,256]{1,0:T(1,128)S(1)}, s32[1,256]{1,0:T(1,128)}, u32[]{:S(2)}) copy-start(s32[1,256]{1,0:T(1,128)} %param.15) | copy-start | bytes 3076
  62.3 5.6 %copy-start.5 = (bf16[1,256,512]{2,1,0:T(8,128)(2,1)S(1)}, bf16[1,256,512]{2,1,0:T(8,128)(2,1)}, u32[]{:S(2)}) copy-start(bf16[1,256,512]{2,1,0:T(8,128)(2,1)} %param.10) | copy-start | bytes 786436
  65.5 4.5 %collective-permute-start.2 = (bf16[256,512]{1,0:T(8,128)(2,1)S(1)}, bf16[256,512]{1,0:T(8,128)(2,1)S(1)}, u32[]{:S(2)}, u32[]{:S(2)}) collective-permute-start(bf16[256,512]{1,0:T(8,128)(2,1)S(1)} %fusion.7), channel_id=1, source_target_pairs={{0,1},{1,0},{2,3},{3,2},{4,5},{5,4},{6,7},{7,6},{8,9},{9,8},{10,11... | collective-permute-start | bytes 786440 | tf_op jit(solution)/shard_map/ppermute | solution.py:26
  68.0 23.6 %collective-permute-start.4 = (bf16[256,512]{1,0:T(8,128)(2,1)S(1)}, bf16[256,512]{1,0:T(8,128)(2,1)S(1)}, u32[]{:S(2)}, u32[]{:S(2)}) collective-permute-start(bf16[256,512]{1,0:T(8,128)(2,1)S(1)} %bitcast_multiply_fusion), channel_id=1, source_target_pairs={{0,1},{1,0},{2,3},{3,2},{4,5},{5,4},{6,7},{7,6},{8,9},{9,8},{10,11... | collective-permute-start | bytes 786440 | tf_op jit(solution)/shard_map/ppermute | solution.py:26
  91.6 3.5 %copy-start.3 = (bf16[8,2,64,512]{3,2,0,1:T(8,128)(2,1)}, bf16[8,2,64,512]{3,2,0,1:T(8,128)(2,1)S(1)}, u32[]{:S(2)}) copy-start(bf16[8,2,64,512]{3,2,0,1:T(8,128)(2,1)S(1)} %copy.13) | copy-start | bytes 3145732
  112.3 21.5 %copy-start.4 = (f32[1,8,2048]{2,1,0:T(8,128)S(1)}, f32[1,8,2048]{2,1,0:T(8,128)}, u32[]{:S(2)}) copy-start(f32[1,8,2048]{2,1,0:T(8,128)} %param.16) | copy-start | bytes 196612
  112.5 43.7 %copy-start = (f32[512,1024]{1,0:T(8,128)S(1)}, f32[512,1024]{1,0:T(8,128)}, u32[]{:S(2)}) copy-start(f32[512,1024]{1,0:T(8,128)} %fusion.46) | copy-start | bytes 6291460
  152.2 18.3 %all-to-all-start.7 = ((bf16[32,16,384]{2,1,0:T(8,128)(2,1)}), bf16[32,16,384]{2,1,0:T(8,128)(2,1)S(1)}, u32[]{:S(2)}, u32[]{:S(2)}) async-start(bf16[32,16,384]{2,1,0:T(8,128)(2,1)} %broadcast_in_dim.30), calls=%async_computation.7 | async-start | bytes 786432 | tf_op jit(solution)/shard_map/all_to_all | solution.py:38
  160.1 21.7 %collective-permute-start.3 = (f32[256,512]{1,0:T(8,128)S(1)}, f32[256,512]{1,0:T(8,128)S(1)}, u32[]{:S(2)}, u32[]{:S(2)}) collective-permute-start(f32[256,512]{1,0:T(8,128)S(1)} %slice.312), channel_id=1, source_target_pairs={{0,1},{1,0},{2,3},{3,2},{4,5},{5,4},{6,7},{7,6},{8,9},{9,8},{10,11... | collective-permute-start | bytes 1572872 | tf_op jit(solution)/shard_map/ppermute | solution.py:26
  170.5 0.8 copy-start.1
  177.6 12.1 %all-to-all-start.8 = ((f32[16,8,128]{2,1,0:T(8,128)}), f32[16,8,128]{2,1,0:T(8,128)S(1)}, u32[]{:S(2)}, u32[]{:S(2)}) async-start(f32[16,8,128]{2,1,0:T(8,128)} %bitcast.59), calls=%async_computation.8 | async-start | bytes 131072 | tf_op jit(solution)/shard_map/all_to_all | solution.py:196

commit v3 on v2

--- a/solution.py
+++ b/solution.py
@@ -6,15 +6,18 @@
 from jax.sharding import Mesh
 from jax.sharding import PartitionSpec as P
 
-Y, X, Z, C = 8, 4, 8, 2
-CHIPS = X * Z
+Y, XH, XL, Z, C = 8, 2, 2, 8, 2
 RANK = 32
-SEQ = ("x", "z", "c")
+CHIP = ("xh", "xl", "z")
+SEQ = ("xh", "xl", "z", "c")
+GROUP = ("xl", "c")
+GROUPS = ("xh", "z")
+QUARTERS = XL * C
 HIGHEST = lax.Precision.HIGHEST
 
 
 def halo(block, width):
-    count = CHIPS * C
+    count = XH * XL * Z * C
     forward = [(i, i + 1) for i in range(count - 1)]
     backward = [(target, source) for source, target in forward]
     low = lax.ppermute(block[block.shape[0] - width :], SEQ, forward)
@@ -22,8 +25,13 @@
     return low, high
 
 
-def swap_cores(block):
-    return lax.ppermute(block, "c", [(0, 1), (1, 0)])
+def swap(block, axis):
+    return lax.ppermute(block, axis, [(0, 1), (1, 0)])
+
+
+def group_frames(block):
+    pair = jnp.stack([block, swap(block, "xl")])
+    return jnp.concatenate([pair, swap(pair, "c")]).reshape(-1, block.shape[1])
 
 
 def layer_norm(stream, norm_gain):
@@ -38,19 +46,26 @@
     return lax.all_to_all(copies, axis, 0, 0, tiled=True)
 
 
-def half_weights(up_weight, down_weight):
+def quarter_weights(up_weight, down_weight):
     rows, hidden = up_weight.shape
-    half = hidden // C
-    up_split = up_weight.reshape(rows, C, half).transpose(1, 0, 2)
-    up_split = jnp.broadcast_to(up_split[None], (Z, C, rows, half)).reshape(Z * C, rows, half)
-    up_line = lax.all_to_all(up_split, ("z", "c"), 0, 0, tiled=True).reshape(Z * C * rows, half)
-    up_half = gather_by_exchange(up_line, "x").reshape(X * Z * C * rows, half)
-
+    quarter = hidden // QUARTERS
     down_rows, features = down_weight.shape
-    down_line = gather_by_exchange(down_weight, ("x", "c")).reshape(X, C * down_rows, features)
-    pair = lax.dynamic_slice_in_dim(down_line, lax.axis_index("c") * (X // C), X // C, axis=0)
-    down_half = gather_by_exchange(pair, "z").transpose(1, 0, 2, 3).reshape(half, features)
-    return up_half, down_half
+    moves = []
+    for q in range(QUARTERS):
+        for z in range(Z):
+            for c in range(C):
+                source = (q * Z + z) * C + c
+                target = ((c * XL + q // C) * Z + z) * C + q % C
+                moves.append((source, target))
+    down_block = lax.ppermute(down_weight, SEQ, moves)
+    up_split = up_weight.reshape(rows, QUARTERS, quarter).transpose(1, 0, 2)
+    up_block = lax.all_to_all(up_split, GROUP, 0, 0, tiled=True).reshape(QUARTERS * rows, quarter)
+    whole = gather_by_exchange(jnp.concatenate([up_block, down_block], axis=0), GROUPS)
+    whole = whole.reshape(XH, Z, QUARTERS * rows + down_rows, features)
+    up = whole[:, :, : QUARTERS * rows].reshape(XH, Z, XL, C * rows, quarter)
+    up = up.transpose(0, 2, 1, 3, 4).reshape(-1, quarter)
+    down = whole[:, :, QUARTERS * rows :].transpose(1, 0, 2, 3).reshape(quarter, features)
+    return up, down
 
 
 def top_bits(values):
@@ -125,8 +140,8 @@
     frames, features = tokens.shape[1:]
     low, high = halo(tokens[0], half_width)
     masked = cotangent[0] * frame_mask[0][:, None].astype(jnp.bfloat16)
-    masked_other = swap_cores(masked)
-    up_half, down_half = half_weights(up_weight, down_weight)
+    masked_all = group_frames(masked)
+    up, down = quarter_weights(up_weight, down_weight)
 
     widened = jnp.concatenate([low, tokens[0], high], axis=0).astype(jnp.float32)
     filtered = kernel[0] * widened[0:frames]
@@ -136,14 +151,12 @@
         jnp.bfloat16
     )
     normed = layer_norm(stream, norm_gain)
-    normed_other = swap_cores(normed)
-    normed_all = jnp.concatenate([normed, normed_other], axis=0)
-    masked_all = jnp.concatenate([masked, masked_other], axis=0)
-    projected = jnp.dot(normed_all, up_half, preferred_element_type=jnp.float32)
+    normed_all = group_frames(normed)
+    projected = jnp.dot(normed_all, up, preferred_element_type=jnp.float32)
     squashed = jax.nn.sigmoid(projected)
     hidden = (projected * squashed).astype(jnp.bfloat16)
     upstream = lax.dot_general(
-        masked_all, down_half, (((1,), (1,)), ((), ())), preferred_element_type=jnp.float32
+        masked_all, down, (((1,), (1,)), ((), ())), preferred_element_type=jnp.float32
     )
     delta_hidden = (0.5 * upstream * squashed * (1.0 + projected * (1.0 - squashed))).astype(
         jnp.bfloat16
@@ -152,21 +165,20 @@
         normed_all, delta_hidden, (((0,), (0,)), ((), ())), preferred_element_type=jnp.float32
     ).astype(jnp.bfloat16)
 
-    half = grad_part.shape[1]
-    line_rows = features // X
-    rows = line_rows // (Z * C)
-    lines = lax.all_to_all(grad_part.reshape(X, line_rows, half), "x", 0, 0, tiled=True)
-    line_sum = jnp.sum(lines.astype(jnp.float32), axis=0).reshape(Z * C, rows, half)
-    pieces = lax.all_to_all(line_sum, ("z", "c"), 0, 0, tiled=True)
-    grad_rows = jnp.sum(pieces.reshape(Z, C, rows, half), axis=0)
-    grad_rows = grad_rows.transpose(1, 0, 2).reshape(rows, C * half)
+    quarter = grad_part.shape[1]
+    devices = XH * XL * Z * C
+    rows = features // devices
+    pieces = lax.all_to_all(grad_part.reshape(devices, rows, quarter), SEQ, 0, 0, tiled=True)
+    pieces = pieces.reshape(XH, XL, Z, C, rows, quarter).astype(jnp.float32)
+    grad_rows = jnp.sum(pieces, axis=(0, 2)).reshape(QUARTERS, rows, quarter)
+    grad_rows = grad_rows.transpose(1, 0, 2).reshape(rows, QUARTERS * quarter)
     memory_rows = grad_rows + error_memory[0]
 
-    mixed_part = jnp.dot(hidden, down_half, preferred_element_type=jnp.float32)
-    mixed_other = swap_cores(mixed_part[frames:])
-    mixed = (stream.astype(jnp.float32) + 0.5 * (mixed_part[:frames] + mixed_other)).astype(
-        jnp.bfloat16
-    )
+    mixed_part = jnp.dot(hidden, down, preferred_element_type=jnp.float32)
+    mixed_part = mixed_part.reshape(C, XL, frames, features)
+    chip_part = mixed_part[0] + swap(mixed_part[1], "c")
+    other_chip = swap(chip_part[1].astype(jnp.bfloat16), "xl").astype(jnp.float32)
+    mixed = (stream.astype(jnp.float32) + 0.5 * (chip_part[0] + other_chip)).astype(jnp.bfloat16)
 
     chunks = Y * C
     width = memory_rows.shape[1] // chunks
@@ -188,8 +200,8 @@
         ],
         axis=1,
     )
-    columns = gather_by_exchange(packed, ("x", "z")).reshape(features, packed.shape[1])
-    chip = lax.axis_index(("x", "z")).astype(jnp.int32).reshape(1)
+    columns = gather_by_exchange(packed, CHIP).reshape(features, packed.shape[1])
+    chip = lax.axis_index(CHIP).astype(jnp.int32).reshape(1)
     piece = tail(chip, columns, chip_rows, width)
 
     piece = jnp.broadcast_to(piece.reshape(1, C, rows, width), (Y, C, rows, width))
@@ -200,7 +212,7 @@
 
 
 def solution(mesh):
-    fine = Mesh(mesh.devices.reshape(Y, X, Z, C), ("y", "x", "z", "c"))
+    fine = Mesh(mesh.devices.reshape(Y, XH, XL, Z, C), ("y", *SEQ))
     in_specs = (
         P("y", SEQ, None),
         P("y", SEQ, None),

time: 192 us -> 159 us (0.83)
  blocking collectives: 89.5 us -> 0 us
  starting transfers between devices: 25.7 us -> 69.2 us
  waiting for transfers between devices: 45.1 us -> 52.3 us
  other arithmetic: 6.14 us -> 12.1 us
    all_to_all x5 -> x0, blocking collectives: 89.5 us -> none  [the longest x1 21.2 us: per_device(): pieces = lax.all_to_all(line_sum, ('z', 'c'), 0, 0, tiled=True)]
    all_to_all x0 -> x3, starting transfers between devices: none -> 25.8 us  [the longest x1 10.3 us: quarter_weights(): lax.all_to_all(up_split, GROUP, 0, 0, tiled=True)]
    all_to_all x0 -> x3, waiting for transfers between devices: none -> 19.6 us  [the longest x1 14.1 us: per_device(): lax.all_to_all(grad_part.reshape(devices, rows, quarter), SEQ, 0, 0, tile...]
    all_to_all x3 -> x2, waiting for transfers between devices: 36.2 us -> 17.6 us  [gather_by_exchange(): return lax.all_to_all(copies, axis, 0, 0, tiled=True)]
    ppermute x3 -> x7, starting transfers between devices: 6.25 us -> 23.1 us  [the longest x6 15.2 us: swap(): return lax.ppermute(block, axis, [(0, 1), (1, 0)])]
    ppermute x3 -> x7, waiting for transfers between devices: 0.01 us -> 8.05 us  [the longest x6 8.05 us: swap(): return lax.ppermute(block, axis, [(0, 1), (1, 0)])]
    ppermute x1, waiting for transfers between devices: 2.85 us -> 0.01 us  [halo(): high = lax.ppermute(block[:width], SEQ, backward)]
    mul x1 -> x2, other arithmetic: 0.1 us -> 2.1 us  [per_device(): masked = cotangent[0] * frame_mask[0][:, None].astype(jnp.bfloat16)]
  transfers between devices with their start and end apart: 9 -> 15, of which waited for: 5 -> 7; matrix products, arithmetic and copies ran while one was open for 7% -> 14% of each run, Pallas kernels for 3% -> 3%
where the time goes in v3:
time: 159 us; the launch traced here: 158 us
  starting transfers between devices  69.2 us (44%)
  waiting for transfers between devices  52.3 us (33%)
  other arithmetic  12.1 us (8%)
  local copies, waits for them, and re-layouts  10.4 us (7%)
  matrix products  8.01 us (5%)
  Pallas kernels  5.02 us (3%)
    all_to_all x2, waiting for transfers between devices, gather_by_exchange(): return lax.all_to_all(copies, axis, 0, 0, tiled=True)  17.6 us
    ppermute x6, starting transfers between devices, swap(): return lax.ppermute(block, axis, [(0, 1), (1, 0)])  15.2 us
    all_to_all x1, waiting for transfers between devices, per_device(): lax.all_to_all(grad_part.reshape(devices, rows, quarter), SEQ, 0, 0, tile...  14.1 us
    all_to_all x2, starting transfers between devices, gather_by_exchange(): return lax.all_to_all(copies, axis, 0, 0, tiled=True)  10.7 us
    all_to_all x1, starting transfers between devices, quarter_weights(): lax.all_to_all(up_split, GROUP, 0, 0, tiled=True)  10.3 us
    all_to_all x1, starting transfers between devices, per_device(): lax.all_to_all(grad_part.reshape(devices, rows, quarter), SEQ, 0, 0, tile...  8.15 us
    ppermute x6, waiting for transfers between devices, swap(): return lax.ppermute(block, axis, [(0, 1), (1, 0)])  8.05 us
    ppermute x1, starting transfers between devices, quarter_weights(): down_block = lax.ppermute(down_weight, SEQ, moves)  7.97 us
  transfers between devices with their start and end apart: 15, of which 7 were waited for; matrix products, arithmetic and copies ran while one was open for 14% of the time, Pallas kernels for 3%

profile of v3, /device:TPU:1, one launch (start us, length us, event | category | flops | bytes accessed | tf_op | source)
XLA Modules:
  0.0 158.1 jit_solution(4648615873995490241)
XLA Ops:
  0.6 0.0 copy-start.1
  0.6 10.3 %all-to-all-start = ((bf16[4,8,512]{2,1,0:T(8,128)(2,1)}), bf16[4,8,512]{2,1,0:T(8,128)(2,1)S(1)}, u32[]{:S(2)}, u32[]{:S(2)}) async-start(bf16[4,8,512]{2,1,0:T(8,128)(2,1)} %bitcast.139), calls=%async_computation | async-start | bytes 65536 | tf_op jit(solution)/shard_map/all_to_all | solution.py:62
  10.9 0.7 slice_bitcast_fusion.3
  11.6 1.9 %collective-permute-start = (bf16[15,512]{1,0:T(8,128)(2,1)S(1)}, bf16[15,512]{1,0:T(8,128)(2,1)S(1)}, u32[]{:S(2)}, u32[]{:S(2)}) collective-permute-start(bf16[15,512]{1,0:T(8,128)(2,1)S(1)} %get-tuple-element.9), channel_id=1, source_target_pairs={{0,1},{1,2},{2,3},{3,4},{4,5},{5,6},{6,7},{7,8},{8,9},{9,10},{10,1... | collective-permute-start | bytes 46088 | tf_op jit(solution)/shard_map/ppermute | solution.py:23
  13.6 2.4 %collective-permute-start.1 = (bf16[15,512]{1,0:T(8,128)(2,1)S(1)}, bf16[15,512]{1,0:T(8,128)(2,1)S(1)}, u32[]{:S(2)}, u32[]{:S(2)}) collective-permute-start(bf16[15,512]{1,0:T(8,128)(2,1)S(1)} %get-tuple-element.10), channel_id=1, source_target_pairs={{1,0},{2,1},{3,2},{4,3},{5,4},{6,5},{7,6},{8,7},{9,8},{10,9},{11,1... | collective-permute-start | bytes 46088 | tf_op jit(solution)/shard_map/ppermute | solution.py:24
  16.0 8.0 %collective-permute-start.4 = (bf16[32,512]{1,0:T(8,128)(2,1)}, bf16[32,512]{1,0:T(8,128)(2,1)S(1)}, u32[]{:S(2)}, u32[]{:S(2)}) collective-permute-start(bf16[32,512]{1,0:T(8,128)(2,1)} %param.12), channel_id=1, source_target_pairs={{0,0},{1,32},{2,2},{3,34},{4,4},{5,36},{6,6},{7,38},{8,8},{9,40},{... | collective-permute-start | bytes 98312 | tf_op jit(solution)/shard_map/ppermute | solution.py:60
  23.9 0.7 convert_reduce_fusion.2
  24.6 1.0 bitcast_multiply_fusion
  25.7 1.9 %collective-permute-start.7 = (bf16[256,512]{1,0:T(8,128)(2,1)S(1)}, bf16[256,512]{1,0:T(8,128)(2,1)S(1)}, u32[]{:S(2)}, u32[]{:S(2)}) collective-permute-start(bf16[256,512]{1,0:T(8,128)(2,1)S(1)} %bitcast_multiply_fusion), channel_id=1, source_target_pairs={{0,16},{16,0},{1,17},{17,1},{2,18},{18,2},{3,19},{19,3},{4,20},{20... | collective-permute-start | bytes 786440 | tf_op jit(solution)/shard_map/ppermute | solution.py:29
  27.6 1.1 broadcast_multiply_fusion
  28.7 1.2 fusion.57
  29.9 1.0 fusion.58
  30.9 0.0 collective-permute-done
  30.9 0.0 collective-permute-done.1
  30.9 1.0 maximum_convert_fusion
  31.9 2.8 %convert_reduce_fusion.1 = (f32[256]{0:T(256)S(1)}, bf16[256,512]{1,0:T(8,128)(2,1)S(1)}) fusion(f32[286,512]{1,0:T(8,128)S(1)} %maximum_convert_fusion, f32[512]{0:T(512)S(1)} %bitcast.169, f32[512]{0:T(512)S(1)} %bitcast.170, f32[512]{0:T(512)S(1)} %bitcast.141, f32[512]{0:T(512)S(1)} %bitcast.142, f32[512]{0:T(512)S(1)} %bitcast.143, ...), kind=kLoop, calls=%fused_computation.11 | loop fusion | flops 9174784 | bytes 16841728 | tf_op jit(solution)/shard_map/reduce_sum | solution.py:39
  34.7 0.0 copy-start.4
  34.8 1.1 broadcast_in_dim.14
  35.9 5.2 %all-to-all-start.1 = ((bf16[16,64,512]{2,1,0:T(8,128)(2,1)}), bf16[16,64,512]{2,1,0:T(8,128)(2,1)S(1)}, u32[]{:S(2)}, u32[]{:S(2)}) async-start(bf16[16,64,512]{2,1,0:T(8,128)(2,1)} %broadcast_in_dim.14), calls=%async_computation.1 | async-start | bytes 2097152 | tf_op jit(solution)/shard_map/all_to_all | solution.py:46
  41.1 0.2 fusion.4
  41.3 0.1 fusion.6
  41.5 2.8 %collective-permute-start.2 = (bf16[256,512]{1,0:T(8,128)(2,1)S(1)}, bf16[256,512]{1,0:T(8,128)(2,1)S(1)}, u32[]{:S(2)}, u32[]{:S(2)}) collective-permute-start(bf16[256,512]{1,0:T(8,128)(2,1)S(1)} %fusion.6), channel_id=1, source_target_pairs={{0,16},{16,0},{1,17},{17,1},{2,18},{18,2},{3,19},{19,3},{4,20},{20... | collective-permute-start | bytes 786440 | tf_op jit(solution)/shard_map/ppermute | solution.py:29
  44.2 0.0 collective-permute-done.7
  44.3 0.1 pad_maximum_fusion.3
  44.3 2.2 %collective-permute-start.8 = (bf16[2,256,512]{2,1,0:T(8,128)(2,1)S(1)}, bf16[2,256,512]{2,1,0:T(8,128)(2,1)S(1)}, u32[]{:S(2)}, u32[]{:S(2)}) collective-permute-start(bf16[2,256,512]{2,1,0:T(8,128)(2,1)S(1)} %pad_maximum_fusion.3), channel_id=1, source_target_pairs={{0,1},{1,0},{2,3},{3,2},{4,5},{5,4},{6,7},{7,6},{8,9},{9,8},{10,11... | collective-permute-start | bytes 1572872 | tf_op jit(solution)/shard_map/ppermute | solution.py:29
  46.5 0.1 fusion.66
  46.7 7.6 %collective-permute-done.2 = bf16[256,512]{1,0:T(8,128)(2,1)S(1)} collective-permute-done((bf16[256,512]{1,0:T(8,128)(2,1)S(1)}, bf16[256,512]{1,0:T(8,128)(2,1)S(1)}, u32[]{:S(2)}, u32[]{:S(2)}) %collective-permute-start.2) | collective-permute-done | bytes 262176 | tf_op jit(solution)/shard_map/ppermute | solution.py:29
  54.3 0.1 pad_maximum_fusion.2
  54.3 3.1 %collective-permute-start.3 = (bf16[2,256,512]{2,1,0:T(8,128)(2,1)S(1)}, bf16[2,256,512]{2,1,0:T(8,128)(2,1)S(1)}, u32[]{:S(2)}, u32[]{:S(2)}) collective-permute-start(bf16[2,256,512]{2,1,0:T(8,128)(2,1)S(1)} %pad_maximum_fusion.2), channel_id=1, source_target_pairs={{0,1},{1,0},{2,3},{3,2},{4,5},{5,4},{6,7},{7,6},{8,9},{9,8},{10,11... | collective-permute-start | bytes 1572872 | tf_op jit(solution)/shard_map/ppermute | solution.py:29
  57.5 1.1 pad_maximum_fusion.1
  58.6 0.4 collective-permute-done.3
  59.0 0.1 pad_maximum_fusion
  59.1 9.0 %all-to-all-done.1 = bf16[16,64,512]{2,1,0:T(8,128)(2,1)S(1)} async-done(((bf16[16,64,512]{2,1,0:T(8,128)(2,1)}), bf16[16,64,512]{2,1,0:T(8,128)(2,1)S(1)}, u32[]{:S(2)}, u32[]{:S(2)}) %all-to-all-start.1) | async-done | bytes 1048608 | tf_op jit(solution)/shard_map/all_to_all | solution.py:46
  68.1 0.1 fusion.56
  68.3 0.8 copy.13
  69.1 0.7 fusion.59
  69.8 3.9 %fusion = bf16[64,8,512]{2,1,0:T(8,128)(2,1)} fusion(bf16[1024,512]{1,0:T(8,128)(2,1)S(1)} %bitcast.116, f32[1024,512]{1,0:T(8,128)S(1)} %fusion.59, bf16[1024,512]{1,0:T(8,128)(2,1)} %bitcast.127, bf16[512,512]{1,0:T(8,128)(2,1)} %bitcast.134), kind=kOutput, calls=%fused_computation.4 | convolution fusion | flops 1079246848 | bytes 5242880 | tf_op jit(solution)/shard_map/dot_general | solution.py:164
  73.7 8.1 %all-to-all-start.2 = ((bf16[64,8,512]{2,1,0:T(8,128)(2,1)}), bf16[64,8,512]{2,1,0:T(8,128)(2,1)S(1)}, u32[]{:S(2)}, u32[]{:S(2)}) async-start(bf16[64,8,512]{2,1,0:T(8,128)(2,1)} %fusion), calls=%async_computation.2 | async-start | bytes 1048576 | tf_op jit(solution)/shard_map/all_to_all | solution.py:171
  81.9 0.0 copy-start.2
  81.9 0.0 copy-start.3
  81.9 3.2 %fusion.1 = f32[1024,512]{1,0:T(8,128)} fusion(bf16[512,512]{1,0:T(8,128)(2,1)} %bitcast.135, f32[1024,512]{1,0:T(8,128)S(1)} %fusion.59), kind=kOutput, calls=%fused_computation.8 | convolution fusion | flops 539492352 | bytes 4718592 | tf_op jit(solution)/shard_map/dot_general | solution.py:177
  85.0 14.1 %all-to-all-done.2 = bf16[64,8,512]{2,1,0:T(8,128)(2,1)S(1)} async-done(((bf16[64,8,512]{2,1,0:T(8,128)(2,1)}), bf16[64,8,512]{2,1,0:T(8,128)(2,1)S(1)}, u32[]{:S(2)}, u32[]{:S(2)}) %all-to-all-start.2) | async-done | bytes 524320 | tf_op jit(solution)/shard_map/all_to_all | solution.py:171
  99.2 0.1 convert_reduce_fusion
  99.3 0.3 fusion.42
  99.6 0.1 broadcast_in_dim.16
  99.6 0.7 pad_maximum_fusion.4
  100.3 7.4 %all-to-all-start.3 = ((f32[16,8,160]{2,1,0:T(8,128)}), f32[16,8,160]{2,1,0:T(8,128)S(1)}, u32[]{:S(2)}, u32[]{:S(2)}) async-start(f32[16,8,160]{2,1,0:T(8,128)} %pad_maximum_fusion.4), calls=%async_computation.3 | async-start | bytes 262144 | tf_op jit(solution)/shard_map/all_to_all | solution.py:193
  107.8 1.7 %fusion.55 = (f32[512,512]{1,0:T(8,128)S(1)}, f32[512,512]{1,0:T(8,128)S(1)}) fusion(f32[1024,512]{1,0:T(8,128)} %fusion.1), kind=kLoop, calls=%fused_computation.123 | loop fusion | bytes 4194304 | tf_op jit(solution)/shard_map/slice | solution.py:179
  109.5 2.0 %collective-permute-start.5 = (f32[2,256,512]{2,1,0:T(8,128)S(1)}, f32[2,256,512]{2,1,0:T(8,128)}, u32[]{:S(2)}, u32[]{:S(2)}) collective-permute-start(f32[2,256,512]{2,1,0:T(8,128)S(1)} %bitcast.128), channel_id=1, source_target_pairs={{0,1},{1,0},{2,3},{3,2},{4,5},{5,4},{6,7},{7,6},{8,9},{9,8},{10,11... | collective-permute-start | bytes 3145736 | tf_op jit(solution)/shard_map/ppermute | solution.py:29
  111.5 5.4 %all-to-all-done.3 = f32[16,8,160]{2,1,0:T(8,128)S(1)} async-done(((f32[16,8,160]{2,1,0:T(8,128)}), f32[16,8,160]{2,1,0:T(8,128)S(1)}, u32[]{:S(2)}, u32[]{:S(2)}) %all-to-all-start.3) | async-done | bytes 81952 | tf_op jit(solution)/shard_map/all_to_all | solution.py:193
  117.0 0.1 concatenate.25
  117.1 0.8 broadcast_in_dim.18
  117.9 5.5 %all-to-all-start.4 = ((bf16[32,16,384]{2,1,0:T(8,128)(2,1)}), bf16[32,16,384]{2,1,0:T(8,128)(2,1)S(1)}, u32[]{:S(2)}, u32[]{:S(2)}) async-start(bf16[32,16,384]{2,1,0:T(8,128)(2,1)} %broadcast_in_dim.18), calls=%async_computation.4 | async-start | bytes 786432 | tf_op jit(solution)/shard_map/all_to_all | solution.py:46
  123.4 1.4 add.172
  124.9 3.1 %collective-permute-start.6 = (bf16[256,512]{1,0:T(8,128)(2,1)S(1)}, bf16[256,512]{1,0:T(8,128)(2,1)S(1)}, u32[]{:S(2)}, u32[]{:S(2)}) collective-permute-start(bf16[256,512]{1,0:T(8,128)(2,1)S(1)} %fusion.40), channel_id=1, source_target_pairs={{0,16},{16,0},{1,17},{17,1},{2,18},{18,2},{3,19},{19,3},{4,20},{20... | collective-permute-start | bytes 786440 | tf_op jit(solution)/shard_map/ppermute | solution.py:29
  128.1 8.6 %all-to-all-done.4 = bf16[32,16,384]{2,1,0:T(8,128)(2,1)S(1)} async-done(((bf16[32,16,384]{2,1,0:T(8,128)(2,1)}), bf16[32,16,384]{2,1,0:T(8,128)(2,1)S(1)}, u32[]{:S(2)}, u32[]{:S(2)}) %all-to-all-start.4) | async-done | bytes 393248 | tf_op jit(solution)/shard_map/all_to_all | solution.py:46
  136.7 0.7 copy-done
  137.4 5.0 %tail.1 = f32[16,128]{1,0:T(8,128)} custom-call(s32[1]{0:T(128)} %bitcast.59.chip_ref, bf16[512,384]{1,0:T(8,128)(2,1)} %bitcast.122), custom_call_target="tpu_custom_call" | custom-call | tf_op jit(solution)/shard_map/tail/pallas_call | solution.py:115
  142.4 1.3 broadcast_in_dim.20
  143.7 5.2 %all-to-all-start.5 = ((f32[16,8,128]{2,1,0:T(8,128)}), f32[16,8,128]{2,1,0:T(8,128)S(1)}, u32[]{:S(2)}, u32[]{:S(2)}) async-start(f32[16,8,128]{2,1,0:T(8,128)} %bitcast.69), calls=%async_computation.5 | async-start | bytes 131072 | tf_op jit(solution)/shard_map/all_to_all | solution.py:208
  149.0 0.8 fusion.41
  149.8 7.0 %all-to-all-done.5 = f32[16,8,128]{2,1,0:T(8,128)S(1)} async-done(((f32[16,8,128]{2,1,0:T(8,128)}), f32[16,8,128]{2,1,0:T(8,128)S(1)}, u32[]{:S(2)}, u32[]{:S(2)}) %all-to-all-start.5) | async-done | bytes 65568 | tf_op jit(solution)/shard_map/all_to_all | solution.py:208
  156.8 0.6 bitcast_subtract_fusion
  157.5 0.6 copy.15
  (21 shorter events, 0.2 us)
Async XLA Ops:
  0.6 31.3 %copy-start.1 = (bf16[1,256,512]{2,1,0:T(8,128)(2,1)S(1)}, bf16[1,256,512]{2,1,0:T(8,128)(2,1)}, u32[]{:S(2)}) copy-start(bf16[1,256,512]{2,1,0:T(8,128)(2,1)} %param.9) | copy-start | bytes 786436
  0.6 34.1 %all-to-all-start = ((bf16[4,8,512]{2,1,0:T(8,128)(2,1)}), bf16[4,8,512]{2,1,0:T(8,128)(2,1)S(1)}, u32[]{:S(2)}, u32[]{:S(2)}) async-start(bf16[4,8,512]{2,1,0:T(8,128)(2,1)} %bitcast.139), calls=%async_computation | async-start | bytes 65536 | tf_op jit(solution)/shard_map/all_to_all | solution.py:62
  11.6 19.2 %collective-permute-start = (bf16[15,512]{1,0:T(8,128)(2,1)S(1)}, bf16[15,512]{1,0:T(8,128)(2,1)S(1)}, u32[]{:S(2)}, u32[]{:S(2)}) collective-permute-start(bf16[15,512]{1,0:T(8,128)(2,1)S(1)} %get-tuple-element.9), channel_id=1, source_target_pairs={{0,1},{1,2},{2,3},{3,4},{4,5},{5,6},{6,7},{7,8},{8,9},{9,10},{10,1... | collective-permute-start | bytes 46088 | tf_op jit(solution)/shard_map/ppermute | solution.py:23
  13.6 17.3 %collective-permute-start.1 = (bf16[15,512]{1,0:T(8,128)(2,1)S(1)}, bf16[15,512]{1,0:T(8,128)(2,1)S(1)}, u32[]{:S(2)}, u32[]{:S(2)}) collective-permute-start(bf16[15,512]{1,0:T(8,128)(2,1)S(1)} %get-tuple-element.10), channel_id=1, source_target_pairs={{1,0},{2,1},{3,2},{4,3},{5,4},{6,5},{7,6},{8,7},{9,8},{10,9},{11,1... | collective-permute-start | bytes 46088 | tf_op jit(solution)/shard_map/ppermute | solution.py:24
  16.0 18.8 %collective-permute-start.4 = (bf16[32,512]{1,0:T(8,128)(2,1)}, bf16[32,512]{1,0:T(8,128)(2,1)S(1)}, u32[]{:S(2)}, u32[]{:S(2)}) collective-permute-start(bf16[32,512]{1,0:T(8,128)(2,1)} %param.12), channel_id=1, source_target_pairs={{0,0},{1,32},{2,2},{3,34},{4,4},{5,36},{6,6},{7,38},{8,8},{9,40},{... | collective-permute-start | bytes 98312 | tf_op jit(solution)/shard_map/ppermute | solution.py:60
  25.7 18.6 %collective-permute-start.7 = (bf16[256,512]{1,0:T(8,128)(2,1)S(1)}, bf16[256,512]{1,0:T(8,128)(2,1)S(1)}, u32[]{:S(2)}, u32[]{:S(2)}) collective-permute-start(bf16[256,512]{1,0:T(8,128)(2,1)S(1)} %bitcast_multiply_fusion), channel_id=1, source_target_pairs={{0,16},{16,0},{1,17},{17,1},{2,18},{18,2},{3,19},{19,3},{4,20},{20... | collective-permute-start | bytes 786440 | tf_op jit(solution)/shard_map/ppermute | solution.py:29
  34.7 6.6 %copy-start.4 = (f32[512]{0:T(512)S(1)}, f32[512]{0:T(512)}, u32[]{:S(2)}) copy-start(f32[512]{0:T(512)} %param.14) | copy-start | bytes 6148
  35.9 32.3 %all-to-all-start.1 = ((bf16[16,64,512]{2,1,0:T(8,128)(2,1)}), bf16[16,64,512]{2,1,0:T(8,128)(2,1)S(1)}, u32[]{:S(2)}, u32[]{:S(2)}) async-start(bf16[16,64,512]{2,1,0:T(8,128)(2,1)} %broadcast_in_dim.14), calls=%async_computation.1 | async-start | bytes 2097152 | tf_op jit(solution)/shard_map/all_to_all | solution.py:46
  41.5 12.8 %collective-permute-start.2 = (bf16[256,512]{1,0:T(8,128)(2,1)S(1)}, bf16[256,512]{1,0:T(8,128)(2,1)S(1)}, u32[]{:S(2)}, u32[]{:S(2)}) collective-permute-start(bf16[256,512]{1,0:T(8,128)(2,1)S(1)} %fusion.6), channel_id=1, source_target_pairs={{0,16},{16,0},{1,17},{17,1},{2,18},{18,2},{3,19},{19,3},{4,20},{20... | collective-permute-start | bytes 786440 | tf_op jit(solution)/shard_map/ppermute | solution.py:29
  44.3 13.2 %collective-permute-start.8 = (bf16[2,256,512]{2,1,0:T(8,128)(2,1)S(1)}, bf16[2,256,512]{2,1,0:T(8,128)(2,1)S(1)}, u32[]{:S(2)}, u32[]{:S(2)}) collective-permute-start(bf16[2,256,512]{2,1,0:T(8,128)(2,1)S(1)} %pad_maximum_fusion.3), channel_id=1, source_target_pairs={{0,1},{1,0},{2,3},{3,2},{4,5},{5,4},{6,7},{7,6},{8,9},{9,8},{10,11... | collective-permute-start | bytes 1572872 | tf_op jit(solution)/shard_map/ppermute | solution.py:29
  54.3 4.7 %collective-permute-start.3 = (bf16[2,256,512]{2,1,0:T(8,128)(2,1)S(1)}, bf16[2,256,512]{2,1,0:T(8,128)(2,1)S(1)}, u32[]{:S(2)}, u32[]{:S(2)}) collective-permute-start(bf16[2,256,512]{2,1,0:T(8,128)(2,1)S(1)} %pad_maximum_fusion.2), channel_id=1, source_target_pairs={{0,1},{1,0},{2,3},{3,2},{4,5},{5,4},{6,7},{7,6},{8,9},{9,8},{10,11... | collective-permute-start | bytes 1572872 | tf_op jit(solution)/shard_map/ppermute | solution.py:29
  73.7 25.5 %all-to-all-start.2 = ((bf16[64,8,512]{2,1,0:T(8,128)(2,1)}), bf16[64,8,512]{2,1,0:T(8,128)(2,1)S(1)}, u32[]{:S(2)}, u32[]{:S(2)}) async-start(bf16[64,8,512]{2,1,0:T(8,128)(2,1)} %fusion), calls=%async_computation.2 | async-start | bytes 1048576 | tf_op jit(solution)/shard_map/all_to_all | solution.py:171
  81.9 17.4 %copy-start.2 = (f32[1,8,2048]{2,1,0:T(8,128)S(1)}, f32[1,8,2048]{2,1,0:T(8,128)}, u32[]{:S(2)}) copy-start(f32[1,8,2048]{2,1,0:T(8,128)} %param.16) | copy-start | bytes 196612
  81.9 17.4 %copy-start.3 = (s32[2048,32]{0,1:T(8,128)S(1)}, s32[2048,32]{0,1:T(8,128)}, u32[]{:S(2)}) copy-start(s32[2048,32]{0,1:T(8,128)} %param.17) | copy-start | bytes 786436
  100.3 16.6 %all-to-all-start.3 = ((f32[16,8,160]{2,1,0:T(8,128)}), f32[16,8,160]{2,1,0:T(8,128)S(1)}, u32[]{:S(2)}, u32[]{:S(2)}) async-start(f32[16,8,160]{2,1,0:T(8,128)} %pad_maximum_fusion.4), calls=%async_computation.3 | async-start | bytes 262144 | tf_op jit(solution)/shard_map/all_to_all | solution.py:193
  109.5 13.9 %collective-permute-start.5 = (f32[2,256,512]{2,1,0:T(8,128)S(1)}, f32[2,256,512]{2,1,0:T(8,128)}, u32[]{:S(2)}, u32[]{:S(2)}) collective-permute-start(f32[2,256,512]{2,1,0:T(8,128)S(1)} %bitcast.128), channel_id=1, source_target_pairs={{0,1},{1,0},{2,3},{3,2},{4,5},{5,4},{6,7},{7,6},{8,9},{9,8},{10,11... | collective-permute-start | bytes 3145736 | tf_op jit(solution)/shard_map/ppermute | solution.py:29
  117.9 18.8 %all-to-all-start.4 = ((bf16[32,16,384]{2,1,0:T(8,128)(2,1)}), bf16[32,16,384]{2,1,0:T(8,128)(2,1)S(1)}, u32[]{:S(2)}, u32[]{:S(2)}) async-start(bf16[32,16,384]{2,1,0:T(8,128)(2,1)} %broadcast_in_dim.18), calls=%async_computation.4 | async-start | bytes 786432 | tf_op jit(solution)/shard_map/all_to_all | solution.py:46
  124.9 24.1 %collective-permute-start.6 = (bf16[256,512]{1,0:T(8,128)(2,1)S(1)}, bf16[256,512]{1,0:T(8,128)(2,1)S(1)}, u32[]{:S(2)}, u32[]{:S(2)}) collective-permute-start(bf16[256,512]{1,0:T(8,128)(2,1)S(1)} %fusion.40), channel_id=1, source_target_pairs={{0,16},{16,0},{1,17},{17,1},{2,18},{18,2},{3,19},{19,3},{4,20},{20... | collective-permute-start | bytes 786440 | tf_op jit(solution)/shard_map/ppermute | solution.py:29
  136.6 0.7 copy-start
  143.7 13.1 %all-to-all-start.5 = ((f32[16,8,128]{2,1,0:T(8,128)}), f32[16,8,128]{2,1,0:T(8,128)S(1)}, u32[]{:S(2)}, u32[]{:S(2)}) async-start(f32[16,8,128]{2,1,0:T(8,128)} %bitcast.69), calls=%async_computation.5 | async-start | bytes 131072 | tf_op jit(solution)/shard_map/all_to_all | solution.py:208

commit v4 on v3

--- a/solution.py
+++ b/solution.py
@@ -46,7 +46,7 @@
     return lax.all_to_all(copies, axis, 0, 0, tiled=True)
 
 
-def quarter_weights(up_weight, down_weight):
+def quarter_block(up_weight, down_weight):
     rows, hidden = up_weight.shape
     quarter = hidden // QUARTERS
     down_rows, features = down_weight.shape
@@ -60,11 +60,15 @@
     down_block = lax.ppermute(down_weight, SEQ, moves)
     up_split = up_weight.reshape(rows, QUARTERS, quarter).transpose(1, 0, 2)
     up_block = lax.all_to_all(up_split, GROUP, 0, 0, tiled=True).reshape(QUARTERS * rows, quarter)
-    whole = gather_by_exchange(jnp.concatenate([up_block, down_block], axis=0), GROUPS)
-    whole = whole.reshape(XH, Z, QUARTERS * rows + down_rows, features)
-    up = whole[:, :, : QUARTERS * rows].reshape(XH, Z, XL, C * rows, quarter)
-    up = up.transpose(0, 2, 1, 3, 4).reshape(-1, quarter)
-    down = whole[:, :, QUARTERS * rows :].transpose(1, 0, 2, 3).reshape(quarter, features)
+    return jnp.concatenate([up_block, down_block], axis=0)
+
+
+def quarter_weights(block):
+    half, width = block.shape[0] // 2, block.shape[1]
+    whole = gather_by_exchange(block, GROUPS).reshape(XH, Z, 2 * half, width)
+    up = whole[:, :, :half].reshape(XH, Z, XL, half // XL, width)
+    up = up.transpose(0, 2, 1, 3, 4).reshape(-1, width)
+    down = whole[:, :, half:].transpose(1, 0, 2, 3).reshape(-1, width)
     return up, down
 
 
@@ -81,8 +85,8 @@
     return parts
 
 
-def tail_kernel(chip_ref, columns_ref, piece_ref, rows_scratch):
-    width = piece_ref.shape[1]
+def tail_kernel(chip_ref, columns_ref, message_ref, rows_scratch):
+    chunks, rows, width = message_ref.shape
     rank = RANK
     columns = columns_ref[...].astype(jnp.float32)
     mean_columns = columns[:, :width] + columns[:, width : 2 * width]
@@ -103,24 +107,26 @@
         solved = jnp.where(row_index == k, solved_row, solved - factor * solved_row)
     right_t = jnp.dot(solved, mean_columns, precision=HIGHEST, preferred_element_type=jnp.float32)
     rows_scratch[...] = solved.T
-    chip_rows = piece_ref.shape[0]
+    chip_rows = C * rows
     basis_rows = rows_scratch[pl.ds(pl.multiple_of(chip_ref[0] * chip_rows, chip_rows), chip_rows), :]
-    piece_ref[...] = jnp.dot(
-        basis_rows, right_t, precision=HIGHEST, preferred_element_type=jnp.float32
-    )
-
-
-def tail(chip, columns, chip_rows, width):
+    piece = jnp.dot(basis_rows, right_t, precision=HIGHEST, preferred_element_type=jnp.float32)
+    for chunk in range(chunks):
+        half = chunk % C
+        message_ref[chunk] = piece[half * rows : (half + 1) * rows]
+
+
+def tail(chip, columns, chunks, rows, width):
     features = columns.shape[0]
     return pl.pallas_call(
         tail_kernel,
-        out_shape=jax.ShapeDtypeStruct((chip_rows, width), jnp.float32),
+        out_shape=jax.ShapeDtypeStruct((chunks, rows, width), jnp.float32),
         in_specs=[
             pl.BlockSpec(memory_space=pltpu.SMEM),
             pl.BlockSpec(memory_space=pltpu.VMEM),
         ],
         out_specs=pl.BlockSpec(memory_space=pltpu.VMEM),
         scratch_shapes=[pltpu.VMEM((features, RANK), jnp.float32)],
+        compiler_params=pltpu.CompilerParams(vmem_limit_bytes=8 * 1024 * 1024),
         name="tail",
     )(chip, columns)
 
@@ -140,8 +146,10 @@
     frames, features = tokens.shape[1:]
     low, high = halo(tokens[0], half_width)
     masked = cotangent[0] * frame_mask[0][:, None].astype(jnp.bfloat16)
+    block = quarter_block(up_weight, down_weight)
+    block, masked, low, high = lax.optimization_barrier((block, masked, low, high))
+    up, down = quarter_weights(block)
     masked_all = group_frames(masked)
-    up, down = quarter_weights(up_weight, down_weight)
 
     widened = jnp.concatenate([low, tokens[0], high], axis=0).astype(jnp.float32)
     filtered = kernel[0] * widened[0:frames]
@@ -164,6 +172,10 @@
     grad_part = lax.dot_general(
         normed_all, delta_hidden, (((0,), (0,)), ((), ())), preferred_element_type=jnp.float32
     ).astype(jnp.bfloat16)
+
+    mixed_part = jnp.dot(hidden, down, preferred_element_type=jnp.float32)
+    mixed_part = mixed_part.reshape(C, XL, frames, features)
+    chip_part = mixed_part[0] + swap(mixed_part[1], "c")
 
     quarter = grad_part.shape[1]
     devices = XH * XL * Z * C
@@ -173,12 +185,6 @@
     grad_rows = jnp.sum(pieces, axis=(0, 2)).reshape(QUARTERS, rows, quarter)
     grad_rows = grad_rows.transpose(1, 0, 2).reshape(rows, QUARTERS * quarter)
     memory_rows = grad_rows + error_memory[0]
-
-    mixed_part = jnp.dot(hidden, down, preferred_element_type=jnp.float32)
-    mixed_part = mixed_part.reshape(C, XL, frames, features)
-    chip_part = mixed_part[0] + swap(mixed_part[1], "c")
-    other_chip = swap(chip_part[1].astype(jnp.bfloat16), "xl").astype(jnp.float32)
-    mixed = (stream.astype(jnp.float32) + 0.5 * (chip_part[0] + other_chip)).astype(jnp.bfloat16)
 
     chunks = Y * C
     width = memory_rows.shape[1] // chunks
@@ -190,6 +196,8 @@
     message = jnp.concatenate(
         [by_chunk, jnp.broadcast_to(left_term[None], (chunks, rows, rank))], axis=2
     )
+    message, chip_part = lax.optimization_barrier((message, chip_part))
+    other_chip = swap(chip_part[1].astype(jnp.bfloat16), "xl")
     arrived = lax.all_to_all(message, ("y", "c"), 0, 0, tiled=True)
     mean_rows = jnp.sum(arrived.reshape(Y, chip_rows, width + rank), axis=0) / Y
     packed = jnp.concatenate(
@@ -200,12 +208,14 @@
         ],
         axis=1,
     )
+    packed, other_chip = lax.optimization_barrier((packed, other_chip))
+    mixed = (
+        stream.astype(jnp.float32) + 0.5 * (chip_part[0] + other_chip.astype(jnp.float32))
+    ).astype(jnp.bfloat16)
     columns = gather_by_exchange(packed, CHIP).reshape(features, packed.shape[1])
     chip = lax.axis_index(CHIP).astype(jnp.int32).reshape(1)
-    piece = tail(chip, columns, chip_rows, width)
-
-    piece = jnp.broadcast_to(piece.reshape(1, C, rows, width), (Y, C, rows, width))
-    compressed = lax.all_to_all(piece.reshape(chunks, rows, width), ("y", "c"), 0, 0, tiled=True)
+    message = tail(chip, columns, chunks, rows, width)
+    compressed = lax.all_to_all(message, ("y", "c"), 0, 0, tiled=True)
     compressed = compressed.transpose(1, 0, 2).reshape(rows, chunks * width)
     new_memory = memory_rows - compressed
     return (mixed[None], new_memory[None], compressed)

time: 159 us -> 155 us (0.975)
  starting transfers between devices: 69.2 us -> 81.4 us
  waiting for transfers between devices: 52.3 us -> 42.7 us
  local copies, waits for them, and re-layouts: 10.4 us -> 6.96 us
  other arithmetic: 12.1 us -> 8.85 us
    all_to_all x2, starting transfers between devices: 15.5 us -> 21.1 us  [the longest x1 10.9 us: per_device(): compressed = lax.all_to_all(message, ('y', 'c'), 0, 0, tiled=True)]
    ppermute x6, starting transfers between devices: 15.2 us -> 19.8 us  [swap(): return lax.ppermute(block, axis, [(0, 1), (1, 0)])]
    all_to_all x2, waiting for transfers between devices: 17.6 us -> 13.1 us  [gather_by_exchange(): return lax.all_to_all(copies, axis, 0, 0, tiled=True)]
    ppermute x6, waiting for transfers between devices: 8.05 us -> 4.95 us  [swap(): return lax.ppermute(block, axis, [(0, 1), (1, 0)])]
    all_to_all x1, waiting for transfers between devices: 14.1 us -> 11.5 us  [per_device(): lax.all_to_all(grad_part.reshape(devices, rows, quarter), SEQ, 0, 0, tile...]
    all_to_all x1, starting transfers between devices: 8.15 us -> 10.7 us  [per_device(): lax.all_to_all(grad_part.reshape(devices, rows, quarter), SEQ, 0, 0, tile...]
    ppermute x1, starting transfers between devices: 1.91 us -> 3.61 us  [halo(): low = lax.ppermute(block[block.shape[0] - width:], SEQ, forward)]
  transfers between devices with their start and end apart: 15 -> 15, of which waited for: 7 -> 8; matrix products, arithmetic and copies ran while one was open for 14% -> 10% of each run, Pallas kernels for 3% -> 0%
where the time goes in v4:
time: 155 us; the launch traced here: 154 us
  starting transfers between devices  81.4 us (53%)
  waiting for transfers between devices  42.7 us (28%)
  matrix products  9.07 us (6%)
  other arithmetic  8.85 us (6%)
  local copies, waits for them, and re-layouts  6.96 us (4%)
  Pallas kernels  4.06 us (3%)
    ppermute x6, starting transfers between devices, swap(): return lax.ppermute(block, axis, [(0, 1), (1, 0)])  19.8 us
    all_to_all x2, waiting for transfers between devices, gather_by_exchange(): return lax.all_to_all(copies, axis, 0, 0, tiled=True)  13.1 us
    all_to_all x1, waiting for transfers between devices, per_device(): lax.all_to_all(grad_part.reshape(devices, rows, quarter), SEQ, 0, 0, tile...  11.5 us
    all_to_all x1, starting transfers between devices, per_device(): compressed = lax.all_to_all(message, ('y', 'c'), 0, 0, tiled=True)  10.9 us
    all_to_all x1, starting transfers between devices, per_device(): lax.all_to_all(grad_part.reshape(devices, rows, quarter), SEQ, 0, 0, tile...  10.7 us
    all_to_all x1, starting transfers between devices, quarter_block(): lax.all_to_all(up_split, GROUP, 0, 0, tiled=True)  10.3 us
    all_to_all x2, starting transfers between devices, gather_by_exchange(): return lax.all_to_all(copies, axis, 0, 0, tiled=True)  10 us
    all_to_all x1, starting transfers between devices, per_device(): arrived = lax.all_to_all(message, ('y', 'c'), 0, 0, tiled=True)  7.45 us
  transfers between devices with their start and end apart: 15, of which 8 were waited for; matrix products, arithmetic and copies ran while one was open for 10% of the time, Pallas kernels for 0%

profile of v4, /device:TPU:1, one launch (start us, length us, event | category | flops | bytes accessed | tf_op | source)
XLA Modules:
  0.0 154.1 jit_solution(13606231775948544626)
XLA Ops:
  0.6 10.3 %all-to-all-start = ((bf16[4,8,512]{2,1,0:T(8,128)(2,1)}), bf16[4,8,512]{2,1,0:T(8,128)(2,1)S(1)}, u32[]{:S(2)}, u32[]{:S(2)}) async-start(bf16[4,8,512]{2,1,0:T(8,128)(2,1)} %bitcast.136), calls=%async_computation | async-start | bytes 65536 | tf_op jit(solution)/shard_map/all_to_all | solution.py:62
  10.9 0.7 slice_bitcast_fusion.1
  11.6 1.9 %collective-permute-start.2 = (bf16[15,512]{1,0:T(8,128)(2,1)S(1)}, bf16[15,512]{1,0:T(8,128)(2,1)S(1)}, u32[]{:S(2)}, u32[]{:S(2)}) collective-permute-start(bf16[15,512]{1,0:T(8,128)(2,1)S(1)} %get-tuple-element.25), channel_id=1, source_target_pairs={{1,0},{2,1},{3,2},{4,3},{5,4},{6,5},{7,6},{8,7},{9,8},{10,9},{11,1... | collective-permute-start | bytes 46088 | tf_op jit(solution)/shard_map/ppermute | solution.py:24
  13.6 3.6 %collective-permute-start.1 = (bf16[15,512]{1,0:T(8,128)(2,1)S(1)}, bf16[15,512]{1,0:T(8,128)(2,1)S(1)}, u32[]{:S(2)}, u32[]{:S(2)}) collective-permute-start(bf16[15,512]{1,0:T(8,128)(2,1)S(1)} %get-tuple-element.26), channel_id=1, source_target_pairs={{0,1},{1,2},{2,3},{3,4},{4,5},{5,6},{6,7},{7,8},{8,9},{9,10},{10,1... | collective-permute-start | bytes 46088 | tf_op jit(solution)/shard_map/ppermute | solution.py:23
  17.2 6.7 %collective-permute-start = (bf16[32,512]{1,0:T(8,128)(2,1)}, bf16[32,512]{1,0:T(8,128)(2,1)S(1)}, u32[]{:S(2)}, u32[]{:S(2)}) collective-permute-start(bf16[32,512]{1,0:T(8,128)(2,1)} %param.12), channel_id=1, source_target_pairs={{0,0},{1,32},{2,2},{3,34},{4,4},{5,36},{6,6},{7,38},{8,8},{9,40},{... | collective-permute-start | bytes 98312 | tf_op jit(solution)/shard_map/ppermute | solution.py:60
  23.9 0.7 convert_reduce_fusion.2
  24.6 1.2 fusion.55
  25.8 1.1 bitcast_multiply_fusion
  26.9 1.0 fusion.56
  27.9 0.0 all-to-all-done
  27.9 0.0 collective-permute-done
  27.9 0.0 collective-permute-done.2
  27.9 0.0 collective-permute-done.1
  27.9 1.9 %collective-permute-start.5 = (bf16[256,512]{1,0:T(8,128)(2,1)S(1)}, bf16[256,512]{1,0:T(8,128)(2,1)S(1)}, u32[]{:S(2)}, u32[]{:S(2)}) collective-permute-start(bf16[256,512]{1,0:T(8,128)(2,1)S(1)} %bitcast_multiply_fusion), channel_id=1, source_target_pairs={{0,16},{16,0},{1,17},{17,1},{2,18},{18,2},{3,19},{19,3},{4,20},{20... | collective-permute-start | bytes 786440 | tf_op jit(solution)/shard_map/ppermute | solution.py:29
  29.9 1.1 broadcast_in_dim.10
  30.9 4.5 %all-to-all-start.1 = ((bf16[16,64,512]{2,1,0:T(8,128)(2,1)}), bf16[16,64,512]{2,1,0:T(8,128)(2,1)S(1)}, u32[]{:S(2)}, u32[]{:S(2)}) async-start(bf16[16,64,512]{2,1,0:T(8,128)(2,1)} %broadcast_in_dim.10), calls=%async_computation.1 | async-start | bytes 2097152 | tf_op jit(solution)/shard_map/all_to_all | solution.py:46
  35.5 0.1 maximum_convert_fusion
  35.6 0.0 copy-start.3
  35.6 2.8 %convert_reduce_fusion.1 = (f32[256]{0:T(256)S(1)}, bf16[256,512]{1,0:T(8,128)(2,1)S(1)}) fusion(f32[286,512]{1,0:T(8,128)S(1)} %maximum_convert_fusion, f32[512]{0:T(512)S(1)} %bitcast.166, f32[512]{0:T(512)S(1)} %bitcast.167, f32[512]{0:T(512)S(1)} %bitcast.138, f32[512]{0:T(512)S(1)} %bitcast.139, f32[512]{0:T(512)S(1)} %bitcast.140, ...), kind=kLoop, calls=%fused_computation.11 | loop fusion | flops 9174784 | bytes 16841728 | tf_op jit(solution)/shard_map/reduce_sum | solution.py:39
  38.4 0.2 fusion.4
  38.6 0.1 fusion.6
  38.8 2.8 %collective-permute-start.3 = (bf16[256,512]{1,0:T(8,128)(2,1)S(1)}, bf16[256,512]{1,0:T(8,128)(2,1)S(1)}, u32[]{:S(2)}, u32[]{:S(2)}) collective-permute-start(bf16[256,512]{1,0:T(8,128)(2,1)S(1)} %fusion.6), channel_id=1, source_target_pairs={{0,16},{16,0},{1,17},{17,1},{2,18},{18,2},{3,19},{19,3},{4,20},{20... | collective-permute-start | bytes 786440 | tf_op jit(solution)/shard_map/ppermute | solution.py:29
  41.5 0.0 collective-permute-done.5
  41.5 0.1 pad_maximum_fusion.3
  41.6 4.2 %collective-permute-start.6 = (bf16[2,256,512]{2,1,0:T(8,128)(2,1)S(1)}, bf16[2,256,512]{2,1,0:T(8,128)(2,1)S(1)}, u32[]{:S(2)}, u32[]{:S(2)}) collective-permute-start(bf16[2,256,512]{2,1,0:T(8,128)(2,1)S(1)} %pad_maximum_fusion.3), channel_id=1, source_target_pairs={{0,1},{1,0},{2,3},{3,2},{4,5},{5,4},{6,7},{7,6},{8,9},{9,8},{10,11... | collective-permute-start | bytes 1572872 | tf_op jit(solution)/shard_map/ppermute | solution.py:29
  45.8 0.1 fusion.64
  46.0 4.0 %collective-permute-done.3 = bf16[256,512]{1,0:T(8,128)(2,1)S(1)} collective-permute-done((bf16[256,512]{1,0:T(8,128)(2,1)S(1)}, bf16[256,512]{1,0:T(8,128)(2,1)S(1)}, u32[]{:S(2)}, u32[]{:S(2)}) %collective-permute-start.3) | collective-permute-done | bytes 262176 | tf_op jit(solution)/shard_map/ppermute | solution.py:29
  50.0 0.1 pad_maximum_fusion.2
  50.1 5.6 %collective-permute-start.4 = (bf16[2,256,512]{2,1,0:T(8,128)(2,1)S(1)}, bf16[2,256,512]{2,1,0:T(8,128)(2,1)S(1)}, u32[]{:S(2)}, u32[]{:S(2)}) collective-permute-start(bf16[2,256,512]{2,1,0:T(8,128)(2,1)S(1)} %pad_maximum_fusion.2), channel_id=1, source_target_pairs={{0,1},{1,0},{2,3},{3,2},{4,5},{5,4},{6,7},{7,6},{8,9},{9,8},{10,11... | collective-permute-start | bytes 1572872 | tf_op jit(solution)/shard_map/ppermute | solution.py:29
  55.7 0.0 collective-permute-done.6
  55.7 1.1 pad_maximum_fusion.1
  56.8 0.4 collective-permute-done.4
  57.2 0.1 pad_maximum_fusion
  57.3 2.1 %all-to-all-done.1 = bf16[16,64,512]{2,1,0:T(8,128)(2,1)S(1)} async-done(((bf16[16,64,512]{2,1,0:T(8,128)(2,1)}), bf16[16,64,512]{2,1,0:T(8,128)(2,1)S(1)}, u32[]{:S(2)}, u32[]{:S(2)}) %all-to-all-start.1) | async-done | bytes 1048608 | tf_op jit(solution)/shard_map/all_to_all | solution.py:46
  59.4 0.1 slice_bitcast_fusion
  59.6 2.0 %fusion.57 = f32[1024,512]{1,0:T(8,128)} fusion(bf16[1024,512]{1,0:T(8,128)(2,1)S(1)} %bitcast.113, bf16[512,512]{1,0:T(8,128)(2,1)S(1)} %bitcast.119), kind=kOutput, calls=%fused_computation.124 | convolution fusion | flops 536870912 | bytes 3670016 | tf_op jit(solution)/shard_map/dot_general | solution.py:163
  61.7 4.4 %fusion = bf16[64,8,512]{2,1,0:T(8,128)(2,1)} fusion(bf16[1024,512]{1,0:T(8,128)(2,1)S(1)} %bitcast.114, f32[1024,512]{1,0:T(8,128)} %fusion.57, bf16[1024,512]{1,0:T(8,128)(2,1)} %bitcast.126, bf16[512,512]{1,0:T(8,128)(2,1)S(1)} %bitcast.132), kind=kOutput, calls=%fused_computation.4 | convolution fusion | flops 1079246848 | bytes 5242880 | tf_op jit(solution)/shard_map/dot_general | solution.py:172
  66.1 10.7 %all-to-all-start.2 = ((bf16[64,8,512]{2,1,0:T(8,128)(2,1)}), bf16[64,8,512]{2,1,0:T(8,128)(2,1)S(1)}, u32[]{:S(2)}, u32[]{:S(2)}) async-start(bf16[64,8,512]{2,1,0:T(8,128)(2,1)} %fusion), calls=%async_computation.2 | async-start | bytes 1048576 | tf_op jit(solution)/shard_map/all_to_all | solution.py:183
  76.8 2.3 %fusion.1 = f32[1024,512]{1,0:T(8,128)S(1)} fusion(bf16[512,512]{1,0:T(8,128)(2,1)S(1)} %bitcast.133, f32[1024,512]{1,0:T(8,128)} %fusion.57), kind=kOutput, calls=%fused_computation.8 | convolution fusion | flops 539492352 | bytes 4718592 | tf_op jit(solution)/shard_map/dot_general | solution.py:176
  79.1 0.0 copy-start.1
  79.2 0.0 copy-start.2
  79.2 1.2 fusion.54
  80.3 2.4 %collective-permute-start.7 = (f32[2,256,512]{2,1,0:T(8,128)}, f32[2,256,512]{2,1,0:T(8,128)S(1)}, u32[]{:S(2)}, u32[]{:S(2)}) collective-permute-start(f32[2,256,512]{2,1,0:T(8,128)} %bitcast.61), channel_id=1, source_target_pairs={{0,1},{1,0},{2,3},{3,2},{4,5},{5,4},{6,7},{7,6},{8,9},{9,8},{10,11... | collective-permute-start | bytes 3145736 | tf_op jit(solution)/shard_map/ppermute | solution.py:29
  82.7 11.5 %all-to-all-done.2 = bf16[64,8,512]{2,1,0:T(8,128)(2,1)S(1)} async-done(((bf16[64,8,512]{2,1,0:T(8,128)(2,1)}), bf16[64,8,512]{2,1,0:T(8,128)(2,1)S(1)}, u32[]{:S(2)}, u32[]{:S(2)}) %all-to-all-start.2) | async-done | bytes 524320 | tf_op jit(solution)/shard_map/all_to_all | solution.py:183
  94.2 0.1 convert_reduce_fusion
  94.3 0.3 fusion.41
  94.5 0.1 broadcast_in_dim.11
  94.6 0.7 pad_maximum_fusion.4
  95.3 0.0 collective-permute-done.7
  95.3 0.2 add.175
  95.5 7.5 %all-to-all-start.3 = ((f32[16,8,160]{2,1,0:T(8,128)}), f32[16,8,160]{2,1,0:T(8,128)S(1)}, u32[]{:S(2)}, u32[]{:S(2)}) async-start(f32[16,8,160]{2,1,0:T(8,128)} %pad_maximum_fusion.4), calls=%async_computation.3 | async-start | bytes 262144 | tf_op jit(solution)/shard_map/all_to_all | solution.py:201
  103.0 2.9 %collective-permute-start.8 = (bf16[256,512]{1,0:T(8,128)(2,1)S(1)}, bf16[256,512]{1,0:T(8,128)(2,1)S(1)}, u32[]{:S(2)}, u32[]{:S(2)}) collective-permute-start(bf16[256,512]{1,0:T(8,128)(2,1)S(1)} %fusion.39), channel_id=1, source_target_pairs={{0,16},{16,0},{1,17},{17,1},{2,18},{18,2},{3,19},{19,3},{4,20},{20... | collective-permute-start | bytes 786440 | tf_op jit(solution)/shard_map/ppermute | solution.py:29
  105.9 6.2 %all-to-all-done.3 = f32[16,8,160]{2,1,0:T(8,128)S(1)} async-done(((f32[16,8,160]{2,1,0:T(8,128)}), f32[16,8,160]{2,1,0:T(8,128)S(1)}, u32[]{:S(2)}, u32[]{:S(2)}) %all-to-all-start.3) | async-done | bytes 81952 | tf_op jit(solution)/shard_map/all_to_all | solution.py:201
  112.2 0.1 concatenate.25
  112.3 0.5 collective-permute-done.8
  112.7 0.8 broadcast_in_dim.14
  113.5 5.5 %all-to-all-start.4 = ((bf16[32,16,384]{2,1,0:T(8,128)(2,1)}), bf16[32,16,384]{2,1,0:T(8,128)(2,1)S(1)}, u32[]{:S(2)}, u32[]{:S(2)}) async-start(bf16[32,16,384]{2,1,0:T(8,128)(2,1)} %broadcast_in_dim.14), calls=%async_computation.4 | async-start | bytes 786432 | tf_op jit(solution)/shard_map/all_to_all | solution.py:46
  119.1 11.1 %all-to-all-done.4 = bf16[32,16,384]{2,1,0:T(8,128)(2,1)S(1)} async-done(((bf16[32,16,384]{2,1,0:T(8,128)(2,1)}), bf16[32,16,384]{2,1,0:T(8,128)(2,1)S(1)}, u32[]{:S(2)}, u32[]{:S(2)}) %all-to-all-start.4) | async-done | bytes 393248 | tf_op jit(solution)/shard_map/all_to_all | solution.py:46
  130.1 4.1 %tail.1 = f32[16,8,128]{2,1,0:T(8,128)} custom-call(s32[1]{0:T(128)} %bitcast.67.chip_ref, bf16[512,384]{1,0:T(8,128)(2,1)S(1)} %bitcast.112), custom_call_target="tpu_custom_call" | custom-call | tf_op jit(solution)/shard_map/tail/pallas_call | solution.py:120
  134.2 10.9 %all-to-all-start.5 = ((f32[16,8,128]{2,1,0:T(8,128)}), f32[16,8,128]{2,1,0:T(8,128)S(1)}, u32[]{:S(2)}, u32[]{:S(2)}) async-start(f32[16,8,128]{2,1,0:T(8,128)} %tail.1), calls=%async_computation.5 | async-start | bytes 131072 | tf_op jit(solution)/shard_map/all_to_all | solution.py:218
  145.0 0.8 fusion.40
  145.9 7.0 %all-to-all-done.5 = f32[16,8,128]{2,1,0:T(8,128)S(1)} async-done(((f32[16,8,128]{2,1,0:T(8,128)}), f32[16,8,128]{2,1,0:T(8,128)S(1)}, u32[]{:S(2)}, u32[]{:S(2)}) %all-to-all-start.5) | async-done | bytes 65568 | tf_op jit(solution)/shard_map/all_to_all | solution.py:218
  152.9 0.6 bitcast_subtract_fusion
  153.5 0.6 copy.16
  (17 shorter events, 0.2 us)
Async XLA Ops:
  0.6 34.9 %copy-start = (bf16[1,256,512]{2,1,0:T(8,128)(2,1)S(1)}, bf16[1,256,512]{2,1,0:T(8,128)(2,1)}, u32[]{:S(2)}) copy-start(bf16[1,256,512]{2,1,0:T(8,128)(2,1)} %param.9) | copy-start | bytes 786436
  0.6 27.2 %all-to-all-start = ((bf16[4,8,512]{2,1,0:T(8,128)(2,1)}), bf16[4,8,512]{2,1,0:T(8,128)(2,1)S(1)}, u32[]{:S(2)}, u32[]{:S(2)}) async-start(bf16[4,8,512]{2,1,0:T(8,128)(2,1)} %bitcast.136), calls=%async_computation | async-start | bytes 65536 | tf_op jit(solution)/shard_map/all_to_all | solution.py:62
  11.6 16.3 %collective-permute-start.2 = (bf16[15,512]{1,0:T(8,128)(2,1)S(1)}, bf16[15,512]{1,0:T(8,128)(2,1)S(1)}, u32[]{:S(2)}, u32[]{:S(2)}) collective-permute-start(bf16[15,512]{1,0:T(8,128)(2,1)S(1)} %get-tuple-element.25), channel_id=1, source_target_pairs={{1,0},{2,1},{3,2},{4,3},{5,4},{6,5},{7,6},{8,7},{9,8},{10,9},{11,1... | collective-permute-start | bytes 46088 | tf_op jit(solution)/shard_map/ppermute | solution.py:24
  13.6 14.3 %collective-permute-start.1 = (bf16[15,512]{1,0:T(8,128)(2,1)S(1)}, bf16[15,512]{1,0:T(8,128)(2,1)S(1)}, u32[]{:S(2)}, u32[]{:S(2)}) collective-permute-start(bf16[15,512]{1,0:T(8,128)(2,1)S(1)} %get-tuple-element.26), channel_id=1, source_target_pairs={{0,1},{1,2},{2,3},{3,4},{4,5},{5,6},{6,7},{7,8},{8,9},{9,10},{10,1... | collective-permute-start | bytes 46088 | tf_op jit(solution)/shard_map/ppermute | solution.py:23
  17.2 10.7 %collective-permute-start = (bf16[32,512]{1,0:T(8,128)(2,1)}, bf16[32,512]{1,0:T(8,128)(2,1)S(1)}, u32[]{:S(2)}, u32[]{:S(2)}) collective-permute-start(bf16[32,512]{1,0:T(8,128)(2,1)} %param.12), channel_id=1, source_target_pairs={{0,0},{1,32},{2,2},{3,34},{4,4},{5,36},{6,6},{7,38},{8,8},{9,40},{... | collective-permute-start | bytes 98312 | tf_op jit(solution)/shard_map/ppermute | solution.py:60
  27.9 13.6 %collective-permute-start.5 = (bf16[256,512]{1,0:T(8,128)(2,1)S(1)}, bf16[256,512]{1,0:T(8,128)(2,1)S(1)}, u32[]{:S(2)}, u32[]{:S(2)}) collective-permute-start(bf16[256,512]{1,0:T(8,128)(2,1)S(1)} %bitcast_multiply_fusion), channel_id=1, source_target_pairs={{0,16},{16,0},{1,17},{17,1},{2,18},{18,2},{3,19},{19,3},{4,20},{20... | collective-permute-start | bytes 786440 | tf_op jit(solution)/shard_map/ppermute | solution.py:29
  30.9 28.5 %all-to-all-start.1 = ((bf16[16,64,512]{2,1,0:T(8,128)(2,1)}), bf16[16,64,512]{2,1,0:T(8,128)(2,1)S(1)}, u32[]{:S(2)}, u32[]{:S(2)}) async-start(bf16[16,64,512]{2,1,0:T(8,128)(2,1)} %broadcast_in_dim.10), calls=%async_computation.1 | async-start | bytes 2097152 | tf_op jit(solution)/shard_map/all_to_all | solution.py:46
  35.6 3.0 %copy-start.3 = (f32[512]{0:T(512)S(1)}, f32[512]{0:T(512)}, u32[]{:S(2)}) copy-start(f32[512]{0:T(512)} %param.14) | copy-start | bytes 6148
  38.8 11.3 %collective-permute-start.3 = (bf16[256,512]{1,0:T(8,128)(2,1)S(1)}, bf16[256,512]{1,0:T(8,128)(2,1)S(1)}, u32[]{:S(2)}, u32[]{:S(2)}) collective-permute-start(bf16[256,512]{1,0:T(8,128)(2,1)S(1)} %fusion.6), channel_id=1, source_target_pairs={{0,16},{16,0},{1,17},{17,1},{2,18},{18,2},{3,19},{19,3},{4,20},{20... | collective-permute-start | bytes 786440 | tf_op jit(solution)/shard_map/ppermute | solution.py:29
  41.6 14.1 %collective-permute-start.6 = (bf16[2,256,512]{2,1,0:T(8,128)(2,1)S(1)}, bf16[2,256,512]{2,1,0:T(8,128)(2,1)S(1)}, u32[]{:S(2)}, u32[]{:S(2)}) collective-permute-start(bf16[2,256,512]{2,1,0:T(8,128)(2,1)S(1)} %pad_maximum_fusion.3), channel_id=1, source_target_pairs={{0,1},{1,0},{2,3},{3,2},{4,5},{5,4},{6,7},{7,6},{8,9},{9,8},{10,11... | collective-permute-start | bytes 1572872 | tf_op jit(solution)/shard_map/ppermute | solution.py:29
  50.1 7.1 %collective-permute-start.4 = (bf16[2,256,512]{2,1,0:T(8,128)(2,1)S(1)}, bf16[2,256,512]{2,1,0:T(8,128)(2,1)S(1)}, u32[]{:S(2)}, u32[]{:S(2)}) collective-permute-start(bf16[2,256,512]{2,1,0:T(8,128)(2,1)S(1)} %pad_maximum_fusion.2), channel_id=1, source_target_pairs={{0,1},{1,0},{2,3},{3,2},{4,5},{5,4},{6,7},{7,6},{8,9},{9,8},{10,11... | collective-permute-start | bytes 1572872 | tf_op jit(solution)/shard_map/ppermute | solution.py:29
  66.1 28.1 %all-to-all-start.2 = ((bf16[64,8,512]{2,1,0:T(8,128)(2,1)}), bf16[64,8,512]{2,1,0:T(8,128)(2,1)S(1)}, u32[]{:S(2)}, u32[]{:S(2)}) async-start(bf16[64,8,512]{2,1,0:T(8,128)(2,1)} %fusion), calls=%async_computation.2 | async-start | bytes 1048576 | tf_op jit(solution)/shard_map/all_to_all | solution.py:183
  79.1 15.1 %copy-start.1 = (f32[1,8,2048]{2,1,0:T(8,128)S(1)}, f32[1,8,2048]{2,1,0:T(8,128)}, u32[]{:S(2)}) copy-start(f32[1,8,2048]{2,1,0:T(8,128)} %param.16) | copy-start | bytes 196612
  79.2 15.1 %copy-start.2 = (s32[2048,32]{0,1:T(8,128)S(1)}, s32[2048,32]{0,1:T(8,128)}, u32[]{:S(2)}) copy-start(s32[2048,32]{0,1:T(8,128)} %param.17) | copy-start | bytes 786436
  80.3 15.0 %collective-permute-start.7 = (f32[2,256,512]{2,1,0:T(8,128)}, f32[2,256,512]{2,1,0:T(8,128)S(1)}, u32[]{:S(2)}, u32[]{:S(2)}) collective-permute-start(f32[2,256,512]{2,1,0:T(8,128)} %bitcast.61), channel_id=1, source_target_pairs={{0,1},{1,0},{2,3},{3,2},{4,5},{5,4},{6,7},{7,6},{8,9},{9,8},{10,11... | collective-permute-start | bytes 3145736 | tf_op jit(solution)/shard_map/ppermute | solution.py:29
  95.5 16.6 %all-to-all-start.3 = ((f32[16,8,160]{2,1,0:T(8,128)}), f32[16,8,160]{2,1,0:T(8,128)S(1)}, u32[]{:S(2)}, u32[]{:S(2)}) async-start(f32[16,8,160]{2,1,0:T(8,128)} %pad_maximum_fusion.4), calls=%async_computation.3 | async-start | bytes 262144 | tf_op jit(solution)/shard_map/all_to_all | solution.py:201
  103.0 9.8 %collective-permute-start.8 = (bf16[256,512]{1,0:T(8,128)(2,1)S(1)}, bf16[256,512]{1,0:T(8,128)(2,1)S(1)}, u32[]{:S(2)}, u32[]{:S(2)}) collective-permute-start(bf16[256,512]{1,0:T(8,128)(2,1)S(1)} %fusion.39), channel_id=1, source_target_pairs={{0,16},{16,0},{1,17},{17,1},{2,18},{18,2},{3,19},{19,3},{4,20},{20... | collective-permute-start | bytes 786440 | tf_op jit(solution)/shard_map/ppermute | solution.py:29
  113.5 16.6 %all-to-all-start.4 = ((bf16[32,16,384]{2,1,0:T(8,128)(2,1)}), bf16[32,16,384]{2,1,0:T(8,128)(2,1)S(1)}, u32[]{:S(2)}, u32[]{:S(2)}) async-start(bf16[32,16,384]{2,1,0:T(8,128)(2,1)} %broadcast_in_dim.14), calls=%async_computation.4 | async-start | bytes 786432 | tf_op jit(solution)/shard_map/all_to_all | solution.py:46
  134.2 18.7 %all-to-all-start.5 = ((f32[16,8,128]{2,1,0:T(8,128)}), f32[16,8,128]{2,1,0:T(8,128)S(1)}, u32[]{:S(2)}, u32[]{:S(2)}) async-start(f32[16,8,128]{2,1,0:T(8,128)} %tail.1), calls=%async_computation.5 | async-start | bytes 131072 | tf_op jit(solution)/shard_map/all_to_all | solution.py:218

commit v5 on v4

--- a/solution.py
+++ b/solution.py
@@ -29,16 +29,123 @@
     return lax.ppermute(block, axis, [(0, 1), (1, 0)])
 
 
-def group_frames(block):
-    pair = jnp.stack([block, swap(block, "xl")])
-    return jnp.concatenate([pair, swap(pair, "c")]).reshape(-1, block.shape[1])
-
-
 def layer_norm(stream, norm_gain):
     values = stream.astype(jnp.float32)
     center = jnp.mean(values, axis=1, keepdims=True)
     spread = jnp.mean((values - center) ** 2, axis=1, keepdims=True)
     return ((values - center) * lax.rsqrt(spread + 1e-05) * norm_gain).astype(jnp.bfloat16)
+
+
+def tokens_kernel(
+    tokens_ref, low_ref, high_ref, cotangent_ref, mask_ref, taps_ref, gain_ref, stream_ref, pack_ref, wide, held
+):
+    frames, features = tokens_ref.shape
+    edge = low_ref.shape[0]
+    taps = taps_ref.shape[0]
+    lanes = wide.shape[2]
+    for chunk in range(features // lanes):
+        columns = slice(chunk * lanes, (chunk + 1) * lanes)
+        wide[chunk, :edge] = low_ref[:, columns].astype(jnp.float32)
+        wide[chunk, edge : edge + frames] = tokens_ref[:, columns].astype(jnp.float32)
+        wide[chunk, edge + frames :] = high_ref[:, columns].astype(jnp.float32)
+    block = 64
+
+    @pl.loop(0, frames // block)
+    def _(step):
+        start = pl.multiple_of(step * block, block)
+        for chunk in range(features // lanes):
+            columns = slice(chunk * lanes, (chunk + 1) * lanes)
+            filtered = None
+            for k in range(taps):
+                shifted = wide[chunk, pl.ds(start + (edge - taps // 2 + k), block), :]
+                term = taps_ref[k : k + 1, columns] * shifted
+                filtered = term if filtered is None else filtered + term
+            middle = wide[chunk, pl.ds(start + edge, block), :]
+            held[pl.ds(start, block), columns] = middle + filtered * jax.nn.sigmoid(filtered)
+
+        stream = held[pl.ds(start, block), :].astype(jnp.bfloat16)
+        stream_ref[pl.ds(start, block), :] = stream
+        pack_ref[0, pl.ds(start, block), :] = layer_norm(stream, gain_ref[...])
+
+    mask = jnp.broadcast_to(mask_ref[...].astype(jnp.float32), (lanes, frames)).T
+    for chunk in range(features // lanes):
+        columns = slice(chunk * lanes, (chunk + 1) * lanes)
+        masked = cotangent_ref[:, columns].astype(jnp.float32) * mask
+        pack_ref[1, :, columns] = masked.astype(jnp.bfloat16)
+
+
+def tokens_part(tokens, low, high, cotangent, mask, taps, gain):
+    frames, features = tokens.shape
+    edge = low.shape[0]
+    return pl.pallas_call(
+        tokens_kernel,
+        out_shape=(
+            jax.ShapeDtypeStruct((frames, features), jnp.bfloat16),
+            jax.ShapeDtypeStruct((2, frames, features), jnp.bfloat16),
+        ),
+        scratch_shapes=[
+            pltpu.VMEM((features // 128, frames + 2 * edge, 128), jnp.float32),
+            pltpu.VMEM((frames, features), jnp.float32),
+        ],
+        compiler_params=pltpu.CompilerParams(vmem_limit_bytes=16 * 1024 * 1024),
+        cost_estimate=pl.CostEstimate(flops=8_000_000, bytes_accessed=1_500_000, transcendentals=0),
+        name="tokens_part",
+    )(tokens, low, high, cotangent, mask, taps, gain)
+
+
+def hidden_kernel(own_ref, x_ref, c_ref, xc_ref, whole_ref, grad_ref, hidden_ref, down_ref, up, delta):
+    half = whole_ref.shape[2] // 2
+    part = half // XL
+    for xh in range(XH):
+        for z in range(Z):
+            for xl in range(XL):
+                row = ((xh * XL + xl) * Z + z) * part
+                up[row : row + part] = whole_ref[xh, z, xl * part : (xl + 1) * part]
+            row = (z * XH + xh) * half
+            down_ref[row : row + half] = whole_ref[xh, z, half:]
+    frames = own_ref.shape[1]
+    for index, block in enumerate((own_ref, x_ref, c_ref, xc_ref)):
+        rows = slice(index * frames, (index + 1) * frames)
+        projected = jnp.dot(block[0], up[...], preferred_element_type=jnp.float32)
+        upstream = lax.dot_general(
+            block[1], down_ref[...], (((1,), (1,)), ((), ())), preferred_element_type=jnp.float32
+        )
+        squashed = jax.nn.sigmoid(projected)
+        hidden_ref[rows] = (projected * squashed).astype(jnp.bfloat16)
+        delta[rows] = (0.5 * upstream * squashed * (1.0 + projected * (1.0 - squashed))).astype(
+            jnp.bfloat16
+        )
+    total = None
+    for index, block in enumerate((own_ref, x_ref, c_ref, xc_ref)):
+        rows = slice(index * frames, (index + 1) * frames)
+        term = lax.dot_general(
+            block[0], delta[rows], (((0,), (0,)), ((), ())), preferred_element_type=jnp.float32
+        )
+        total = term if total is None else total + term
+    grad_ref[...] = total.astype(jnp.bfloat16)
+
+
+def hidden_part(own, x_block, c_block, xc_block, whole):
+    frames, features = own.shape[1:]
+    quarter = whole.shape[3]
+    blocks = XL * C
+    return pl.pallas_call(
+        hidden_kernel,
+        out_shape=(
+            jax.ShapeDtypeStruct((features, quarter), jnp.bfloat16),
+            jax.ShapeDtypeStruct((blocks * frames, quarter), jnp.bfloat16),
+            jax.ShapeDtypeStruct((quarter, features), jnp.bfloat16),
+        ),
+        scratch_shapes=[
+            pltpu.VMEM((features, quarter), jnp.bfloat16),
+            pltpu.VMEM((blocks * frames, quarter), jnp.bfloat16),
+        ],
+        compiler_params=pltpu.CompilerParams(vmem_limit_bytes=32 * 1024 * 1024),
+        cost_estimate=pl.CostEstimate(
+            flops=6 * blocks * frames * features * quarter, bytes_accessed=6_000_000, transcendentals=0
+        ),
+        name="hidden_part",
+    )(own, x_block, c_block, xc_block, whole)
 
 
 def gather_by_exchange(block, axis):
@@ -61,15 +168,6 @@
     up_split = up_weight.reshape(rows, QUARTERS, quarter).transpose(1, 0, 2)
     up_block = lax.all_to_all(up_split, GROUP, 0, 0, tiled=True).reshape(QUARTERS * rows, quarter)
     return jnp.concatenate([up_block, down_block], axis=0)
-
-
-def quarter_weights(block):
-    half, width = block.shape[0] // 2, block.shape[1]
-    whole = gather_by_exchange(block, GROUPS).reshape(XH, Z, 2 * half, width)
-    up = whole[:, :, :half].reshape(XH, Z, XL, half // XL, width)
-    up = up.transpose(0, 2, 1, 3, 4).reshape(-1, width)
-    down = whole[:, :, half:].transpose(1, 0, 2, 3).reshape(-1, width)
-    return up, down
 
 
 def top_bits(values):
@@ -142,36 +240,19 @@
     error_memory,
     seed_matrix,
 ):
-    half_width = kernel.shape[0] // 2
     frames, features = tokens.shape[1:]
-    low, high = halo(tokens[0], half_width)
-    masked = cotangent[0] * frame_mask[0][:, None].astype(jnp.bfloat16)
     block = quarter_block(up_weight, down_weight)
-    block, masked, low, high = lax.optimization_barrier((block, masked, low, high))
-    up, down = quarter_weights(block)
-    masked_all = group_frames(masked)
-
-    widened = jnp.concatenate([low, tokens[0], high], axis=0).astype(jnp.float32)
-    filtered = kernel[0] * widened[0:frames]
-    for offset in range(1, kernel.shape[0]):
-        filtered = filtered + kernel[offset] * widened[offset : offset + frames]
-    stream = (tokens[0].astype(jnp.float32) + filtered * jax.nn.sigmoid(filtered)).astype(
-        jnp.bfloat16
-    )
-    normed = layer_norm(stream, norm_gain)
-    normed_all = group_frames(normed)
-    projected = jnp.dot(normed_all, up, preferred_element_type=jnp.float32)
-    squashed = jax.nn.sigmoid(projected)
-    hidden = (projected * squashed).astype(jnp.bfloat16)
-    upstream = lax.dot_general(
-        masked_all, down, (((1,), (1,)), ((), ())), preferred_element_type=jnp.float32
-    )
-    delta_hidden = (0.5 * upstream * squashed * (1.0 + projected * (1.0 - squashed))).astype(
-        jnp.bfloat16
-    )
-    grad_part = lax.dot_general(
-        normed_all, delta_hidden, (((0,), (0,)), ((), ())), preferred_element_type=jnp.float32
-    ).astype(jnp.bfloat16)
+    low, high = halo(tokens[0], 16)
+    block, low, high = lax.optimization_barrier((block, low, high))
+    whole = gather_by_exchange(block, GROUPS).reshape(XH, Z, *block.shape)
+
+    stream, own = tokens_part(
+        tokens[0], low, high, cotangent[0], frame_mask, kernel, norm_gain[None]
+    )
+    x_block = swap(own, "xl")
+    c_block = swap(own, "c")
+    xc_block = swap(x_block, "c")
+    grad_part, hidden, down = hidden_part(own, x_block, c_block, xc_block, whole)
 
     mixed_part = jnp.dot(hidden, down, preferred_element_type=jnp.float32)
     mixed_part = mixed_part.reshape(C, XL, frames, features)

time: 155 us -> 158 us (1.019)
  waiting for transfers between devices: 42.7 us -> 59.7 us
  starting transfers between devices: 81.4 us -> 72.3 us
  matrix products: 9.07 us -> 0.97 us
  other arithmetic: 8.85 us -> 3.68 us
  Pallas kernels: 4.06 us -> 9.03 us
  local copies, waits for them, and re-layouts: 6.96 us -> 10.1 us
    ppermute x6 -> x5, waiting for transfers between devices: 4.95 us -> 19.8 us  [swap(): return lax.ppermute(block, axis, [(0, 1), (1, 0)])]
    ppermute x6 -> x5, starting transfers between devices: 19.8 us -> 11.7 us  [swap(): return lax.ppermute(block, axis, [(0, 1), (1, 0)])]
    dot_general x2 -> x0, matrix products: 6.49 us -> none  [the longest x1 4.44 us: per_device(): lax.dot_general(normed_all, delta_hidden, (((0,), (0,)), ((), ())), prefe...]
    all_to_all x2, starting transfers between devices: 10 us -> 16.2 us  [gather_by_exchange(): return lax.all_to_all(copies, axis, 0, 0, tiled=True)]
    unnamed x9 -> x27, local copies, waits for them, and re-layouts: 0.65 us -> 6.17 us
    pallas_call x0 -> x2, Pallas kernels: none -> 4.96 us  [the longest x1 2.86 us: hidden_part(): pl.pallas_call(hidden_kernel, out_shape=(jax.ShapeDtypeStruct((features,...]
    all_to_all x1, starting transfers between devices: 10.3 us -> 5.47 us  [quarter_block(): lax.all_to_all(up_split, GROUP, 0, 0, tiled=True)]
    reduce_sum x2 -> x0, other arithmetic: 2.99 us -> none  [the longest x1 2.78 us: layer_norm(): center = jnp.mean(values, axis=1, keepdims=True)]
  transfers between devices with their start and end apart: 15 -> 14, of which waited for: 8 -> 8; matrix products, arithmetic and copies ran while one was open for 10% -> 3% of each run, Pallas kernels for 0% -> 1%
where the time goes in v5:
time: 158 us; the launch traced here: 157 us
  starting transfers between devices  72.3 us (46%)
  waiting for transfers between devices  59.7 us (38%)
  local copies, waits for them, and re-layouts  10.1 us (6%)
  Pallas kernels  9.03 us (6%)
  other arithmetic  3.68 us (2%)
    ppermute x5, waiting for transfers between devices, swap(): return lax.ppermute(block, axis, [(0, 1), (1, 0)])  19.8 us
    all_to_all x2, starting transfers between devices, gather_by_exchange(): return lax.all_to_all(copies, axis, 0, 0, tiled=True)  16.2 us
    all_to_all x1, waiting for transfers between devices, per_device(): lax.all_to_all(grad_part.reshape(devices, rows, quarter), SEQ, 0, 0, tile...  13.1 us
    ppermute x5, starting transfers between devices, swap(): return lax.ppermute(block, axis, [(0, 1), (1, 0)])  11.7 us
    all_to_all x2, waiting for transfers between devices, gather_by_exchange(): return lax.all_to_all(copies, axis, 0, 0, tiled=True)  11.1 us
    all_to_all x1, starting transfers between devices, per_device(): compressed = lax.all_to_all(message, ('y', 'c'), 0, 0, tiled=True)  10.9 us
    all_to_all x1, starting transfers between devices, per_device(): lax.all_to_all(grad_part.reshape(devices, rows, quarter), SEQ, 0, 0, tile...  10.2 us
    all_to_all x1, starting transfers between devices, per_device(): arrived = lax.all_to_all(message, ('y', 'c'), 0, 0, tiled=True)  7.45 us
  transfers between devices with their start and end apart: 14, of which 8 were waited for; matrix products, arithmetic and copies ran while one was open for 3% of the time, Pallas kernels for 1%

profile of v5, /device:TPU:1, one launch (start us, length us, event | category | flops | bytes accessed | tf_op | source)
XLA Modules:
  0.0 156.8 jit_solution(354631118906725800)
XLA Ops:
  0.6 0.0 copy-start
  0.6 0.0 copy-start.1
  0.7 0.0 copy-start.3
  0.7 0.0 copy-start.2
  0.7 0.0 copy-start.4
  0.7 6.2 %collective-permute-start = (bf16[32,512]{1,0:T(8,128)(2,1)}, bf16[32,512]{1,0:T(8,128)(2,1)S(1)}, u32[]{:S(2)}, u32[]{:S(2)}) collective-permute-start(bf16[32,512]{1,0:T(8,128)(2,1)} %param.12), channel_id=1, source_target_pairs={{0,0},{1,32},{2,2},{3,34},{4,4},{5,36},{6,6},{7,38},{8,8},{9,40},{... | collective-permute-start | bytes 98312 | tf_op jit(solution)/shard_map/ppermute | solution.py:167
  6.9 5.5 %all-to-all-start = ((bf16[4,8,512]{2,1,0:T(8,128)(2,1)}), bf16[4,8,512]{2,1,0:T(8,128)(2,1)S(1)}, u32[]{:S(2)}, u32[]{:S(2)}) async-start(bf16[4,8,512]{2,1,0:T(8,128)(2,1)} %bitcast.75), calls=%async_computation | async-start | bytes 65536 | tf_op jit(solution)/shard_map/all_to_all | solution.py:169
  12.3 0.7 slice_bitcast_fusion
  13.1 1.9 %collective-permute-start.1 = (bf16[16,512]{1,0:T(8,128)(2,1)S(1)}, bf16[16,512]{1,0:T(8,128)(2,1)S(1)}, u32[]{:S(2)}, u32[]{:S(2)}) collective-permute-start(bf16[16,512]{1,0:T(8,128)(2,1)S(1)} %get-tuple-element.30), channel_id=1, source_target_pairs={{0,1},{1,2},{2,3},{3,4},{4,5},{5,6},{6,7},{7,8},{8,9},{9,10},{10,1... | collective-permute-start | bytes 49160 | tf_op jit(solution)/shard_map/ppermute | solution.py:23
  15.0 2.4 %collective-permute-start.2 = (bf16[16,512]{1,0:T(8,128)(2,1)S(1)}, bf16[16,512]{1,0:T(8,128)(2,1)S(1)}, u32[]{:S(2)}, u32[]{:S(2)}) collective-permute-start(bf16[16,512]{1,0:T(8,128)(2,1)S(1)} %get-tuple-element.29), channel_id=1, source_target_pairs={{1,0},{2,1},{3,2},{4,3},{5,4},{6,5},{7,6},{8,7},{9,8},{10,9},{11,1... | collective-permute-start | bytes 49160 | tf_op jit(solution)/shard_map/ppermute | solution.py:24
  17.4 0.0 all-to-all-done
  17.4 0.0 collective-permute-done
  17.4 0.0 collective-permute-done.1.low_ref
  17.4 2.6 %collective-permute-done.2.high_ref = bf16[16,512]{1,0:T(8,128)(2,1)S(1)} collective-permute-done((bf16[16,512]{1,0:T(8,128)(2,1)S(1)}, bf16[16,512]{1,0:T(8,128)(2,1)S(1)}, u32[]{:S(2)}, u32[]{:S(2)}) %collective-permute-start.2) | collective-permute-done | bytes 16416 | tf_op jit(solution)/shard_map/ppermute | solution.py:24
  20.1 1.1 broadcast_in_dim.13
  21.1 10.7 %all-to-all-start.1 = ((bf16[16,64,512]{2,1,0:T(8,128)(2,1)}), bf16[16,64,512]{2,1,0:T(8,128)(2,1)S(1)}, u32[]{:S(2)}, u32[]{:S(2)}) async-start(bf16[16,64,512]{2,1,0:T(8,128)(2,1)} %broadcast_in_dim.13), calls=%async_computation.1 | async-start | bytes 2097152 | tf_op jit(solution)/shard_map/all_to_all | solution.py:153
  31.8 0.0 copy-done
  31.8 0.0 copy-done.1
  31.8 0.0 copy-done.3
  31.8 0.0 copy-done.2
  31.9 0.0 copy-done.4
  31.9 2.1 %tokens_part.1 = (bf16[256,512]{1,0:T(8,128)(2,1)S(1)}, bf16[2,256,512]{2,1,0:T(8,128)(2,1)S(1)}) custom-call(bf16[256,512]{1,0:T(8,128)(2,1)S(1)} %bitcast.64, bf16[16,512]{1,0:T(8,128)(2,1)S(1)} %collective-permute-done.1.low_ref, bf16[16,512]{1,0:T(8,128)(2,1)S(1)} %collective-permute-done.2.high_ref, bf16[256,512]{1,0:T(8,128)(2,1)S(1)} %bitcast.65, ...), custom_call_target="tpu_custom_call" | custom-call | flops 8000000 | bytes 1500000 | tf_op jit(solution)/shard_map/tokens_part/pallas_call | solution.py:80
  34.0 2.0 %collective-permute-start.3 = (bf16[2,256,512]{2,1,0:T(8,128)(2,1)S(1)}, bf16[2,256,512]{2,1,0:T(8,128)(2,1)S(1)}, u32[]{:S(2)}, u32[]{:S(2)}) collective-permute-start(bf16[2,256,512]{2,1,0:T(8,128)(2,1)S(1)} %get-tuple-element.18.own_ref), channel_id=1, source_target_pairs={{0,16},{16,0},{1,17},{17,1},{2,18},{18,2},{3,19},{19,3},{4,20},{20... | collective-permute-start | bytes 1572872 | tf_op jit(solution)/shard_map/ppermute | solution.py:29
  36.0 2.3 %collective-permute-start.4 = (bf16[2,256,512]{2,1,0:T(8,128)(2,1)S(1)}, bf16[2,256,512]{2,1,0:T(8,128)(2,1)S(1)}, u32[]{:S(2)}, u32[]{:S(2)}) collective-permute-start(bf16[2,256,512]{2,1,0:T(8,128)(2,1)S(1)} %get-tuple-element.18.own_ref), channel_id=1, source_target_pairs={{0,1},{1,0},{2,3},{3,2},{4,5},{5,4},{6,7},{7,6},{8,9},{9,8},{10,11... | collective-permute-start | bytes 1572872 | tf_op jit(solution)/shard_map/ppermute | solution.py:29
  38.3 19.2 %collective-permute-done.3.x_ref = bf16[2,256,512]{2,1,0:T(8,128)(2,1)S(1)} collective-permute-done((bf16[2,256,512]{2,1,0:T(8,128)(2,1)S(1)}, bf16[2,256,512]{2,1,0:T(8,128)(2,1)S(1)}, u32[]{:S(2)}, u32[]{:S(2)}) %collective-permute-start.3) | collective-permute-done | bytes 524320 | tf_op jit(solution)/shard_map/ppermute | solution.py:29
  57.5 2.1 %collective-permute-start.5 = (bf16[2,256,512]{2,1,0:T(8,128)(2,1)S(1)}, bf16[2,256,512]{2,1,0:T(8,128)(2,1)S(1)}, u32[]{:S(2)}, u32[]{:S(2)}) collective-permute-start(bf16[2,256,512]{2,1,0:T(8,128)(2,1)S(1)} %collective-permute-done.3.x_ref), channel_id=1, source_target_pairs={{0,1},{1,0},{2,3},{3,2},{4,5},{5,4},{6,7},{7,6},{8,9},{9,8},{10,11... | collective-permute-start | bytes 1572872 | tf_op jit(solution)/shard_map/ppermute | solution.py:29
  59.5 0.0 copy-start.5
  59.5 0.8 copy-done.5
  60.3 0.0 collective-permute-done.4.c_ref
  60.3 0.8 copy-done.7
  61.1 0.1 collective-permute-done.5.xc_ref
  61.3 0.8 copy-done.9
  62.1 0.0 all-to-all-done.1
  62.1 1.0 copy-done.6
  63.1 1.0 copy-done.8
  64.1 1.0 copy-done.10
  65.2 2.9 %hidden_part.1 = (bf16[512,512]{1,0:T(8,128)(2,1)}, bf16[1024,512]{1,0:T(8,128)(2,1)S(1)}, bf16[512,512]{1,0:T(8,128)(2,1)S(1)}) custom-call(bf16[2,256,512]{2,1,0:T(8,128)(2,1)S(1)} %get-tuple-element.18.own_ref, bf16[2,256,512]{2,1,0:T(8,128)(2,1)S(1)} %copy-done.6, bf16[2,256,512]{2,1,0:T(8,128)(2,1)S(1)} %copy-done.8, ...), custom_call_target="tpu_custom_call" | custom-call | flops 1610612736 | bytes 6000000 | tf_op jit(solution)/shard_map/hidden_part/pallas_call | solution.py:132
  68.0 10.2 %all-to-all-start.2 = ((bf16[64,8,512]{2,1,0:T(8,128)(2,1)}), bf16[64,8,512]{2,1,0:T(8,128)(2,1)S(1)}, u32[]{:S(2)}, u32[]{:S(2)}) async-start(bf16[64,8,512]{2,1,0:T(8,128)(2,1)} %bitcast.9), calls=%async_computation.2 | async-start | bytes 1048576 | tf_op jit(solution)/shard_map/all_to_all | solution.py:264
  78.3 0.7 fusion.16
  79.0 0.0 copy-start.11
  79.0 0.0 copy-start.12
  79.0 1.1 fusion.15
  80.1 2.4 %collective-permute-start.6 = (f32[2,256,512]{2,1,0:T(8,128)}, f32[2,256,512]{2,1,0:T(8,128)}, u32[]{:S(2)}, u32[]{:S(2)}) collective-permute-start(f32[2,256,512]{2,1,0:T(8,128)} %bitcast.20), channel_id=1, source_target_pairs={{0,1},{1,0},{2,3},{3,2},{4,5},{5,4},{6,7},{7,6},{8,9},{9,8},{10,11... | collective-permute-start | bytes 3145736 | tf_op jit(solution)/shard_map/ppermute | solution.py:29
  82.5 13.1 %all-to-all-done.2 = bf16[64,8,512]{2,1,0:T(8,128)(2,1)S(1)} async-done(((bf16[64,8,512]{2,1,0:T(8,128)(2,1)}), bf16[64,8,512]{2,1,0:T(8,128)(2,1)S(1)}, u32[]{:S(2)}, u32[]{:S(2)}) %all-to-all-start.2) | async-done | bytes 524320 | tf_op jit(solution)/shard_map/all_to_all | solution.py:264
  95.6 0.1 convert_reduce_fusion
  95.7 0.3 fusion.5
  96.0 0.1 broadcast_in_dim.14
  96.0 0.7 pad_maximum_fusion
  96.7 0.0 collective-permute-done.6
  96.7 1.4 add.26
  98.1 7.5 %all-to-all-start.3 = ((f32[16,8,160]{2,1,0:T(8,128)}), f32[16,8,160]{2,1,0:T(8,128)S(1)}, u32[]{:S(2)}, u32[]{:S(2)}) async-start(f32[16,8,160]{2,1,0:T(8,128)} %pad_maximum_fusion), calls=%async_computation.3 | async-start | bytes 262144 | tf_op jit(solution)/shard_map/all_to_all | solution.py:282
  105.6 2.9 %collective-permute-start.7 = (bf16[256,512]{1,0:T(8,128)(2,1)S(1)}, bf16[256,512]{1,0:T(8,128)(2,1)S(1)}, u32[]{:S(2)}, u32[]{:S(2)}) collective-permute-start(bf16[256,512]{1,0:T(8,128)(2,1)S(1)} %fusion.4), channel_id=1, source_target_pairs={{0,16},{16,0},{1,17},{17,1},{2,18},{18,2},{3,19},{19,3},{4,20},{20... | collective-permute-start | bytes 786440 | tf_op jit(solution)/shard_map/ppermute | solution.py:29
  108.6 6.2 %all-to-all-done.3 = f32[16,8,160]{2,1,0:T(8,128)S(1)} async-done(((f32[16,8,160]{2,1,0:T(8,128)}), f32[16,8,160]{2,1,0:T(8,128)S(1)}, u32[]{:S(2)}, u32[]{:S(2)}) %all-to-all-start.3) | async-done | bytes 81952 | tf_op jit(solution)/shard_map/all_to_all | solution.py:282
  114.8 0.1 concatenate.11
  114.9 0.5 collective-permute-done.7
  115.4 0.8 broadcast_in_dim.33
  116.2 5.5 %all-to-all-start.4 = ((bf16[32,16,384]{2,1,0:T(8,128)(2,1)}), bf16[32,16,384]{2,1,0:T(8,128)(2,1)S(1)}, u32[]{:S(2)}, u32[]{:S(2)}) async-start(bf16[32,16,384]{2,1,0:T(8,128)(2,1)} %broadcast_in_dim.33), calls=%async_computation.4 | async-start | bytes 786432 | tf_op jit(solution)/shard_map/all_to_all | solution.py:153
  121.7 11.1 %all-to-all-done.4 = bf16[32,16,384]{2,1,0:T(8,128)(2,1)S(1)} async-done(((bf16[32,16,384]{2,1,0:T(8,128)(2,1)}), bf16[32,16,384]{2,1,0:T(8,128)(2,1)S(1)}, u32[]{:S(2)}, u32[]{:S(2)}) %all-to-all-start.4) | async-done | bytes 393248 | tf_op jit(solution)/shard_map/all_to_all | solution.py:153
  132.7 4.1 %tail.1 = f32[16,8,128]{2,1,0:T(8,128)} custom-call(s32[1]{0:T(128)} %bitcast.26.chip_ref, bf16[512,384]{1,0:T(8,128)(2,1)S(1)} %bitcast.62), custom_call_target="tpu_custom_call" | custom-call | tf_op jit(solution)/shard_map/tail/pallas_call | solution.py:218
  136.8 10.9 %all-to-all-start.5 = ((f32[16,8,128]{2,1,0:T(8,128)}), f32[16,8,128]{2,1,0:T(8,128)S(1)}, u32[]{:S(2)}, u32[]{:S(2)}) async-start(f32[16,8,128]{2,1,0:T(8,128)} %tail.1), calls=%async_computation.5 | async-start | bytes 131072 | tf_op jit(solution)/shard_map/all_to_all | solution.py:299
  147.7 0.8 fusion.3
  148.5 7.0 %all-to-all-done.5 = f32[16,8,128]{2,1,0:T(8,128)S(1)} async-done(((f32[16,8,128]{2,1,0:T(8,128)}), f32[16,8,128]{2,1,0:T(8,128)S(1)}, u32[]{:S(2)}, u32[]{:S(2)}) %all-to-all-start.5) | async-done | bytes 65568 | tf_op jit(solution)/shard_map/all_to_all | solution.py:299
  155.5 0.6 bitcast_subtract_fusion
  156.1 0.6 copy.13
  (15 shorter events, 0.1 us)
Async XLA Ops:
  0.6 31.2 %copy-start = (bf16[1,256,512]{2,1,0:T(8,128)(2,1)S(1)}, bf16[1,256,512]{2,1,0:T(8,128)(2,1)}, u32[]{:S(2)}) copy-start(bf16[1,256,512]{2,1,0:T(8,128)(2,1)} %param.9) | copy-start | bytes 786436
  0.6 31.2 %copy-start.1 = (bf16[1,256,512]{2,1,0:T(8,128)(2,1)S(1)}, bf16[1,256,512]{2,1,0:T(8,128)(2,1)}, u32[]{:S(2)}) copy-start(bf16[1,256,512]{2,1,0:T(8,128)(2,1)} %param.10) | copy-start | bytes 786436
  0.7 31.2 %copy-start.3 = (f32[512]{0:T(512)S(1)}, f32[512]{0:T(512)}, u32[]{:S(2)}) copy-start(f32[512]{0:T(512)} %param.14) | copy-start | bytes 6148
  0.7 31.2 %copy-start.2 = (f32[31,512]{1,0:T(8,128)S(1)}, f32[31,512]{1,0:T(8,128)}, u32[]{:S(2)}) copy-start(f32[31,512]{1,0:T(8,128)} %taps_ref.1) | copy-start | bytes 190468
  0.7 31.2 %copy-start.4 = (s32[1,256]{1,0:T(1,128)S(1)}, s32[1,256]{1,0:T(1,128)}, u32[]{:S(2)}) copy-start(s32[1,256]{1,0:T(1,128)} %mask_ref.1) | copy-start | bytes 3076
  0.7 16.7 %collective-permute-start = (bf16[32,512]{1,0:T(8,128)(2,1)}, bf16[32,512]{1,0:T(8,128)(2,1)S(1)}, u32[]{:S(2)}, u32[]{:S(2)}) collective-permute-start(bf16[32,512]{1,0:T(8,128)(2,1)} %param.12), channel_id=1, source_target_pairs={{0,0},{1,32},{2,2},{3,34},{4,4},{5,36},{6,6},{7,38},{8,8},{9,40},{... | collective-permute-start | bytes 98312 | tf_op jit(solution)/shard_map/ppermute | solution.py:167
  6.9 10.5 %all-to-all-start = ((bf16[4,8,512]{2,1,0:T(8,128)(2,1)}), bf16[4,8,512]{2,1,0:T(8,128)(2,1)S(1)}, u32[]{:S(2)}, u32[]{:S(2)}) async-start(bf16[4,8,512]{2,1,0:T(8,128)(2,1)} %bitcast.75), calls=%async_computation | async-start | bytes 65536 | tf_op jit(solution)/shard_map/all_to_all | solution.py:169
  13.1 4.4 %collective-permute-start.1 = (bf16[16,512]{1,0:T(8,128)(2,1)S(1)}, bf16[16,512]{1,0:T(8,128)(2,1)S(1)}, u32[]{:S(2)}, u32[]{:S(2)}) collective-permute-start(bf16[16,512]{1,0:T(8,128)(2,1)S(1)} %get-tuple-element.30), channel_id=1, source_target_pairs={{0,1},{1,2},{2,3},{3,4},{4,5},{5,6},{6,7},{7,8},{8,9},{9,10},{10,1... | collective-permute-start | bytes 49160 | tf_op jit(solution)/shard_map/ppermute | solution.py:23
  15.0 5.1 %collective-permute-start.2 = (bf16[16,512]{1,0:T(8,128)(2,1)S(1)}, bf16[16,512]{1,0:T(8,128)(2,1)S(1)}, u32[]{:S(2)}, u32[]{:S(2)}) collective-permute-start(bf16[16,512]{1,0:T(8,128)(2,1)S(1)} %get-tuple-element.29), channel_id=1, source_target_pairs={{1,0},{2,1},{3,2},{4,3},{5,4},{6,5},{7,6},{8,7},{9,8},{10,9},{11,1... | collective-permute-start | bytes 49160 | tf_op jit(solution)/shard_map/ppermute | solution.py:24
  21.1 40.9 %all-to-all-start.1 = ((bf16[16,64,512]{2,1,0:T(8,128)(2,1)}), bf16[16,64,512]{2,1,0:T(8,128)(2,1)S(1)}, u32[]{:S(2)}, u32[]{:S(2)}) async-start(bf16[16,64,512]{2,1,0:T(8,128)(2,1)} %broadcast_in_dim.13), calls=%async_computation.1 | async-start | bytes 2097152 | tf_op jit(solution)/shard_map/all_to_all | solution.py:153
  34.0 23.5 %collective-permute-start.3 = (bf16[2,256,512]{2,1,0:T(8,128)(2,1)S(1)}, bf16[2,256,512]{2,1,0:T(8,128)(2,1)S(1)}, u32[]{:S(2)}, u32[]{:S(2)}) collective-permute-start(bf16[2,256,512]{2,1,0:T(8,128)(2,1)S(1)} %get-tuple-element.18.own_ref), channel_id=1, source_target_pairs={{0,16},{16,0},{1,17},{17,1},{2,18},{18,2},{3,19},{19,3},{4,20},{20... | collective-permute-start | bytes 1572872 | tf_op jit(solution)/shard_map/ppermute | solution.py:29
  36.0 24.4 %collective-permute-start.4 = (bf16[2,256,512]{2,1,0:T(8,128)(2,1)S(1)}, bf16[2,256,512]{2,1,0:T(8,128)(2,1)S(1)}, u32[]{:S(2)}, u32[]{:S(2)}) collective-permute-start(bf16[2,256,512]{2,1,0:T(8,128)(2,1)S(1)} %get-tuple-element.18.own_ref), channel_id=1, source_target_pairs={{0,1},{1,0},{2,3},{3,2},{4,5},{5,4},{6,7},{7,6},{8,9},{9,8},{10,11... | collective-permute-start | bytes 1572872 | tf_op jit(solution)/shard_map/ppermute | solution.py:29
  57.5 3.8 %collective-permute-start.5 = (bf16[2,256,512]{2,1,0:T(8,128)(2,1)S(1)}, bf16[2,256,512]{2,1,0:T(8,128)(2,1)S(1)}, u32[]{:S(2)}, u32[]{:S(2)}) collective-permute-start(bf16[2,256,512]{2,1,0:T(8,128)(2,1)S(1)} %collective-permute-done.3.x_ref), channel_id=1, source_target_pairs={{0,1},{1,0},{2,3},{3,2},{4,5},{5,4},{6,7},{7,6},{8,9},{9,8},{10,11... | collective-permute-start | bytes 1572872 | tf_op jit(solution)/shard_map/ppermute | solution.py:29
  59.5 0.8 copy-start.5
  60.3 0.8 copy-start.7
  61.2 0.8 copy-start.9
  62.1 1.0 copy-start.6
  63.1 1.0 copy-start.8
  64.1 1.0 copy-start.10
  68.0 27.5 %all-to-all-start.2 = ((bf16[64,8,512]{2,1,0:T(8,128)(2,1)}), bf16[64,8,512]{2,1,0:T(8,128)(2,1)S(1)}, u32[]{:S(2)}, u32[]{:S(2)}) async-start(bf16[64,8,512]{2,1,0:T(8,128)(2,1)} %bitcast.9), calls=%async_computation.2 | async-start | bytes 1048576 | tf_op jit(solution)/shard_map/all_to_all | solution.py:264
  79.0 16.7 %copy-start.11 = (f32[1,8,2048]{2,1,0:T(8,128)S(1)}, f32[1,8,2048]{2,1,0:T(8,128)}, u32[]{:S(2)}) copy-start(f32[1,8,2048]{2,1,0:T(8,128)} %param.16) | copy-start | bytes 196612
  79.0 16.7 %copy-start.12 = (s32[2048,32]{0,1:T(8,128)S(1)}, s32[2048,32]{0,1:T(8,128)}, u32[]{:S(2)}) copy-start(s32[2048,32]{0,1:T(8,128)} %param.17) | copy-start | bytes 786436
  80.1 16.6 %collective-permute-start.6 = (f32[2,256,512]{2,1,0:T(8,128)}, f32[2,256,512]{2,1,0:T(8,128)}, u32[]{:S(2)}, u32[]{:S(2)}) collective-permute-start(f32[2,256,512]{2,1,0:T(8,128)} %bitcast.20), channel_id=1, source_target_pairs={{0,1},{1,0},{2,3},{3,2},{4,5},{5,4},{6,7},{7,6},{8,9},{9,8},{10,11... | collective-permute-start | bytes 3145736 | tf_op jit(solution)/shard_map/ppermute | solution.py:29
  98.1 16.6 %all-to-all-start.3 = ((f32[16,8,160]{2,1,0:T(8,128)}), f32[16,8,160]{2,1,0:T(8,128)S(1)}, u32[]{:S(2)}, u32[]{:S(2)}) async-start(f32[16,8,160]{2,1,0:T(8,128)} %pad_maximum_fusion), calls=%async_computation.3 | async-start | bytes 262144 | tf_op jit(solution)/shard_map/all_to_all | solution.py:282
  105.6 9.8 %collective-permute-start.7 = (bf16[256,512]{1,0:T(8,128)(2,1)S(1)}, bf16[256,512]{1,0:T(8,128)(2,1)S(1)}, u32[]{:S(2)}, u32[]{:S(2)}) collective-permute-start(bf16[256,512]{1,0:T(8,128)(2,1)S(1)} %fusion.4), channel_id=1, source_target_pairs={{0,16},{16,0},{1,17},{17,1},{2,18},{18,2},{3,19},{19,3},{4,20},{20... | collective-permute-start | bytes 786440 | tf_op jit(solution)/shard_map/ppermute | solution.py:29
  116.2 16.6 %all-to-all-start.4 = ((bf16[32,16,384]{2,1,0:T(8,128)(2,1)}), bf16[32,16,384]{2,1,0:T(8,128)(2,1)S(1)}, u32[]{:S(2)}, u32[]{:S(2)}) async-start(bf16[32,16,384]{2,1,0:T(8,128)(2,1)} %broadcast_in_dim.33), calls=%async_computation.4 | async-start | bytes 786432 | tf_op jit(solution)/shard_map/all_to_all | solution.py:153
  136.8 18.7 %all-to-all-start.5 = ((f32[16,8,128]{2,1,0:T(8,128)}), f32[16,8,128]{2,1,0:T(8,128)S(1)}, u32[]{:S(2)}, u32[]{:S(2)}) async-start(f32[16,8,128]{2,1,0:T(8,128)} %tail.1), calls=%async_computation.5 | async-start | bytes 131072 | tf_op jit(solution)/shard_map/all_to_all | solution.py:299

commit v6 on v5

--- a/solution.py
+++ b/solution.py
@@ -8,6 +8,7 @@
 
 Y, XH, XL, Z, C = 8, 2, 2, 8, 2
 RANK = 32
+MASK_ROWS = 16
 CHIP = ("xh", "xl", "z")
 SEQ = ("xh", "xl", "z", "c")
 GROUP = ("xl", "c")
@@ -37,7 +38,7 @@
 
 
 def tokens_kernel(
-    tokens_ref, low_ref, high_ref, cotangent_ref, mask_ref, taps_ref, gain_ref, stream_ref, pack_ref, wide, held
+    tokens_ref, low_ref, high_ref, mask_ref, taps_ref, gain_ref, stream_ref, pack_ref, wide, held
 ):
     frames, features = tokens_ref.shape
     edge = low_ref.shape[0]
@@ -65,35 +66,35 @@
 
         stream = held[pl.ds(start, block), :].astype(jnp.bfloat16)
         stream_ref[pl.ds(start, block), :] = stream
-        pack_ref[0, pl.ds(start, block), :] = layer_norm(stream, gain_ref[...])
-
-    mask = jnp.broadcast_to(mask_ref[...].astype(jnp.float32), (lanes, frames)).T
-    for chunk in range(features // lanes):
-        columns = slice(chunk * lanes, (chunk + 1) * lanes)
-        masked = cotangent_ref[:, columns].astype(jnp.float32) * mask
-        pack_ref[1, :, columns] = masked.astype(jnp.bfloat16)
-
-
-def tokens_part(tokens, low, high, cotangent, mask, taps, gain):
+        pack_ref[pl.ds(start, block), :] = layer_norm(stream, gain_ref[...])
+
+    mask = jnp.broadcast_to(mask_ref[...].astype(jnp.float32), (MASK_ROWS, frames))
+    pack_ref[frames:, :frames] = mask.astype(jnp.bfloat16)
+    pack_ref[frames:, frames:] = jnp.zeros((MASK_ROWS, features - frames), jnp.bfloat16)
+
+
+def tokens_part(tokens, low, high, mask, taps, gain):
     frames, features = tokens.shape
     edge = low.shape[0]
     return pl.pallas_call(
         tokens_kernel,
         out_shape=(
             jax.ShapeDtypeStruct((frames, features), jnp.bfloat16),
-            jax.ShapeDtypeStruct((2, frames, features), jnp.bfloat16),
+            jax.ShapeDtypeStruct((frames + MASK_ROWS, features), jnp.bfloat16),
         ),
         scratch_shapes=[
             pltpu.VMEM((features // 128, frames + 2 * edge, 128), jnp.float32),
             pltpu.VMEM((frames, features), jnp.float32),
         ],
-        compiler_params=pltpu.CompilerParams(vmem_limit_bytes=16 * 1024 * 1024),
+        compiler_params=pltpu.CompilerParams(vmem_limit_bytes=48 * 1024 * 1024),
         cost_estimate=pl.CostEstimate(flops=8_000_000, bytes_accessed=1_500_000, transcendentals=0),
         name="tokens_part",
-    )(tokens, low, high, cotangent, mask, taps, gain)
-
-
-def hidden_kernel(own_ref, x_ref, c_ref, xc_ref, whole_ref, grad_ref, hidden_ref, down_ref, up, delta):
+    )(tokens, low, high, mask, taps, gain)
+
+
+def hidden_kernel(
+    packs_ref, cotangents_ref, whole_ref, grad_ref, hidden_ref, down_ref, up, delta, masked
+):
     half = whole_ref.shape[2] // 2
     part = half // XL
     for xh in range(XH):
@@ -103,12 +104,23 @@
                 up[row : row + part] = whole_ref[xh, z, xl * part : (xl + 1) * part]
             row = (z * XH + xh) * half
             down_ref[row : row + half] = whole_ref[xh, z, half:]
-    frames = own_ref.shape[1]
-    for index, block in enumerate((own_ref, x_ref, c_ref, xc_ref)):
+    blocks, frames, features = cotangents_ref.shape
+    lanes = 128
+    for index in range(blocks):
         rows = slice(index * frames, (index + 1) * frames)
-        projected = jnp.dot(block[0], up[...], preferred_element_type=jnp.float32)
+        mask = packs_ref[index, frames:, :frames][:1].astype(jnp.float32)
+        mask = jnp.broadcast_to(mask, (lanes, frames)).T
+        for chunk in range(features // lanes):
+            columns = slice(chunk * lanes, (chunk + 1) * lanes)
+            kept = cotangents_ref[index, :, columns].astype(jnp.float32) * mask
+            masked[:, columns] = kept.astype(jnp.bfloat16)
+        normed = packs_ref[index, :frames]
+        projected = jnp.dot(normed, up[...], preferred_element_type=jnp.float32)
         upstream = lax.dot_general(
-            block[1], down_ref[...], (((1,), (1,)), ((), ())), preferred_element_type=jnp.float32
+            masked[...],
+            down_ref[...],
+            (((1,), (1,)), ((), ())),
+            preferred_element_type=jnp.float32,
         )
         squashed = jax.nn.sigmoid(projected)
         hidden_ref[rows] = (projected * squashed).astype(jnp.bfloat16)
@@ -116,36 +128,45 @@
             jnp.bfloat16
         )
     total = None
-    for index, block in enumerate((own_ref, x_ref, c_ref, xc_ref)):
+    for index in range(blocks):
         rows = slice(index * frames, (index + 1) * frames)
         term = lax.dot_general(
-            block[0], delta[rows], (((0,), (0,)), ((), ())), preferred_element_type=jnp.float32
+            packs_ref[index, :frames],
+            delta[rows],
+            (((0,), (0,)), ((), ())),
+            preferred_element_type=jnp.float32,
         )
         total = term if total is None else total + term
     grad_ref[...] = total.astype(jnp.bfloat16)
 
 
-def hidden_part(own, x_block, c_block, xc_block, whole):
-    frames, features = own.shape[1:]
+def hidden_part(packs, cotangents, whole):
+    blocks, frames, features = cotangents.shape
     quarter = whole.shape[3]
-    blocks = XL * C
+    bf16 = jnp.bfloat16
     return pl.pallas_call(
         hidden_kernel,
         out_shape=(
-            jax.ShapeDtypeStruct((features, quarter), jnp.bfloat16),
-            jax.ShapeDtypeStruct((blocks * frames, quarter), jnp.bfloat16),
-            jax.ShapeDtypeStruct((quarter, features), jnp.bfloat16),
+            jax.ShapeDtypeStruct((features, quarter), bf16),
+            jax.ShapeDtypeStruct((blocks * frames, quarter), bf16),
+            jax.ShapeDtypeStruct((quarter, features), bf16),
         ),
         scratch_shapes=[
-            pltpu.VMEM((features, quarter), jnp.bfloat16),
-            pltpu.VMEM((blocks * frames, quarter), jnp.bfloat16),
+            pltpu.VMEM((features, quarter), bf16),
+            pltpu.VMEM((blocks * frames, quarter), bf16),
+            pltpu.VMEM((frames, features), bf16),
         ],
-        compiler_params=pltpu.CompilerParams(vmem_limit_bytes=32 * 1024 * 1024),
+        compiler_params=pltpu.CompilerParams(vmem_limit_bytes=16 * 1024 * 1024),
         cost_estimate=pl.CostEstimate(
             flops=6 * blocks * frames * features * quarter, bytes_accessed=6_000_000, transcendentals=0
         ),
         name="hidden_part",
-    )(own, x_block, c_block, xc_block, whole)
+    )(packs, cotangents, whole)
+
+
+def group_frames(block, x_block):
+    pair = jnp.stack([block, x_block])
+    return jnp.concatenate([pair, swap(pair, "c")])
 
 
 def gather_by_exchange(block, axis):
@@ -241,18 +262,15 @@
     seed_matrix,
 ):
     frames, features = tokens.shape[1:]
+    cotangent_x = swap(cotangent[0], "xl")
+    low, high = halo(tokens[0], 16)
     block = quarter_block(up_weight, down_weight)
-    low, high = halo(tokens[0], 16)
-    block, low, high = lax.optimization_barrier((block, low, high))
+    block, low, high, cotangent_x = lax.optimization_barrier((block, low, high, cotangent_x))
     whole = gather_by_exchange(block, GROUPS).reshape(XH, Z, *block.shape)
-
-    stream, own = tokens_part(
-        tokens[0], low, high, cotangent[0], frame_mask, kernel, norm_gain[None]
-    )
-    x_block = swap(own, "xl")
-    c_block = swap(own, "c")
-    xc_block = swap(x_block, "c")
-    grad_part, hidden, down = hidden_part(own, x_block, c_block, xc_block, whole)
+    stream, own = tokens_part(tokens[0], low, high, frame_mask, kernel, norm_gain[None])
+    packs = group_frames(own, swap(own, "xl"))
+    cotangents = group_frames(cotangent[0], cotangent_x)
+    grad_part, hidden, down = hidden_part(packs, cotangents, whole)
 
     mixed_part = jnp.dot(hidden, down, preferred_element_type=jnp.float32)
     mixed_part = mixed_part.reshape(C, XL, frames, features)
@@ -289,7 +307,6 @@
         ],
         axis=1,
     )
-    packed, other_chip = lax.optimization_barrier((packed, other_chip))
     mixed = (
         stream.astype(jnp.float32) + 0.5 * (chip_part[0] + other_chip.astype(jnp.float32))
     ).astype(jnp.bfloat16)

time: 158 us -> 147 us (0.930)
  blocking collectives: 0 us -> 16.4 us
  starting transfers between devices: 72.3 us -> 57.3 us
  waiting for transfers between devices: 59.7 us -> 51.9 us
  local copies, waits for them, and re-layouts: 10.1 us -> 7.48 us
    all_to_all x0 -> x1, blocking collectives: none -> 16.4 us  [per_device(): arrived = lax.all_to_all(message, ('y', 'c'), 0, 0, tiled=True)]
    ppermute x5 -> x6, waiting for transfers between devices: 19.8 us -> 11.9 us  [swap(): return lax.ppermute(block, axis, [(0, 1), (1, 0)])]
    all_to_all x1 -> x0, starting transfers between devices: 7.45 us -> none  [per_device(): arrived = lax.all_to_all(message, ('y', 'c'), 0, 0, tiled=True)]
    all_to_all x1 -> x0, waiting for transfers between devices: 6.18 us -> none  [per_device(): arrived = lax.all_to_all(message, ('y', 'c'), 0, 0, tiled=True)]
    all_to_all x2, waiting for transfers between devices: 11.1 us -> 17.2 us  [gather_by_exchange(): return lax.all_to_all(copies, axis, 0, 0, tiled=True)]
    all_to_all x1, starting transfers between devices: 10.9 us -> 5.24 us  [per_device(): compressed = lax.all_to_all(message, ('y', 'c'), 0, 0, tiled=True)]
    all_to_all x1, starting transfers between devices: 10.2 us -> 5.56 us  [per_device(): lax.all_to_all(grad_part.reshape(devices, rows, quarter), SEQ, 0, 0, tile...]
    ppermute x5 -> x6, starting transfers between devices: 11.7 us -> 15.5 us  [swap(): return lax.ppermute(block, axis, [(0, 1), (1, 0)])]
  transfers between devices with their start and end apart: 14 -> 14, of which waited for: 8 -> 7; matrix products, arithmetic and copies ran while one was open for 3% -> 4% of each run, Pallas kernels for 1% -> 4%
where the time goes in v6:
time: 147 us; the launch traced here: 146 us
  starting transfers between devices  57.3 us (39%)
  waiting for transfers between devices  51.9 us (35%)
  blocking collectives  16.4 us (11%)
  Pallas kernels  8.25 us (6%)
  local copies, waits for them, and re-layouts  7.48 us (5%)
  other arithmetic  3.11 us (2%)
    all_to_all x2, waiting for transfers between devices, gather_by_exchange(): return lax.all_to_all(copies, axis, 0, 0, tiled=True)  17.2 us
    all_to_all x2, starting transfers between devices, gather_by_exchange(): return lax.all_to_all(copies, axis, 0, 0, tiled=True)  16.6 us
    all_to_all x1, blocking collectives, per_device(): arrived = lax.all_to_all(message, ('y', 'c'), 0, 0, tiled=True)  16.4 us
    ppermute x6, starting transfers between devices, swap(): return lax.ppermute(block, axis, [(0, 1), (1, 0)])  15.5 us
    all_to_all x1, waiting for transfers between devices, per_device(): lax.all_to_all(grad_part.reshape(devices, rows, quarter), SEQ, 0, 0, tile...  13.1 us
    ppermute x6, waiting for transfers between devices, swap(): return lax.ppermute(block, axis, [(0, 1), (1, 0)])  11.9 us
    all_to_all x1, waiting for transfers between devices, per_device(): compressed = lax.all_to_all(message, ('y', 'c'), 0, 0, tiled=True)  7.01 us
    all_to_all x1, starting transfers between devices, per_device(): lax.all_to_all(grad_part.reshape(devices, rows, quarter), SEQ, 0, 0, tile...  5.56 us
  transfers between devices with their start and end apart: 14, of which 7 were waited for; matrix products, arithmetic and copies ran while one was open for 4% of the time, Pallas kernels for 4%

profile of v6, /device:TPU:1, one launch (start us, length us, event | category | flops | bytes accessed | tf_op | source)
XLA Modules:
  0.0 146.3 jit_solution(11440594961745939987)
XLA Ops:
  0.6 4.0 %collective-permute-start.3 = (bf16[256,512]{1,0:T(8,128)(2,1)}, bf16[256,512]{1,0:T(8,128)(2,1)S(1)}, u32[]{:S(2)}, u32[]{:S(2)}) collective-permute-start(bf16[256,512]{1,0:T(8,128)(2,1)} %bitcast.79), channel_id=1, source_target_pairs={{0,16},{16,0},{1,17},{17,1},{2,18},{18,2},{3,19},{19,3},{4,20},{20... | collective-permute-start | bytes 786440 | tf_op jit(solution)/shard_map/ppermute | solution.py:30
  4.6 5.2 %collective-permute-start = (bf16[32,512]{1,0:T(8,128)(2,1)}, bf16[32,512]{1,0:T(8,128)(2,1)S(1)}, u32[]{:S(2)}, u32[]{:S(2)}) collective-permute-start(bf16[32,512]{1,0:T(8,128)(2,1)} %param.12), channel_id=1, source_target_pairs={{0,0},{1,32},{2,2},{3,34},{4,4},{5,36},{6,6},{7,38},{8,8},{9,40},{... | collective-permute-start | bytes 98312 | tf_op jit(solution)/shard_map/ppermute | solution.py:188
  9.8 4.9 %all-to-all-start = ((bf16[4,8,512]{2,1,0:T(8,128)(2,1)}), bf16[4,8,512]{2,1,0:T(8,128)(2,1)S(1)}, u32[]{:S(2)}, u32[]{:S(2)}) async-start(bf16[4,8,512]{2,1,0:T(8,128)(2,1)} %bitcast.85), calls=%async_computation | async-start | bytes 65536 | tf_op jit(solution)/shard_map/all_to_all | solution.py:190
  14.7 0.7 slice_bitcast_fusion
  15.4 1.9 %collective-permute-start.1 = (bf16[16,512]{1,0:T(8,128)(2,1)S(1)}, bf16[16,512]{1,0:T(8,128)(2,1)S(1)}, u32[]{:S(2)}, u32[]{:S(2)}) collective-permute-start(bf16[16,512]{1,0:T(8,128)(2,1)S(1)} %get-tuple-element.28), channel_id=1, source_target_pairs={{0,1},{1,2},{2,3},{3,4},{4,5},{5,6},{6,7},{7,8},{8,9},{9,10},{10,1... | collective-permute-start | bytes 49160 | tf_op jit(solution)/shard_map/ppermute | solution.py:24
  17.3 2.4 %collective-permute-start.2 = (bf16[16,512]{1,0:T(8,128)(2,1)S(1)}, bf16[16,512]{1,0:T(8,128)(2,1)S(1)}, u32[]{:S(2)}, u32[]{:S(2)}) collective-permute-start(bf16[16,512]{1,0:T(8,128)(2,1)S(1)} %get-tuple-element.27), channel_id=1, source_target_pairs={{1,0},{2,1},{3,2},{4,3},{5,4},{6,5},{7,6},{8,7},{9,8},{10,9},{11,1... | collective-permute-start | bytes 49160 | tf_op jit(solution)/shard_map/ppermute | solution.py:25
  19.7 0.0 all-to-all-done
  19.7 0.0 collective-permute-done
  19.8 0.0 collective-permute-done.1.low_ref
  19.8 2.6 %collective-permute-done.2.high_ref = bf16[16,512]{1,0:T(8,128)(2,1)S(1)} collective-permute-done((bf16[16,512]{1,0:T(8,128)(2,1)S(1)}, bf16[16,512]{1,0:T(8,128)(2,1)S(1)}, u32[]{:S(2)}, u32[]{:S(2)}) %collective-permute-start.2) | collective-permute-done | bytes 16416 | tf_op jit(solution)/shard_map/ppermute | solution.py:25
  22.4 0.0 collective-permute-done.3
  22.4 1.1 broadcast_in_dim.13
  23.5 0.0 copy-start.8
  23.5 11.1 %all-to-all-start.1 = ((bf16[16,64,512]{2,1,0:T(8,128)(2,1)}), bf16[16,64,512]{2,1,0:T(8,128)(2,1)S(1)}, u32[]{:S(2)}, u32[]{:S(2)}) async-start(bf16[16,64,512]{2,1,0:T(8,128)(2,1)} %broadcast_in_dim.13), calls=%async_computation.1 | async-start | bytes 2097152 | tf_op jit(solution)/shard_map/all_to_all | solution.py:174
  34.6 0.0 copy-done.4
  34.6 0.0 copy-done.5
  34.6 0.0 copy-done.6
  34.6 0.0 copy-done.7
  34.6 2.0 %tokens_part.1 = (bf16[256,512]{1,0:T(8,128)(2,1)S(1)}, bf16[272,512]{1,0:T(8,128)(2,1)S(1)}) custom-call(bf16[256,512]{1,0:T(8,128)(2,1)S(1)} %bitcast.70, bf16[16,512]{1,0:T(8,128)(2,1)S(1)} %collective-permute-done.1.low_ref, bf16[16,512]{1,0:T(8,128)(2,1)S(1)} %collective-permute-done.2.high_ref, s32[1,256]{1,0:T(1,128)S(1)} %copy-done.7, ...), custom_call_target="tpu_custom_call" | custom-call | flops 8000000 | bytes 1500000 | tf_op jit(solution)/shard_map/tokens_part/pallas_call | solution.py:79
  36.6 1.9 %collective-permute-start.4 = (bf16[272,512]{1,0:T(8,128)(2,1)S(1)}, bf16[272,512]{1,0:T(8,128)(2,1)S(1)}, u32[]{:S(2)}, u32[]{:S(2)}) collective-permute-start(bf16[272,512]{1,0:T(8,128)(2,1)S(1)} %get-tuple-element.17), channel_id=1, source_target_pairs={{0,16},{16,0},{1,17},{17,1},{2,18},{18,2},{3,19},{19,3},{4,20},{20... | collective-permute-start | bytes 835592 | tf_op jit(solution)/shard_map/ppermute | solution.py:30
  38.5 0.0 copy-done.8
  38.5 0.1 pad_maximum_fusion.3
  38.6 2.2 %collective-permute-start.6 = (bf16[2,256,512]{2,1,0:T(8,128)(2,1)S(1)}, bf16[2,256,512]{2,1,0:T(8,128)(2,1)S(1)}, u32[]{:S(2)}, u32[]{:S(2)}) collective-permute-start(bf16[2,256,512]{2,1,0:T(8,128)(2,1)S(1)} %pad_maximum_fusion.3), channel_id=1, source_target_pairs={{0,1},{1,0},{2,3},{3,2},{4,5},{5,4},{6,7},{7,6},{8,9},{9,8},{10,11... | collective-permute-start | bytes 1572872 | tf_op jit(solution)/shard_map/ppermute | solution.py:30
  40.8 11.1 %collective-permute-done.4 = bf16[272,512]{1,0:T(8,128)(2,1)S(1)} collective-permute-done((bf16[272,512]{1,0:T(8,128)(2,1)S(1)}, bf16[272,512]{1,0:T(8,128)(2,1)S(1)}, u32[]{:S(2)}, u32[]{:S(2)}) %collective-permute-start.4) | collective-permute-done | bytes 278560 | tf_op jit(solution)/shard_map/ppermute | solution.py:30
  51.9 0.1 pad_maximum_fusion.2
  52.0 1.9 %collective-permute-start.5 = (bf16[2,272,512]{2,1,0:T(8,128)(2,1)S(1)}, bf16[2,272,512]{2,1,0:T(8,128)(2,1)S(1)}, u32[]{:S(2)}, u32[]{:S(2)}) collective-permute-start(bf16[2,272,512]{2,1,0:T(8,128)(2,1)S(1)} %pad_maximum_fusion.2), channel_id=1, source_target_pairs={{0,1},{1,0},{2,3},{3,2},{4,5},{5,4},{6,7},{7,6},{8,9},{9,8},{10,11... | collective-permute-start | bytes 1671176 | tf_op jit(solution)/shard_map/ppermute | solution.py:30
  53.9 0.0 collective-permute-done.6
  53.9 1.1 pad_maximum_fusion.1.cotangents_ref
  55.0 0.8 collective-permute-done.5
  55.8 0.1 pad_maximum_fusion.packs_ref
  55.9 7.2 %all-to-all-done.1 = bf16[16,64,512]{2,1,0:T(8,128)(2,1)S(1)} async-done(((bf16[16,64,512]{2,1,0:T(8,128)(2,1)}), bf16[16,64,512]{2,1,0:T(8,128)(2,1)S(1)}, u32[]{:S(2)}, u32[]{:S(2)}) %all-to-all-start.1) | async-done | bytes 1048608 | tf_op jit(solution)/shard_map/all_to_all | solution.py:174
  63.1 1.2 copy-done
  64.4 2.2 %hidden_part.1 = (bf16[512,512]{1,0:T(8,128)(2,1)S(1)}, bf16[1024,512]{1,0:T(8,128)(2,1)S(1)}, bf16[512,512]{1,0:T(8,128)(2,1)S(1)}) custom-call(bf16[4,272,512]{2,1,0:T(8,128)(2,1)S(1)} %pad_maximum_fusion.packs_ref, bf16[4,256,512]{2,1,0:T(8,128)(2,1)S(1)} %copy-done, bf16[2,8,64,512]{3,2,1,0:T(8,128)(2,1)S(1)} %bitcast.68), custom_call_target="tpu_custom_call" | custom-call | flops 1610612736 | bytes 6000000 | tf_op jit(solution)/shard_map/hidden_part/pallas_call | solution.py:147
  66.6 0.0 copy-start.1
  66.6 0.8 copy-done.1
  67.4 0.8 copy-done.3
  68.2 5.6 %all-to-all-start.2 = ((bf16[64,8,512]{2,1,0:T(8,128)(2,1)}), bf16[64,8,512]{2,1,0:T(8,128)(2,1)S(1)}, u32[]{:S(2)}, u32[]{:S(2)}) async-start(bf16[64,8,512]{2,1,0:T(8,128)(2,1)} %bitcast.69), calls=%async_computation.2 | async-start | bytes 1048576 | tf_op jit(solution)/shard_map/all_to_all | solution.py:282
  73.8 0.0 copy-done.2
  73.8 0.7 fusion.16
  74.5 0.0 copy-start.9
  74.5 0.0 copy-start.10
  74.5 1.2 fusion.15
  75.7 2.4 %collective-permute-start.7 = (f32[2,256,512]{2,1,0:T(8,128)}, f32[2,256,512]{2,1,0:T(8,128)S(1)}, u32[]{:S(2)}, u32[]{:S(2)}) collective-permute-start(f32[2,256,512]{2,1,0:T(8,128)} %bitcast.23), channel_id=1, source_target_pairs={{0,1},{1,0},{2,3},{3,2},{4,5},{5,4},{6,7},{7,6},{8,9},{9,8},{10,11... | collective-permute-start | bytes 3145736 | tf_op jit(solution)/shard_map/ppermute | solution.py:30
  78.0 13.1 %all-to-all-done.2 = bf16[64,8,512]{2,1,0:T(8,128)(2,1)S(1)} async-done(((bf16[64,8,512]{2,1,0:T(8,128)(2,1)}), bf16[64,8,512]{2,1,0:T(8,128)(2,1)S(1)}, u32[]{:S(2)}, u32[]{:S(2)}) %all-to-all-start.2) | async-done | bytes 524320 | tf_op jit(solution)/shard_map/all_to_all | solution.py:282
  91.1 0.1 convert_reduce_fusion
  91.2 0.0 copy-done.9
  91.2 0.0 copy-done.10
  91.2 0.3 fusion.5
  91.5 0.1 broadcast_in_dim.14
  91.6 0.0 collective-permute-done.7
  91.6 0.2 add.26
  91.8 16.4 %all_to_all.30 = f32[16,8,160]{2,1,0:T(8,128)S(1)} all-to-all(f32[16,8,160]{2,1,0:T(8,128)S(1)} %pad_maximum_fusion.4), channel_id=1, replica_groups=mesh['y'=8,'xh'=2,'xl'=2,'z'=8,'c'=2] {'y','c'}, dimensions={0} | all-to-all | bytes 163840 | tf_op jit(solution)/shard_map/all_to_all | solution.py:300
  108.3 0.1 concatenate.21
  108.4 0.8 broadcast_in_dim.33
  109.2 5.5 %all-to-all-start.4 = ((bf16[32,16,384]{2,1,0:T(8,128)(2,1)}), bf16[32,16,384]{2,1,0:T(8,128)(2,1)S(1)}, u32[]{:S(2)}, u32[]{:S(2)}) async-start(bf16[32,16,384]{2,1,0:T(8,128)(2,1)} %broadcast_in_dim.33), calls=%async_computation.4 | async-start | bytes 786432 | tf_op jit(solution)/shard_map/all_to_all | solution.py:174
  114.7 3.1 %collective-permute-start.8 = (bf16[256,512]{1,0:T(8,128)(2,1)S(1)}, bf16[256,512]{1,0:T(8,128)(2,1)S(1)}, u32[]{:S(2)}, u32[]{:S(2)}) collective-permute-start(bf16[256,512]{1,0:T(8,128)(2,1)S(1)} %fusion.4), channel_id=1, source_target_pairs={{0,16},{16,0},{1,17},{17,1},{2,18},{18,2},{3,19},{19,3},{4,20},{20... | collective-permute-start | bytes 786440 | tf_op jit(solution)/shard_map/ppermute | solution.py:30
  117.9 10.0 %all-to-all-done.4 = bf16[32,16,384]{2,1,0:T(8,128)(2,1)S(1)} async-done(((bf16[32,16,384]{2,1,0:T(8,128)(2,1)}), bf16[32,16,384]{2,1,0:T(8,128)(2,1)S(1)}, u32[]{:S(2)}, u32[]{:S(2)}) %all-to-all-start.4) | async-done | bytes 393248 | tf_op jit(solution)/shard_map/all_to_all | solution.py:174
  127.9 4.1 %tail.1 = f32[16,8,128]{2,1,0:T(8,128)} custom-call(s32[1]{0:T(128)} %bitcast.28.chip_ref, bf16[512,384]{1,0:T(8,128)(2,1)S(1)} %bitcast.65), custom_call_target="tpu_custom_call" | custom-call | tf_op jit(solution)/shard_map/tail/pallas_call | solution.py:239
  132.0 5.2 %all-to-all-start.5 = ((f32[16,8,128]{2,1,0:T(8,128)}), f32[16,8,128]{2,1,0:T(8,128)S(1)}, u32[]{:S(2)}, u32[]{:S(2)}) async-start(f32[16,8,128]{2,1,0:T(8,128)} %tail.1), calls=%async_computation.5 | async-start | bytes 131072 | tf_op jit(solution)/shard_map/all_to_all | solution.py:316
  137.2 0.0 collective-permute-done.8
  137.2 0.8 fusion.3
  138.1 7.0 %all-to-all-done.5 = f32[16,8,128]{2,1,0:T(8,128)S(1)} async-done(((f32[16,8,128]{2,1,0:T(8,128)}), f32[16,8,128]{2,1,0:T(8,128)S(1)}, u32[]{:S(2)}, u32[]{:S(2)}) %all-to-all-start.5) | async-done | bytes 65568 | tf_op jit(solution)/shard_map/all_to_all | solution.py:316
  145.1 0.6 bitcast_subtract_fusion
  145.7 0.6 copy.13
  (16 shorter events, 0.1 us)
Async XLA Ops:
  0.6 21.7 %collective-permute-start.3 = (bf16[256,512]{1,0:T(8,128)(2,1)}, bf16[256,512]{1,0:T(8,128)(2,1)S(1)}, u32[]{:S(2)}, u32[]{:S(2)}) collective-permute-start(bf16[256,512]{1,0:T(8,128)(2,1)} %bitcast.79), channel_id=1, source_target_pairs={{0,16},{16,0},{1,17},{17,1},{2,18},{18,2},{3,19},{19,3},{4,20},{20... | collective-permute-start | bytes 786440 | tf_op jit(solution)/shard_map/ppermute | solution.py:30
  4.6 15.1 %collective-permute-start = (bf16[32,512]{1,0:T(8,128)(2,1)}, bf16[32,512]{1,0:T(8,128)(2,1)S(1)}, u32[]{:S(2)}, u32[]{:S(2)}) collective-permute-start(bf16[32,512]{1,0:T(8,128)(2,1)} %param.12), channel_id=1, source_target_pairs={{0,0},{1,32},{2,2},{3,34},{4,4},{5,36},{6,6},{7,38},{8,8},{9,40},{... | collective-permute-start | bytes 98312 | tf_op jit(solution)/shard_map/ppermute | solution.py:188
  9.8 9.9 %all-to-all-start = ((bf16[4,8,512]{2,1,0:T(8,128)(2,1)}), bf16[4,8,512]{2,1,0:T(8,128)(2,1)S(1)}, u32[]{:S(2)}, u32[]{:S(2)}) async-start(bf16[4,8,512]{2,1,0:T(8,128)(2,1)} %bitcast.85), calls=%async_computation | async-start | bytes 65536 | tf_op jit(solution)/shard_map/all_to_all | solution.py:190
  15.4 4.4 %collective-permute-start.1 = (bf16[16,512]{1,0:T(8,128)(2,1)S(1)}, bf16[16,512]{1,0:T(8,128)(2,1)S(1)}, u32[]{:S(2)}, u32[]{:S(2)}) collective-permute-start(bf16[16,512]{1,0:T(8,128)(2,1)S(1)} %get-tuple-element.28), channel_id=1, source_target_pairs={{0,1},{1,2},{2,3},{3,4},{4,5},{5,6},{6,7},{7,8},{8,9},{9,10},{10,1... | collective-permute-start | bytes 49160 | tf_op jit(solution)/shard_map/ppermute | solution.py:24
  17.3 5.1 %collective-permute-start.2 = (bf16[16,512]{1,0:T(8,128)(2,1)S(1)}, bf16[16,512]{1,0:T(8,128)(2,1)S(1)}, u32[]{:S(2)}, u32[]{:S(2)}) collective-permute-start(bf16[16,512]{1,0:T(8,128)(2,1)S(1)} %get-tuple-element.27), channel_id=1, source_target_pairs={{1,0},{2,1},{3,2},{4,3},{5,4},{6,5},{7,6},{8,7},{9,8},{10,9},{11,1... | collective-permute-start | bytes 49160 | tf_op jit(solution)/shard_map/ppermute | solution.py:25
  23.4 11.1 %copy-start.4 = (bf16[1,256,512]{2,1,0:T(8,128)(2,1)S(1)}, bf16[1,256,512]{2,1,0:T(8,128)(2,1)}, u32[]{:S(2)}) copy-start(bf16[1,256,512]{2,1,0:T(8,128)(2,1)} %param.9) | copy-start | bytes 786436
  23.4 11.1 %copy-start.5 = (f32[31,512]{1,0:T(8,128)S(1)}, f32[31,512]{1,0:T(8,128)}, u32[]{:S(2)}) copy-start(f32[31,512]{1,0:T(8,128)} %taps_ref.1) | copy-start | bytes 190468
  23.4 11.2 %copy-start.6 = (f32[512]{0:T(512)S(1)}, f32[512]{0:T(512)}, u32[]{:S(2)}) copy-start(f32[512]{0:T(512)} %param.14) | copy-start | bytes 6148
  23.5 11.2 %copy-start.7 = (s32[1,256]{1,0:T(1,128)S(1)}, s32[1,256]{1,0:T(1,128)}, u32[]{:S(2)}) copy-start(s32[1,256]{1,0:T(1,128)} %mask_ref.1) | copy-start | bytes 3076
  23.5 15.1 %copy-start.8 = (bf16[1,256,512]{2,1,0:T(8,128)(2,1)S(1)}, bf16[1,256,512]{2,1,0:T(8,128)(2,1)}, u32[]{:S(2)}) copy-start(bf16[1,256,512]{2,1,0:T(8,128)(2,1)} %param.10) | copy-start | bytes 786436
  23.5 39.7 %all-to-all-start.1 = ((bf16[16,64,512]{2,1,0:T(8,128)(2,1)}), bf16[16,64,512]{2,1,0:T(8,128)(2,1)S(1)}, u32[]{:S(2)}, u32[]{:S(2)}) async-start(bf16[16,64,512]{2,1,0:T(8,128)(2,1)} %broadcast_in_dim.13), calls=%async_computation.1 | async-start | bytes 2097152 | tf_op jit(solution)/shard_map/all_to_all | solution.py:174
  36.6 15.3 %collective-permute-start.4 = (bf16[272,512]{1,0:T(8,128)(2,1)S(1)}, bf16[272,512]{1,0:T(8,128)(2,1)S(1)}, u32[]{:S(2)}, u32[]{:S(2)}) collective-permute-start(bf16[272,512]{1,0:T(8,128)(2,1)S(1)} %get-tuple-element.17), channel_id=1, source_target_pairs={{0,16},{16,0},{1,17},{17,1},{2,18},{18,2},{3,19},{19,3},{4,20},{20... | collective-permute-start | bytes 835592 | tf_op jit(solution)/shard_map/ppermute | solution.py:30
  38.6 15.3 %collective-permute-start.6 = (bf16[2,256,512]{2,1,0:T(8,128)(2,1)S(1)}, bf16[2,256,512]{2,1,0:T(8,128)(2,1)S(1)}, u32[]{:S(2)}, u32[]{:S(2)}) collective-permute-start(bf16[2,256,512]{2,1,0:T(8,128)(2,1)S(1)} %pad_maximum_fusion.3), channel_id=1, source_target_pairs={{0,1},{1,0},{2,3},{3,2},{4,5},{5,4},{6,7},{7,6},{8,9},{9,8},{10,11... | collective-permute-start | bytes 1572872 | tf_op jit(solution)/shard_map/ppermute | solution.py:30
  52.0 3.9 %collective-permute-start.5 = (bf16[2,272,512]{2,1,0:T(8,128)(2,1)S(1)}, bf16[2,272,512]{2,1,0:T(8,128)(2,1)S(1)}, u32[]{:S(2)}, u32[]{:S(2)}) collective-permute-start(bf16[2,272,512]{2,1,0:T(8,128)(2,1)S(1)} %pad_maximum_fusion.2), channel_id=1, source_target_pairs={{0,1},{1,0},{2,3},{3,2},{4,5},{5,4},{6,7},{7,6},{8,9},{9,8},{10,11... | collective-permute-start | bytes 1671176 | tf_op jit(solution)/shard_map/ppermute | solution.py:30
  63.1 1.2 copy-start
  66.6 0.8 copy-start.1
  67.4 0.8 copy-start.3
  68.2 5.6 %copy-start.2 = (bf16[512,512]{1,0:T(8,128)(2,1)S(1)}, bf16[512,512]{1,0:T(8,128)(2,1)}, u32[]{:S(2)}) copy-start(bf16[512,512]{1,0:T(8,128)(2,1)} %copy-done.1) | copy-start | bytes 1572868
  68.2 22.9 %all-to-all-start.2 = ((bf16[64,8,512]{2,1,0:T(8,128)(2,1)}), bf16[64,8,512]{2,1,0:T(8,128)(2,1)S(1)}, u32[]{:S(2)}, u32[]{:S(2)}) async-start(bf16[64,8,512]{2,1,0:T(8,128)(2,1)} %bitcast.69), calls=%async_computation.2 | async-start | bytes 1048576 | tf_op jit(solution)/shard_map/all_to_all | solution.py:282
  74.5 16.7 %copy-start.9 = (f32[1,8,2048]{2,1,0:T(8,128)S(1)}, f32[1,8,2048]{2,1,0:T(8,128)}, u32[]{:S(2)}) copy-start(f32[1,8,2048]{2,1,0:T(8,128)} %param.16) | copy-start | bytes 196612
  74.5 16.7 %copy-start.10 = (s32[2048,32]{0,1:T(8,128)S(1)}, s32[2048,32]{0,1:T(8,128)}, u32[]{:S(2)}) copy-start(s32[2048,32]{0,1:T(8,128)} %param.17) | copy-start | bytes 786436
  75.7 15.9 %collective-permute-start.7 = (f32[2,256,512]{2,1,0:T(8,128)}, f32[2,256,512]{2,1,0:T(8,128)S(1)}, u32[]{:S(2)}, u32[]{:S(2)}) collective-permute-start(f32[2,256,512]{2,1,0:T(8,128)} %bitcast.23), channel_id=1, source_target_pairs={{0,1},{1,0},{2,3},{3,2},{4,5},{5,4},{6,7},{7,6},{8,9},{9,8},{10,11... | collective-permute-start | bytes 3145736 | tf_op jit(solution)/shard_map/ppermute | solution.py:30
  109.2 18.8 %all-to-all-start.4 = ((bf16[32,16,384]{2,1,0:T(8,128)(2,1)}), bf16[32,16,384]{2,1,0:T(8,128)(2,1)S(1)}, u32[]{:S(2)}, u32[]{:S(2)}) async-start(bf16[32,16,384]{2,1,0:T(8,128)(2,1)} %broadcast_in_dim.33), calls=%async_computation.4 | async-start | bytes 786432 | tf_op jit(solution)/shard_map/all_to_all | solution.py:174
  114.7 22.5 %collective-permute-start.8 = (bf16[256,512]{1,0:T(8,128)(2,1)S(1)}, bf16[256,512]{1,0:T(8,128)(2,1)S(1)}, u32[]{:S(2)}, u32[]{:S(2)}) collective-permute-start(bf16[256,512]{1,0:T(8,128)(2,1)S(1)} %fusion.4), channel_id=1, source_target_pairs={{0,16},{16,0},{1,17},{17,1},{2,18},{18,2},{3,19},{19,3},{4,20},{20... | collective-permute-start | bytes 786440 | tf_op jit(solution)/shard_map/ppermute | solution.py:30
  132.0 13.1 %all-to-all-start.5 = ((f32[16,8,128]{2,1,0:T(8,128)}), f32[16,8,128]{2,1,0:T(8,128)S(1)}, u32[]{:S(2)}, u32[]{:S(2)}) async-start(f32[16,8,128]{2,1,0:T(8,128)} %tail.1), calls=%async_computation.5 | async-start | bytes 131072 | tf_op jit(solution)/shard_map/all_to_all | solution.py:316

commit v7 on v6

--- a/solution.py
+++ b/solution.py
@@ -157,9 +157,6 @@
             pltpu.VMEM((frames, features), bf16),
         ],
         compiler_params=pltpu.CompilerParams(vmem_limit_bytes=16 * 1024 * 1024),
-        cost_estimate=pl.CostEstimate(
-            flops=6 * blocks * frames * features * quarter, bytes_accessed=6_000_000, transcendentals=0
-        ),
         name="hidden_part",
     )(packs, cotangents, whole)
 
@@ -191,26 +188,116 @@
     return jnp.concatenate([up_block, down_block], axis=0)
 
 
-def top_bits(values):
-    return lax.reduce_precision(values, exponent_bits=8, mantissa_bits=7)
-
-
-def terms(values, count):
-    parts = []
-    for _ in range(count):
-        part = top_bits(values)
-        parts.append(part.astype(jnp.bfloat16))
-        values = values - part
-    return parts
+def rows_kernel(pieces_ref, error_ref, start_ref, message_ref, memory_ref):
+    chips, rows, quarter = pieces_ref.shape
+    for xl in range(XL):
+        total = None
+        for chip in range(chips):
+            if chip // Z % XL == xl:
+                piece = pieces_ref[chip].astype(jnp.float32)
+                total = piece if total is None else total + piece
+        columns = slice(xl * quarter, (xl + 1) * quarter)
+        memory_ref[:, columns] = total + error_ref[:, columns]
+    memory = memory_ref[...]
+    left = lax.dot_general(
+        memory,
+        start_ref[...],
+        (((1,), (1,)), ((), ())),
+        precision=HIGHEST,
+        preferred_element_type=jnp.float32,
+    )
+    chunks, _, width = message_ref.shape
+    part = width // C
+    filler = jnp.zeros((rows, width - part - RANK), jnp.float32)
+    for chunk in range(chunks):
+        columns = slice(chunk * part, (chunk + 1) * part)
+        message_ref[chunk] = jnp.concatenate([memory[:, columns], left, filler], axis=1)
+
+
+def rows_part(pieces, error_rows, start):
+    rows, columns = error_rows.shape
+    chunks = Y * C
+    return pl.pallas_call(
+        rows_kernel,
+        out_shape=(
+            jax.ShapeDtypeStruct((chunks, rows, C * columns // chunks), jnp.float32),
+            jax.ShapeDtypeStruct((rows, columns), jnp.float32),
+        ),
+        compiler_params=pltpu.CompilerParams(vmem_limit_bytes=8 * 1024 * 1024),
+        name="rows_part",
+    )(pieces, error_rows, start)
+
+
+def mean_kernel(arrived_ref, message_ref):
+    senders, rows, width = arrived_ref.shape
+    part = width // C
+    sums = []
+    for c in range(C):
+        total = arrived_ref[c]
+        for sender in range(c + C, senders, C):
+            total = total + arrived_ref[sender]
+        sums.append(total / Y)
+    left = sums[0][:, part : part + RANK] + sums[1][:, part : part + RANK]
+    parts = [jnp.concatenate([total[:, :part] for total in sums], axis=1).astype(jnp.bfloat16)]
+    for _ in range(3):
+        parts.append(left.astype(jnp.bfloat16))
+        left = left - parts[-1].astype(jnp.float32)
+    parts.append(jnp.zeros((rows, width - 3 * RANK), jnp.bfloat16))
+    row = jnp.concatenate(parts, axis=1)
+    for chip in range(message_ref.shape[0]):
+        message_ref[chip] = row
+
+
+def mean_part(arrived, chips):
+    _, rows, width = arrived.shape
+    return pl.pallas_call(
+        mean_kernel,
+        out_shape=jax.ShapeDtypeStruct((chips, rows, 2 * width), jnp.bfloat16),
+        compiler_params=pltpu.CompilerParams(vmem_limit_bytes=8 * 1024 * 1024),
+        name="mean_part",
+    )(arrived)
+
+
+def last_kernel(arrived_ref, memory_ref, new_ref, compressed_ref):
+    chunks, rows, width = arrived_ref.shape
+    part = width // C
+    per_quarter = chunks // XL
+    for xl in range(XL):
+        for c in range(C):
+            mine = slice(c * part, (c + 1) * part)
+            pieces = [arrived_ref[xl * per_quarter + k][:, mine] for k in range(per_quarter)]
+            compressed = jnp.concatenate(pieces, axis=1)
+            quarter = per_quarter * part
+            columns = slice((xl * C + c) * quarter, (xl * C + c + 1) * quarter)
+            compressed_ref[:, columns] = compressed
+            new_ref[:, columns] = memory_ref[c, :, xl * quarter : (xl + 1) * quarter] - compressed
+
+
+def last_part(arrived, memory_rows):
+    _, rows, columns = memory_rows.shape
+    shape = jax.ShapeDtypeStruct((rows, C * columns), jnp.float32)
+    return pl.pallas_call(
+        last_kernel,
+        out_shape=(shape, shape),
+        compiler_params=pltpu.CompilerParams(vmem_limit_bytes=8 * 1024 * 1024),
+        name="last_part",
+    )(arrived, memory_rows)
+
+
+def by_core(mine, theirs, axis=0):
+    first = lax.axis_index("c") == 0
+    return jnp.concatenate(
+        [jnp.where(first, mine, theirs), jnp.where(first, theirs, mine)], axis=axis
+    )
 
 
 def tail_kernel(chip_ref, columns_ref, message_ref, rows_scratch):
     chunks, rows, width = message_ref.shape
     rank = RANK
     columns = columns_ref[...].astype(jnp.float32)
-    mean_columns = columns[:, :width] + columns[:, width : 2 * width]
+    mean_columns = columns[:, :width]
     first, second, third = (
-        columns[:, 2 * width + rank * i : 2 * width + rank * (i + 1)] for i in range(3)
+        columns[:, width + rank * i : width + rank * (i + 1)] for i in range(3)
     )
     left = first + second + third
     left_t = left.T
@@ -276,46 +363,40 @@
     mixed_part = mixed_part.reshape(C, XL, frames, features)
     chip_part = mixed_part[0] + swap(mixed_part[1], "c")
 
-    quarter = grad_part.shape[1]
-    devices = XH * XL * Z * C
-    rows = features // devices
-    pieces = lax.all_to_all(grad_part.reshape(devices, rows, quarter), SEQ, 0, 0, tiled=True)
-    pieces = pieces.reshape(XH, XL, Z, C, rows, quarter).astype(jnp.float32)
-    grad_rows = jnp.sum(pieces, axis=(0, 2)).reshape(QUARTERS, rows, quarter)
-    grad_rows = grad_rows.transpose(1, 0, 2).reshape(rows, QUARTERS * quarter)
-    memory_rows = grad_rows + error_memory[0]
-
-    chunks = Y * C
-    width = memory_rows.shape[1] // chunks
+    core = lax.axis_index("c")
+    rows, quarter = error_memory.shape[1], error_memory.shape[2] // QUARTERS
+    error = error_memory[0].reshape(rows, XL, C, quarter).transpose(2, 0, 1, 3)
+    error = error.reshape(C, rows, XL * quarter)
+    error_rows = by_core(
+        lax.dynamic_index_in_dim(error, core, keepdims=False),
+        swap(lax.dynamic_index_in_dim(error, 1 - core, keepdims=False), "c"),
+    )
+    start = (seed_matrix.astype(jnp.float32) / 128.0).T.reshape(RANK, XL, C, quarter)
+    start = lax.dynamic_index_in_dim(start, core, axis=2, keepdims=False).reshape(RANK, -1)
+
+    chips = XH * XL * Z
     chip_rows = C * rows
-    start_matrix = seed_matrix.astype(jnp.float32) / 128.0
-    left_term = jnp.dot(memory_rows, start_matrix, precision=HIGHEST)
-    rank = left_term.shape[1]
-    by_chunk = memory_rows.reshape(rows, chunks, width).transpose(1, 0, 2)
-    message = jnp.concatenate(
-        [by_chunk, jnp.broadcast_to(left_term[None], (chunks, rows, rank))], axis=2
-    )
-    message, chip_part = lax.optimization_barrier((message, chip_part))
+    pieces = lax.all_to_all(grad_part.reshape(chips, chip_rows, quarter), CHIP, 0, 0, tiled=True)
+    message, memory = rows_part(pieces, error_rows, start)
+
+    arrived = lax.all_to_all(message, ("y", "c"), 0, 0, tiled=True)
+    arrived, memory = lax.optimization_barrier((arrived, memory))
     other_chip = swap(chip_part[1].astype(jnp.bfloat16), "xl")
-    arrived = lax.all_to_all(message, ("y", "c"), 0, 0, tiled=True)
-    mean_rows = jnp.sum(arrived.reshape(Y, chip_rows, width + rank), axis=0) / Y
-    packed = jnp.concatenate(
-        [
-            *terms(mean_rows[:, :width], 2),
-            *terms(mean_rows[:, width:], 3),
-            jnp.zeros((chip_rows, width - 3 * rank), jnp.bfloat16),
-        ],
-        axis=1,
-    )
     mixed = (
         stream.astype(jnp.float32) + 0.5 * (chip_part[0] + other_chip.astype(jnp.float32))
     ).astype(jnp.bfloat16)
-    columns = gather_by_exchange(packed, CHIP).reshape(features, packed.shape[1])
+    memory = memory.reshape(C, rows, XL * quarter)
+    memory_rows = by_core(
+        lax.dynamic_index_in_dim(memory, core),
+        swap(lax.dynamic_index_in_dim(memory, 1 - core), "c"),
+    )
+    packed = mean_part(arrived, chips)
+    columns = lax.all_to_all(packed, CHIP, 0, 0, tiled=True).reshape(features, -1)
     chip = lax.axis_index(CHIP).astype(jnp.int32).reshape(1)
-    message = tail(chip, columns, chunks, rows, width)
-    compressed = lax.all_to_all(message, ("y", "c"), 0, 0, tiled=True)
-    compressed = compressed.transpose(1, 0, 2).reshape(rows, chunks * width)
-    new_memory = memory_rows - compressed
+    width = arrived.shape[2]
+    message = tail(chip, columns, Y * C, rows, width)
+    arrived = lax.all_to_all(message, ("y", "c"), 0, 0, tiled=True)
+    new_memory, compressed = last_part(arrived, memory_rows)
     return (mixed[None], new_memory[None], compressed)
 
 

time: 147 us -> 145 us (0.986)
  blocking collectives: 16.4 us -> 0 us
  starting transfers between devices: 57.3 us -> 72.8 us
  waiting for transfers between devices: 51.9 us -> 45.4 us
  Pallas kernels: 8.25 us -> 10.8 us
    all_to_all x1 -> x0, blocking collectives: 16.4 us -> none  [per_device(): arrived = lax.all_to_all(message, ('y', 'c'), 0, 0, tiled=True)]
    all_to_all x2 -> x4, starting transfers between devices: 10.8 us -> 26.9 us  [the longest x2 15.7 us: per_device(): arrived = lax.all_to_all(message, ('y', 'c'), 0, 0, tiled=True)]
    all_to_all x2 -> x1, waiting for transfers between devices: 17.2 us -> 3.54 us  [gather_by_exchange(): return lax.all_to_all(copies, axis, 0, 0, tiled=True)]
    all_to_all x2 -> x4, waiting for transfers between devices: 20.1 us -> 28.3 us  [the longest x2 15.9 us: per_device(): arrived = lax.all_to_all(message, ('y', 'c'), 0, 0, tiled=True)]
    all_to_all x2 -> x1, starting transfers between devices: 16.6 us -> 10.5 us  [gather_by_exchange(): return lax.all_to_all(copies, axis, 0, 0, tiled=True)]
    ppermute x6 -> x8, starting transfers between devices: 15.5 us -> 19.5 us  [swap(): return lax.ppermute(block, axis, [(0, 1), (1, 0)])]
    pallas_call x0 -> x3, Pallas kernels: none -> 2.54 us  [the longest x1 1.01 us: rows_part(): pl.pallas_call(rows_kernel, out_shape=(jax.ShapeDtypeStruct((chunks, rows...]
    ppermute x6 -> x8, waiting for transfers between devices: 11.9 us -> 11 us  [swap(): return lax.ppermute(block, axis, [(0, 1), (1, 0)])]
  transfers between devices with their start and end apart: 14 -> 17, of which waited for: 7 -> 7; matrix products, arithmetic and copies ran while one was open for 4% -> 6% of each run, Pallas kernels for 4% -> 6%
where the time goes in v7:
time: 145 us; the launch traced here: 144 us
  starting transfers between devices  72.8 us (50%)
  waiting for transfers between devices  45.4 us (31%)
  Pallas kernels  10.8 us (7%)
  local copies, waits for them, and re-layouts  7.71 us (5%)
  other arithmetic  4.35 us (3%)
  matrix products  1.74 us (1%)
    ppermute x8, starting transfers between devices, swap(): return lax.ppermute(block, axis, [(0, 1), (1, 0)])  19.5 us
    all_to_all x2, waiting for transfers between devices, per_device(): arrived = lax.all_to_all(message, ('y', 'c'), 0, 0, tiled=True)  15.9 us
    all_to_all x2, starting transfers between devices, per_device(): arrived = lax.all_to_all(message, ('y', 'c'), 0, 0, tiled=True)  15.7 us
    ppermute x8, waiting for transfers between devices, swap(): return lax.ppermute(block, axis, [(0, 1), (1, 0)])  11 us
    all_to_all x1, starting transfers between devices, gather_by_exchange(): return lax.all_to_all(copies, axis, 0, 0, tiled=True)  10.5 us
    all_to_all x1, waiting for transfers between devices, per_device(): lax.all_to_all(grad_part.reshape(chips, chip_rows, quarter), CHIP, 0, 0,...  7.06 us
    ppermute x1, starting transfers between devices, quarter_block(): down_block = lax.ppermute(down_weight, SEQ, moves)  6.04 us
    all_to_all x1, starting transfers between devices, per_device(): lax.all_to_all(grad_part.reshape(chips, chip_rows, quarter), CHIP, 0, 0,...  5.77 us
  transfers between devices with their start and end apart: 17, of which 7 were waited for; matrix products, arithmetic and copies ran while one was open for 6% of the time, Pallas kernels for 6%

profile of v7, /device:TPU:1, one launch (start us, length us, event | category | flops | bytes accessed | tf_op | source)
XLA Modules:
  0.0 143.8 jit_solution(14999822023091915997)
XLA Ops:
  0.6 6.0 %collective-permute-start = (bf16[32,512]{1,0:T(8,128)(2,1)}, bf16[32,512]{1,0:T(8,128)(2,1)S(1)}, u32[]{:S(2)}, u32[]{:S(2)}) collective-permute-start(bf16[32,512]{1,0:T(8,128)(2,1)} %param.12), channel_id=1, source_target_pairs={{0,0},{1,32},{2,2},{3,34},{4,4},{5,36},{6,6},{7,38},{8,8},{9,40},{... | collective-permute-start | bytes 98312 | tf_op jit(solution)/shard_map/ppermute | solution.py:185
  6.7 5.5 %all-to-all-start = ((bf16[4,8,512]{2,1,0:T(8,128)(2,1)}), bf16[4,8,512]{2,1,0:T(8,128)(2,1)S(1)}, u32[]{:S(2)}, u32[]{:S(2)}) async-start(bf16[4,8,512]{2,1,0:T(8,128)(2,1)} %bitcast.74), calls=%async_computation | async-start | bytes 65536 | tf_op jit(solution)/shard_map/all_to_all | solution.py:187
  12.2 3.3 %collective-permute-start.3 = (bf16[256,512]{1,0:T(8,128)(2,1)}, bf16[256,512]{1,0:T(8,128)(2,1)S(1)}, u32[]{:S(2)}, u32[]{:S(2)}) collective-permute-start(bf16[256,512]{1,0:T(8,128)(2,1)} %bitcast.66), channel_id=1, source_target_pairs={{0,16},{16,0},{1,17},{17,1},{2,18},{18,2},{3,19},{19,3},{4,20},{20... | collective-permute-start | bytes 786440 | tf_op jit(solution)/shard_map/ppermute | solution.py:30
  15.4 0.7 slice_bitcast_fusion.1
  16.2 1.9 %collective-permute-start.1 = (bf16[16,512]{1,0:T(8,128)(2,1)S(1)}, bf16[16,512]{1,0:T(8,128)(2,1)S(1)}, u32[]{:S(2)}, u32[]{:S(2)}) collective-permute-start(bf16[16,512]{1,0:T(8,128)(2,1)S(1)} %get-tuple-element.36), channel_id=1, source_target_pairs={{0,1},{1,2},{2,3},{3,4},{4,5},{5,6},{6,7},{7,8},{8,9},{9,10},{10,1... | collective-permute-start | bytes 49160 | tf_op jit(solution)/shard_map/ppermute | solution.py:24
  18.1 2.4 %collective-permute-start.2 = (bf16[16,512]{1,0:T(8,128)(2,1)S(1)}, bf16[16,512]{1,0:T(8,128)(2,1)S(1)}, u32[]{:S(2)}, u32[]{:S(2)}) collective-permute-start(bf16[16,512]{1,0:T(8,128)(2,1)S(1)} %get-tuple-element.35), channel_id=1, source_target_pairs={{1,0},{2,1},{3,2},{4,3},{5,4},{6,5},{7,6},{8,7},{9,8},{10,9},{11,1... | collective-permute-start | bytes 49160 | tf_op jit(solution)/shard_map/ppermute | solution.py:25
  20.5 0.0 all-to-all-done
  20.5 0.0 collective-permute-done
  20.6 0.0 collective-permute-done.1.low_ref
  20.6 2.6 %collective-permute-done.2.high_ref = bf16[16,512]{1,0:T(8,128)(2,1)S(1)} collective-permute-done((bf16[16,512]{1,0:T(8,128)(2,1)S(1)}, bf16[16,512]{1,0:T(8,128)(2,1)S(1)}, u32[]{:S(2)}, u32[]{:S(2)}) %collective-permute-start.2) | collective-permute-done | bytes 16416 | tf_op jit(solution)/shard_map/ppermute | solution.py:25
  23.2 0.0 collective-permute-done.3
  23.2 1.1 broadcast_in_dim.16
  24.3 0.0 copy-start.11
  24.3 10.5 %all-to-all-start.1 = ((bf16[16,64,512]{2,1,0:T(8,128)(2,1)}), bf16[16,64,512]{2,1,0:T(8,128)(2,1)S(1)}, u32[]{:S(2)}, u32[]{:S(2)}) async-start(bf16[16,64,512]{2,1,0:T(8,128)(2,1)} %broadcast_in_dim.16), calls=%async_computation.1 | async-start | bytes 2097152 | tf_op jit(solution)/shard_map/all_to_all | solution.py:171
  34.8 0.0 copy-done.4
  34.8 0.0 copy-done.7
  34.9 2.0 %tokens_part.1 = (bf16[256,512]{1,0:T(8,128)(2,1)S(1)}, bf16[272,512]{1,0:T(8,128)(2,1)S(1)}) custom-call(bf16[256,512]{1,0:T(8,128)(2,1)S(1)} %bitcast.59, bf16[16,512]{1,0:T(8,128)(2,1)S(1)} %collective-permute-done.1.low_ref, bf16[16,512]{1,0:T(8,128)(2,1)S(1)} %collective-permute-done.2.high_ref, s32[1,256]{1,0:T(1,128)S(1)} %copy-done.9, ...), custom_call_target="tpu_custom_call" | custom-call | flops 8000000 | bytes 1500000 | tf_op jit(solution)/shard_map/tokens_part/pallas_call | solution.py:79
  36.8 0.0 copy-start.5
  36.9 0.0 copy-start.13
  36.9 2.1 %collective-permute-start.4 = (bf16[272,512]{1,0:T(8,128)(2,1)S(1)}, bf16[272,512]{1,0:T(8,128)(2,1)S(1)}, u32[]{:S(2)}, u32[]{:S(2)}) collective-permute-start(bf16[272,512]{1,0:T(8,128)(2,1)S(1)} %get-tuple-element.21), channel_id=1, source_target_pairs={{0,16},{16,0},{1,17},{17,1},{2,18},{18,2},{3,19},{19,3},{4,20},{20... | collective-permute-start | bytes 835592 | tf_op jit(solution)/shard_map/ppermute | solution.py:30
  38.9 0.1 pad_maximum_fusion.3
  39.0 1.9 %collective-permute-start.6 = (bf16[2,256,512]{2,1,0:T(8,128)(2,1)S(1)}, bf16[2,256,512]{2,1,0:T(8,128)(2,1)}, u32[]{:S(2)}, u32[]{:S(2)}) collective-permute-start(bf16[2,256,512]{2,1,0:T(8,128)(2,1)S(1)} %pad_maximum_fusion.3), channel_id=1, source_target_pairs={{0,1},{1,0},{2,3},{3,2},{4,5},{5,4},{6,7},{7,6},{8,9},{9,8},{10,11... | collective-permute-start | bytes 1572872 | tf_op jit(solution)/shard_map/ppermute | solution.py:30
  40.9 10.9 %collective-permute-done.4 = bf16[272,512]{1,0:T(8,128)(2,1)S(1)} collective-permute-done((bf16[272,512]{1,0:T(8,128)(2,1)S(1)}, bf16[272,512]{1,0:T(8,128)(2,1)S(1)}, u32[]{:S(2)}, u32[]{:S(2)}) %collective-permute-start.4) | collective-permute-done | bytes 278560 | tf_op jit(solution)/shard_map/ppermute | solution.py:30
  51.9 0.7 copy-done.10
  52.6 0.1 pad_maximum_fusion.2
  52.7 2.4 %collective-permute-start.5 = (bf16[2,272,512]{2,1,0:T(8,128)(2,1)S(1)}, bf16[2,272,512]{2,1,0:T(8,128)(2,1)}, u32[]{:S(2)}, u32[]{:S(2)}) collective-permute-start(bf16[2,272,512]{2,1,0:T(8,128)(2,1)S(1)} %pad_maximum_fusion.2), channel_id=1, source_target_pairs={{0,1},{1,0},{2,3},{3,2},{4,5},{5,4},{6,7},{7,6},{8,9},{9,8},{10,11... | collective-permute-start | bytes 1671176 | tf_op jit(solution)/shard_map/ppermute | solution.py:30
  55.1 0.6 dynamic-slice_bitcast_fusion
  55.7 1.9 %collective-permute-start.9 = (f32[8,1024]{1,0:T(8,128)}, f32[8,1024]{1,0:T(8,128)}, u32[]{:S(2)}, u32[]{:S(2)}) collective-permute-start(f32[8,1024]{1,0:T(8,128)} %dynamic-slice_bitcast_fusion), channel_id=1, source_target_pairs={{0,1},{1,0},{2,3},{3,2},{4,5},{5,4},{6,7},{7,6},{8,9},{9,8},{10,11... | collective-permute-start | bytes 98312 | tf_op jit(solution)/shard_map/ppermute | solution.py:30
  57.6 0.0 collective-permute-done.6
  57.7 1.1 pad_maximum_fusion.1.cotangents_ref
  58.8 0.0 collective-permute-done.5
  58.8 1.2 pad_maximum_fusion.packs_ref
  60.0 3.5 %all-to-all-done.1 = bf16[16,64,512]{2,1,0:T(8,128)(2,1)S(1)} async-done(((bf16[16,64,512]{2,1,0:T(8,128)(2,1)}), bf16[16,64,512]{2,1,0:T(8,128)(2,1)S(1)}, u32[]{:S(2)}, u32[]{:S(2)}) %all-to-all-start.1) | async-done | bytes 1048608 | tf_op jit(solution)/shard_map/all_to_all | solution.py:171
  63.6 2.2 %hidden_part.1 = (bf16[512,512]{1,0:T(8,128)(2,1)S(1)}, bf16[1024,512]{1,0:T(8,128)(2,1)S(1)}, bf16[512,512]{1,0:T(8,128)(2,1)S(1)}) custom-call(bf16[4,272,512]{2,1,0:T(8,128)(2,1)S(1)} %pad_maximum_fusion.packs_ref, bf16[4,256,512]{2,1,0:T(8,128)(2,1)S(1)} %pad_maximum_fusion.1.cotangents_ref, bf16[2,8,64,512]{3,2,1,0:T(8,128)(2,1)S(1)} %bitcast.53), custom_call_target="tpu_custom_call" | custom-call | tf_op jit(solution)/shard_map/hidden_part/pallas_call | solution.py:147
  65.8 1.0 copy-done
  66.8 0.8 copy-done.2
  67.6 0.8 copy-done.3
  68.4 5.8 %all-to-all-start.2 = ((bf16[32,16,512]{2,1,0:T(8,128)(2,1)}), bf16[32,16,512]{2,1,0:T(8,128)(2,1)S(1)}, u32[]{:S(2)}, u32[]{:S(2)}) async-start(bf16[32,16,512]{2,1,0:T(8,128)(2,1)} %bitcast.57), calls=%async_computation.2 | async-start | bytes 1048576 | tf_op jit(solution)/shard_map/all_to_all | solution.py:379
  74.2 1.7 %fusion.7 = f32[1024,512]{1,0:T(8,128)S(1)} fusion(bf16[1024,512]{1,0:T(8,128)(2,1)S(1)} %copy-done.1, bf16[512,512]{1,0:T(8,128)(2,1)} %copy-done.2), kind=kOutput, calls=%fused_computation.26 | convolution fusion | flops 536870912 | bytes 3670016 | tf_op jit(solution)/shard_map/dot_general | solution.py:362
  75.9 0.0 copy-start.12
  75.9 1.2 fusion.6
  77.1 2.6 %collective-permute-start.7 = (f32[2,256,512]{2,1,0:T(8,128)}, f32[2,256,512]{2,1,0:T(8,128)S(1)}, u32[]{:S(2)}, u32[]{:S(2)}) collective-permute-start(f32[2,256,512]{2,1,0:T(8,128)} %bitcast.13), channel_id=1, source_target_pairs={{0,1},{1,0},{2,3},{3,2},{4,5},{5,4},{6,7},{7,6},{8,9},{9,8},{10,11... | collective-permute-start | bytes 3145736 | tf_op jit(solution)/shard_map/ppermute | solution.py:30
  79.8 0.2 reshape.52
  80.0 0.4 dynamic-slice_reduce_fusion
  80.5 0.0 collective-permute-done.9
  80.5 0.8 bitcast_select_fusion.1
  81.2 7.1 %all-to-all-done.2.pieces_ref = bf16[32,16,512]{2,1,0:T(8,128)(2,1)S(1)} async-done(((bf16[32,16,512]{2,1,0:T(8,128)(2,1)}), bf16[32,16,512]{2,1,0:T(8,128)(2,1)S(1)}, u32[]{:S(2)}, u32[]{:S(2)}) %all-to-all-start.2) | async-done | bytes 524320 | tf_op jit(solution)/shard_map/all_to_all | solution.py:379
  88.3 1.0 rows_part.1
  89.3 10.6 %all-to-all-start.3 = ((f32[16,16,128]{2,1,0:T(8,128)}), f32[16,16,128]{2,1,0:T(8,128)S(1)}, u32[]{:S(2)}, u32[]{:S(2)}) async-start(f32[16,16,128]{2,1,0:T(8,128)} %get-tuple-element.27), calls=%async_computation.3 | async-start | bytes 262144 | tf_op jit(solution)/shard_map/all_to_all | solution.py:382
  100.0 0.0 collective-permute-done.7
  100.0 0.2 add.28
  100.2 8.9 %all-to-all-done.3.arrived_ref = f32[16,16,128]{2,1,0:T(8,128)S(1)} async-done(((f32[16,16,128]{2,1,0:T(8,128)}), f32[16,16,128]{2,1,0:T(8,128)S(1)}, u32[]{:S(2)}, u32[]{:S(2)}) %all-to-all-start.3) | async-done | bytes 131104 | tf_op jit(solution)/shard_map/all_to_all | solution.py:382
  109.1 0.8 mean_part.1
  109.9 5.5 %all-to-all-start.4 = ((bf16[32,16,256]{2,1,0:T(8,128)(2,1)}), bf16[32,16,256]{2,1,0:T(8,128)(2,1)S(1)}, u32[]{:S(2)}, u32[]{:S(2)}) async-start(bf16[32,16,256]{2,1,0:T(8,128)(2,1)} %mean_part.1), calls=%async_computation.4 | async-start | bytes 524288 | tf_op jit(solution)/shard_map/all_to_all | solution.py:394
  115.5 1.9 %collective-permute-start.10 = (f32[1,8,1024]{2,1,0:T(8,128)S(1)}, f32[1,8,1024]{2,1,0:T(8,128)S(1)}, u32[]{:S(2)}, u32[]{:S(2)}) collective-permute-start(f32[1,8,1024]{2,1,0:T(8,128)S(1)} %constant_dynamic-slice_fusion), channel_id=1, source_target_pairs={{0,1},{1,0},{2,3},{3,2},{4,5},{5,4},{6,7},{7,6},{8,9},{9,8},{10,11... | collective-permute-start | bytes 98312 | tf_op jit(solution)/shard_map/ppermute | solution.py:30
  117.4 3.4 %collective-permute-start.8 = (bf16[256,512]{1,0:T(8,128)(2,1)S(1)}, bf16[256,512]{1,0:T(8,128)(2,1)S(1)}, u32[]{:S(2)}, u32[]{:S(2)}) collective-permute-start(bf16[256,512]{1,0:T(8,128)(2,1)S(1)} %fusion.5), channel_id=1, source_target_pairs={{0,16},{16,0},{1,17},{17,1},{2,18},{18,2},{3,19},{19,3},{4,20},{20... | collective-permute-start | bytes 786440 | tf_op jit(solution)/shard_map/ppermute | solution.py:30
  120.8 0.0 collective-permute-done.10
  120.8 5.3 %all-to-all-done.4 = bf16[32,16,256]{2,1,0:T(8,128)(2,1)S(1)} async-done(((bf16[32,16,256]{2,1,0:T(8,128)(2,1)}), bf16[32,16,256]{2,1,0:T(8,128)(2,1)S(1)}, u32[]{:S(2)}, u32[]{:S(2)}) %all-to-all-start.4) | async-done | bytes 262176 | tf_op jit(solution)/shard_map/all_to_all | solution.py:394
  126.1 4.1 %tail.1 = f32[16,8,128]{2,1,0:T(8,128)} custom-call(s32[1]{0:T(128)} %bitcast.17.chip_ref, bf16[512,256]{1,0:T(8,128)(2,1)S(1)} %bitcast.56), custom_call_target="tpu_custom_call" | custom-call | tf_op jit(solution)/shard_map/tail/pallas_call | solution.py:326
  130.2 5.0 %all-to-all-start.5 = ((f32[16,8,128]{2,1,0:T(8,128)}), f32[16,8,128]{2,1,0:T(8,128)S(1)}, u32[]{:S(2)}, u32[]{:S(2)}) async-start(f32[16,8,128]{2,1,0:T(8,128)} %tail.1), calls=%async_computation.5 | async-start | bytes 131072 | tf_op jit(solution)/shard_map/all_to_all | solution.py:398
  135.2 0.0 collective-permute-done.8
  135.2 0.8 fusion.4
  136.1 7.0 %all-to-all-done.5.arrived_ref = f32[16,8,128]{2,1,0:T(8,128)S(1)} async-done(((f32[16,8,128]{2,1,0:T(8,128)}), f32[16,8,128]{2,1,0:T(8,128)S(1)}, u32[]{:S(2)}, u32[]{:S(2)}) %all-to-all-start.5) | async-done | bytes 65568 | tf_op jit(solution)/shard_map/all_to_all | solution.py:398
  143.1 0.7 last_part.1
  (27 shorter events, 0.2 us)
Async XLA Ops:
  0.6 19.9 %collective-permute-start = (bf16[32,512]{1,0:T(8,128)(2,1)}, bf16[32,512]{1,0:T(8,128)(2,1)S(1)}, u32[]{:S(2)}, u32[]{:S(2)}) collective-permute-start(bf16[32,512]{1,0:T(8,128)(2,1)} %param.12), channel_id=1, source_target_pairs={{0,0},{1,32},{2,2},{3,34},{4,4},{5,36},{6,6},{7,38},{8,8},{9,40},{... | collective-permute-start | bytes 98312 | tf_op jit(solution)/shard_map/ppermute | solution.py:185
  6.7 13.8 %all-to-all-start = ((bf16[4,8,512]{2,1,0:T(8,128)(2,1)}), bf16[4,8,512]{2,1,0:T(8,128)(2,1)S(1)}, u32[]{:S(2)}, u32[]{:S(2)}) async-start(bf16[4,8,512]{2,1,0:T(8,128)(2,1)} %bitcast.74), calls=%async_computation | async-start | bytes 65536 | tf_op jit(solution)/shard_map/all_to_all | solution.py:187
  12.2 11.0 %collective-permute-start.3 = (bf16[256,512]{1,0:T(8,128)(2,1)}, bf16[256,512]{1,0:T(8,128)(2,1)S(1)}, u32[]{:S(2)}, u32[]{:S(2)}) collective-permute-start(bf16[256,512]{1,0:T(8,128)(2,1)} %bitcast.66), channel_id=1, source_target_pairs={{0,16},{16,0},{1,17},{17,1},{2,18},{18,2},{3,19},{19,3},{4,20},{20... | collective-permute-start | bytes 786440 | tf_op jit(solution)/shard_map/ppermute | solution.py:30
  16.2 4.4 %collective-permute-start.1 = (bf16[16,512]{1,0:T(8,128)(2,1)S(1)}, bf16[16,512]{1,0:T(8,128)(2,1)S(1)}, u32[]{:S(2)}, u32[]{:S(2)}) collective-permute-start(bf16[16,512]{1,0:T(8,128)(2,1)S(1)} %get-tuple-element.36), channel_id=1, source_target_pairs={{0,1},{1,2},{2,3},{3,4},{4,5},{5,6},{6,7},{7,8},{8,9},{9,10},{10,1... | collective-permute-start | bytes 49160 | tf_op jit(solution)/shard_map/ppermute | solution.py:24
  18.1 5.1 %collective-permute-start.2 = (bf16[16,512]{1,0:T(8,128)(2,1)S(1)}, bf16[16,512]{1,0:T(8,128)(2,1)S(1)}, u32[]{:S(2)}, u32[]{:S(2)}) collective-permute-start(bf16[16,512]{1,0:T(8,128)(2,1)S(1)} %get-tuple-element.35), channel_id=1, source_target_pairs={{1,0},{2,1},{3,2},{4,3},{5,4},{6,5},{7,6},{8,7},{9,8},{10,9},{11,1... | collective-permute-start | bytes 49160 | tf_op jit(solution)/shard_map/ppermute | solution.py:25
  24.3 10.6 %copy-start.4 = (bf16[1,256,512]{2,1,0:T(8,128)(2,1)S(1)}, bf16[1,256,512]{2,1,0:T(8,128)(2,1)}, u32[]{:S(2)}) copy-start(bf16[1,256,512]{2,1,0:T(8,128)(2,1)} %param.9) | copy-start | bytes 786436
  24.3 10.6 %copy-start.7 = (f32[31,512]{1,0:T(8,128)S(1)}, f32[31,512]{1,0:T(8,128)}, u32[]{:S(2)}) copy-start(f32[31,512]{1,0:T(8,128)} %taps_ref.1) | copy-start | bytes 190468
  24.3 10.6 %copy-start.8 = (f32[512]{0:T(512)S(1)}, f32[512]{0:T(512)}, u32[]{:S(2)}) copy-start(f32[512]{0:T(512)} %param.14) | copy-start | bytes 6148
  24.3 10.6 %copy-start.9 = (s32[1,256]{1,0:T(1,128)S(1)}, s32[1,256]{1,0:T(1,128)}, u32[]{:S(2)}) copy-start(s32[1,256]{1,0:T(1,128)} %mask_ref.1) | copy-start | bytes 3076
  24.3 14.6 %copy-start.11 = (bf16[1,256,512]{2,1,0:T(8,128)(2,1)S(1)}, bf16[1,256,512]{2,1,0:T(8,128)(2,1)}, u32[]{:S(2)}) copy-start(bf16[1,256,512]{2,1,0:T(8,128)(2,1)} %param.10) | copy-start | bytes 786436
  24.3 39.3 %all-to-all-start.1 = ((bf16[16,64,512]{2,1,0:T(8,128)(2,1)}), bf16[16,64,512]{2,1,0:T(8,128)(2,1)S(1)}, u32[]{:S(2)}, u32[]{:S(2)}) async-start(bf16[16,64,512]{2,1,0:T(8,128)(2,1)} %broadcast_in_dim.16), calls=%async_computation.1 | async-start | bytes 2097152 | tf_op jit(solution)/shard_map/all_to_all | solution.py:171
  36.8 15.0 %copy-start.5 = (bf16[256,512]{1,0:T(8,128)(2,1)}, bf16[256,512]{1,0:T(8,128)(2,1)S(1)}, u32[]{:S(2)}) copy-start(bf16[256,512]{1,0:T(8,128)(2,1)S(1)} %get-tuple-element.20) | copy-start | bytes 786436
  36.9 18.2 %copy-start.13 = (f32[1,8,2048]{2,1,0:T(8,128)S(1)}, f32[1,8,2048]{2,1,0:T(8,128)}, u32[]{:S(2)}) copy-start(f32[1,8,2048]{2,1,0:T(8,128)} %param.16) | copy-start | bytes 196612
  36.9 15.0 %collective-permute-start.4 = (bf16[272,512]{1,0:T(8,128)(2,1)S(1)}, bf16[272,512]{1,0:T(8,128)(2,1)S(1)}, u32[]{:S(2)}, u32[]{:S(2)}) collective-permute-start(bf16[272,512]{1,0:T(8,128)(2,1)S(1)} %get-tuple-element.21), channel_id=1, source_target_pairs={{0,16},{16,0},{1,17},{17,1},{2,18},{18,2},{3,19},{19,3},{4,20},{20... | collective-permute-start | bytes 835592 | tf_op jit(solution)/shard_map/ppermute | solution.py:30
  39.0 18.7 %collective-permute-start.6 = (bf16[2,256,512]{2,1,0:T(8,128)(2,1)S(1)}, bf16[2,256,512]{2,1,0:T(8,128)(2,1)}, u32[]{:S(2)}, u32[]{:S(2)}) collective-permute-start(bf16[2,256,512]{2,1,0:T(8,128)(2,1)S(1)} %pad_maximum_fusion.3), channel_id=1, source_target_pairs={{0,1},{1,0},{2,3},{3,2},{4,5},{5,4},{6,7},{7,6},{8,9},{9,8},{10,11... | collective-permute-start | bytes 1572872 | tf_op jit(solution)/shard_map/ppermute | solution.py:30
  51.9 0.7 copy-start.10
  52.7 6.2 %collective-permute-start.5 = (bf16[2,272,512]{2,1,0:T(8,128)(2,1)S(1)}, bf16[2,272,512]{2,1,0:T(8,128)(2,1)}, u32[]{:S(2)}, u32[]{:S(2)}) collective-permute-start(bf16[2,272,512]{2,1,0:T(8,128)(2,1)S(1)} %pad_maximum_fusion.2), channel_id=1, source_target_pairs={{0,1},{1,0},{2,3},{3,2},{4,5},{5,4},{6,7},{7,6},{8,9},{9,8},{10,11... | collective-permute-start | bytes 1671176 | tf_op jit(solution)/shard_map/ppermute | solution.py:30
  55.7 24.7 %collective-permute-start.9 = (f32[8,1024]{1,0:T(8,128)}, f32[8,1024]{1,0:T(8,128)}, u32[]{:S(2)}, u32[]{:S(2)}) collective-permute-start(f32[8,1024]{1,0:T(8,128)} %dynamic-slice_bitcast_fusion), channel_id=1, source_target_pairs={{0,1},{1,0},{2,3},{3,2},{4,5},{5,4},{6,7},{7,6},{8,9},{9,8},{10,11... | collective-permute-start | bytes 98312 | tf_op jit(solution)/shard_map/ppermute | solution.py:30
  65.8 1.0 copy-start
  66.8 0.8 copy-start.2
  67.6 0.8 copy-start.3
  68.4 5.8 %copy-start.1 = (bf16[1024,512]{1,0:T(8,128)(2,1)S(1)}, bf16[1024,512]{1,0:T(8,128)(2,1)}, u32[]{:S(2)}) copy-start(bf16[1024,512]{1,0:T(8,128)(2,1)} %copy-done) | copy-start | bytes 3145732
  68.4 19.9 %all-to-all-start.2 = ((bf16[32,16,512]{2,1,0:T(8,128)(2,1)}), bf16[32,16,512]{2,1,0:T(8,128)(2,1)S(1)}, u32[]{:S(2)}, u32[]{:S(2)}) async-start(bf16[32,16,512]{2,1,0:T(8,128)(2,1)} %bitcast.57), calls=%async_computation.2 | async-start | bytes 1048576 | tf_op jit(solution)/shard_map/all_to_all | solution.py:379
  75.9 3.8 %copy-start.12 = (s32[2048,32]{0,1:T(8,128)S(1)}, s32[2048,32]{0,1:T(8,128)}, u32[]{:S(2)}) copy-start(s32[2048,32]{0,1:T(8,128)} %param.17) | copy-start | bytes 786436
  77.1 22.8 %collective-permute-start.7 = (f32[2,256,512]{2,1,0:T(8,128)}, f32[2,256,512]{2,1,0:T(8,128)S(1)}, u32[]{:S(2)}, u32[]{:S(2)}) collective-permute-start(f32[2,256,512]{2,1,0:T(8,128)} %bitcast.13), channel_id=1, source_target_pairs={{0,1},{1,0},{2,3},{3,2},{4,5},{5,4},{6,7},{7,6},{8,9},{9,8},{10,11... | collective-permute-start | bytes 3145736 | tf_op jit(solution)/shard_map/ppermute | solution.py:30
  89.3 19.8 %all-to-all-start.3 = ((f32[16,16,128]{2,1,0:T(8,128)}), f32[16,16,128]{2,1,0:T(8,128)S(1)}, u32[]{:S(2)}, u32[]{:S(2)}) async-start(f32[16,16,128]{2,1,0:T(8,128)} %get-tuple-element.27), calls=%async_computation.3 | async-start | bytes 262144 | tf_op jit(solution)/shard_map/all_to_all | solution.py:382
  109.1 26.1 %copy-start.6 = (bf16[256,512]{1,0:T(8,128)(2,1)S(1)}, bf16[256,512]{1,0:T(8,128)(2,1)}, u32[]{:S(2)}) copy-start(bf16[256,512]{1,0:T(8,128)(2,1)} %copy-done.5) | copy-start | bytes 786436
  109.9 16.2 %all-to-all-start.4 = ((bf16[32,16,256]{2,1,0:T(8,128)(2,1)}), bf16[32,16,256]{2,1,0:T(8,128)(2,1)S(1)}, u32[]{:S(2)}, u32[]{:S(2)}) async-start(bf16[32,16,256]{2,1,0:T(8,128)(2,1)} %mean_part.1), calls=%async_computation.4 | async-start | bytes 524288 | tf_op jit(solution)/shard_map/all_to_all | solution.py:394
  115.5 5.3 %collective-permute-start.10 = (f32[1,8,1024]{2,1,0:T(8,128)S(1)}, f32[1,8,1024]{2,1,0:T(8,128)S(1)}, u32[]{:S(2)}, u32[]{:S(2)}) collective-permute-start(f32[1,8,1024]{2,1,0:T(8,128)S(1)} %constant_dynamic-slice_fusion), channel_id=1, source_target_pairs={{0,1},{1,0},{2,3},{3,2},{4,5},{5,4},{6,7},{7,6},{8,9},{9,8},{10,11... | collective-permute-start | bytes 98312 | tf_op jit(solution)/shard_map/ppermute | solution.py:30
  117.4 17.8 %collective-permute-start.8 = (bf16[256,512]{1,0:T(8,128)(2,1)S(1)}, bf16[256,512]{1,0:T(8,128)(2,1)S(1)}, u32[]{:S(2)}, u32[]{:S(2)}) collective-permute-start(bf16[256,512]{1,0:T(8,128)(2,1)S(1)} %fusion.5), channel_id=1, source_target_pairs={{0,16},{16,0},{1,17},{17,1},{2,18},{18,2},{3,19},{19,3},{4,20},{20... | collective-permute-start | bytes 786440 | tf_op jit(solution)/shard_map/ppermute | solution.py:30
  130.2 12.9 %all-to-all-start.5 = ((f32[16,8,128]{2,1,0:T(8,128)}), f32[16,8,128]{2,1,0:T(8,128)S(1)}, u32[]{:S(2)}, u32[]{:S(2)}) async-start(f32[16,8,128]{2,1,0:T(8,128)} %tail.1), calls=%async_computation.5 | async-start | bytes 131072 | tf_op jit(solution)/shard_map/all_to_all | solution.py:398

commit v8 on v7

--- a/solution.py
+++ b/solution.py
@@ -93,8 +93,10 @@
 
 
 def hidden_kernel(
-    packs_ref, cotangents_ref, whole_ref, grad_ref, hidden_ref, down_ref, up, delta, masked
+    packs_ref, cotangents_ref, whole_ref, grad_ref, both_ref, up, delta, masked
 ):
+    blocks, frames, features = cotangents_ref.shape
+    hidden_ref, down_ref = both_ref.at[: blocks * frames], both_ref.at[blocks * frames :]
     half = whole_ref.shape[2] // 2
     part = half // XL
     for xh in range(XH):
@@ -104,7 +106,6 @@
                 up[row : row + part] = whole_ref[xh, z, xl * part : (xl + 1) * part]
             row = (z * XH + xh) * half
             down_ref[row : row + half] = whole_ref[xh, z, half:]
-    blocks, frames, features = cotangents_ref.shape
     lanes = 128
     for index in range(blocks):
         rows = slice(index * frames, (index + 1) * frames)
@@ -148,8 +149,7 @@
         hidden_kernel,
         out_shape=(
             jax.ShapeDtypeStruct((features, quarter), bf16),
-            jax.ShapeDtypeStruct((blocks * frames, quarter), bf16),
-            jax.ShapeDtypeStruct((quarter, features), bf16),
+            jax.ShapeDtypeStruct((blocks * frames + quarter, features), bf16),
         ),
         scratch_shapes=[
             pltpu.VMEM((features, quarter), bf16),
@@ -188,48 +188,58 @@
     return jnp.concatenate([up_block, down_block], axis=0)
 
 
-def rows_kernel(pieces_ref, error_ref, start_ref, message_ref, memory_ref):
-    chips, rows, quarter = pieces_ref.shape
+def rows_kernel(pieces_ref, error_ref, start_ref, error_left_ref, message_ref, grad_ref):
+    chips, chip_rows, quarter = pieces_ref.shape
     for xl in range(XL):
         total = None
         for chip in range(chips):
             if chip // Z % XL == xl:
                 piece = pieces_ref[chip].astype(jnp.float32)
                 total = piece if total is None else total + piece
-        columns = slice(xl * quarter, (xl + 1) * quarter)
-        memory_ref[:, columns] = total + error_ref[:, columns]
-    memory = memory_ref[...]
+        grad_ref[:, xl * quarter : (xl + 1) * quarter] = total
+    grad = grad_ref[...]
     left = lax.dot_general(
-        memory,
+        grad,
         start_ref[...],
         (((1,), (1,)), ((), ())),
         precision=HIGHEST,
         preferred_element_type=jnp.float32,
     )
+    rows = error_ref.shape[0]
+    error_left = jnp.concatenate(
+        [error_left_ref[...], jnp.zeros((chip_rows - rows, RANK), jnp.float32)], axis=0
+    )
     chunks, _, width = message_ref.shape
     part = width // C
-    filler = jnp.zeros((rows, width - part - RANK), jnp.float32)
     for chunk in range(chunks):
-        columns = slice(chunk * part, (chunk + 1) * part)
-        message_ref[chunk] = jnp.concatenate([memory[:, columns], left, filler], axis=1)
-
-
-def rows_part(pieces, error_rows, start):
-    rows, columns = error_rows.shape
+        own = slice(chunk * part, (chunk + 1) * part)
+        message_ref[chunk, :chip_rows] = jnp.concatenate([grad[:, own], left, error_left], axis=1)
+        first = chunk * part // quarter * C * quarter + chunk * part % quarter
+        message_ref[chunk, chip_rows:] = jnp.concatenate(
+            [error_ref[:, first + c * quarter : first + c * quarter + part] for c in range(C)],
+            axis=1,
+        )
+
+
+def rows_part(pieces, error, start, error_left):
+    _, chip_rows, quarter = pieces.shape
+    rows, columns = error.shape
     chunks = Y * C
     return pl.pallas_call(
         rows_kernel,
         out_shape=(
-            jax.ShapeDtypeStruct((chunks, rows, C * columns // chunks), jnp.float32),
-            jax.ShapeDtypeStruct((rows, columns), jnp.float32),
+            jax.ShapeDtypeStruct((chunks, chip_rows + rows, columns // chunks), jnp.float32),
+            jax.ShapeDtypeStruct((chip_rows, XL * quarter), jnp.float32),
         ),
         compiler_params=pltpu.CompilerParams(vmem_limit_bytes=8 * 1024 * 1024),
         name="rows_part",
-    )(pieces, error_rows, start)
+    )(pieces, error, start, error_left)
 
 
 def mean_kernel(arrived_ref, message_ref):
-    senders, rows, width = arrived_ref.shape
+    senders, _, width = arrived_ref.shape
+    chip_rows = message_ref.shape[1]
+    rows = chip_rows // C
     part = width // C
     sums = []
     for c in range(C):
@@ -237,28 +247,31 @@
         for sender in range(c + C, senders, C):
             total = total + arrived_ref[sender]
         sums.append(total / Y)
-    left = sums[0][:, part : part + RANK] + sums[1][:, part : part + RANK]
-    parts = [jnp.concatenate([total[:, :part] for total in sums], axis=1).astype(jnp.bfloat16)]
+    mean = jnp.concatenate([total[:chip_rows, :part] for total in sums], axis=1)
+    mean = mean + jnp.concatenate([total[chip_rows:] for total in sums], axis=0)
+    left = sum(total[:chip_rows, part : part + RANK] for total in sums)
+    left = left + jnp.concatenate([total[:rows, part + RANK :] for total in sums], axis=0)
+    parts = [mean.astype(jnp.bfloat16)]
     for _ in range(3):
         parts.append(left.astype(jnp.bfloat16))
         left = left - parts[-1].astype(jnp.float32)
-    parts.append(jnp.zeros((rows, width - 3 * RANK), jnp.bfloat16))
+    parts.append(jnp.zeros((chip_rows, width - 3 * RANK), jnp.bfloat16))
     row = jnp.concatenate(parts, axis=1)
     for chip in range(message_ref.shape[0]):
         message_ref[chip] = row
 
 
-def mean_part(arrived, chips):
-    _, rows, width = arrived.shape
+def mean_part(arrived, chips, chip_rows):
+    width = arrived.shape[2]
     return pl.pallas_call(
         mean_kernel,
-        out_shape=jax.ShapeDtypeStruct((chips, rows, 2 * width), jnp.bfloat16),
+        out_shape=jax.ShapeDtypeStruct((chips, chip_rows, 2 * width), jnp.bfloat16),
         compiler_params=pltpu.CompilerParams(vmem_limit_bytes=8 * 1024 * 1024),
         name="mean_part",
     )(arrived)
 
 
-def last_kernel(arrived_ref, memory_ref, new_ref, compressed_ref):
+def last_kernel(arrived_ref, grad_ref, error_ref, new_ref, compressed_ref):
     chunks, rows, width = arrived_ref.shape
     part = width // C
     per_quarter = chunks // XL
@@ -270,18 +283,18 @@
             quarter = per_quarter * part
             columns = slice((xl * C + c) * quarter, (xl * C + c + 1) * quarter)
             compressed_ref[:, columns] = compressed
-            new_ref[:, columns] = memory_ref[c, :, xl * quarter : (xl + 1) * quarter] - compressed
-
-
-def last_part(arrived, memory_rows):
-    _, rows, columns = memory_rows.shape
-    shape = jax.ShapeDtypeStruct((rows, C * columns), jnp.float32)
+            memory = grad_ref[c, :, xl * quarter : (xl + 1) * quarter] + error_ref[:, columns]
+            new_ref[:, columns] = memory - compressed
+
+
+def last_part(arrived, grad_rows, error):
+    shape = jax.ShapeDtypeStruct(error.shape, jnp.float32)
     return pl.pallas_call(
         last_kernel,
         out_shape=(shape, shape),
         compiler_params=pltpu.CompilerParams(vmem_limit_bytes=8 * 1024 * 1024),
         name="last_part",
-    )(arrived, memory_rows)
+    )(arrived, grad_rows, error)
 
 
 def by_core(mine, theirs, axis=0):
@@ -357,46 +370,43 @@
     stream, own = tokens_part(tokens[0], low, high, frame_mask, kernel, norm_gain[None])
     packs = group_frames(own, swap(own, "xl"))
     cotangents = group_frames(cotangent[0], cotangent_x)
-    grad_part, hidden, down = hidden_part(packs, cotangents, whole)
-
+    grad_part, both = hidden_part(packs, cotangents, whole)
+
+    hidden, down = both[: QUARTERS * frames], both[QUARTERS * frames :]
     mixed_part = jnp.dot(hidden, down, preferred_element_type=jnp.float32)
+    core = lax.axis_index("c")
+    error = error_memory[0]
+    rows, quarter = error.shape[0], error.shape[1] // QUARTERS
+    start = seed_matrix.astype(jnp.float32) / 128.0
+    error_left = jnp.dot(error, start, precision=HIGHEST)
+    start = start.T.reshape(RANK, XL, C, quarter)
+    start = lax.dynamic_index_in_dim(start, core, axis=2, keepdims=False).reshape(RANK, -1)
+
     mixed_part = mixed_part.reshape(C, XL, frames, features)
     chip_part = mixed_part[0] + swap(mixed_part[1], "c")
-
-    core = lax.axis_index("c")
-    rows, quarter = error_memory.shape[1], error_memory.shape[2] // QUARTERS
-    error = error_memory[0].reshape(rows, XL, C, quarter).transpose(2, 0, 1, 3)
-    error = error.reshape(C, rows, XL * quarter)
-    error_rows = by_core(
-        lax.dynamic_index_in_dim(error, core, keepdims=False),
-        swap(lax.dynamic_index_in_dim(error, 1 - core, keepdims=False), "c"),
-    )
-    start = (seed_matrix.astype(jnp.float32) / 128.0).T.reshape(RANK, XL, C, quarter)
-    start = lax.dynamic_index_in_dim(start, core, axis=2, keepdims=False).reshape(RANK, -1)
 
     chips = XH * XL * Z
     chip_rows = C * rows
     pieces = lax.all_to_all(grad_part.reshape(chips, chip_rows, quarter), CHIP, 0, 0, tiled=True)
-    message, memory = rows_part(pieces, error_rows, start)
+    message, grad = rows_part(pieces, error, start, error_left)
 
     arrived = lax.all_to_all(message, ("y", "c"), 0, 0, tiled=True)
-    arrived, memory = lax.optimization_barrier((arrived, memory))
     other_chip = swap(chip_part[1].astype(jnp.bfloat16), "xl")
     mixed = (
         stream.astype(jnp.float32) + 0.5 * (chip_part[0] + other_chip.astype(jnp.float32))
     ).astype(jnp.bfloat16)
-    memory = memory.reshape(C, rows, XL * quarter)
-    memory_rows = by_core(
-        lax.dynamic_index_in_dim(memory, core),
-        swap(lax.dynamic_index_in_dim(memory, 1 - core), "c"),
-    )
-    packed = mean_part(arrived, chips)
+    grad = grad.reshape(C, rows, XL * quarter)
+    grad_rows = by_core(
+        lax.dynamic_index_in_dim(grad, core),
+        swap(lax.dynamic_index_in_dim(grad, 1 - core), "c"),
+    )
+    packed = mean_part(arrived, chips, chip_rows)
     columns = lax.all_to_all(packed, CHIP, 0, 0, tiled=True).reshape(features, -1)
     chip = lax.axis_index(CHIP).astype(jnp.int32).reshape(1)
     width = arrived.shape[2]
     message = tail(chip, columns, Y * C, rows, width)
     arrived = lax.all_to_all(message, ("y", "c"), 0, 0, tiled=True)
-    new_memory, compressed = last_part(arrived, memory_rows)
+    new_memory, compressed = last_part(arrived, grad_rows, error)
     return (mixed[None], new_memory[None], compressed)
 
 

time: 145 us -> 144 us (level)
  starting transfers between devices: 72.8 us -> 69.3 us
  waiting for transfers between devices: 45.4 us -> 47.7 us
    all_to_all x1, waiting for transfers between devices: 5.29 us -> 7.41 us  [per_device(): lax.all_to_all(packed, CHIP, 0, 0, tiled=True).reshape(features, -1)]
    all_to_all x1, waiting for transfers between devices: 3.54 us -> 5.28 us  [gather_by_exchange(): return lax.all_to_all(copies, axis, 0, 0, tiled=True)]
    ppermute x8 -> x7, starting transfers between devices: 19.5 us -> 17.9 us  [swap(): return lax.ppermute(block, axis, [(0, 1), (1, 0)])]
    all_to_all x1, waiting for transfers between devices: 7.06 us -> 5.51 us  [per_device(): lax.all_to_all(grad_part.reshape(chips, chip_rows, quarter), CHIP, 0, 0,...]
    ppermute x8 -> x7, waiting for transfers between devices: 11 us -> 12 us  [swap(): return lax.ppermute(block, axis, [(0, 1), (1, 0)])]
    unnamed x29 -> x27, local copies, waits for them, and re-layouts: 3.38 us -> 2.77 us
  transfers between devices with their start and end apart: 17 -> 16, of which waited for: 7 -> 8; matrix products, arithmetic and copies ran while one was open for 6% -> 7% of each run, Pallas kernels for 6% -> 6%
where the time goes in v8:
time: 144 us; the launch traced here: 143 us
  starting transfers between devices  69.3 us (48%)
  waiting for transfers between devices  47.7 us (33%)
  Pallas kernels  10.9 us (8%)
  local copies, waits for them, and re-layouts  8.08 us (6%)
  other arithmetic  3.54 us (2%)
  matrix products  2.33 us (2%)
    ppermute x7, starting transfers between devices, swap(): return lax.ppermute(block, axis, [(0, 1), (1, 0)])  17.9 us
    all_to_all x2, starting transfers between devices, per_device(): arrived = lax.all_to_all(message, ('y', 'c'), 0, 0, tiled=True)  16 us
    all_to_all x2, waiting for transfers between devices, per_device(): arrived = lax.all_to_all(message, ('y', 'c'), 0, 0, tiled=True)  15 us
    ppermute x7, waiting for transfers between devices, swap(): return lax.ppermute(block, axis, [(0, 1), (1, 0)])  12 us
    all_to_all x1, starting transfers between devices, gather_by_exchange(): return lax.all_to_all(copies, axis, 0, 0, tiled=True)  11 us
    all_to_all x1, waiting for transfers between devices, per_device(): lax.all_to_all(packed, CHIP, 0, 0, tiled=True).reshape(features, -1)  7.41 us
    all_to_all x1, waiting for transfers between devices, per_device(): lax.all_to_all(grad_part.reshape(chips, chip_rows, quarter), CHIP, 0, 0,...  5.51 us
    all_to_all x1, starting transfers between devices, per_device(): lax.all_to_all(packed, CHIP, 0, 0, tiled=True).reshape(features, -1)  5.5 us
  transfers between devices with their start and end apart: 16, of which 8 were waited for; matrix products, arithmetic and copies ran while one was open for 7% of the time, Pallas kernels for 6%

profile of v8, /device:TPU:1, one launch (start us, length us, event | category | flops | bytes accessed | tf_op | source)
XLA Modules:
  0.0 142.9 jit_solution(8033002113384748827)
XLA Ops:
  0.6 4.0 %collective-permute-start.3 = (bf16[256,512]{1,0:T(8,128)(2,1)}, bf16[256,512]{1,0:T(8,128)(2,1)S(1)}, u32[]{:S(2)}, u32[]{:S(2)}) collective-permute-start(bf16[256,512]{1,0:T(8,128)(2,1)} %bitcast.62), channel_id=1, source_target_pairs={{0,16},{16,0},{1,17},{17,1},{2,18},{18,2},{3,19},{19,3},{4,20},{20... | collective-permute-start | bytes 786440 | tf_op jit(solution)/shard_map/ppermute | solution.py:30
  4.6 5.2 %collective-permute-start = (bf16[32,512]{1,0:T(8,128)(2,1)}, bf16[32,512]{1,0:T(8,128)(2,1)S(1)}, u32[]{:S(2)}, u32[]{:S(2)}) collective-permute-start(bf16[32,512]{1,0:T(8,128)(2,1)} %param.12), channel_id=1, source_target_pairs={{0,0},{1,32},{2,2},{3,34},{4,4},{5,36},{6,6},{7,38},{8,8},{9,40},{... | collective-permute-start | bytes 98312 | tf_op jit(solution)/shard_map/ppermute | solution.py:185
  9.8 4.9 %all-to-all-start = ((bf16[4,8,512]{2,1,0:T(8,128)(2,1)}), bf16[4,8,512]{2,1,0:T(8,128)(2,1)S(1)}, u32[]{:S(2)}, u32[]{:S(2)}) async-start(bf16[4,8,512]{2,1,0:T(8,128)(2,1)} %bitcast.67), calls=%async_computation | async-start | bytes 65536 | tf_op jit(solution)/shard_map/all_to_all | solution.py:187
  14.7 0.7 slice_bitcast_fusion.1
  15.4 1.9 %collective-permute-start.1 = (bf16[16,512]{1,0:T(8,128)(2,1)S(1)}, bf16[16,512]{1,0:T(8,128)(2,1)S(1)}, u32[]{:S(2)}, u32[]{:S(2)}) collective-permute-start(bf16[16,512]{1,0:T(8,128)(2,1)S(1)} %get-tuple-element.30), channel_id=1, source_target_pairs={{0,1},{1,2},{2,3},{3,4},{4,5},{5,6},{6,7},{7,8},{8,9},{9,10},{10,1... | collective-permute-start | bytes 49160 | tf_op jit(solution)/shard_map/ppermute | solution.py:24
  17.3 2.4 %collective-permute-start.2 = (bf16[16,512]{1,0:T(8,128)(2,1)S(1)}, bf16[16,512]{1,0:T(8,128)(2,1)S(1)}, u32[]{:S(2)}, u32[]{:S(2)}) collective-permute-start(bf16[16,512]{1,0:T(8,128)(2,1)S(1)} %get-tuple-element.29), channel_id=1, source_target_pairs={{1,0},{2,1},{3,2},{4,3},{5,4},{6,5},{7,6},{8,7},{9,8},{10,9},{11,1... | collective-permute-start | bytes 49160 | tf_op jit(solution)/shard_map/ppermute | solution.py:25
  19.7 0.0 all-to-all-done
  19.7 0.0 collective-permute-done
  19.8 0.0 copy-start.3
  19.8 0.0 copy-start.6
  19.8 0.0 copy-start.7
  19.8 0.0 copy-start.8
  19.8 0.0 copy-start.12
  19.8 0.0 collective-permute-done.1.low_ref
  19.8 2.5 %collective-permute-done.2.high_ref = bf16[16,512]{1,0:T(8,128)(2,1)S(1)} collective-permute-done((bf16[16,512]{1,0:T(8,128)(2,1)S(1)}, bf16[16,512]{1,0:T(8,128)(2,1)S(1)}, u32[]{:S(2)}, u32[]{:S(2)}) %collective-permute-start.2) | collective-permute-done | bytes 16416 | tf_op jit(solution)/shard_map/ppermute | solution.py:25
  22.4 0.0 collective-permute-done.3
  22.4 1.1 broadcast_in_dim.16
  23.5 11.0 %all-to-all-start.1 = ((bf16[16,64,512]{2,1,0:T(8,128)(2,1)}), bf16[16,64,512]{2,1,0:T(8,128)(2,1)S(1)}, u32[]{:S(2)}, u32[]{:S(2)}) async-start(bf16[16,64,512]{2,1,0:T(8,128)(2,1)} %broadcast_in_dim.16), calls=%async_computation.1 | async-start | bytes 2097152 | tf_op jit(solution)/shard_map/all_to_all | solution.py:171
  34.5 2.0 %tokens_part.1 = (bf16[256,512]{1,0:T(8,128)(2,1)S(1)}, bf16[272,512]{1,0:T(8,128)(2,1)S(1)}) custom-call(bf16[256,512]{1,0:T(8,128)(2,1)S(1)} %bitcast.55, bf16[16,512]{1,0:T(8,128)(2,1)S(1)} %collective-permute-done.1.low_ref, bf16[16,512]{1,0:T(8,128)(2,1)S(1)} %collective-permute-done.2.high_ref, s32[1,256]{1,0:T(1,128)S(1)} %copy-done.8, ...), custom_call_target="tpu_custom_call" | custom-call | flops 8000000 | bytes 1500000 | tf_op jit(solution)/shard_map/tokens_part/pallas_call | solution.py:79
  36.4 0.0 copy-start.4
  36.5 1.9 %collective-permute-start.4 = (bf16[272,512]{1,0:T(8,128)(2,1)S(1)}, bf16[272,512]{1,0:T(8,128)(2,1)S(1)}, u32[]{:S(2)}, u32[]{:S(2)}) collective-permute-start(bf16[272,512]{1,0:T(8,128)(2,1)S(1)} %get-tuple-element.18), channel_id=1, source_target_pairs={{0,16},{16,0},{1,17},{17,1},{2,18},{18,2},{3,19},{19,3},{4,20},{20... | collective-permute-start | bytes 835592 | tf_op jit(solution)/shard_map/ppermute | solution.py:30
  38.4 0.0 copy-done.12
  38.4 0.1 pad_maximum_fusion.3
  38.5 2.2 %collective-permute-start.6 = (bf16[2,256,512]{2,1,0:T(8,128)(2,1)S(1)}, bf16[2,256,512]{2,1,0:T(8,128)(2,1)}, u32[]{:S(2)}, u32[]{:S(2)}) collective-permute-start(bf16[2,256,512]{2,1,0:T(8,128)(2,1)S(1)} %pad_maximum_fusion.3), channel_id=1, source_target_pairs={{0,1},{1,0},{2,3},{3,2},{4,5},{5,4},{6,7},{7,6},{8,9},{9,8},{10,11... | collective-permute-start | bytes 1572872 | tf_op jit(solution)/shard_map/ppermute | solution.py:30
  40.7 11.1 %collective-permute-done.4 = bf16[272,512]{1,0:T(8,128)(2,1)S(1)} collective-permute-done((bf16[272,512]{1,0:T(8,128)(2,1)S(1)}, bf16[272,512]{1,0:T(8,128)(2,1)S(1)}, u32[]{:S(2)}, u32[]{:S(2)}) %collective-permute-start.4) | collective-permute-done | bytes 278560 | tf_op jit(solution)/shard_map/ppermute | solution.py:30
  51.8 0.0 copy-done.4
  51.8 0.7 copy-done.9
  52.5 0.1 pad_maximum_fusion.2
  52.5 1.9 %collective-permute-start.5 = (bf16[2,272,512]{2,1,0:T(8,128)(2,1)S(1)}, bf16[2,272,512]{2,1,0:T(8,128)(2,1)}, u32[]{:S(2)}, u32[]{:S(2)}) collective-permute-start(bf16[2,272,512]{2,1,0:T(8,128)(2,1)S(1)} %pad_maximum_fusion.2), channel_id=1, source_target_pairs={{0,1},{1,0},{2,3},{3,2},{4,5},{5,4},{6,7},{7,6},{8,9},{9,8},{10,11... | collective-permute-start | bytes 1671176 | tf_op jit(solution)/shard_map/ppermute | solution.py:30
  54.5 0.0 collective-permute-done.6
  54.5 1.2 pad_maximum_fusion.1.cotangents_ref
  55.7 0.8 collective-permute-done.5
  56.5 1.2 pad_maximum_fusion.packs_ref
  57.7 5.3 %all-to-all-done.1 = bf16[16,64,512]{2,1,0:T(8,128)(2,1)S(1)} async-done(((bf16[16,64,512]{2,1,0:T(8,128)(2,1)}), bf16[16,64,512]{2,1,0:T(8,128)(2,1)S(1)}, u32[]{:S(2)}, u32[]{:S(2)}) %all-to-all-start.1) | async-done | bytes 1048608 | tf_op jit(solution)/shard_map/all_to_all | solution.py:171
  63.0 2.2 %hidden_part.1 = (bf16[512,512]{1,0:T(8,128)(2,1)S(1)}, bf16[1536,512]{1,0:T(8,128)(2,1)S(1)}) custom-call(bf16[4,272,512]{2,1,0:T(8,128)(2,1)S(1)} %pad_maximum_fusion.packs_ref, bf16[4,256,512]{2,1,0:T(8,128)(2,1)S(1)} %pad_maximum_fusion.1.cotangents_ref, bf16[2,8,64,512]{3,2,1,0:T(8,128)(2,1)S(1)} %bitcast.47), custom_call_target="tpu_custom_call" | custom-call | tf_op jit(solution)/shard_map/hidden_part/pallas_call | solution.py:148
  65.2 1.2 copy-done
  66.4 0.8 copy-done.2
  67.2 4.5 %all-to-all-start.2 = ((bf16[32,16,512]{2,1,0:T(8,128)(2,1)}), bf16[32,16,512]{2,1,0:T(8,128)(2,1)S(1)}, u32[]{:S(2)}, u32[]{:S(2)}) async-start(bf16[32,16,512]{2,1,0:T(8,128)(2,1)} %bitcast.53), calls=%async_computation.2 | async-start | bytes 1048576 | tf_op jit(solution)/shard_map/all_to_all | solution.py:390
  71.7 2.1 %fusion = f32[1024,512]{1,0:T(8,128)S(1)} fusion(bf16[1536,512]{1,0:T(8,128)(2,1)} %copy-done), kind=kOutput, calls=%fused_computation.3 | convolution fusion | flops 536870912 | bytes 3670016 | tf_op jit(solution)/shard_map/dot_general | solution.py:376
  73.8 0.0 copy-start.11
  73.8 1.2 fusion.13
  75.0 2.7 %collective-permute-start.7 = (f32[2,256,512]{2,1,0:T(8,128)}, f32[2,256,512]{2,1,0:T(8,128)S(1)}, u32[]{:S(2)}, u32[]{:S(2)}) collective-permute-start(f32[2,256,512]{2,1,0:T(8,128)} %bitcast.13), channel_id=1, source_target_pairs={{0,1},{1,0},{2,3},{3,2},{4,5},{5,4},{6,7},{7,6},{8,9},{9,8},{10,11... | collective-permute-start | bytes 3145736 | tf_op jit(solution)/shard_map/ppermute | solution.py:30
  77.7 0.9 reshape.48
  78.6 1.4 dynamic-slice_reduce_fusion
  80.1 0.3 convolution_bitcast_fusion.error_left_ref
  80.4 5.5 %all-to-all-done.2.pieces_ref = bf16[32,16,512]{2,1,0:T(8,128)(2,1)S(1)} async-done(((bf16[32,16,512]{2,1,0:T(8,128)(2,1)}), bf16[32,16,512]{2,1,0:T(8,128)(2,1)S(1)}, u32[]{:S(2)}, u32[]{:S(2)}) %all-to-all-start.2) | async-done | bytes 524320 | tf_op jit(solution)/shard_map/all_to_all | solution.py:390
  85.9 1.0 rows_part.1
  86.9 10.7 %all-to-all-start.3 = ((f32[16,24,128]{2,1,0:T(8,128)}), f32[16,24,128]{2,1,0:T(8,128)S(1)}, u32[]{:S(2)}, u32[]{:S(2)}) async-start(f32[16,24,128]{2,1,0:T(8,128)} %get-tuple-element.23), calls=%async_computation.3 | async-start | bytes 393216 | tf_op jit(solution)/shard_map/all_to_all | solution.py:393
  97.6 2.0 %collective-permute-start.9 = (f32[1,8,1024]{2,1,0:T(8,128)S(1)}, f32[1,8,1024]{2,1,0:T(8,128)S(1)}, u32[]{:S(2)}, u32[]{:S(2)}) collective-permute-start(f32[1,8,1024]{2,1,0:T(8,128)S(1)} %constant_dynamic-slice_fusion), channel_id=1, source_target_pairs={{0,1},{1,0},{2,3},{3,2},{4,5},{5,4},{6,7},{7,6},{8,9},{9,8},{10,11... | collective-permute-start | bytes 98312 | tf_op jit(solution)/shard_map/ppermute | solution.py:30
  99.6 0.0 collective-permute-done.7
  99.7 0.2 add.25
  99.9 0.0 copy-start.5
  99.9 8.0 %all-to-all-done.3.arrived_ref = f32[16,24,128]{2,1,0:T(8,128)S(1)} async-done(((f32[16,24,128]{2,1,0:T(8,128)}), f32[16,24,128]{2,1,0:T(8,128)S(1)}, u32[]{:S(2)}, u32[]{:S(2)}) %all-to-all-start.3) | async-done | bytes 196640 | tf_op jit(solution)/shard_map/all_to_all | solution.py:393
  107.9 0.9 mean_part.1
  108.8 5.5 %all-to-all-start.4 = ((bf16[32,16,256]{2,1,0:T(8,128)(2,1)}), bf16[32,16,256]{2,1,0:T(8,128)(2,1)S(1)}, u32[]{:S(2)}, u32[]{:S(2)}) async-start(bf16[32,16,256]{2,1,0:T(8,128)(2,1)} %mean_part.1), calls=%async_computation.4 | async-start | bytes 524288 | tf_op jit(solution)/shard_map/all_to_all | solution.py:404
  114.3 3.1 %collective-permute-start.8 = (bf16[256,512]{1,0:T(8,128)(2,1)S(1)}, bf16[256,512]{1,0:T(8,128)(2,1)S(1)}, u32[]{:S(2)}, u32[]{:S(2)}) collective-permute-start(bf16[256,512]{1,0:T(8,128)(2,1)S(1)} %fusion.8), channel_id=1, source_target_pairs={{0,16},{16,0},{1,17},{17,1},{2,18},{18,2},{3,19},{19,3},{4,20},{20... | collective-permute-start | bytes 786440 | tf_op jit(solution)/shard_map/ppermute | solution.py:30
  117.5 0.0 collective-permute-done.9
  117.5 7.4 %all-to-all-done.4 = bf16[32,16,256]{2,1,0:T(8,128)(2,1)S(1)} async-done(((bf16[32,16,256]{2,1,0:T(8,128)(2,1)}), bf16[32,16,256]{2,1,0:T(8,128)(2,1)S(1)}, u32[]{:S(2)}, u32[]{:S(2)}) %all-to-all-start.4) | async-done | bytes 262176 | tf_op jit(solution)/shard_map/all_to_all | solution.py:404
  124.9 4.1 %tail.1 = f32[16,8,128]{2,1,0:T(8,128)} custom-call(s32[1]{0:T(128)} %bitcast.17.chip_ref, bf16[512,256]{1,0:T(8,128)(2,1)S(1)} %bitcast.50), custom_call_target="tpu_custom_call" | custom-call | tf_op jit(solution)/shard_map/tail/pallas_call | solution.py:339
  129.0 5.3 %all-to-all-start.5 = ((f32[16,8,128]{2,1,0:T(8,128)}), f32[16,8,128]{2,1,0:T(8,128)S(1)}, u32[]{:S(2)}, u32[]{:S(2)}) async-start(f32[16,8,128]{2,1,0:T(8,128)} %tail.1), calls=%async_computation.5 | async-start | bytes 131072 | tf_op jit(solution)/shard_map/all_to_all | solution.py:408
  134.3 0.0 collective-permute-done.8
  134.3 0.8 fusion.7
  135.2 7.0 %all-to-all-done.5.arrived_ref = f32[16,8,128]{2,1,0:T(8,128)S(1)} async-done(((f32[16,8,128]{2,1,0:T(8,128)}), f32[16,8,128]{2,1,0:T(8,128)S(1)}, u32[]{:S(2)}, u32[]{:S(2)}) %all-to-all-start.5) | async-done | bytes 65568 | tf_op jit(solution)/shard_map/all_to_all | solution.py:408
  142.1 0.7 last_part.1
  (20 shorter events, 0.1 us)
Async XLA Ops:
  0.6 21.7 %collective-permute-start.3 = (bf16[256,512]{1,0:T(8,128)(2,1)}, bf16[256,512]{1,0:T(8,128)(2,1)S(1)}, u32[]{:S(2)}, u32[]{:S(2)}) collective-permute-start(bf16[256,512]{1,0:T(8,128)(2,1)} %bitcast.62), channel_id=1, source_target_pairs={{0,16},{16,0},{1,17},{17,1},{2,18},{18,2},{3,19},{19,3},{4,20},{20... | collective-permute-start | bytes 786440 | tf_op jit(solution)/shard_map/ppermute | solution.py:30
  4.6 15.1 %collective-permute-start = (bf16[32,512]{1,0:T(8,128)(2,1)}, bf16[32,512]{1,0:T(8,128)(2,1)S(1)}, u32[]{:S(2)}, u32[]{:S(2)}) collective-permute-start(bf16[32,512]{1,0:T(8,128)(2,1)} %param.12), channel_id=1, source_target_pairs={{0,0},{1,32},{2,2},{3,34},{4,4},{5,36},{6,6},{7,38},{8,8},{9,40},{... | collective-permute-start | bytes 98312 | tf_op jit(solution)/shard_map/ppermute | solution.py:185
  9.8 9.9 %all-to-all-start = ((bf16[4,8,512]{2,1,0:T(8,128)(2,1)}), bf16[4,8,512]{2,1,0:T(8,128)(2,1)S(1)}, u32[]{:S(2)}, u32[]{:S(2)}) async-start(bf16[4,8,512]{2,1,0:T(8,128)(2,1)} %bitcast.67), calls=%async_computation | async-start | bytes 65536 | tf_op jit(solution)/shard_map/all_to_all | solution.py:187
  15.4 4.4 %collective-permute-start.1 = (bf16[16,512]{1,0:T(8,128)(2,1)S(1)}, bf16[16,512]{1,0:T(8,128)(2,1)S(1)}, u32[]{:S(2)}, u32[]{:S(2)}) collective-permute-start(bf16[16,512]{1,0:T(8,128)(2,1)S(1)} %get-tuple-element.30), channel_id=1, source_target_pairs={{0,1},{1,2},{2,3},{3,4},{4,5},{5,6},{6,7},{7,8},{8,9},{9,10},{10,1... | collective-permute-start | bytes 49160 | tf_op jit(solution)/shard_map/ppermute | solution.py:24
  17.3 5.1 %collective-permute-start.2 = (bf16[16,512]{1,0:T(8,128)(2,1)S(1)}, bf16[16,512]{1,0:T(8,128)(2,1)S(1)}, u32[]{:S(2)}, u32[]{:S(2)}) collective-permute-start(bf16[16,512]{1,0:T(8,128)(2,1)S(1)} %get-tuple-element.29), channel_id=1, source_target_pairs={{1,0},{2,1},{3,2},{4,3},{5,4},{6,5},{7,6},{8,7},{9,8},{10,9},{11,1... | collective-permute-start | bytes 49160 | tf_op jit(solution)/shard_map/ppermute | solution.py:25
  19.8 14.7 %copy-start.3 = (bf16[1,256,512]{2,1,0:T(8,128)(2,1)S(1)}, bf16[1,256,512]{2,1,0:T(8,128)(2,1)}, u32[]{:S(2)}) copy-start(bf16[1,256,512]{2,1,0:T(8,128)(2,1)} %param.9) | copy-start | bytes 786436
  19.8 14.7 %copy-start.6 = (f32[31,512]{1,0:T(8,128)S(1)}, f32[31,512]{1,0:T(8,128)}, u32[]{:S(2)}) copy-start(f32[31,512]{1,0:T(8,128)} %taps_ref.1) | copy-start | bytes 190468
  19.8 14.7 %copy-start.7 = (f32[512]{0:T(512)S(1)}, f32[512]{0:T(512)}, u32[]{:S(2)}) copy-start(f32[512]{0:T(512)} %param.14) | copy-start | bytes 6148
  19.8 14.7 %copy-start.8 = (s32[1,256]{1,0:T(1,128)S(1)}, s32[1,256]{1,0:T(1,128)}, u32[]{:S(2)}) copy-start(s32[1,256]{1,0:T(1,128)} %mask_ref.1) | copy-start | bytes 3076
  19.8 18.6 %copy-start.12 = (bf16[1,256,512]{2,1,0:T(8,128)(2,1)S(1)}, bf16[1,256,512]{2,1,0:T(8,128)(2,1)}, u32[]{:S(2)}) copy-start(bf16[1,256,512]{2,1,0:T(8,128)(2,1)} %param.10) | copy-start | bytes 786436
  23.5 39.5 %all-to-all-start.1 = ((bf16[16,64,512]{2,1,0:T(8,128)(2,1)}), bf16[16,64,512]{2,1,0:T(8,128)(2,1)S(1)}, u32[]{:S(2)}, u32[]{:S(2)}) async-start(bf16[16,64,512]{2,1,0:T(8,128)(2,1)} %broadcast_in_dim.16), calls=%async_computation.1 | async-start | bytes 2097152 | tf_op jit(solution)/shard_map/all_to_all | solution.py:171
  36.4 15.3 %copy-start.4 = (bf16[256,512]{1,0:T(8,128)(2,1)}, bf16[256,512]{1,0:T(8,128)(2,1)S(1)}, u32[]{:S(2)}) copy-start(bf16[256,512]{1,0:T(8,128)(2,1)S(1)} %get-tuple-element.17) | copy-start | bytes 786436
  36.5 15.3 %collective-permute-start.4 = (bf16[272,512]{1,0:T(8,128)(2,1)S(1)}, bf16[272,512]{1,0:T(8,128)(2,1)S(1)}, u32[]{:S(2)}, u32[]{:S(2)}) collective-permute-start(bf16[272,512]{1,0:T(8,128)(2,1)S(1)} %get-tuple-element.18), channel_id=1, source_target_pairs={{0,16},{16,0},{1,17},{17,1},{2,18},{18,2},{3,19},{19,3},{4,20},{20... | collective-permute-start | bytes 835592 | tf_op jit(solution)/shard_map/ppermute | solution.py:30
  38.5 16.0 %collective-permute-start.6 = (bf16[2,256,512]{2,1,0:T(8,128)(2,1)S(1)}, bf16[2,256,512]{2,1,0:T(8,128)(2,1)}, u32[]{:S(2)}, u32[]{:S(2)}) collective-permute-start(bf16[2,256,512]{2,1,0:T(8,128)(2,1)S(1)} %pad_maximum_fusion.3), channel_id=1, source_target_pairs={{0,1},{1,0},{2,3},{3,2},{4,5},{5,4},{6,7},{7,6},{8,9},{9,8},{10,11... | collective-permute-start | bytes 1572872 | tf_op jit(solution)/shard_map/ppermute | solution.py:30
  51.8 0.7 copy-start.9
  52.5 4.0 %collective-permute-start.5 = (bf16[2,272,512]{2,1,0:T(8,128)(2,1)S(1)}, bf16[2,272,512]{2,1,0:T(8,128)(2,1)}, u32[]{:S(2)}, u32[]{:S(2)}) collective-permute-start(bf16[2,272,512]{2,1,0:T(8,128)(2,1)S(1)} %pad_maximum_fusion.2), channel_id=1, source_target_pairs={{0,1},{1,0},{2,3},{3,2},{4,5},{5,4},{6,7},{7,6},{8,9},{9,8},{10,11... | collective-permute-start | bytes 1671176 | tf_op jit(solution)/shard_map/ppermute | solution.py:30
  54.5 2.1 %copy-start.10 = (bf16[272,512]{1,0:T(8,128)(2,1)S(1)}, bf16[272,512]{1,0:T(8,128)(2,1)}, u32[]{:S(2)}) copy-start(bf16[272,512]{1,0:T(8,128)(2,1)} %copy-done.9) | copy-start | bytes 835588
  65.2 1.2 copy-start
  66.4 0.8 copy-start.2
  67.2 18.7 %all-to-all-start.2 = ((bf16[32,16,512]{2,1,0:T(8,128)(2,1)}), bf16[32,16,512]{2,1,0:T(8,128)(2,1)S(1)}, u32[]{:S(2)}, u32[]{:S(2)}) async-start(bf16[32,16,512]{2,1,0:T(8,128)(2,1)} %bitcast.53), calls=%async_computation.2 | async-start | bytes 1048576 | tf_op jit(solution)/shard_map/all_to_all | solution.py:390
  73.8 3.9 %copy-start.11 = (s32[2048,32]{0,1:T(8,128)S(1)}, s32[2048,32]{0,1:T(8,128)}, u32[]{:S(2)}) copy-start(s32[2048,32]{0,1:T(8,128)} %param.17) | copy-start | bytes 786436
  75.0 5.1 %copy-start.1 = (f32[1,8,2048]{2,1,0:T(8,128)S(1)}, f32[1,8,2048]{2,1,0:T(8,128)}, u32[]{:S(2)}) copy-start(f32[1,8,2048]{2,1,0:T(8,128)} %param.16) | copy-start | bytes 196612
  75.0 24.7 %collective-permute-start.7 = (f32[2,256,512]{2,1,0:T(8,128)}, f32[2,256,512]{2,1,0:T(8,128)S(1)}, u32[]{:S(2)}, u32[]{:S(2)}) collective-permute-start(f32[2,256,512]{2,1,0:T(8,128)} %bitcast.13), channel_id=1, source_target_pairs={{0,1},{1,0},{2,3},{3,2},{4,5},{5,4},{6,7},{7,6},{8,9},{9,8},{10,11... | collective-permute-start | bytes 3145736 | tf_op jit(solution)/shard_map/ppermute | solution.py:30
  86.9 21.0 %all-to-all-start.3 = ((f32[16,24,128]{2,1,0:T(8,128)}), f32[16,24,128]{2,1,0:T(8,128)S(1)}, u32[]{:S(2)}, u32[]{:S(2)}) async-start(f32[16,24,128]{2,1,0:T(8,128)} %get-tuple-element.23), calls=%async_computation.3 | async-start | bytes 393216 | tf_op jit(solution)/shard_map/all_to_all | solution.py:393
  97.6 19.9 %collective-permute-start.9 = (f32[1,8,1024]{2,1,0:T(8,128)S(1)}, f32[1,8,1024]{2,1,0:T(8,128)S(1)}, u32[]{:S(2)}, u32[]{:S(2)}) collective-permute-start(f32[1,8,1024]{2,1,0:T(8,128)S(1)} %constant_dynamic-slice_fusion), channel_id=1, source_target_pairs={{0,1},{1,0},{2,3},{3,2},{4,5},{5,4},{6,7},{7,6},{8,9},{9,8},{10,11... | collective-permute-start | bytes 98312 | tf_op jit(solution)/shard_map/ppermute | solution.py:30
  99.9 34.5 %copy-start.5 = (bf16[256,512]{1,0:T(8,128)(2,1)S(1)}, bf16[256,512]{1,0:T(8,128)(2,1)}, u32[]{:S(2)}) copy-start(bf16[256,512]{1,0:T(8,128)(2,1)} %copy-done.4) | copy-start | bytes 786436
  108.8 16.2 %all-to-all-start.4 = ((bf16[32,16,256]{2,1,0:T(8,128)(2,1)}), bf16[32,16,256]{2,1,0:T(8,128)(2,1)S(1)}, u32[]{:S(2)}, u32[]{:S(2)}) async-start(bf16[32,16,256]{2,1,0:T(8,128)(2,1)} %mean_part.1), calls=%async_computation.4 | async-start | bytes 524288 | tf_op jit(solution)/shard_map/all_to_all | solution.py:404
  114.3 20.0 %collective-permute-start.8 = (bf16[256,512]{1,0:T(8,128)(2,1)S(1)}, bf16[256,512]{1,0:T(8,128)(2,1)S(1)}, u32[]{:S(2)}, u32[]{:S(2)}) collective-permute-start(bf16[256,512]{1,0:T(8,128)(2,1)S(1)} %fusion.8), channel_id=1, source_target_pairs={{0,16},{16,0},{1,17},{17,1},{2,18},{18,2},{3,19},{19,3},{4,20},{20... | collective-permute-start | bytes 786440 | tf_op jit(solution)/shard_map/ppermute | solution.py:30
  129.0 13.1 %all-to-all-start.5 = ((f32[16,8,128]{2,1,0:T(8,128)}), f32[16,8,128]{2,1,0:T(8,128)S(1)}, u32[]{:S(2)}, u32[]{:S(2)}) async-start(f32[16,8,128]{2,1,0:T(8,128)} %tail.1), calls=%async_computation.5 | async-start | bytes 131072 | tf_op jit(solution)/shard_map/all_to_all | solution.py:408

commit v9 on v7

--- a/solution.py
+++ b/solution.py
@@ -93,8 +93,10 @@
 
 
 def hidden_kernel(
-    packs_ref, cotangents_ref, whole_ref, grad_ref, hidden_ref, down_ref, up, delta, masked
+    packs_ref, cotangents_ref, whole_ref, grad_ref, both_ref, up, delta, masked
 ):
+    blocks, frames, features = cotangents_ref.shape
+    hidden_ref, down_ref = both_ref.at[: blocks * frames], both_ref.at[blocks * frames :]
     half = whole_ref.shape[2] // 2
     part = half // XL
     for xh in range(XH):
@@ -104,7 +106,6 @@
                 up[row : row + part] = whole_ref[xh, z, xl * part : (xl + 1) * part]
             row = (z * XH + xh) * half
             down_ref[row : row + half] = whole_ref[xh, z, half:]
-    blocks, frames, features = cotangents_ref.shape
     lanes = 128
     for index in range(blocks):
         rows = slice(index * frames, (index + 1) * frames)
@@ -148,8 +149,7 @@
         hidden_kernel,
         out_shape=(
             jax.ShapeDtypeStruct((features, quarter), bf16),
-            jax.ShapeDtypeStruct((blocks * frames, quarter), bf16),
-            jax.ShapeDtypeStruct((quarter, features), bf16),
+            jax.ShapeDtypeStruct((blocks * frames + quarter, features), bf16),
         ),
         scratch_shapes=[
             pltpu.VMEM((features, quarter), bf16),
@@ -208,10 +208,12 @@
     )
     chunks, _, width = message_ref.shape
     part = width // C
-    filler = jnp.zeros((rows, width - part - RANK), jnp.float32)
+    high = left.astype(jnp.bfloat16)
+    low = (left - high.astype(jnp.float32)).astype(jnp.bfloat16)
+    kept = memory.astype(jnp.bfloat16)
     for chunk in range(chunks):
         columns = slice(chunk * part, (chunk + 1) * part)
-        message_ref[chunk] = jnp.concatenate([memory[:, columns], left, filler], axis=1)
+        message_ref[chunk] = jnp.concatenate([kept[:, columns], high, low], axis=1)
 
 
 def rows_part(pieces, error_rows, start):
@@ -220,7 +222,7 @@
     return pl.pallas_call(
         rows_kernel,
         out_shape=(
-            jax.ShapeDtypeStruct((chunks, rows, C * columns // chunks), jnp.float32),
+            jax.ShapeDtypeStruct((chunks, rows, C * columns // chunks), jnp.bfloat16),
             jax.ShapeDtypeStruct((rows, columns), jnp.float32),
         ),
         compiler_params=pltpu.CompilerParams(vmem_limit_bytes=8 * 1024 * 1024),
@@ -233,11 +235,11 @@
     part = width // C
     sums = []
     for c in range(C):
-        total = arrived_ref[c]
+        total = arrived_ref[c].astype(jnp.float32)
         for sender in range(c + C, senders, C):
-            total = total + arrived_ref[sender]
+            total = total + arrived_ref[sender].astype(jnp.float32)
         sums.append(total / Y)
-    left = sums[0][:, part : part + RANK] + sums[1][:, part : part + RANK]
+    left = sum(total[:, part : part + RANK] + total[:, part + RANK :] for total in sums)
     parts = [jnp.concatenate([total[:, :part] for total in sums], axis=1).astype(jnp.bfloat16)]
     for _ in range(3):
         parts.append(left.astype(jnp.bfloat16))
@@ -357,15 +359,17 @@
     stream, own = tokens_part(tokens[0], low, high, frame_mask, kernel, norm_gain[None])
     packs = group_frames(own, swap(own, "xl"))
     cotangents = group_frames(cotangent[0], cotangent_x)
-    grad_part, hidden, down = hidden_part(packs, cotangents, whole)
-
+    grad_part, both = hidden_part(packs, cotangents, whole)
+
+    hidden, down = both[: QUARTERS * frames], both[QUARTERS * frames :]
     mixed_part = jnp.dot(hidden, down, preferred_element_type=jnp.float32)
     mixed_part = mixed_part.reshape(C, XL, frames, features)
-    chip_part = mixed_part[0] + swap(mixed_part[1], "c")
+    mixed_away, error = lax.optimization_barrier((mixed_part[1], error_memory[0]))
+    chip_part = mixed_part[0] + swap(mixed_away, "c")
 
     core = lax.axis_index("c")
-    rows, quarter = error_memory.shape[1], error_memory.shape[2] // QUARTERS
-    error = error_memory[0].reshape(rows, XL, C, quarter).transpose(2, 0, 1, 3)
+    rows, quarter = error.shape[0], error.shape[1] // QUARTERS
+    error = error.reshape(rows, XL, C, quarter).transpose(2, 0, 1, 3)
     error = error.reshape(C, rows, XL * quarter)
     error_rows = by_core(
         lax.dynamic_index_in_dim(error, core, keepdims=False),
@@ -380,7 +384,6 @@
     message, memory = rows_part(pieces, error_rows, start)
 
     arrived = lax.all_to_all(message, ("y", "c"), 0, 0, tiled=True)
-    arrived, memory = lax.optimization_barrier((arrived, memory))
     other_chip = swap(chip_part[1].astype(jnp.bfloat16), "xl")
     mixed = (
         stream.astype(jnp.float32) + 0.5 * (chip_part[0] + other_chip.astype(jnp.float32))

time: 145 us -> 141 us (0.972)
  local copies, waits for them, and re-layouts: 7.71 us -> 4.95 us
    all_to_all x2, waiting for transfers between devices: 15.9 us -> 11.3 us  [per_device(): arrived = lax.all_to_all(message, ('y', 'c'), 0, 0, tiled=True)]
    unnamed x29 -> x27, local copies, waits for them, and re-layouts: 3.38 us -> 0.89 us
    all_to_all x1, waiting for transfers between devices: 3.54 us -> 5.26 us  [gather_by_exchange(): return lax.all_to_all(copies, axis, 0, 0, tiled=True)]
    all_to_all x1, waiting for transfers between devices: 5.29 us -> 6.86 us  [per_device(): lax.all_to_all(packed, CHIP, 0, 0, tiled=True).reshape(features, -1)]
  transfers between devices with their start and end apart: 17 -> 17, of which waited for: 7 -> 9; matrix products, arithmetic and copies ran while one was open for 6% -> 6% of each run, Pallas kernels for 6% -> 6%
where the time goes in v9:
time: 141 us; the launch traced here: 140 us
  starting transfers between devices  72.2 us (51%)
  waiting for transfers between devices  45 us (32%)
  Pallas kernels  10.9 us (8%)
  local copies, waits for them, and re-layouts  4.95 us (4%)
  other arithmetic  4.77 us (3%)
    ppermute x8, starting transfers between devices, swap(): return lax.ppermute(block, axis, [(0, 1), (1, 0)])  19.8 us
    all_to_all x2, starting transfers between devices, per_device(): arrived = lax.all_to_all(message, ('y', 'c'), 0, 0, tiled=True)  17 us
    ppermute x8, waiting for transfers between devices, swap(): return lax.ppermute(block, axis, [(0, 1), (1, 0)])  12.4 us
    all_to_all x2, waiting for transfers between devices, per_device(): arrived = lax.all_to_all(message, ('y', 'c'), 0, 0, tiled=True)  11.3 us
    all_to_all x1, starting transfers between devices, gather_by_exchange(): return lax.all_to_all(copies, axis, 0, 0, tiled=True)  11 us
    all_to_all x1, waiting for transfers between devices, per_device(): lax.all_to_all(packed, CHIP, 0, 0, tiled=True).reshape(features, -1)  6.86 us
    all_to_all x1, waiting for transfers between devices, per_device(): lax.all_to_all(grad_part.reshape(chips, chip_rows, quarter), CHIP, 0, 0,...  6.67 us
    all_to_all x1, starting transfers between devices, per_device(): lax.all_to_all(packed, CHIP, 0, 0, tiled=True).reshape(features, -1)  5.5 us
  transfers between devices with their start and end apart: 17, of which 9 were waited for; matrix products, arithmetic and copies ran while one was open for 6% of the time, Pallas kernels for 6%

profile of v9, /device:TPU:1, one launch (start us, length us, event | category | flops | bytes accessed | tf_op | source)
XLA Modules:
  0.0 139.6 jit_solution(11929692635049832605)
XLA Ops:
  0.6 4.0 %collective-permute-start.3 = (bf16[256,512]{1,0:T(8,128)(2,1)}, bf16[256,512]{1,0:T(8,128)(2,1)S(1)}, u32[]{:S(2)}, u32[]{:S(2)}) collective-permute-start(bf16[256,512]{1,0:T(8,128)(2,1)} %bitcast.65), channel_id=1, source_target_pairs={{0,16},{16,0},{1,17},{17,1},{2,18},{18,2},{3,19},{19,3},{4,20},{20... | collective-permute-start | bytes 786440 | tf_op jit(solution)/shard_map/ppermute | solution.py:30
  4.6 5.2 %collective-permute-start = (bf16[32,512]{1,0:T(8,128)(2,1)}, bf16[32,512]{1,0:T(8,128)(2,1)S(1)}, u32[]{:S(2)}, u32[]{:S(2)}) collective-permute-start(bf16[32,512]{1,0:T(8,128)(2,1)} %param.12), channel_id=1, source_target_pairs={{0,0},{1,32},{2,2},{3,34},{4,4},{5,36},{6,6},{7,38},{8,8},{9,40},{... | collective-permute-start | bytes 98312 | tf_op jit(solution)/shard_map/ppermute | solution.py:185
  9.8 4.9 %all-to-all-start = ((bf16[4,8,512]{2,1,0:T(8,128)(2,1)}), bf16[4,8,512]{2,1,0:T(8,128)(2,1)S(1)}, u32[]{:S(2)}, u32[]{:S(2)}) async-start(bf16[4,8,512]{2,1,0:T(8,128)(2,1)} %bitcast.73), calls=%async_computation | async-start | bytes 65536 | tf_op jit(solution)/shard_map/all_to_all | solution.py:187
  14.7 0.7 slice_bitcast_fusion.1
  15.4 1.9 %collective-permute-start.1 = (bf16[16,512]{1,0:T(8,128)(2,1)S(1)}, bf16[16,512]{1,0:T(8,128)(2,1)S(1)}, u32[]{:S(2)}, u32[]{:S(2)}) collective-permute-start(bf16[16,512]{1,0:T(8,128)(2,1)S(1)} %get-tuple-element.34), channel_id=1, source_target_pairs={{0,1},{1,2},{2,3},{3,4},{4,5},{5,6},{6,7},{7,8},{8,9},{9,10},{10,1... | collective-permute-start | bytes 49160 | tf_op jit(solution)/shard_map/ppermute | solution.py:24
  17.3 2.4 %collective-permute-start.2 = (bf16[16,512]{1,0:T(8,128)(2,1)S(1)}, bf16[16,512]{1,0:T(8,128)(2,1)S(1)}, u32[]{:S(2)}, u32[]{:S(2)}) collective-permute-start(bf16[16,512]{1,0:T(8,128)(2,1)S(1)} %get-tuple-element.33), channel_id=1, source_target_pairs={{1,0},{2,1},{3,2},{4,3},{5,4},{6,5},{7,6},{8,7},{9,8},{10,9},{11,1... | collective-permute-start | bytes 49160 | tf_op jit(solution)/shard_map/ppermute | solution.py:25
  19.7 0.0 all-to-all-done
  19.7 0.0 collective-permute-done
  19.8 0.0 copy-start.1
  19.8 0.0 copy-start.4
  19.8 0.0 copy-start.5
  19.8 0.0 copy-start.6
  19.8 0.0 copy-start.10
  19.8 0.0 collective-permute-done.1.low_ref
  19.8 2.5 %collective-permute-done.2.high_ref = bf16[16,512]{1,0:T(8,128)(2,1)S(1)} collective-permute-done((bf16[16,512]{1,0:T(8,128)(2,1)S(1)}, bf16[16,512]{1,0:T(8,128)(2,1)S(1)}, u32[]{:S(2)}, u32[]{:S(2)}) %collective-permute-start.2) | collective-permute-done | bytes 16416 | tf_op jit(solution)/shard_map/ppermute | solution.py:25
  22.4 0.0 collective-permute-done.3
  22.4 1.1 broadcast_in_dim.16
  23.5 11.0 %all-to-all-start.1 = ((bf16[16,64,512]{2,1,0:T(8,128)(2,1)}), bf16[16,64,512]{2,1,0:T(8,128)(2,1)S(1)}, u32[]{:S(2)}, u32[]{:S(2)}) async-start(bf16[16,64,512]{2,1,0:T(8,128)(2,1)} %broadcast_in_dim.16), calls=%async_computation.1 | async-start | bytes 2097152 | tf_op jit(solution)/shard_map/all_to_all | solution.py:171
  34.5 2.0 %tokens_part.1 = (bf16[256,512]{1,0:T(8,128)(2,1)S(1)}, bf16[272,512]{1,0:T(8,128)(2,1)S(1)}) custom-call(bf16[256,512]{1,0:T(8,128)(2,1)S(1)} %bitcast.58, bf16[16,512]{1,0:T(8,128)(2,1)S(1)} %collective-permute-done.1.low_ref, bf16[16,512]{1,0:T(8,128)(2,1)S(1)} %collective-permute-done.2.high_ref, s32[1,256]{1,0:T(1,128)S(1)} %copy-done.6, ...), custom_call_target="tpu_custom_call" | custom-call | flops 8000000 | bytes 1500000 | tf_op jit(solution)/shard_map/tokens_part/pallas_call | solution.py:79
  36.5 0.0 copy-start.2
  36.5 1.9 %collective-permute-start.4 = (bf16[272,512]{1,0:T(8,128)(2,1)S(1)}, bf16[272,512]{1,0:T(8,128)(2,1)S(1)}, u32[]{:S(2)}, u32[]{:S(2)}) collective-permute-start(bf16[272,512]{1,0:T(8,128)(2,1)S(1)} %get-tuple-element.20), channel_id=1, source_target_pairs={{0,16},{16,0},{1,17},{17,1},{2,18},{18,2},{3,19},{19,3},{4,20},{20... | collective-permute-start | bytes 835592 | tf_op jit(solution)/shard_map/ppermute | solution.py:30
  38.4 0.0 copy-done.10
  38.4 0.1 pad_maximum_fusion.3
  38.5 2.2 %collective-permute-start.6 = (bf16[2,256,512]{2,1,0:T(8,128)(2,1)S(1)}, bf16[2,256,512]{2,1,0:T(8,128)(2,1)}, u32[]{:S(2)}, u32[]{:S(2)}) collective-permute-start(bf16[2,256,512]{2,1,0:T(8,128)(2,1)S(1)} %pad_maximum_fusion.3), channel_id=1, source_target_pairs={{0,1},{1,0},{2,3},{3,2},{4,5},{5,4},{6,7},{7,6},{8,9},{9,8},{10,11... | collective-permute-start | bytes 1572872 | tf_op jit(solution)/shard_map/ppermute | solution.py:30
  40.7 11.1 %collective-permute-done.4 = bf16[272,512]{1,0:T(8,128)(2,1)S(1)} collective-permute-done((bf16[272,512]{1,0:T(8,128)(2,1)S(1)}, bf16[272,512]{1,0:T(8,128)(2,1)S(1)}, u32[]{:S(2)}, u32[]{:S(2)}) %collective-permute-start.4) | collective-permute-done | bytes 278560 | tf_op jit(solution)/shard_map/ppermute | solution.py:30
  51.8 0.7 copy-done.8
  52.5 0.1 pad_maximum_fusion.2
  52.6 1.9 %collective-permute-start.5 = (bf16[2,272,512]{2,1,0:T(8,128)(2,1)S(1)}, bf16[2,272,512]{2,1,0:T(8,128)(2,1)}, u32[]{:S(2)}, u32[]{:S(2)}) collective-permute-start(bf16[2,272,512]{2,1,0:T(8,128)(2,1)S(1)} %pad_maximum_fusion.2), channel_id=1, source_target_pairs={{0,1},{1,0},{2,3},{3,2},{4,5},{5,4},{6,7},{7,6},{8,9},{9,8},{10,11... | collective-permute-start | bytes 1671176 | tf_op jit(solution)/shard_map/ppermute | solution.py:30
  54.5 0.0 collective-permute-done.6
  54.5 1.2 pad_maximum_fusion.1.cotangents_ref
  55.7 0.8 collective-permute-done.5
  56.6 1.2 pad_maximum_fusion.packs_ref
  57.7 5.3 %all-to-all-done.1 = bf16[16,64,512]{2,1,0:T(8,128)(2,1)S(1)} async-done(((bf16[16,64,512]{2,1,0:T(8,128)(2,1)}), bf16[16,64,512]{2,1,0:T(8,128)(2,1)S(1)}, u32[]{:S(2)}, u32[]{:S(2)}) %all-to-all-start.1) | async-done | bytes 1048608 | tf_op jit(solution)/shard_map/all_to_all | solution.py:171
  63.0 2.2 %hidden_part.1 = (bf16[512,512]{1,0:T(8,128)(2,1)S(1)}, bf16[1536,512]{1,0:T(8,128)(2,1)S(1)}) custom-call(bf16[4,272,512]{2,1,0:T(8,128)(2,1)S(1)} %pad_maximum_fusion.packs_ref, bf16[4,256,512]{2,1,0:T(8,128)(2,1)S(1)} %pad_maximum_fusion.1.cotangents_ref, bf16[2,8,64,512]{3,2,1,0:T(8,128)(2,1)S(1)} %bitcast.52), custom_call_target="tpu_custom_call" | custom-call | tf_op jit(solution)/shard_map/hidden_part/pallas_call | solution.py:148
  65.2 0.7 fusion
  65.9 0.1 copy-done
  66.0 4.5 %all-to-all-start.2 = ((bf16[32,16,512]{2,1,0:T(8,128)(2,1)}), bf16[32,16,512]{2,1,0:T(8,128)(2,1)S(1)}, u32[]{:S(2)}, u32[]{:S(2)}) async-start(bf16[32,16,512]{2,1,0:T(8,128)(2,1)} %bitcast.56), calls=%async_computation.2 | async-start | bytes 1048576 | tf_op jit(solution)/shard_map/all_to_all | solution.py:383
  70.5 0.0 copy-start.12
  70.5 0.0 copy-start.11
  70.6 1.5 %fusion.9 = (f32[512,512]{1,0:T(8,128)}, f32[512,512]{1,0:T(8,128)}) fusion(f32[1024,512]{1,0:T(8,128)S(1)} %fusion), kind=kLoop, calls=%fused_computation.28 | loop fusion | bytes 4194304 | tf_op jit(solution)/shard_map/slice | solution.py:367
  72.1 2.7 %collective-permute-start.7 = (f32[2,256,512]{2,1,0:T(8,128)}, f32[2,256,512]{2,1,0:T(8,128)}, u32[]{:S(2)}, u32[]{:S(2)}) collective-permute-start(f32[2,256,512]{2,1,0:T(8,128)} %bitcast.13), channel_id=1, source_target_pairs={{0,1},{1,0},{2,3},{3,2},{4,5},{5,4},{6,7},{7,6},{8,9},{9,8},{10,11... | collective-permute-start | bytes 3145736 | tf_op jit(solution)/shard_map/ppermute | solution.py:30
  74.9 1.9 %collective-permute-start.9 = (f32[8,1024]{1,0:T(8,128)S(1)}, f32[8,1024]{1,0:T(8,128)S(1)}, u32[]{:S(2)}, u32[]{:S(2)}) collective-permute-start(f32[8,1024]{1,0:T(8,128)S(1)} %dynamic-slice_bitcast_fusion), channel_id=1, source_target_pairs={{0,1},{1,0},{2,3},{3,2},{4,5},{5,4},{6,7},{7,6},{8,9},{9,8},{10,11... | collective-permute-start | bytes 98312 | tf_op jit(solution)/shard_map/ppermute | solution.py:30
  76.8 0.2 reshape.56
  77.1 0.4 dynamic-slice_reduce_fusion
  77.5 0.4 collective-permute-done.9
  78.0 6.7 %all-to-all-done.2.pieces_ref = bf16[32,16,512]{2,1,0:T(8,128)(2,1)S(1)} async-done(((bf16[32,16,512]{2,1,0:T(8,128)(2,1)}), bf16[32,16,512]{2,1,0:T(8,128)(2,1)S(1)}, u32[]{:S(2)}, u32[]{:S(2)}) %all-to-all-start.2) | async-done | bytes 524320 | tf_op jit(solution)/shard_map/all_to_all | solution.py:383
  84.7 1.0 rows_part.1
  85.7 10.7 %all-to-all-start.3 = ((bf16[16,16,128]{2,1,0:T(8,128)(2,1)}), bf16[16,16,128]{2,1,0:T(8,128)(2,1)S(1)}, u32[]{:S(2)}, u32[]{:S(2)}) async-start(bf16[16,16,128]{2,1,0:T(8,128)(2,1)} %get-tuple-element.27), calls=%async_computation.3 | async-start | bytes 131072 | tf_op jit(solution)/shard_map/all_to_all | solution.py:386
  96.4 2.0 %collective-permute-start.10 = (f32[1,8,1024]{2,1,0:T(8,128)S(1)}, f32[1,8,1024]{2,1,0:T(8,128)S(1)}, u32[]{:S(2)}, u32[]{:S(2)}) collective-permute-start(f32[1,8,1024]{2,1,0:T(8,128)S(1)} %constant_dynamic-slice_fusion), channel_id=1, source_target_pairs={{0,1},{1,0},{2,3},{3,2},{4,5},{5,4},{6,7},{7,6},{8,9},{9,8},{10,11... | collective-permute-start | bytes 98312 | tf_op jit(solution)/shard_map/ppermute | solution.py:30
  98.4 0.0 collective-permute-done.7
  98.4 1.4 %add.28 = f32[2,256,512]{2,1,0:T(8,128)S(1)} add(f32[2,256,512]{2,1,0:T(8,128)S(1)} %bitcast.62, f32[2,256,512]{2,1,0:T(8,128)} %collective-permute-done.7) | non-fusion elementwise | flops 262144 | bytes 3145728 | tf_op jit(solution)/shard_map/add | solution.py:368
  99.9 0.0 copy-start.3
  99.9 4.3 %all-to-all-done.3.arrived_ref = bf16[16,16,128]{2,1,0:T(8,128)(2,1)S(1)} async-done(((bf16[16,16,128]{2,1,0:T(8,128)(2,1)}), bf16[16,16,128]{2,1,0:T(8,128)(2,1)S(1)}, u32[]{:S(2)}, u32[]{:S(2)}) %all-to-all-start.3) | async-done | bytes 65568 | tf_op jit(solution)/shard_map/all_to_all | solution.py:386
  104.2 0.9 mean_part.1
  105.0 5.5 %all-to-all-start.4 = ((bf16[32,16,256]{2,1,0:T(8,128)(2,1)}), bf16[32,16,256]{2,1,0:T(8,128)(2,1)S(1)}, u32[]{:S(2)}, u32[]{:S(2)}) async-start(bf16[32,16,256]{2,1,0:T(8,128)(2,1)} %mean_part.1), calls=%async_computation.4 | async-start | bytes 524288 | tf_op jit(solution)/shard_map/all_to_all | solution.py:397
  110.6 3.1 %collective-permute-start.8 = (bf16[256,512]{1,0:T(8,128)(2,1)S(1)}, bf16[256,512]{1,0:T(8,128)(2,1)S(1)}, u32[]{:S(2)}, u32[]{:S(2)}) collective-permute-start(bf16[256,512]{1,0:T(8,128)(2,1)S(1)} %fusion.8), channel_id=1, source_target_pairs={{0,16},{16,0},{1,17},{17,1},{2,18},{18,2},{3,19},{19,3},{4,20},{20... | collective-permute-start | bytes 786440 | tf_op jit(solution)/shard_map/ppermute | solution.py:30
  113.7 0.0 collective-permute-done.10
  113.8 6.9 %all-to-all-done.4 = bf16[32,16,256]{2,1,0:T(8,128)(2,1)S(1)} async-done(((bf16[32,16,256]{2,1,0:T(8,128)(2,1)}), bf16[32,16,256]{2,1,0:T(8,128)(2,1)S(1)}, u32[]{:S(2)}, u32[]{:S(2)}) %all-to-all-start.4) | async-done | bytes 262176 | tf_op jit(solution)/shard_map/all_to_all | solution.py:397
  120.6 4.1 %tail.1 = f32[16,8,128]{2,1,0:T(8,128)} custom-call(s32[1]{0:T(128)} %bitcast.18.chip_ref, bf16[512,256]{1,0:T(8,128)(2,1)S(1)} %bitcast.55), custom_call_target="tpu_custom_call" | custom-call | tf_op jit(solution)/shard_map/tail/pallas_call | solution.py:328
  124.7 6.3 %all-to-all-start.5 = ((f32[16,8,128]{2,1,0:T(8,128)}), f32[16,8,128]{2,1,0:T(8,128)S(1)}, u32[]{:S(2)}, u32[]{:S(2)}) async-start(f32[16,8,128]{2,1,0:T(8,128)} %tail.1), calls=%async_computation.5 | async-start | bytes 131072 | tf_op jit(solution)/shard_map/all_to_all | solution.py:401
  131.0 0.0 collective-permute-done.8
  131.0 0.8 fusion.7
  131.8 7.0 %all-to-all-done.5.arrived_ref = f32[16,8,128]{2,1,0:T(8,128)S(1)} async-done(((f32[16,8,128]{2,1,0:T(8,128)}), f32[16,8,128]{2,1,0:T(8,128)S(1)}, u32[]{:S(2)}, u32[]{:S(2)}) %all-to-all-start.5) | async-done | bytes 65568 | tf_op jit(solution)/shard_map/all_to_all | solution.py:401
  138.8 0.7 last_part.1
  (25 shorter events, 0.2 us)
Async XLA Ops:
  0.6 21.7 %collective-permute-start.3 = (bf16[256,512]{1,0:T(8,128)(2,1)}, bf16[256,512]{1,0:T(8,128)(2,1)S(1)}, u32[]{:S(2)}, u32[]{:S(2)}) collective-permute-start(bf16[256,512]{1,0:T(8,128)(2,1)} %bitcast.65), channel_id=1, source_target_pairs={{0,16},{16,0},{1,17},{17,1},{2,18},{18,2},{3,19},{19,3},{4,20},{20... | collective-permute-start | bytes 786440 | tf_op jit(solution)/shard_map/ppermute | solution.py:30
  4.6 15.1 %collective-permute-start = (bf16[32,512]{1,0:T(8,128)(2,1)}, bf16[32,512]{1,0:T(8,128)(2,1)S(1)}, u32[]{:S(2)}, u32[]{:S(2)}) collective-permute-start(bf16[32,512]{1,0:T(8,128)(2,1)} %param.12), channel_id=1, source_target_pairs={{0,0},{1,32},{2,2},{3,34},{4,4},{5,36},{6,6},{7,38},{8,8},{9,40},{... | collective-permute-start | bytes 98312 | tf_op jit(solution)/shard_map/ppermute | solution.py:185
  9.8 9.9 %all-to-all-start = ((bf16[4,8,512]{2,1,0:T(8,128)(2,1)}), bf16[4,8,512]{2,1,0:T(8,128)(2,1)S(1)}, u32[]{:S(2)}, u32[]{:S(2)}) async-start(bf16[4,8,512]{2,1,0:T(8,128)(2,1)} %bitcast.73), calls=%async_computation | async-start | bytes 65536 | tf_op jit(solution)/shard_map/all_to_all | solution.py:187
  15.4 4.4 %collective-permute-start.1 = (bf16[16,512]{1,0:T(8,128)(2,1)S(1)}, bf16[16,512]{1,0:T(8,128)(2,1)S(1)}, u32[]{:S(2)}, u32[]{:S(2)}) collective-permute-start(bf16[16,512]{1,0:T(8,128)(2,1)S(1)} %get-tuple-element.34), channel_id=1, source_target_pairs={{0,1},{1,2},{2,3},{3,4},{4,5},{5,6},{6,7},{7,8},{8,9},{9,10},{10,1... | collective-permute-start | bytes 49160 | tf_op jit(solution)/shard_map/ppermute | solution.py:24
  17.3 5.1 %collective-permute-start.2 = (bf16[16,512]{1,0:T(8,128)(2,1)S(1)}, bf16[16,512]{1,0:T(8,128)(2,1)S(1)}, u32[]{:S(2)}, u32[]{:S(2)}) collective-permute-start(bf16[16,512]{1,0:T(8,128)(2,1)S(1)} %get-tuple-element.33), channel_id=1, source_target_pairs={{1,0},{2,1},{3,2},{4,3},{5,4},{6,5},{7,6},{8,7},{9,8},{10,9},{11,1... | collective-permute-start | bytes 49160 | tf_op jit(solution)/shard_map/ppermute | solution.py:25
  19.8 14.7 %copy-start.1 = (bf16[1,256,512]{2,1,0:T(8,128)(2,1)S(1)}, bf16[1,256,512]{2,1,0:T(8,128)(2,1)}, u32[]{:S(2)}) copy-start(bf16[1,256,512]{2,1,0:T(8,128)(2,1)} %param.9) | copy-start | bytes 786436
  19.8 14.7 %copy-start.4 = (f32[31,512]{1,0:T(8,128)S(1)}, f32[31,512]{1,0:T(8,128)}, u32[]{:S(2)}) copy-start(f32[31,512]{1,0:T(8,128)} %taps_ref.1) | copy-start | bytes 190468
  19.8 14.7 %copy-start.5 = (f32[512]{0:T(512)S(1)}, f32[512]{0:T(512)}, u32[]{:S(2)}) copy-start(f32[512]{0:T(512)} %param.14) | copy-start | bytes 6148
  19.8 14.7 %copy-start.6 = (s32[1,256]{1,0:T(1,128)S(1)}, s32[1,256]{1,0:T(1,128)}, u32[]{:S(2)}) copy-start(s32[1,256]{1,0:T(1,128)} %mask_ref.1) | copy-start | bytes 3076
  19.8 18.6 %copy-start.10 = (bf16[1,256,512]{2,1,0:T(8,128)(2,1)S(1)}, bf16[1,256,512]{2,1,0:T(8,128)(2,1)}, u32[]{:S(2)}) copy-start(bf16[1,256,512]{2,1,0:T(8,128)(2,1)} %param.10) | copy-start | bytes 786436
  23.5 39.5 %all-to-all-start.1 = ((bf16[16,64,512]{2,1,0:T(8,128)(2,1)}), bf16[16,64,512]{2,1,0:T(8,128)(2,1)S(1)}, u32[]{:S(2)}, u32[]{:S(2)}) async-start(bf16[16,64,512]{2,1,0:T(8,128)(2,1)} %broadcast_in_dim.16), calls=%async_computation.1 | async-start | bytes 2097152 | tf_op jit(solution)/shard_map/all_to_all | solution.py:171
  36.5 15.3 %copy-start.2 = (bf16[256,512]{1,0:T(8,128)(2,1)}, bf16[256,512]{1,0:T(8,128)(2,1)S(1)}, u32[]{:S(2)}) copy-start(bf16[256,512]{1,0:T(8,128)(2,1)S(1)} %get-tuple-element.19) | copy-start | bytes 786436
  36.5 15.3 %collective-permute-start.4 = (bf16[272,512]{1,0:T(8,128)(2,1)S(1)}, bf16[272,512]{1,0:T(8,128)(2,1)S(1)}, u32[]{:S(2)}, u32[]{:S(2)}) collective-permute-start(bf16[272,512]{1,0:T(8,128)(2,1)S(1)} %get-tuple-element.20), channel_id=1, source_target_pairs={{0,16},{16,0},{1,17},{17,1},{2,18},{18,2},{3,19},{19,3},{4,20},{20... | collective-permute-start | bytes 835592 | tf_op jit(solution)/shard_map/ppermute | solution.py:30
  38.5 16.1 %collective-permute-start.6 = (bf16[2,256,512]{2,1,0:T(8,128)(2,1)S(1)}, bf16[2,256,512]{2,1,0:T(8,128)(2,1)}, u32[]{:S(2)}, u32[]{:S(2)}) collective-permute-start(bf16[2,256,512]{2,1,0:T(8,128)(2,1)S(1)} %pad_maximum_fusion.3), channel_id=1, source_target_pairs={{0,1},{1,0},{2,3},{3,2},{4,5},{5,4},{6,7},{7,6},{8,9},{9,8},{10,11... | collective-permute-start | bytes 1572872 | tf_op jit(solution)/shard_map/ppermute | solution.py:30
  51.8 0.7 copy-start.8
  52.6 4.0 %collective-permute-start.5 = (bf16[2,272,512]{2,1,0:T(8,128)(2,1)S(1)}, bf16[2,272,512]{2,1,0:T(8,128)(2,1)}, u32[]{:S(2)}, u32[]{:S(2)}) collective-permute-start(bf16[2,272,512]{2,1,0:T(8,128)(2,1)S(1)} %pad_maximum_fusion.2), channel_id=1, source_target_pairs={{0,1},{1,0},{2,3},{3,2},{4,5},{5,4},{6,7},{7,6},{8,9},{9,8},{10,11... | collective-permute-start | bytes 1671176 | tf_op jit(solution)/shard_map/ppermute | solution.py:30
  54.5 2.1 %copy-start.9 = (bf16[272,512]{1,0:T(8,128)(2,1)S(1)}, bf16[272,512]{1,0:T(8,128)(2,1)}, u32[]{:S(2)}) copy-start(bf16[272,512]{1,0:T(8,128)(2,1)} %copy-done.8) | copy-start | bytes 835588
  65.2 0.8 copy-start
  66.0 18.7 %all-to-all-start.2 = ((bf16[32,16,512]{2,1,0:T(8,128)(2,1)}), bf16[32,16,512]{2,1,0:T(8,128)(2,1)S(1)}, u32[]{:S(2)}, u32[]{:S(2)}) async-start(bf16[32,16,512]{2,1,0:T(8,128)(2,1)} %bitcast.56), calls=%async_computation.2 | async-start | bytes 1048576 | tf_op jit(solution)/shard_map/all_to_all | solution.py:383
  70.5 1.6 %copy-start.12 = (f32[1,8,2048]{2,1,0:T(8,128)S(1)}, f32[1,8,2048]{2,1,0:T(8,128)}, u32[]{:S(2)}) copy-start(f32[1,8,2048]{2,1,0:T(8,128)} %param.16) | copy-start | bytes 196612
  70.5 6.3 %copy-start.11 = (s32[2048,32]{0,1:T(8,128)S(1)}, s32[2048,32]{0,1:T(8,128)}, u32[]{:S(2)}) copy-start(s32[2048,32]{0,1:T(8,128)} %param.17) | copy-start | bytes 786436
  72.1 26.3 %copy-start.7 = (f32[512,512]{1,0:T(8,128)S(1)}, f32[512,512]{1,0:T(8,128)}, u32[]{:S(2)}) copy-start(f32[512,512]{1,0:T(8,128)} %get-tuple-element.32) | copy-start | bytes 3145732
  72.1 26.3 %collective-permute-start.7 = (f32[2,256,512]{2,1,0:T(8,128)}, f32[2,256,512]{2,1,0:T(8,128)}, u32[]{:S(2)}, u32[]{:S(2)}) collective-permute-start(f32[2,256,512]{2,1,0:T(8,128)} %bitcast.13), channel_id=1, source_target_pairs={{0,1},{1,0},{2,3},{3,2},{4,5},{5,4},{6,7},{7,6},{8,9},{9,8},{10,11... | collective-permute-start | bytes 3145736 | tf_op jit(solution)/shard_map/ppermute | solution.py:30
  74.9 3.1 %collective-permute-start.9 = (f32[8,1024]{1,0:T(8,128)S(1)}, f32[8,1024]{1,0:T(8,128)S(1)}, u32[]{:S(2)}, u32[]{:S(2)}) collective-permute-start(f32[8,1024]{1,0:T(8,128)S(1)} %dynamic-slice_bitcast_fusion), channel_id=1, source_target_pairs={{0,1},{1,0},{2,3},{3,2},{4,5},{5,4},{6,7},{7,6},{8,9},{9,8},{10,11... | collective-permute-start | bytes 98312 | tf_op jit(solution)/shard_map/ppermute | solution.py:30
  85.7 18.5 %all-to-all-start.3 = ((bf16[16,16,128]{2,1,0:T(8,128)(2,1)}), bf16[16,16,128]{2,1,0:T(8,128)(2,1)S(1)}, u32[]{:S(2)}, u32[]{:S(2)}) async-start(bf16[16,16,128]{2,1,0:T(8,128)(2,1)} %get-tuple-element.27), calls=%async_computation.3 | async-start | bytes 131072 | tf_op jit(solution)/shard_map/all_to_all | solution.py:386
  96.4 17.4 %collective-permute-start.10 = (f32[1,8,1024]{2,1,0:T(8,128)S(1)}, f32[1,8,1024]{2,1,0:T(8,128)S(1)}, u32[]{:S(2)}, u32[]{:S(2)}) collective-permute-start(f32[1,8,1024]{2,1,0:T(8,128)S(1)} %constant_dynamic-slice_fusion), channel_id=1, source_target_pairs={{0,1},{1,0},{2,3},{3,2},{4,5},{5,4},{6,7},{7,6},{8,9},{9,8},{10,11... | collective-permute-start | bytes 98312 | tf_op jit(solution)/shard_map/ppermute | solution.py:30
  99.9 31.2 %copy-start.3 = (bf16[256,512]{1,0:T(8,128)(2,1)S(1)}, bf16[256,512]{1,0:T(8,128)(2,1)}, u32[]{:S(2)}) copy-start(bf16[256,512]{1,0:T(8,128)(2,1)} %copy-done.2) | copy-start | bytes 786436
  105.0 15.6 %all-to-all-start.4 = ((bf16[32,16,256]{2,1,0:T(8,128)(2,1)}), bf16[32,16,256]{2,1,0:T(8,128)(2,1)S(1)}, u32[]{:S(2)}, u32[]{:S(2)}) async-start(bf16[32,16,256]{2,1,0:T(8,128)(2,1)} %mean_part.1), calls=%async_computation.4 | async-start | bytes 524288 | tf_op jit(solution)/shard_map/all_to_all | solution.py:397
  110.6 20.4 %collective-permute-start.8 = (bf16[256,512]{1,0:T(8,128)(2,1)S(1)}, bf16[256,512]{1,0:T(8,128)(2,1)S(1)}, u32[]{:S(2)}, u32[]{:S(2)}) collective-permute-start(bf16[256,512]{1,0:T(8,128)(2,1)S(1)} %fusion.8), channel_id=1, source_target_pairs={{0,16},{16,0},{1,17},{17,1},{2,18},{18,2},{3,19},{19,3},{4,20},{20... | collective-permute-start | bytes 786440 | tf_op jit(solution)/shard_map/ppermute | solution.py:30
  124.7 14.1 %all-to-all-start.5 = ((f32[16,8,128]{2,1,0:T(8,128)}), f32[16,8,128]{2,1,0:T(8,128)S(1)}, u32[]{:S(2)}, u32[]{:S(2)}) async-start(f32[16,8,128]{2,1,0:T(8,128)} %tail.1), calls=%async_computation.5 | async-start | bytes 131072 | tf_op jit(solution)/shard_map/all_to_all | solution.py:401

commit v10 on v9

--- a/solution.py
+++ b/solution.py
@@ -296,24 +296,44 @@
 def tail_kernel(chip_ref, columns_ref, message_ref, rows_scratch):
     chunks, rows, width = message_ref.shape
     rank = RANK
-    columns = columns_ref[...].astype(jnp.float32)
-    mean_columns = columns[:, :width]
-    first, second, third = (
-        columns[:, width + rank * i : width + rank * (i + 1)] for i in range(3)
-    )
-    left = first + second + third
-    left_t = left.T
-    gram = jnp.dot(left_t, left, precision=HIGHEST, preferred_element_type=jnp.float32)
-    row_index = lax.broadcasted_iota(jnp.int32, (rank, 1), 0)
-    solved = left_t
+    terms = columns_ref[:, width:].astype(jnp.float32).T
+    left_t = terms[:rank] + terms[rank : 2 * rank] + terms[2 * rank : 3 * rank]
+    gram = lax.dot_general(
+        left_t,
+        left_t,
+        (((1,), (1,)), ((), ())),
+        precision=HIGHEST,
+        preferred_element_type=jnp.float32,
+    )
+    index = lax.broadcasted_iota(jnp.int32, (rank, rank), 0)
+    diagonal = index == lax.broadcasted_iota(jnp.int32, (rank, rank), 1)
+    pivots = jnp.sum(jnp.where(diagonal, gram, 0.0), axis=1, keepdims=True)
+    pivots = jnp.broadcast_to(pivots, (rank, width))
+    gram = jnp.concatenate([gram, jnp.zeros((rank, width - rank), jnp.float32)], axis=1)
+    row_index = lax.broadcasted_iota(jnp.int32, (rank, width), 0)
+    parts = [left_t[:, at : at + width] for at in range(0, left_t.shape[1], width)]
     for k in range(rank):
-        scale = lax.rsqrt(gram[k : k + 1, k : k + 1])
-        factor = jnp.where(row_index > k, gram[:, k : k + 1] * scale, 0.0)
-        gram_row = gram[k : k + 1, :] * scale
-        solved_row = solved[k : k + 1, :] * scale
-        gram = gram - factor * gram_row
-        solved = jnp.where(row_index == k, solved_row, solved - factor * solved_row)
-    right_t = jnp.dot(solved, mean_columns, precision=HIGHEST, preferred_element_type=jnp.float32)
+        scale = lax.rsqrt(pivots[k : k + 1, :])
+        column = jnp.broadcast_to(gram[:, k : k + 1], (rank, width))
+        factor = jnp.where(row_index > k, column * scale, 0.0)
+        gram = gram - factor * (gram[k : k + 1, :] * scale)
+        solved_rows = [part[k : k + 1, :] * scale for part in parts]
+        parts = [
+            jnp.where(row_index == k, row, part - factor * row)
+            for part, row in zip(parts, solved_rows)
+        ]
+        pivots = pivots - factor * factor
+    solved = jnp.concatenate(parts, axis=1)
+    rest, pieces = solved, []
+    for _ in range(3):
+        pieces.append(rest.astype(jnp.bfloat16))
+        rest = rest - pieces[-1].astype(jnp.float32)
+    products = jnp.dot(
+        jnp.concatenate(pieces, axis=0),
+        columns_ref[:, :width],
+        preferred_element_type=jnp.float32,
+    )
+    right_t = products[:rank] + products[rank : 2 * rank] + products[2 * rank :]
     rows_scratch[...] = solved.T
     chip_rows = C * rows
     basis_rows = rows_scratch[pl.ds(pl.multiple_of(chip_ref[0] * chip_rows, chip_rows), chip_rows), :]

time: 141 us -> 140 us (level)
  transfers between devices with their start and end apart: 17 -> 17, of which waited for: 9 -> 9; matrix products, arithmetic and copies ran while one was open for 6% -> 6% of each run, Pallas kernels for 6% -> 5%
where the time goes in v10:
time: 140 us; the launch traced here: 139 us
  starting transfers between devices  72.2 us (52%)
  waiting for transfers between devices  45 us (32%)
  Pallas kernels  10.3 us (7%)
  local copies, waits for them, and re-layouts  4.95 us (4%)
  other arithmetic  4.77 us (3%)
    ppermute x8, starting transfers between devices, swap(): return lax.ppermute(block, axis, [(0, 1), (1, 0)])  19.8 us
    all_to_all x2, starting transfers between devices, per_device(): arrived = lax.all_to_all(message, ('y', 'c'), 0, 0, tiled=True)  17 us
    ppermute x8, waiting for transfers between devices, swap(): return lax.ppermute(block, axis, [(0, 1), (1, 0)])  12.4 us
    all_to_all x2, waiting for transfers between devices, per_device(): arrived = lax.all_to_all(message, ('y', 'c'), 0, 0, tiled=True)  11.3 us
    all_to_all x1, starting transfers between devices, gather_by_exchange(): return lax.all_to_all(copies, axis, 0, 0, tiled=True)  11 us
    all_to_all x1, waiting for transfers between devices, per_device(): lax.all_to_all(packed, CHIP, 0, 0, tiled=True).reshape(features, -1)  6.86 us
    all_to_all x1, waiting for transfers between devices, per_device(): lax.all_to_all(grad_part.reshape(chips, chip_rows, quarter), CHIP, 0, 0,...  6.67 us
    all_to_all x1, starting transfers between devices, per_device(): lax.all_to_all(packed, CHIP, 0, 0, tiled=True).reshape(features, -1)  5.5 us
  transfers between devices with their start and end apart: 17, of which 9 were waited for; matrix products, arithmetic and copies ran while one was open for 6% of the time, Pallas kernels for 5%

profile of v10, /device:TPU:1, one launch (start us, length us, event | category | flops | bytes accessed | tf_op | source)
XLA Modules:
  0.0 139.0 jit_solution(1152109737358975699)
XLA Ops:
  0.6 4.0 %collective-permute-start.3 = (bf16[256,512]{1,0:T(8,128)(2,1)}, bf16[256,512]{1,0:T(8,128)(2,1)S(1)}, u32[]{:S(2)}, u32[]{:S(2)}) collective-permute-start(bf16[256,512]{1,0:T(8,128)(2,1)} %bitcast.65), channel_id=1, source_target_pairs={{0,16},{16,0},{1,17},{17,1},{2,18},{18,2},{3,19},{19,3},{4,20},{20... | collective-permute-start | bytes 786440 | tf_op jit(solution)/shard_map/ppermute | solution.py:30
  4.6 5.2 %collective-permute-start = (bf16[32,512]{1,0:T(8,128)(2,1)}, bf16[32,512]{1,0:T(8,128)(2,1)S(1)}, u32[]{:S(2)}, u32[]{:S(2)}) collective-permute-start(bf16[32,512]{1,0:T(8,128)(2,1)} %param.12), channel_id=1, source_target_pairs={{0,0},{1,32},{2,2},{3,34},{4,4},{5,36},{6,6},{7,38},{8,8},{9,40},{... | collective-permute-start | bytes 98312 | tf_op jit(solution)/shard_map/ppermute | solution.py:185
  9.8 4.9 %all-to-all-start = ((bf16[4,8,512]{2,1,0:T(8,128)(2,1)}), bf16[4,8,512]{2,1,0:T(8,128)(2,1)S(1)}, u32[]{:S(2)}, u32[]{:S(2)}) async-start(bf16[4,8,512]{2,1,0:T(8,128)(2,1)} %bitcast.73), calls=%async_computation | async-start | bytes 65536 | tf_op jit(solution)/shard_map/all_to_all | solution.py:187
  14.7 0.7 slice_bitcast_fusion.1
  15.4 1.9 %collective-permute-start.1 = (bf16[16,512]{1,0:T(8,128)(2,1)S(1)}, bf16[16,512]{1,0:T(8,128)(2,1)S(1)}, u32[]{:S(2)}, u32[]{:S(2)}) collective-permute-start(bf16[16,512]{1,0:T(8,128)(2,1)S(1)} %get-tuple-element.34), channel_id=1, source_target_pairs={{0,1},{1,2},{2,3},{3,4},{4,5},{5,6},{6,7},{7,8},{8,9},{9,10},{10,1... | collective-permute-start | bytes 49160 | tf_op jit(solution)/shard_map/ppermute | solution.py:24
  17.3 2.4 %collective-permute-start.2 = (bf16[16,512]{1,0:T(8,128)(2,1)S(1)}, bf16[16,512]{1,0:T(8,128)(2,1)S(1)}, u32[]{:S(2)}, u32[]{:S(2)}) collective-permute-start(bf16[16,512]{1,0:T(8,128)(2,1)S(1)} %get-tuple-element.33), channel_id=1, source_target_pairs={{1,0},{2,1},{3,2},{4,3},{5,4},{6,5},{7,6},{8,7},{9,8},{10,9},{11,1... | collective-permute-start | bytes 49160 | tf_op jit(solution)/shard_map/ppermute | solution.py:25
  19.7 0.0 all-to-all-done
  19.7 0.0 collective-permute-done
  19.8 0.0 copy-start.1
  19.8 0.0 copy-start.4
  19.8 0.0 copy-start.5
  19.8 0.0 copy-start.6
  19.8 0.0 copy-start.10
  19.8 0.0 collective-permute-done.1.low_ref
  19.8 2.5 %collective-permute-done.2.high_ref = bf16[16,512]{1,0:T(8,128)(2,1)S(1)} collective-permute-done((bf16[16,512]{1,0:T(8,128)(2,1)S(1)}, bf16[16,512]{1,0:T(8,128)(2,1)S(1)}, u32[]{:S(2)}, u32[]{:S(2)}) %collective-permute-start.2) | collective-permute-done | bytes 16416 | tf_op jit(solution)/shard_map/ppermute | solution.py:25
  22.4 0.0 collective-permute-done.3
  22.4 1.1 broadcast_in_dim.16
  23.5 11.0 %all-to-all-start.1 = ((bf16[16,64,512]{2,1,0:T(8,128)(2,1)}), bf16[16,64,512]{2,1,0:T(8,128)(2,1)S(1)}, u32[]{:S(2)}, u32[]{:S(2)}) async-start(bf16[16,64,512]{2,1,0:T(8,128)(2,1)} %broadcast_in_dim.16), calls=%async_computation.1 | async-start | bytes 2097152 | tf_op jit(solution)/shard_map/all_to_all | solution.py:171
  34.5 2.0 %tokens_part.1 = (bf16[256,512]{1,0:T(8,128)(2,1)S(1)}, bf16[272,512]{1,0:T(8,128)(2,1)S(1)}) custom-call(bf16[256,512]{1,0:T(8,128)(2,1)S(1)} %bitcast.58, bf16[16,512]{1,0:T(8,128)(2,1)S(1)} %collective-permute-done.1.low_ref, bf16[16,512]{1,0:T(8,128)(2,1)S(1)} %collective-permute-done.2.high_ref, s32[1,256]{1,0:T(1,128)S(1)} %copy-done.6, ...), custom_call_target="tpu_custom_call" | custom-call | flops 8000000 | bytes 1500000 | tf_op jit(solution)/shard_map/tokens_part/pallas_call | solution.py:79
  36.5 0.0 copy-start.2
  36.5 1.9 %collective-permute-start.4 = (bf16[272,512]{1,0:T(8,128)(2,1)S(1)}, bf16[272,512]{1,0:T(8,128)(2,1)S(1)}, u32[]{:S(2)}, u32[]{:S(2)}) collective-permute-start(bf16[272,512]{1,0:T(8,128)(2,1)S(1)} %get-tuple-element.20), channel_id=1, source_target_pairs={{0,16},{16,0},{1,17},{17,1},{2,18},{18,2},{3,19},{19,3},{4,20},{20... | collective-permute-start | bytes 835592 | tf_op jit(solution)/shard_map/ppermute | solution.py:30
  38.4 0.0 copy-done.10
  38.4 0.1 pad_maximum_fusion.3
  38.5 2.2 %collective-permute-start.6 = (bf16[2,256,512]{2,1,0:T(8,128)(2,1)S(1)}, bf16[2,256,512]{2,1,0:T(8,128)(2,1)}, u32[]{:S(2)}, u32[]{:S(2)}) collective-permute-start(bf16[2,256,512]{2,1,0:T(8,128)(2,1)S(1)} %pad_maximum_fusion.3), channel_id=1, source_target_pairs={{0,1},{1,0},{2,3},{3,2},{4,5},{5,4},{6,7},{7,6},{8,9},{9,8},{10,11... | collective-permute-start | bytes 1572872 | tf_op jit(solution)/shard_map/ppermute | solution.py:30
  40.7 11.1 %collective-permute-done.4 = bf16[272,512]{1,0:T(8,128)(2,1)S(1)} collective-permute-done((bf16[272,512]{1,0:T(8,128)(2,1)S(1)}, bf16[272,512]{1,0:T(8,128)(2,1)S(1)}, u32[]{:S(2)}, u32[]{:S(2)}) %collective-permute-start.4) | collective-permute-done | bytes 278560 | tf_op jit(solution)/shard_map/ppermute | solution.py:30
  51.8 0.7 copy-done.8
  52.5 0.1 pad_maximum_fusion.2
  52.6 1.9 %collective-permute-start.5 = (bf16[2,272,512]{2,1,0:T(8,128)(2,1)S(1)}, bf16[2,272,512]{2,1,0:T(8,128)(2,1)}, u32[]{:S(2)}, u32[]{:S(2)}) collective-permute-start(bf16[2,272,512]{2,1,0:T(8,128)(2,1)S(1)} %pad_maximum_fusion.2), channel_id=1, source_target_pairs={{0,1},{1,0},{2,3},{3,2},{4,5},{5,4},{6,7},{7,6},{8,9},{9,8},{10,11... | collective-permute-start | bytes 1671176 | tf_op jit(solution)/shard_map/ppermute | solution.py:30
  54.5 0.0 collective-permute-done.6
  54.5 1.2 pad_maximum_fusion.1.cotangents_ref
  55.7 0.8 collective-permute-done.5
  56.6 1.2 pad_maximum_fusion.packs_ref
  57.7 5.3 %all-to-all-done.1 = bf16[16,64,512]{2,1,0:T(8,128)(2,1)S(1)} async-done(((bf16[16,64,512]{2,1,0:T(8,128)(2,1)}), bf16[16,64,512]{2,1,0:T(8,128)(2,1)S(1)}, u32[]{:S(2)}, u32[]{:S(2)}) %all-to-all-start.1) | async-done | bytes 1048608 | tf_op jit(solution)/shard_map/all_to_all | solution.py:171
  63.0 2.2 %hidden_part.1 = (bf16[512,512]{1,0:T(8,128)(2,1)S(1)}, bf16[1536,512]{1,0:T(8,128)(2,1)S(1)}) custom-call(bf16[4,272,512]{2,1,0:T(8,128)(2,1)S(1)} %pad_maximum_fusion.packs_ref, bf16[4,256,512]{2,1,0:T(8,128)(2,1)S(1)} %pad_maximum_fusion.1.cotangents_ref, bf16[2,8,64,512]{3,2,1,0:T(8,128)(2,1)S(1)} %bitcast.52), custom_call_target="tpu_custom_call" | custom-call | tf_op jit(solution)/shard_map/hidden_part/pallas_call | solution.py:148
  65.2 0.7 fusion
  65.9 0.1 copy-done
  66.0 4.5 %all-to-all-start.2 = ((bf16[32,16,512]{2,1,0:T(8,128)(2,1)}), bf16[32,16,512]{2,1,0:T(8,128)(2,1)S(1)}, u32[]{:S(2)}, u32[]{:S(2)}) async-start(bf16[32,16,512]{2,1,0:T(8,128)(2,1)} %bitcast.56), calls=%async_computation.2 | async-start | bytes 1048576 | tf_op jit(solution)/shard_map/all_to_all | solution.py:403
  70.5 0.0 copy-start.12
  70.5 0.0 copy-start.11
  70.6 1.5 %fusion.9 = (f32[512,512]{1,0:T(8,128)}, f32[512,512]{1,0:T(8,128)}) fusion(f32[1024,512]{1,0:T(8,128)S(1)} %fusion), kind=kLoop, calls=%fused_computation.28 | loop fusion | bytes 4194304 | tf_op jit(solution)/shard_map/slice | solution.py:387
  72.1 2.7 %collective-permute-start.7 = (f32[2,256,512]{2,1,0:T(8,128)}, f32[2,256,512]{2,1,0:T(8,128)}, u32[]{:S(2)}, u32[]{:S(2)}) collective-permute-start(f32[2,256,512]{2,1,0:T(8,128)} %bitcast.13), channel_id=1, source_target_pairs={{0,1},{1,0},{2,3},{3,2},{4,5},{5,4},{6,7},{7,6},{8,9},{9,8},{10,11... | collective-permute-start | bytes 3145736 | tf_op jit(solution)/shard_map/ppermute | solution.py:30
  74.9 1.9 %collective-permute-start.9 = (f32[8,1024]{1,0:T(8,128)S(1)}, f32[8,1024]{1,0:T(8,128)S(1)}, u32[]{:S(2)}, u32[]{:S(2)}) collective-permute-start(f32[8,1024]{1,0:T(8,128)S(1)} %dynamic-slice_bitcast_fusion), channel_id=1, source_target_pairs={{0,1},{1,0},{2,3},{3,2},{4,5},{5,4},{6,7},{7,6},{8,9},{9,8},{10,11... | collective-permute-start | bytes 98312 | tf_op jit(solution)/shard_map/ppermute | solution.py:30
  76.8 0.2 reshape.56
  77.1 0.4 dynamic-slice_reduce_fusion
  77.5 0.4 collective-permute-done.9
  78.0 6.7 %all-to-all-done.2.pieces_ref = bf16[32,16,512]{2,1,0:T(8,128)(2,1)S(1)} async-done(((bf16[32,16,512]{2,1,0:T(8,128)(2,1)}), bf16[32,16,512]{2,1,0:T(8,128)(2,1)S(1)}, u32[]{:S(2)}, u32[]{:S(2)}) %all-to-all-start.2) | async-done | bytes 524320 | tf_op jit(solution)/shard_map/all_to_all | solution.py:403
  84.7 1.0 rows_part.1
  85.7 10.7 %all-to-all-start.3 = ((bf16[16,16,128]{2,1,0:T(8,128)(2,1)}), bf16[16,16,128]{2,1,0:T(8,128)(2,1)S(1)}, u32[]{:S(2)}, u32[]{:S(2)}) async-start(bf16[16,16,128]{2,1,0:T(8,128)(2,1)} %get-tuple-element.27), calls=%async_computation.3 | async-start | bytes 131072 | tf_op jit(solution)/shard_map/all_to_all | solution.py:406
  96.4 2.0 %collective-permute-start.10 = (f32[1,8,1024]{2,1,0:T(8,128)S(1)}, f32[1,8,1024]{2,1,0:T(8,128)S(1)}, u32[]{:S(2)}, u32[]{:S(2)}) collective-permute-start(f32[1,8,1024]{2,1,0:T(8,128)S(1)} %constant_dynamic-slice_fusion), channel_id=1, source_target_pairs={{0,1},{1,0},{2,3},{3,2},{4,5},{5,4},{6,7},{7,6},{8,9},{9,8},{10,11... | collective-permute-start | bytes 98312 | tf_op jit(solution)/shard_map/ppermute | solution.py:30
  98.4 0.0 collective-permute-done.7
  98.4 1.4 %add.28 = f32[2,256,512]{2,1,0:T(8,128)S(1)} add(f32[2,256,512]{2,1,0:T(8,128)S(1)} %bitcast.62, f32[2,256,512]{2,1,0:T(8,128)} %collective-permute-done.7) | non-fusion elementwise | flops 262144 | bytes 3145728 | tf_op jit(solution)/shard_map/add | solution.py:388
  99.9 0.0 copy-start.3
  99.9 4.3 %all-to-all-done.3.arrived_ref = bf16[16,16,128]{2,1,0:T(8,128)(2,1)S(1)} async-done(((bf16[16,16,128]{2,1,0:T(8,128)(2,1)}), bf16[16,16,128]{2,1,0:T(8,128)(2,1)S(1)}, u32[]{:S(2)}, u32[]{:S(2)}) %all-to-all-start.3) | async-done | bytes 65568 | tf_op jit(solution)/shard_map/all_to_all | solution.py:406
  104.2 0.9 mean_part.1
  105.0 5.5 %all-to-all-start.4 = ((bf16[32,16,256]{2,1,0:T(8,128)(2,1)}), bf16[32,16,256]{2,1,0:T(8,128)(2,1)S(1)}, u32[]{:S(2)}, u32[]{:S(2)}) async-start(bf16[32,16,256]{2,1,0:T(8,128)(2,1)} %mean_part.1), calls=%async_computation.4 | async-start | bytes 524288 | tf_op jit(solution)/shard_map/all_to_all | solution.py:417
  110.6 3.1 %collective-permute-start.8 = (bf16[256,512]{1,0:T(8,128)(2,1)S(1)}, bf16[256,512]{1,0:T(8,128)(2,1)S(1)}, u32[]{:S(2)}, u32[]{:S(2)}) collective-permute-start(bf16[256,512]{1,0:T(8,128)(2,1)S(1)} %fusion.8), channel_id=1, source_target_pairs={{0,16},{16,0},{1,17},{17,1},{2,18},{18,2},{3,19},{19,3},{4,20},{20... | collective-permute-start | bytes 786440 | tf_op jit(solution)/shard_map/ppermute | solution.py:30
  113.7 0.0 collective-permute-done.10
  113.8 6.9 %all-to-all-done.4 = bf16[32,16,256]{2,1,0:T(8,128)(2,1)S(1)} async-done(((bf16[32,16,256]{2,1,0:T(8,128)(2,1)}), bf16[32,16,256]{2,1,0:T(8,128)(2,1)S(1)}, u32[]{:S(2)}, u32[]{:S(2)}) %all-to-all-start.4) | async-done | bytes 262176 | tf_op jit(solution)/shard_map/all_to_all | solution.py:417
  120.6 3.5 %tail.1 = f32[16,8,128]{2,1,0:T(8,128)} custom-call(s32[1]{0:T(128)} %bitcast.18.chip_ref, bf16[512,256]{1,0:T(8,128)(2,1)S(1)} %bitcast.55), custom_call_target="tpu_custom_call" | custom-call | tf_op jit(solution)/shard_map/tail/pallas_call | solution.py:348
  124.1 6.3 %all-to-all-start.5 = ((f32[16,8,128]{2,1,0:T(8,128)}), f32[16,8,128]{2,1,0:T(8,128)S(1)}, u32[]{:S(2)}, u32[]{:S(2)}) async-start(f32[16,8,128]{2,1,0:T(8,128)} %tail.1), calls=%async_computation.5 | async-start | bytes 131072 | tf_op jit(solution)/shard_map/all_to_all | solution.py:421
  130.4 0.0 collective-permute-done.8
  130.5 0.8 fusion.7
  131.3 7.0 %all-to-all-done.5.arrived_ref = f32[16,8,128]{2,1,0:T(8,128)S(1)} async-done(((f32[16,8,128]{2,1,0:T(8,128)}), f32[16,8,128]{2,1,0:T(8,128)S(1)}, u32[]{:S(2)}, u32[]{:S(2)}) %all-to-all-start.5) | async-done | bytes 65568 | tf_op jit(solution)/shard_map/all_to_all | solution.py:421
  138.3 0.7 last_part.1
  (25 shorter events, 0.2 us)
Async XLA Ops:
  0.6 21.7 %collective-permute-start.3 = (bf16[256,512]{1,0:T(8,128)(2,1)}, bf16[256,512]{1,0:T(8,128)(2,1)S(1)}, u32[]{:S(2)}, u32[]{:S(2)}) collective-permute-start(bf16[256,512]{1,0:T(8,128)(2,1)} %bitcast.65), channel_id=1, source_target_pairs={{0,16},{16,0},{1,17},{17,1},{2,18},{18,2},{3,19},{19,3},{4,20},{20... | collective-permute-start | bytes 786440 | tf_op jit(solution)/shard_map/ppermute | solution.py:30
  4.6 15.1 %collective-permute-start = (bf16[32,512]{1,0:T(8,128)(2,1)}, bf16[32,512]{1,0:T(8,128)(2,1)S(1)}, u32[]{:S(2)}, u32[]{:S(2)}) collective-permute-start(bf16[32,512]{1,0:T(8,128)(2,1)} %param.12), channel_id=1, source_target_pairs={{0,0},{1,32},{2,2},{3,34},{4,4},{5,36},{6,6},{7,38},{8,8},{9,40},{... | collective-permute-start | bytes 98312 | tf_op jit(solution)/shard_map/ppermute | solution.py:185
  9.8 9.9 %all-to-all-start = ((bf16[4,8,512]{2,1,0:T(8,128)(2,1)}), bf16[4,8,512]{2,1,0:T(8,128)(2,1)S(1)}, u32[]{:S(2)}, u32[]{:S(2)}) async-start(bf16[4,8,512]{2,1,0:T(8,128)(2,1)} %bitcast.73), calls=%async_computation | async-start | bytes 65536 | tf_op jit(solution)/shard_map/all_to_all | solution.py:187
  15.4 4.4 %collective-permute-start.1 = (bf16[16,512]{1,0:T(8,128)(2,1)S(1)}, bf16[16,512]{1,0:T(8,128)(2,1)S(1)}, u32[]{:S(2)}, u32[]{:S(2)}) collective-permute-start(bf16[16,512]{1,0:T(8,128)(2,1)S(1)} %get-tuple-element.34), channel_id=1, source_target_pairs={{0,1},{1,2},{2,3},{3,4},{4,5},{5,6},{6,7},{7,8},{8,9},{9,10},{10,1... | collective-permute-start | bytes 49160 | tf_op jit(solution)/shard_map/ppermute | solution.py:24
  17.3 5.1 %collective-permute-start.2 = (bf16[16,512]{1,0:T(8,128)(2,1)S(1)}, bf16[16,512]{1,0:T(8,128)(2,1)S(1)}, u32[]{:S(2)}, u32[]{:S(2)}) collective-permute-start(bf16[16,512]{1,0:T(8,128)(2,1)S(1)} %get-tuple-element.33), channel_id=1, source_target_pairs={{1,0},{2,1},{3,2},{4,3},{5,4},{6,5},{7,6},{8,7},{9,8},{10,9},{11,1... | collective-permute-start | bytes 49160 | tf_op jit(solution)/shard_map/ppermute | solution.py:25
  19.8 14.7 %copy-start.1 = (bf16[1,256,512]{2,1,0:T(8,128)(2,1)S(1)}, bf16[1,256,512]{2,1,0:T(8,128)(2,1)}, u32[]{:S(2)}) copy-start(bf16[1,256,512]{2,1,0:T(8,128)(2,1)} %param.9) | copy-start | bytes 786436
  19.8 14.7 %copy-start.4 = (f32[31,512]{1,0:T(8,128)S(1)}, f32[31,512]{1,0:T(8,128)}, u32[]{:S(2)}) copy-start(f32[31,512]{1,0:T(8,128)} %taps_ref.1) | copy-start | bytes 190468
  19.8 14.7 %copy-start.5 = (f32[512]{0:T(512)S(1)}, f32[512]{0:T(512)}, u32[]{:S(2)}) copy-start(f32[512]{0:T(512)} %param.14) | copy-start | bytes 6148
  19.8 14.7 %copy-start.6 = (s32[1,256]{1,0:T(1,128)S(1)}, s32[1,256]{1,0:T(1,128)}, u32[]{:S(2)}) copy-start(s32[1,256]{1,0:T(1,128)} %mask_ref.1) | copy-start | bytes 3076
  19.8 18.6 %copy-start.10 = (bf16[1,256,512]{2,1,0:T(8,128)(2,1)S(1)}, bf16[1,256,512]{2,1,0:T(8,128)(2,1)}, u32[]{:S(2)}) copy-start(bf16[1,256,512]{2,1,0:T(8,128)(2,1)} %param.10) | copy-start | bytes 786436
  23.5 39.5 %all-to-all-start.1 = ((bf16[16,64,512]{2,1,0:T(8,128)(2,1)}), bf16[16,64,512]{2,1,0:T(8,128)(2,1)S(1)}, u32[]{:S(2)}, u32[]{:S(2)}) async-start(bf16[16,64,512]{2,1,0:T(8,128)(2,1)} %broadcast_in_dim.16), calls=%async_computation.1 | async-start | bytes 2097152 | tf_op jit(solution)/shard_map/all_to_all | solution.py:171
  36.5 15.3 %copy-start.2 = (bf16[256,512]{1,0:T(8,128)(2,1)}, bf16[256,512]{1,0:T(8,128)(2,1)S(1)}, u32[]{:S(2)}) copy-start(bf16[256,512]{1,0:T(8,128)(2,1)S(1)} %get-tuple-element.19) | copy-start | bytes 786436
  36.5 15.3 %collective-permute-start.4 = (bf16[272,512]{1,0:T(8,128)(2,1)S(1)}, bf16[272,512]{1,0:T(8,128)(2,1)S(1)}, u32[]{:S(2)}, u32[]{:S(2)}) collective-permute-start(bf16[272,512]{1,0:T(8,128)(2,1)S(1)} %get-tuple-element.20), channel_id=1, source_target_pairs={{0,16},{16,0},{1,17},{17,1},{2,18},{18,2},{3,19},{19,3},{4,20},{20... | collective-permute-start | bytes 835592 | tf_op jit(solution)/shard_map/ppermute | solution.py:30
  38.5 16.1 %collective-permute-start.6 = (bf16[2,256,512]{2,1,0:T(8,128)(2,1)S(1)}, bf16[2,256,512]{2,1,0:T(8,128)(2,1)}, u32[]{:S(2)}, u32[]{:S(2)}) collective-permute-start(bf16[2,256,512]{2,1,0:T(8,128)(2,1)S(1)} %pad_maximum_fusion.3), channel_id=1, source_target_pairs={{0,1},{1,0},{2,3},{3,2},{4,5},{5,4},{6,7},{7,6},{8,9},{9,8},{10,11... | collective-permute-start | bytes 1572872 | tf_op jit(solution)/shard_map/ppermute | solution.py:30
  51.8 0.7 copy-start.8
  52.6 4.0 %collective-permute-start.5 = (bf16[2,272,512]{2,1,0:T(8,128)(2,1)S(1)}, bf16[2,272,512]{2,1,0:T(8,128)(2,1)}, u32[]{:S(2)}, u32[]{:S(2)}) collective-permute-start(bf16[2,272,512]{2,1,0:T(8,128)(2,1)S(1)} %pad_maximum_fusion.2), channel_id=1, source_target_pairs={{0,1},{1,0},{2,3},{3,2},{4,5},{5,4},{6,7},{7,6},{8,9},{9,8},{10,11... | collective-permute-start | bytes 1671176 | tf_op jit(solution)/shard_map/ppermute | solution.py:30
  54.5 2.1 %copy-start.9 = (bf16[272,512]{1,0:T(8,128)(2,1)S(1)}, bf16[272,512]{1,0:T(8,128)(2,1)}, u32[]{:S(2)}) copy-start(bf16[272,512]{1,0:T(8,128)(2,1)} %copy-done.8) | copy-start | bytes 835588
  65.2 0.8 copy-start
  66.0 18.7 %all-to-all-start.2 = ((bf16[32,16,512]{2,1,0:T(8,128)(2,1)}), bf16[32,16,512]{2,1,0:T(8,128)(2,1)S(1)}, u32[]{:S(2)}, u32[]{:S(2)}) async-start(bf16[32,16,512]{2,1,0:T(8,128)(2,1)} %bitcast.56), calls=%async_computation.2 | async-start | bytes 1048576 | tf_op jit(solution)/shard_map/all_to_all | solution.py:403
  70.5 1.6 %copy-start.12 = (f32[1,8,2048]{2,1,0:T(8,128)S(1)}, f32[1,8,2048]{2,1,0:T(8,128)}, u32[]{:S(2)}) copy-start(f32[1,8,2048]{2,1,0:T(8,128)} %param.16) | copy-start | bytes 196612
  70.5 6.3 %copy-start.11 = (s32[2048,32]{0,1:T(8,128)S(1)}, s32[2048,32]{0,1:T(8,128)}, u32[]{:S(2)}) copy-start(s32[2048,32]{0,1:T(8,128)} %param.17) | copy-start | bytes 786436
  72.1 26.3 %copy-start.7 = (f32[512,512]{1,0:T(8,128)S(1)}, f32[512,512]{1,0:T(8,128)}, u32[]{:S(2)}) copy-start(f32[512,512]{1,0:T(8,128)} %get-tuple-element.32) | copy-start | bytes 3145732
  72.1 26.3 %collective-permute-start.7 = (f32[2,256,512]{2,1,0:T(8,128)}, f32[2,256,512]{2,1,0:T(8,128)}, u32[]{:S(2)}, u32[]{:S(2)}) collective-permute-start(f32[2,256,512]{2,1,0:T(8,128)} %bitcast.13), channel_id=1, source_target_pairs={{0,1},{1,0},{2,3},{3,2},{4,5},{5,4},{6,7},{7,6},{8,9},{9,8},{10,11... | collective-permute-start | bytes 3145736 | tf_op jit(solution)/shard_map/ppermute | solution.py:30
  74.9 3.1 %collective-permute-start.9 = (f32[8,1024]{1,0:T(8,128)S(1)}, f32[8,1024]{1,0:T(8,128)S(1)}, u32[]{:S(2)}, u32[]{:S(2)}) collective-permute-start(f32[8,1024]{1,0:T(8,128)S(1)} %dynamic-slice_bitcast_fusion), channel_id=1, source_target_pairs={{0,1},{1,0},{2,3},{3,2},{4,5},{5,4},{6,7},{7,6},{8,9},{9,8},{10,11... | collective-permute-start | bytes 98312 | tf_op jit(solution)/shard_map/ppermute | solution.py:30
  85.7 18.5 %all-to-all-start.3 = ((bf16[16,16,128]{2,1,0:T(8,128)(2,1)}), bf16[16,16,128]{2,1,0:T(8,128)(2,1)S(1)}, u32[]{:S(2)}, u32[]{:S(2)}) async-start(bf16[16,16,128]{2,1,0:T(8,128)(2,1)} %get-tuple-element.27), calls=%async_computation.3 | async-start | bytes 131072 | tf_op jit(solution)/shard_map/all_to_all | solution.py:406
  96.4 17.4 %collective-permute-start.10 = (f32[1,8,1024]{2,1,0:T(8,128)S(1)}, f32[1,8,1024]{2,1,0:T(8,128)S(1)}, u32[]{:S(2)}, u32[]{:S(2)}) collective-permute-start(f32[1,8,1024]{2,1,0:T(8,128)S(1)} %constant_dynamic-slice_fusion), channel_id=1, source_target_pairs={{0,1},{1,0},{2,3},{3,2},{4,5},{5,4},{6,7},{7,6},{8,9},{9,8},{10,11... | collective-permute-start | bytes 98312 | tf_op jit(solution)/shard_map/ppermute | solution.py:30
  99.9 30.6 %copy-start.3 = (bf16[256,512]{1,0:T(8,128)(2,1)S(1)}, bf16[256,512]{1,0:T(8,128)(2,1)}, u32[]{:S(2)}) copy-start(bf16[256,512]{1,0:T(8,128)(2,1)} %copy-done.2) | copy-start | bytes 786436
  105.0 15.6 %all-to-all-start.4 = ((bf16[32,16,256]{2,1,0:T(8,128)(2,1)}), bf16[32,16,256]{2,1,0:T(8,128)(2,1)S(1)}, u32[]{:S(2)}, u32[]{:S(2)}) async-start(bf16[32,16,256]{2,1,0:T(8,128)(2,1)} %mean_part.1), calls=%async_computation.4 | async-start | bytes 524288 | tf_op jit(solution)/shard_map/all_to_all | solution.py:417
  110.6 19.9 %collective-permute-start.8 = (bf16[256,512]{1,0:T(8,128)(2,1)S(1)}, bf16[256,512]{1,0:T(8,128)(2,1)S(1)}, u32[]{:S(2)}, u32[]{:S(2)}) collective-permute-start(bf16[256,512]{1,0:T(8,128)(2,1)S(1)} %fusion.8), channel_id=1, source_target_pairs={{0,16},{16,0},{1,17},{17,1},{2,18},{18,2},{3,19},{19,3},{4,20},{20... | collective-permute-start | bytes 786440 | tf_op jit(solution)/shard_map/ppermute | solution.py:30
  124.1 14.1 %all-to-all-start.5 = ((f32[16,8,128]{2,1,0:T(8,128)}), f32[16,8,128]{2,1,0:T(8,128)S(1)}, u32[]{:S(2)}, u32[]{:S(2)}) async-start(f32[16,8,128]{2,1,0:T(8,128)} %tail.1), calls=%async_computation.5 | async-start | bytes 131072 | tf_op jit(solution)/shard_map/all_to_all | solution.py:421

commit v11 on v10

--- a/solution.py
+++ b/solution.py
@@ -123,11 +123,11 @@
             (((1,), (1,)), ((), ())),
             preferred_element_type=jnp.float32,
         )
-        squashed = jax.nn.sigmoid(projected)
-        hidden_ref[rows] = (projected * squashed).astype(jnp.bfloat16)
-        delta[rows] = (0.5 * upstream * squashed * (1.0 + projected * (1.0 - squashed))).astype(
-            jnp.bfloat16
-        )
+        squashed = 0.5 + 0.5 * jnp.tanh(0.5 * projected)
+        hidden = projected * squashed
+        hidden_ref[rows] = hidden.astype(jnp.bfloat16)
+        slope = squashed + hidden * (1.0 - squashed)
+        delta[rows] = (0.5 * upstream * slope).astype(jnp.bfloat16)
     total = None
     for index in range(blocks):
         rows = slice(index * frames, (index + 1) * frames)

time: 140 us -> 140 us (level)
  no operation moved by 1% of the time
where the time goes in v11:
time: 140 us; the launch traced here: 139 us
  starting transfers between devices  72.2 us (52%)
  waiting for transfers between devices  45.1 us (32%)
  Pallas kernels  10.1 us (7%)
  local copies, waits for them, and re-layouts  4.95 us (4%)
  other arithmetic  4.77 us (3%)
    ppermute x8, starting transfers between devices, swap(): return lax.ppermute(block, axis, [(0, 1), (1, 0)])  19.8 us
    all_to_all x2, starting transfers between devices, per_device(): arrived = lax.all_to_all(message, ('y', 'c'), 0, 0, tiled=True)  17 us
    ppermute x8, waiting for transfers between devices, swap(): return lax.ppermute(block, axis, [(0, 1), (1, 0)])  12.4 us
    all_to_all x2, waiting for transfers between devices, per_device(): arrived = lax.all_to_all(message, ('y', 'c'), 0, 0, tiled=True)  11.3 us
    all_to_all x1, starting transfers between devices, gather_by_exchange(): return lax.all_to_all(copies, axis, 0, 0, tiled=True)  11 us
    all_to_all x1, waiting for transfers between devices, per_device(): lax.all_to_all(packed, CHIP, 0, 0, tiled=True).reshape(features, -1)  6.86 us
    all_to_all x1, waiting for transfers between devices, per_device(): lax.all_to_all(grad_part.reshape(chips, chip_rows, quarter), CHIP, 0, 0,...  6.68 us
    all_to_all x1, starting transfers between devices, per_device(): lax.all_to_all(packed, CHIP, 0, 0, tiled=True).reshape(features, -1)  5.5 us
  transfers between devices with their start and end apart: 17, of which 9 were waited for; matrix products, arithmetic and copies ran while one was open for 6% of the time, Pallas kernels for 5%

profile of v11, /device:TPU:1, one launch (start us, length us, event | category | flops | bytes accessed | tf_op | source)
XLA Modules:
  0.0 138.8 jit_solution(10656210180763628646)
XLA Ops:
  0.6 4.0 %collective-permute-start.3 = (bf16[256,512]{1,0:T(8,128)(2,1)}, bf16[256,512]{1,0:T(8,128)(2,1)S(1)}, u32[]{:S(2)}, u32[]{:S(2)}) collective-permute-start(bf16[256,512]{1,0:T(8,128)(2,1)} %bitcast.65), channel_id=1, source_target_pairs={{0,16},{16,0},{1,17},{17,1},{2,18},{18,2},{3,19},{19,3},{4,20},{20... | collective-permute-start | bytes 786440 | tf_op jit(solution)/shard_map/ppermute | solution.py:30
  4.6 5.2 %collective-permute-start = (bf16[32,512]{1,0:T(8,128)(2,1)}, bf16[32,512]{1,0:T(8,128)(2,1)S(1)}, u32[]{:S(2)}, u32[]{:S(2)}) collective-permute-start(bf16[32,512]{1,0:T(8,128)(2,1)} %param.12), channel_id=1, source_target_pairs={{0,0},{1,32},{2,2},{3,34},{4,4},{5,36},{6,6},{7,38},{8,8},{9,40},{... | collective-permute-start | bytes 98312 | tf_op jit(solution)/shard_map/ppermute | solution.py:185
  9.8 4.9 %all-to-all-start = ((bf16[4,8,512]{2,1,0:T(8,128)(2,1)}), bf16[4,8,512]{2,1,0:T(8,128)(2,1)S(1)}, u32[]{:S(2)}, u32[]{:S(2)}) async-start(bf16[4,8,512]{2,1,0:T(8,128)(2,1)} %bitcast.73), calls=%async_computation | async-start | bytes 65536 | tf_op jit(solution)/shard_map/all_to_all | solution.py:187
  14.7 0.7 slice_bitcast_fusion.1
  15.4 1.9 %collective-permute-start.1 = (bf16[16,512]{1,0:T(8,128)(2,1)S(1)}, bf16[16,512]{1,0:T(8,128)(2,1)S(1)}, u32[]{:S(2)}, u32[]{:S(2)}) collective-permute-start(bf16[16,512]{1,0:T(8,128)(2,1)S(1)} %get-tuple-element.34), channel_id=1, source_target_pairs={{0,1},{1,2},{2,3},{3,4},{4,5},{5,6},{6,7},{7,8},{8,9},{9,10},{10,1... | collective-permute-start | bytes 49160 | tf_op jit(solution)/shard_map/ppermute | solution.py:24
  17.3 2.4 %collective-permute-start.2 = (bf16[16,512]{1,0:T(8,128)(2,1)S(1)}, bf16[16,512]{1,0:T(8,128)(2,1)S(1)}, u32[]{:S(2)}, u32[]{:S(2)}) collective-permute-start(bf16[16,512]{1,0:T(8,128)(2,1)S(1)} %get-tuple-element.33), channel_id=1, source_target_pairs={{1,0},{2,1},{3,2},{4,3},{5,4},{6,5},{7,6},{8,7},{9,8},{10,9},{11,1... | collective-permute-start | bytes 49160 | tf_op jit(solution)/shard_map/ppermute | solution.py:25
  19.7 0.0 all-to-all-done
  19.7 0.0 collective-permute-done
  19.8 0.0 copy-start.1
  19.8 0.0 copy-start.4
  19.8 0.0 copy-start.5
  19.8 0.0 copy-start.6
  19.8 0.0 copy-start.10
  19.8 0.0 collective-permute-done.1.low_ref
  19.8 2.5 %collective-permute-done.2.high_ref = bf16[16,512]{1,0:T(8,128)(2,1)S(1)} collective-permute-done((bf16[16,512]{1,0:T(8,128)(2,1)S(1)}, bf16[16,512]{1,0:T(8,128)(2,1)S(1)}, u32[]{:S(2)}, u32[]{:S(2)}) %collective-permute-start.2) | collective-permute-done | bytes 16416 | tf_op jit(solution)/shard_map/ppermute | solution.py:25
  22.4 0.0 collective-permute-done.3
  22.4 1.1 broadcast_in_dim.16
  23.5 11.0 %all-to-all-start.1 = ((bf16[16,64,512]{2,1,0:T(8,128)(2,1)}), bf16[16,64,512]{2,1,0:T(8,128)(2,1)S(1)}, u32[]{:S(2)}, u32[]{:S(2)}) async-start(bf16[16,64,512]{2,1,0:T(8,128)(2,1)} %broadcast_in_dim.16), calls=%async_computation.1 | async-start | bytes 2097152 | tf_op jit(solution)/shard_map/all_to_all | solution.py:171
  34.4 0.0 copy-done.1
  34.5 2.0 %tokens_part.1 = (bf16[256,512]{1,0:T(8,128)(2,1)S(1)}, bf16[272,512]{1,0:T(8,128)(2,1)S(1)}) custom-call(bf16[256,512]{1,0:T(8,128)(2,1)S(1)} %bitcast.58, bf16[16,512]{1,0:T(8,128)(2,1)S(1)} %collective-permute-done.1.low_ref, bf16[16,512]{1,0:T(8,128)(2,1)S(1)} %collective-permute-done.2.high_ref, s32[1,256]{1,0:T(1,128)S(1)} %copy-done.6, ...), custom_call_target="tpu_custom_call" | custom-call | flops 8000000 | bytes 1500000 | tf_op jit(solution)/shard_map/tokens_part/pallas_call | solution.py:79
  36.5 0.0 copy-start.2
  36.5 1.9 %collective-permute-start.4 = (bf16[272,512]{1,0:T(8,128)(2,1)S(1)}, bf16[272,512]{1,0:T(8,128)(2,1)S(1)}, u32[]{:S(2)}, u32[]{:S(2)}) collective-permute-start(bf16[272,512]{1,0:T(8,128)(2,1)S(1)} %get-tuple-element.20), channel_id=1, source_target_pairs={{0,16},{16,0},{1,17},{17,1},{2,18},{18,2},{3,19},{19,3},{4,20},{20... | collective-permute-start | bytes 835592 | tf_op jit(solution)/shard_map/ppermute | solution.py:30
  38.4 0.1 pad_maximum_fusion.3
  38.5 2.2 %collective-permute-start.6 = (bf16[2,256,512]{2,1,0:T(8,128)(2,1)S(1)}, bf16[2,256,512]{2,1,0:T(8,128)(2,1)}, u32[]{:S(2)}, u32[]{:S(2)}) collective-permute-start(bf16[2,256,512]{2,1,0:T(8,128)(2,1)S(1)} %pad_maximum_fusion.3), channel_id=1, source_target_pairs={{0,1},{1,0},{2,3},{3,2},{4,5},{5,4},{6,7},{7,6},{8,9},{9,8},{10,11... | collective-permute-start | bytes 1572872 | tf_op jit(solution)/shard_map/ppermute | solution.py:30
  40.7 11.1 %collective-permute-done.4 = bf16[272,512]{1,0:T(8,128)(2,1)S(1)} collective-permute-done((bf16[272,512]{1,0:T(8,128)(2,1)S(1)}, bf16[272,512]{1,0:T(8,128)(2,1)S(1)}, u32[]{:S(2)}, u32[]{:S(2)}) %collective-permute-start.4) | collective-permute-done | bytes 278560 | tf_op jit(solution)/shard_map/ppermute | solution.py:30
  51.8 0.7 copy-done.8
  52.5 0.1 pad_maximum_fusion.2
  52.6 1.9 %collective-permute-start.5 = (bf16[2,272,512]{2,1,0:T(8,128)(2,1)S(1)}, bf16[2,272,512]{2,1,0:T(8,128)(2,1)}, u32[]{:S(2)}, u32[]{:S(2)}) collective-permute-start(bf16[2,272,512]{2,1,0:T(8,128)(2,1)S(1)} %pad_maximum_fusion.2), channel_id=1, source_target_pairs={{0,1},{1,0},{2,3},{3,2},{4,5},{5,4},{6,7},{7,6},{8,9},{9,8},{10,11... | collective-permute-start | bytes 1671176 | tf_op jit(solution)/shard_map/ppermute | solution.py:30
  54.5 0.0 collective-permute-done.6
  54.5 1.2 pad_maximum_fusion.1.cotangents_ref
  55.7 0.8 collective-permute-done.5
  56.6 1.2 pad_maximum_fusion.packs_ref
  57.7 5.3 %all-to-all-done.1 = bf16[16,64,512]{2,1,0:T(8,128)(2,1)S(1)} async-done(((bf16[16,64,512]{2,1,0:T(8,128)(2,1)}), bf16[16,64,512]{2,1,0:T(8,128)(2,1)S(1)}, u32[]{:S(2)}, u32[]{:S(2)}) %all-to-all-start.1) | async-done | bytes 1048608 | tf_op jit(solution)/shard_map/all_to_all | solution.py:171
  63.0 2.0 %hidden_part.1 = (bf16[512,512]{1,0:T(8,128)(2,1)S(1)}, bf16[1536,512]{1,0:T(8,128)(2,1)S(1)}) custom-call(bf16[4,272,512]{2,1,0:T(8,128)(2,1)S(1)} %pad_maximum_fusion.packs_ref, bf16[4,256,512]{2,1,0:T(8,128)(2,1)S(1)} %pad_maximum_fusion.1.cotangents_ref, bf16[2,8,64,512]{3,2,1,0:T(8,128)(2,1)S(1)} %bitcast.52), custom_call_target="tpu_custom_call" | custom-call | tf_op jit(solution)/shard_map/hidden_part/pallas_call | solution.py:148
  65.0 0.7 fusion
  65.7 0.1 copy-done
  65.8 4.5 %all-to-all-start.2 = ((bf16[32,16,512]{2,1,0:T(8,128)(2,1)}), bf16[32,16,512]{2,1,0:T(8,128)(2,1)S(1)}, u32[]{:S(2)}, u32[]{:S(2)}) async-start(bf16[32,16,512]{2,1,0:T(8,128)(2,1)} %bitcast.56), calls=%async_computation.2 | async-start | bytes 1048576 | tf_op jit(solution)/shard_map/all_to_all | solution.py:403
  70.3 0.0 copy-start.12
  70.3 0.0 copy-start.11
  70.4 1.5 %fusion.9 = (f32[512,512]{1,0:T(8,128)}, f32[512,512]{1,0:T(8,128)}) fusion(f32[1024,512]{1,0:T(8,128)S(1)} %fusion), kind=kLoop, calls=%fused_computation.28 | loop fusion | bytes 4194304 | tf_op jit(solution)/shard_map/slice | solution.py:387
  71.9 2.7 %collective-permute-start.7 = (f32[2,256,512]{2,1,0:T(8,128)}, f32[2,256,512]{2,1,0:T(8,128)}, u32[]{:S(2)}, u32[]{:S(2)}) collective-permute-start(f32[2,256,512]{2,1,0:T(8,128)} %bitcast.13), channel_id=1, source_target_pairs={{0,1},{1,0},{2,3},{3,2},{4,5},{5,4},{6,7},{7,6},{8,9},{9,8},{10,11... | collective-permute-start | bytes 3145736 | tf_op jit(solution)/shard_map/ppermute | solution.py:30
  74.7 1.9 %collective-permute-start.9 = (f32[8,1024]{1,0:T(8,128)S(1)}, f32[8,1024]{1,0:T(8,128)S(1)}, u32[]{:S(2)}, u32[]{:S(2)}) collective-permute-start(f32[8,1024]{1,0:T(8,128)S(1)} %dynamic-slice_bitcast_fusion), channel_id=1, source_target_pairs={{0,1},{1,0},{2,3},{3,2},{4,5},{5,4},{6,7},{7,6},{8,9},{9,8},{10,11... | collective-permute-start | bytes 98312 | tf_op jit(solution)/shard_map/ppermute | solution.py:30
  76.6 0.2 reshape.56
  76.9 0.4 dynamic-slice_reduce_fusion
  77.3 0.4 collective-permute-done.9
  77.8 6.7 %all-to-all-done.2.pieces_ref = bf16[32,16,512]{2,1,0:T(8,128)(2,1)S(1)} async-done(((bf16[32,16,512]{2,1,0:T(8,128)(2,1)}), bf16[32,16,512]{2,1,0:T(8,128)(2,1)S(1)}, u32[]{:S(2)}, u32[]{:S(2)}) %all-to-all-start.2) | async-done | bytes 524320 | tf_op jit(solution)/shard_map/all_to_all | solution.py:403
  84.5 1.0 rows_part.1
  85.5 10.7 %all-to-all-start.3 = ((bf16[16,16,128]{2,1,0:T(8,128)(2,1)}), bf16[16,16,128]{2,1,0:T(8,128)(2,1)S(1)}, u32[]{:S(2)}, u32[]{:S(2)}) async-start(bf16[16,16,128]{2,1,0:T(8,128)(2,1)} %get-tuple-element.27), calls=%async_computation.3 | async-start | bytes 131072 | tf_op jit(solution)/shard_map/all_to_all | solution.py:406
  96.2 2.0 %collective-permute-start.10 = (f32[1,8,1024]{2,1,0:T(8,128)S(1)}, f32[1,8,1024]{2,1,0:T(8,128)S(1)}, u32[]{:S(2)}, u32[]{:S(2)}) collective-permute-start(f32[1,8,1024]{2,1,0:T(8,128)S(1)} %constant_dynamic-slice_fusion), channel_id=1, source_target_pairs={{0,1},{1,0},{2,3},{3,2},{4,5},{5,4},{6,7},{7,6},{8,9},{9,8},{10,11... | collective-permute-start | bytes 98312 | tf_op jit(solution)/shard_map/ppermute | solution.py:30
  98.2 0.0 collective-permute-done.7
  98.2 1.4 %add.28 = f32[2,256,512]{2,1,0:T(8,128)S(1)} add(f32[2,256,512]{2,1,0:T(8,128)S(1)} %bitcast.62, f32[2,256,512]{2,1,0:T(8,128)} %collective-permute-done.7) | non-fusion elementwise | flops 262144 | bytes 3145728 | tf_op jit(solution)/shard_map/add | solution.py:388
  99.7 0.0 copy-start.3
  99.7 4.3 %all-to-all-done.3.arrived_ref = bf16[16,16,128]{2,1,0:T(8,128)(2,1)S(1)} async-done(((bf16[16,16,128]{2,1,0:T(8,128)(2,1)}), bf16[16,16,128]{2,1,0:T(8,128)(2,1)S(1)}, u32[]{:S(2)}, u32[]{:S(2)}) %all-to-all-start.3) | async-done | bytes 65568 | tf_op jit(solution)/shard_map/all_to_all | solution.py:406
  104.0 0.9 mean_part.1
  104.8 5.5 %all-to-all-start.4 = ((bf16[32,16,256]{2,1,0:T(8,128)(2,1)}), bf16[32,16,256]{2,1,0:T(8,128)(2,1)S(1)}, u32[]{:S(2)}, u32[]{:S(2)}) async-start(bf16[32,16,256]{2,1,0:T(8,128)(2,1)} %mean_part.1), calls=%async_computation.4 | async-start | bytes 524288 | tf_op jit(solution)/shard_map/all_to_all | solution.py:417
  110.4 3.1 %collective-permute-start.8 = (bf16[256,512]{1,0:T(8,128)(2,1)S(1)}, bf16[256,512]{1,0:T(8,128)(2,1)S(1)}, u32[]{:S(2)}, u32[]{:S(2)}) collective-permute-start(bf16[256,512]{1,0:T(8,128)(2,1)S(1)} %fusion.8), channel_id=1, source_target_pairs={{0,16},{16,0},{1,17},{17,1},{2,18},{18,2},{3,19},{19,3},{4,20},{20... | collective-permute-start | bytes 786440 | tf_op jit(solution)/shard_map/ppermute | solution.py:30
  113.5 0.0 collective-permute-done.10
  113.6 6.9 %all-to-all-done.4 = bf16[32,16,256]{2,1,0:T(8,128)(2,1)S(1)} async-done(((bf16[32,16,256]{2,1,0:T(8,128)(2,1)}), bf16[32,16,256]{2,1,0:T(8,128)(2,1)S(1)}, u32[]{:S(2)}, u32[]{:S(2)}) %all-to-all-start.4) | async-done | bytes 262176 | tf_op jit(solution)/shard_map/all_to_all | solution.py:417
  120.4 3.5 %tail.1 = f32[16,8,128]{2,1,0:T(8,128)} custom-call(s32[1]{0:T(128)} %bitcast.18.chip_ref, bf16[512,256]{1,0:T(8,128)(2,1)S(1)} %bitcast.55), custom_call_target="tpu_custom_call" | custom-call | tf_op jit(solution)/shard_map/tail/pallas_call | solution.py:348
  123.9 6.3 %all-to-all-start.5 = ((f32[16,8,128]{2,1,0:T(8,128)}), f32[16,8,128]{2,1,0:T(8,128)S(1)}, u32[]{:S(2)}, u32[]{:S(2)}) async-start(f32[16,8,128]{2,1,0:T(8,128)} %tail.1), calls=%async_computation.5 | async-start | bytes 131072 | tf_op jit(solution)/shard_map/all_to_all | solution.py:421
  130.2 0.0 collective-permute-done.8
  130.3 0.8 fusion.7
  131.1 7.0 %all-to-all-done.5.arrived_ref = f32[16,8,128]{2,1,0:T(8,128)S(1)} async-done(((f32[16,8,128]{2,1,0:T(8,128)}), f32[16,8,128]{2,1,0:T(8,128)S(1)}, u32[]{:S(2)}, u32[]{:S(2)}) %all-to-all-start.5) | async-done | bytes 65568 | tf_op jit(solution)/shard_map/all_to_all | solution.py:421
  138.1 0.7 last_part.1
  (25 shorter events, 0.2 us)
Async XLA Ops:
  0.6 21.7 %collective-permute-start.3 = (bf16[256,512]{1,0:T(8,128)(2,1)}, bf16[256,512]{1,0:T(8,128)(2,1)S(1)}, u32[]{:S(2)}, u32[]{:S(2)}) collective-permute-start(bf16[256,512]{1,0:T(8,128)(2,1)} %bitcast.65), channel_id=1, source_target_pairs={{0,16},{16,0},{1,17},{17,1},{2,18},{18,2},{3,19},{19,3},{4,20},{20... | collective-permute-start | bytes 786440 | tf_op jit(solution)/shard_map/ppermute | solution.py:30
  4.6 15.1 %collective-permute-start = (bf16[32,512]{1,0:T(8,128)(2,1)}, bf16[32,512]{1,0:T(8,128)(2,1)S(1)}, u32[]{:S(2)}, u32[]{:S(2)}) collective-permute-start(bf16[32,512]{1,0:T(8,128)(2,1)} %param.12), channel_id=1, source_target_pairs={{0,0},{1,32},{2,2},{3,34},{4,4},{5,36},{6,6},{7,38},{8,8},{9,40},{... | collective-permute-start | bytes 98312 | tf_op jit(solution)/shard_map/ppermute | solution.py:185
  9.8 9.9 %all-to-all-start = ((bf16[4,8,512]{2,1,0:T(8,128)(2,1)}), bf16[4,8,512]{2,1,0:T(8,128)(2,1)S(1)}, u32[]{:S(2)}, u32[]{:S(2)}) async-start(bf16[4,8,512]{2,1,0:T(8,128)(2,1)} %bitcast.73), calls=%async_computation | async-start | bytes 65536 | tf_op jit(solution)/shard_map/all_to_all | solution.py:187
  15.4 4.4 %collective-permute-start.1 = (bf16[16,512]{1,0:T(8,128)(2,1)S(1)}, bf16[16,512]{1,0:T(8,128)(2,1)S(1)}, u32[]{:S(2)}, u32[]{:S(2)}) collective-permute-start(bf16[16,512]{1,0:T(8,128)(2,1)S(1)} %get-tuple-element.34), channel_id=1, source_target_pairs={{0,1},{1,2},{2,3},{3,4},{4,5},{5,6},{6,7},{7,8},{8,9},{9,10},{10,1... | collective-permute-start | bytes 49160 | tf_op jit(solution)/shard_map/ppermute | solution.py:24
  17.3 5.1 %collective-permute-start.2 = (bf16[16,512]{1,0:T(8,128)(2,1)S(1)}, bf16[16,512]{1,0:T(8,128)(2,1)S(1)}, u32[]{:S(2)}, u32[]{:S(2)}) collective-permute-start(bf16[16,512]{1,0:T(8,128)(2,1)S(1)} %get-tuple-element.33), channel_id=1, source_target_pairs={{1,0},{2,1},{3,2},{4,3},{5,4},{6,5},{7,6},{8,7},{9,8},{10,9},{11,1... | collective-permute-start | bytes 49160 | tf_op jit(solution)/shard_map/ppermute | solution.py:25
  19.8 14.7 %copy-start.1 = (bf16[1,256,512]{2,1,0:T(8,128)(2,1)S(1)}, bf16[1,256,512]{2,1,0:T(8,128)(2,1)}, u32[]{:S(2)}) copy-start(bf16[1,256,512]{2,1,0:T(8,128)(2,1)} %param.9) | copy-start | bytes 786436
  19.8 14.7 %copy-start.4 = (f32[31,512]{1,0:T(8,128)S(1)}, f32[31,512]{1,0:T(8,128)}, u32[]{:S(2)}) copy-start(f32[31,512]{1,0:T(8,128)} %taps_ref.1) | copy-start | bytes 190468
  19.8 14.7 %copy-start.5 = (f32[512]{0:T(512)S(1)}, f32[512]{0:T(512)}, u32[]{:S(2)}) copy-start(f32[512]{0:T(512)} %param.14) | copy-start | bytes 6148
  19.8 14.7 %copy-start.6 = (s32[1,256]{1,0:T(1,128)S(1)}, s32[1,256]{1,0:T(1,128)}, u32[]{:S(2)}) copy-start(s32[1,256]{1,0:T(1,128)} %mask_ref.1) | copy-start | bytes 3076
  19.8 18.6 %copy-start.10 = (bf16[1,256,512]{2,1,0:T(8,128)(2,1)S(1)}, bf16[1,256,512]{2,1,0:T(8,128)(2,1)}, u32[]{:S(2)}) copy-start(bf16[1,256,512]{2,1,0:T(8,128)(2,1)} %param.10) | copy-start | bytes 786436
  23.5 39.5 %all-to-all-start.1 = ((bf16[16,64,512]{2,1,0:T(8,128)(2,1)}), bf16[16,64,512]{2,1,0:T(8,128)(2,1)S(1)}, u32[]{:S(2)}, u32[]{:S(2)}) async-start(bf16[16,64,512]{2,1,0:T(8,128)(2,1)} %broadcast_in_dim.16), calls=%async_computation.1 | async-start | bytes 2097152 | tf_op jit(solution)/shard_map/all_to_all | solution.py:171
  36.5 15.3 %copy-start.2 = (bf16[256,512]{1,0:T(8,128)(2,1)}, bf16[256,512]{1,0:T(8,128)(2,1)S(1)}, u32[]{:S(2)}) copy-start(bf16[256,512]{1,0:T(8,128)(2,1)S(1)} %get-tuple-element.19) | copy-start | bytes 786436
  36.5 15.3 %collective-permute-start.4 = (bf16[272,512]{1,0:T(8,128)(2,1)S(1)}, bf16[272,512]{1,0:T(8,128)(2,1)S(1)}, u32[]{:S(2)}, u32[]{:S(2)}) collective-permute-start(bf16[272,512]{1,0:T(8,128)(2,1)S(1)} %get-tuple-element.20), channel_id=1, source_target_pairs={{0,16},{16,0},{1,17},{17,1},{2,18},{18,2},{3,19},{19,3},{4,20},{20... | collective-permute-start | bytes 835592 | tf_op jit(solution)/shard_map/ppermute | solution.py:30
  38.5 16.1 %collective-permute-start.6 = (bf16[2,256,512]{2,1,0:T(8,128)(2,1)S(1)}, bf16[2,256,512]{2,1,0:T(8,128)(2,1)}, u32[]{:S(2)}, u32[]{:S(2)}) collective-permute-start(bf16[2,256,512]{2,1,0:T(8,128)(2,1)S(1)} %pad_maximum_fusion.3), channel_id=1, source_target_pairs={{0,1},{1,0},{2,3},{3,2},{4,5},{5,4},{6,7},{7,6},{8,9},{9,8},{10,11... | collective-permute-start | bytes 1572872 | tf_op jit(solution)/shard_map/ppermute | solution.py:30
  51.8 0.7 copy-start.8
  52.6 4.0 %collective-permute-start.5 = (bf16[2,272,512]{2,1,0:T(8,128)(2,1)S(1)}, bf16[2,272,512]{2,1,0:T(8,128)(2,1)}, u32[]{:S(2)}, u32[]{:S(2)}) collective-permute-start(bf16[2,272,512]{2,1,0:T(8,128)(2,1)S(1)} %pad_maximum_fusion.2), channel_id=1, source_target_pairs={{0,1},{1,0},{2,3},{3,2},{4,5},{5,4},{6,7},{7,6},{8,9},{9,8},{10,11... | collective-permute-start | bytes 1671176 | tf_op jit(solution)/shard_map/ppermute | solution.py:30
  54.5 2.1 %copy-start.9 = (bf16[272,512]{1,0:T(8,128)(2,1)S(1)}, bf16[272,512]{1,0:T(8,128)(2,1)}, u32[]{:S(2)}) copy-start(bf16[272,512]{1,0:T(8,128)(2,1)} %copy-done.8) | copy-start | bytes 835588
  65.0 0.8 copy-start
  65.8 18.7 %all-to-all-start.2 = ((bf16[32,16,512]{2,1,0:T(8,128)(2,1)}), bf16[32,16,512]{2,1,0:T(8,128)(2,1)S(1)}, u32[]{:S(2)}, u32[]{:S(2)}) async-start(bf16[32,16,512]{2,1,0:T(8,128)(2,1)} %bitcast.56), calls=%async_computation.2 | async-start | bytes 1048576 | tf_op jit(solution)/shard_map/all_to_all | solution.py:403
  70.3 1.6 %copy-start.12 = (f32[1,8,2048]{2,1,0:T(8,128)S(1)}, f32[1,8,2048]{2,1,0:T(8,128)}, u32[]{:S(2)}) copy-start(f32[1,8,2048]{2,1,0:T(8,128)} %param.16) | copy-start | bytes 196612
  70.3 6.2 %copy-start.11 = (s32[2048,32]{0,1:T(8,128)S(1)}, s32[2048,32]{0,1:T(8,128)}, u32[]{:S(2)}) copy-start(s32[2048,32]{0,1:T(8,128)} %param.17) | copy-start | bytes 786436
  71.9 26.3 %copy-start.7 = (f32[512,512]{1,0:T(8,128)S(1)}, f32[512,512]{1,0:T(8,128)}, u32[]{:S(2)}) copy-start(f32[512,512]{1,0:T(8,128)} %get-tuple-element.32) | copy-start | bytes 3145732
  71.9 26.3 %collective-permute-start.7 = (f32[2,256,512]{2,1,0:T(8,128)}, f32[2,256,512]{2,1,0:T(8,128)}, u32[]{:S(2)}, u32[]{:S(2)}) collective-permute-start(f32[2,256,512]{2,1,0:T(8,128)} %bitcast.13), channel_id=1, source_target_pairs={{0,1},{1,0},{2,3},{3,2},{4,5},{5,4},{6,7},{7,6},{8,9},{9,8},{10,11... | collective-permute-start | bytes 3145736 | tf_op jit(solution)/shard_map/ppermute | solution.py:30
  74.7 3.1 %collective-permute-start.9 = (f32[8,1024]{1,0:T(8,128)S(1)}, f32[8,1024]{1,0:T(8,128)S(1)}, u32[]{:S(2)}, u32[]{:S(2)}) collective-permute-start(f32[8,1024]{1,0:T(8,128)S(1)} %dynamic-slice_bitcast_fusion), channel_id=1, source_target_pairs={{0,1},{1,0},{2,3},{3,2},{4,5},{5,4},{6,7},{7,6},{8,9},{9,8},{10,11... | collective-permute-start | bytes 98312 | tf_op jit(solution)/shard_map/ppermute | solution.py:30
  85.5 18.5 %all-to-all-start.3 = ((bf16[16,16,128]{2,1,0:T(8,128)(2,1)}), bf16[16,16,128]{2,1,0:T(8,128)(2,1)S(1)}, u32[]{:S(2)}, u32[]{:S(2)}) async-start(bf16[16,16,128]{2,1,0:T(8,128)(2,1)} %get-tuple-element.27), calls=%async_computation.3 | async-start | bytes 131072 | tf_op jit(solution)/shard_map/all_to_all | solution.py:406
  96.2 17.4 %collective-permute-start.10 = (f32[1,8,1024]{2,1,0:T(8,128)S(1)}, f32[1,8,1024]{2,1,0:T(8,128)S(1)}, u32[]{:S(2)}, u32[]{:S(2)}) collective-permute-start(f32[1,8,1024]{2,1,0:T(8,128)S(1)} %constant_dynamic-slice_fusion), channel_id=1, source_target_pairs={{0,1},{1,0},{2,3},{3,2},{4,5},{5,4},{6,7},{7,6},{8,9},{9,8},{10,11... | collective-permute-start | bytes 98312 | tf_op jit(solution)/shard_map/ppermute | solution.py:30
  99.7 30.6 %copy-start.3 = (bf16[256,512]{1,0:T(8,128)(2,1)S(1)}, bf16[256,512]{1,0:T(8,128)(2,1)}, u32[]{:S(2)}) copy-start(bf16[256,512]{1,0:T(8,128)(2,1)} %copy-done.2) | copy-start | bytes 786436
  104.8 15.6 %all-to-all-start.4 = ((bf16[32,16,256]{2,1,0:T(8,128)(2,1)}), bf16[32,16,256]{2,1,0:T(8,128)(2,1)S(1)}, u32[]{:S(2)}, u32[]{:S(2)}) async-start(bf16[32,16,256]{2,1,0:T(8,128)(2,1)} %mean_part.1), calls=%async_computation.4 | async-start | bytes 524288 | tf_op jit(solution)/shard_map/all_to_all | solution.py:417
  110.4 19.9 %collective-permute-start.8 = (bf16[256,512]{1,0:T(8,128)(2,1)S(1)}, bf16[256,512]{1,0:T(8,128)(2,1)S(1)}, u32[]{:S(2)}, u32[]{:S(2)}) collective-permute-start(bf16[256,512]{1,0:T(8,128)(2,1)S(1)} %fusion.8), channel_id=1, source_target_pairs={{0,16},{16,0},{1,17},{17,1},{2,18},{18,2},{3,19},{19,3},{4,20},{20... | collective-permute-start | bytes 786440 | tf_op jit(solution)/shard_map/ppermute | solution.py:30
  123.9 14.1 %all-to-all-start.5 = ((f32[16,8,128]{2,1,0:T(8,128)}), f32[16,8,128]{2,1,0:T(8,128)S(1)}, u32[]{:S(2)}, u32[]{:S(2)}) async-start(f32[16,8,128]{2,1,0:T(8,128)} %tail.1), calls=%async_computation.5 | async-start | bytes 131072 | tf_op jit(solution)/shard_map/all_to_all | solution.py:421

commit v12 on v11

--- a/solution.py
+++ b/solution.py
@@ -110,11 +110,10 @@
     for index in range(blocks):
         rows = slice(index * frames, (index + 1) * frames)
         mask = packs_ref[index, frames:, :frames][:1].astype(jnp.float32)
-        mask = jnp.broadcast_to(mask, (lanes, frames)).T
+        mask = jnp.broadcast_to(mask, (lanes, frames)).T.astype(jnp.bfloat16)
         for chunk in range(features // lanes):
             columns = slice(chunk * lanes, (chunk + 1) * lanes)
-            kept = cotangents_ref[index, :, columns].astype(jnp.float32) * mask
-            masked[:, columns] = kept.astype(jnp.bfloat16)
+            masked[:, columns] = cotangents_ref[index, :, columns] * mask
         normed = packs_ref[index, :frames]
         projected = jnp.dot(normed, up[...], preferred_element_type=jnp.float32)
         upstream = lax.dot_general(

time: 140 us -> 140 us (level)
  no operation moved by 1% of the time
where the time goes in v12:
time: 140 us; the launch traced here: 139 us
  starting transfers between devices  72.2 us (52%)
  waiting for transfers between devices  45.1 us (32%)
  Pallas kernels  10.1 us (7%)
  local copies, waits for them, and re-layouts  4.95 us (4%)
  other arithmetic  4.77 us (3%)
    ppermute x8, starting transfers between devices, swap(): return lax.ppermute(block, axis, [(0, 1), (1, 0)])  19.8 us
    all_to_all x2, starting transfers between devices, per_device(): arrived = lax.all_to_all(message, ('y', 'c'), 0, 0, tiled=True)  17 us
    ppermute x8, waiting for transfers between devices, swap(): return lax.ppermute(block, axis, [(0, 1), (1, 0)])  12.4 us
    all_to_all x2, waiting for transfers between devices, per_device(): arrived = lax.all_to_all(message, ('y', 'c'), 0, 0, tiled=True)  11.3 us
    all_to_all x1, starting transfers between devices, gather_by_exchange(): return lax.all_to_all(copies, axis, 0, 0, tiled=True)  11 us
    all_to_all x1, waiting for transfers between devices, per_device(): lax.all_to_all(packed, CHIP, 0, 0, tiled=True).reshape(features, -1)  6.86 us
    all_to_all x1, waiting for transfers between devices, per_device(): lax.all_to_all(grad_part.reshape(chips, chip_rows, quarter), CHIP, 0, 0,...  6.68 us
    all_to_all x1, starting transfers between devices, per_device(): lax.all_to_all(packed, CHIP, 0, 0, tiled=True).reshape(features, -1)  5.49 us
  transfers between devices with their start and end apart: 17, of which 9 were waited for; matrix products, arithmetic and copies ran while one was open for 6% of the time, Pallas kernels for 5%

profile of v12, /device:TPU:1, one launch (start us, length us, event | category | flops | bytes accessed | tf_op | source)
XLA Modules:
  0.0 138.9 jit_solution(10695081560571753299)
XLA Ops:
  0.6 4.0 %collective-permute-start.3 = (bf16[256,512]{1,0:T(8,128)(2,1)}, bf16[256,512]{1,0:T(8,128)(2,1)S(1)}, u32[]{:S(2)}, u32[]{:S(2)}) collective-permute-start(bf16[256,512]{1,0:T(8,128)(2,1)} %bitcast.65), channel_id=1, source_target_pairs={{0,16},{16,0},{1,17},{17,1},{2,18},{18,2},{3,19},{19,3},{4,20},{20... | collective-permute-start | bytes 786440 | tf_op jit(solution)/shard_map/ppermute | solution.py:30
  4.6 5.2 %collective-permute-start = (bf16[32,512]{1,0:T(8,128)(2,1)}, bf16[32,512]{1,0:T(8,128)(2,1)S(1)}, u32[]{:S(2)}, u32[]{:S(2)}) collective-permute-start(bf16[32,512]{1,0:T(8,128)(2,1)} %param.12), channel_id=1, source_target_pairs={{0,0},{1,32},{2,2},{3,34},{4,4},{5,36},{6,6},{7,38},{8,8},{9,40},{... | collective-permute-start | bytes 98312 | tf_op jit(solution)/shard_map/ppermute | solution.py:184
  9.8 4.9 %all-to-all-start = ((bf16[4,8,512]{2,1,0:T(8,128)(2,1)}), bf16[4,8,512]{2,1,0:T(8,128)(2,1)S(1)}, u32[]{:S(2)}, u32[]{:S(2)}) async-start(bf16[4,8,512]{2,1,0:T(8,128)(2,1)} %bitcast.73), calls=%async_computation | async-start | bytes 65536 | tf_op jit(solution)/shard_map/all_to_all | solution.py:186
  14.7 0.7 slice_bitcast_fusion.1
  15.4 1.9 %collective-permute-start.1 = (bf16[16,512]{1,0:T(8,128)(2,1)S(1)}, bf16[16,512]{1,0:T(8,128)(2,1)S(1)}, u32[]{:S(2)}, u32[]{:S(2)}) collective-permute-start(bf16[16,512]{1,0:T(8,128)(2,1)S(1)} %get-tuple-element.34), channel_id=1, source_target_pairs={{0,1},{1,2},{2,3},{3,4},{4,5},{5,6},{6,7},{7,8},{8,9},{9,10},{10,1... | collective-permute-start | bytes 49160 | tf_op jit(solution)/shard_map/ppermute | solution.py:24
  17.3 2.4 %collective-permute-start.2 = (bf16[16,512]{1,0:T(8,128)(2,1)S(1)}, bf16[16,512]{1,0:T(8,128)(2,1)S(1)}, u32[]{:S(2)}, u32[]{:S(2)}) collective-permute-start(bf16[16,512]{1,0:T(8,128)(2,1)S(1)} %get-tuple-element.33), channel_id=1, source_target_pairs={{1,0},{2,1},{3,2},{4,3},{5,4},{6,5},{7,6},{8,7},{9,8},{10,9},{11,1... | collective-permute-start | bytes 49160 | tf_op jit(solution)/shard_map/ppermute | solution.py:25
  19.7 0.0 all-to-all-done
  19.7 0.0 collective-permute-done
  19.8 0.0 copy-start.1
  19.8 0.0 copy-start.4
  19.8 0.0 copy-start.5
  19.8 0.0 copy-start.6
  19.8 0.0 copy-start.10
  19.8 0.0 collective-permute-done.1.low_ref
  19.8 2.5 %collective-permute-done.2.high_ref = bf16[16,512]{1,0:T(8,128)(2,1)S(1)} collective-permute-done((bf16[16,512]{1,0:T(8,128)(2,1)S(1)}, bf16[16,512]{1,0:T(8,128)(2,1)S(1)}, u32[]{:S(2)}, u32[]{:S(2)}) %collective-permute-start.2) | collective-permute-done | bytes 16416 | tf_op jit(solution)/shard_map/ppermute | solution.py:25
  22.4 0.0 collective-permute-done.3
  22.4 1.1 broadcast_in_dim.16
  23.5 11.0 %all-to-all-start.1 = ((bf16[16,64,512]{2,1,0:T(8,128)(2,1)}), bf16[16,64,512]{2,1,0:T(8,128)(2,1)S(1)}, u32[]{:S(2)}, u32[]{:S(2)}) async-start(bf16[16,64,512]{2,1,0:T(8,128)(2,1)} %broadcast_in_dim.16), calls=%async_computation.1 | async-start | bytes 2097152 | tf_op jit(solution)/shard_map/all_to_all | solution.py:170
  34.4 0.0 copy-done.1
  34.5 2.0 %tokens_part.1 = (bf16[256,512]{1,0:T(8,128)(2,1)S(1)}, bf16[272,512]{1,0:T(8,128)(2,1)S(1)}) custom-call(bf16[256,512]{1,0:T(8,128)(2,1)S(1)} %bitcast.58, bf16[16,512]{1,0:T(8,128)(2,1)S(1)} %collective-permute-done.1.low_ref, bf16[16,512]{1,0:T(8,128)(2,1)S(1)} %collective-permute-done.2.high_ref, s32[1,256]{1,0:T(1,128)S(1)} %copy-done.6, ...), custom_call_target="tpu_custom_call" | custom-call | flops 8000000 | bytes 1500000 | tf_op jit(solution)/shard_map/tokens_part/pallas_call | solution.py:79
  36.5 0.0 copy-start.2
  36.5 1.9 %collective-permute-start.4 = (bf16[272,512]{1,0:T(8,128)(2,1)S(1)}, bf16[272,512]{1,0:T(8,128)(2,1)S(1)}, u32[]{:S(2)}, u32[]{:S(2)}) collective-permute-start(bf16[272,512]{1,0:T(8,128)(2,1)S(1)} %get-tuple-element.20), channel_id=1, source_target_pairs={{0,16},{16,0},{1,17},{17,1},{2,18},{18,2},{3,19},{19,3},{4,20},{20... | collective-permute-start | bytes 835592 | tf_op jit(solution)/shard_map/ppermute | solution.py:30
  38.4 0.1 pad_maximum_fusion.3
  38.5 2.2 %collective-permute-start.6 = (bf16[2,256,512]{2,1,0:T(8,128)(2,1)S(1)}, bf16[2,256,512]{2,1,0:T(8,128)(2,1)}, u32[]{:S(2)}, u32[]{:S(2)}) collective-permute-start(bf16[2,256,512]{2,1,0:T(8,128)(2,1)S(1)} %pad_maximum_fusion.3), channel_id=1, source_target_pairs={{0,1},{1,0},{2,3},{3,2},{4,5},{5,4},{6,7},{7,6},{8,9},{9,8},{10,11... | collective-permute-start | bytes 1572872 | tf_op jit(solution)/shard_map/ppermute | solution.py:30
  40.7 11.1 %collective-permute-done.4 = bf16[272,512]{1,0:T(8,128)(2,1)S(1)} collective-permute-done((bf16[272,512]{1,0:T(8,128)(2,1)S(1)}, bf16[272,512]{1,0:T(8,128)(2,1)S(1)}, u32[]{:S(2)}, u32[]{:S(2)}) %collective-permute-start.4) | collective-permute-done | bytes 278560 | tf_op jit(solution)/shard_map/ppermute | solution.py:30
  51.8 0.7 copy-done.8
  52.5 0.1 pad_maximum_fusion.2
  52.6 1.9 %collective-permute-start.5 = (bf16[2,272,512]{2,1,0:T(8,128)(2,1)S(1)}, bf16[2,272,512]{2,1,0:T(8,128)(2,1)}, u32[]{:S(2)}, u32[]{:S(2)}) collective-permute-start(bf16[2,272,512]{2,1,0:T(8,128)(2,1)S(1)} %pad_maximum_fusion.2), channel_id=1, source_target_pairs={{0,1},{1,0},{2,3},{3,2},{4,5},{5,4},{6,7},{7,6},{8,9},{9,8},{10,11... | collective-permute-start | bytes 1671176 | tf_op jit(solution)/shard_map/ppermute | solution.py:30
  54.5 0.0 collective-permute-done.6
  54.5 1.2 pad_maximum_fusion.1.cotangents_ref
  55.7 0.8 collective-permute-done.5
  56.6 1.2 pad_maximum_fusion.packs_ref
  57.7 5.3 %all-to-all-done.1 = bf16[16,64,512]{2,1,0:T(8,128)(2,1)S(1)} async-done(((bf16[16,64,512]{2,1,0:T(8,128)(2,1)}), bf16[16,64,512]{2,1,0:T(8,128)(2,1)S(1)}, u32[]{:S(2)}, u32[]{:S(2)}) %all-to-all-start.1) | async-done | bytes 1048608 | tf_op jit(solution)/shard_map/all_to_all | solution.py:170
  63.0 2.1 %hidden_part.1 = (bf16[512,512]{1,0:T(8,128)(2,1)S(1)}, bf16[1536,512]{1,0:T(8,128)(2,1)S(1)}) custom-call(bf16[4,272,512]{2,1,0:T(8,128)(2,1)S(1)} %pad_maximum_fusion.packs_ref, bf16[4,256,512]{2,1,0:T(8,128)(2,1)S(1)} %pad_maximum_fusion.1.cotangents_ref, bf16[2,8,64,512]{3,2,1,0:T(8,128)(2,1)S(1)} %bitcast.52), custom_call_target="tpu_custom_call" | custom-call | tf_op jit(solution)/shard_map/hidden_part/pallas_call | solution.py:147
  65.1 0.7 fusion
  65.8 0.1 copy-done
  65.8 4.5 %all-to-all-start.2 = ((bf16[32,16,512]{2,1,0:T(8,128)(2,1)}), bf16[32,16,512]{2,1,0:T(8,128)(2,1)S(1)}, u32[]{:S(2)}, u32[]{:S(2)}) async-start(bf16[32,16,512]{2,1,0:T(8,128)(2,1)} %bitcast.56), calls=%async_computation.2 | async-start | bytes 1048576 | tf_op jit(solution)/shard_map/all_to_all | solution.py:402
  70.4 0.0 copy-start.12
  70.4 0.0 copy-start.11
  70.4 1.5 %fusion.9 = (f32[512,512]{1,0:T(8,128)}, f32[512,512]{1,0:T(8,128)}) fusion(f32[1024,512]{1,0:T(8,128)S(1)} %fusion), kind=kLoop, calls=%fused_computation.28 | loop fusion | bytes 4194304 | tf_op jit(solution)/shard_map/slice | solution.py:386
  72.0 2.7 %collective-permute-start.7 = (f32[2,256,512]{2,1,0:T(8,128)}, f32[2,256,512]{2,1,0:T(8,128)}, u32[]{:S(2)}, u32[]{:S(2)}) collective-permute-start(f32[2,256,512]{2,1,0:T(8,128)} %bitcast.13), channel_id=1, source_target_pairs={{0,1},{1,0},{2,3},{3,2},{4,5},{5,4},{6,7},{7,6},{8,9},{9,8},{10,11... | collective-permute-start | bytes 3145736 | tf_op jit(solution)/shard_map/ppermute | solution.py:30
  74.7 1.9 %collective-permute-start.9 = (f32[8,1024]{1,0:T(8,128)S(1)}, f32[8,1024]{1,0:T(8,128)S(1)}, u32[]{:S(2)}, u32[]{:S(2)}) collective-permute-start(f32[8,1024]{1,0:T(8,128)S(1)} %dynamic-slice_bitcast_fusion), channel_id=1, source_target_pairs={{0,1},{1,0},{2,3},{3,2},{4,5},{5,4},{6,7},{7,6},{8,9},{9,8},{10,11... | collective-permute-start | bytes 98312 | tf_op jit(solution)/shard_map/ppermute | solution.py:30
  76.7 0.2 reshape.56
  76.9 0.4 dynamic-slice_reduce_fusion
  77.4 0.4 collective-permute-done.9
  77.9 6.7 %all-to-all-done.2.pieces_ref = bf16[32,16,512]{2,1,0:T(8,128)(2,1)S(1)} async-done(((bf16[32,16,512]{2,1,0:T(8,128)(2,1)}), bf16[32,16,512]{2,1,0:T(8,128)(2,1)S(1)}, u32[]{:S(2)}, u32[]{:S(2)}) %all-to-all-start.2) | async-done | bytes 524320 | tf_op jit(solution)/shard_map/all_to_all | solution.py:402
  84.5 1.0 rows_part.1
  85.5 10.7 %all-to-all-start.3 = ((bf16[16,16,128]{2,1,0:T(8,128)(2,1)}), bf16[16,16,128]{2,1,0:T(8,128)(2,1)S(1)}, u32[]{:S(2)}, u32[]{:S(2)}) async-start(bf16[16,16,128]{2,1,0:T(8,128)(2,1)} %get-tuple-element.27), calls=%async_computation.3 | async-start | bytes 131072 | tf_op jit(solution)/shard_map/all_to_all | solution.py:405
  96.2 2.0 %collective-permute-start.10 = (f32[1,8,1024]{2,1,0:T(8,128)S(1)}, f32[1,8,1024]{2,1,0:T(8,128)S(1)}, u32[]{:S(2)}, u32[]{:S(2)}) collective-permute-start(f32[1,8,1024]{2,1,0:T(8,128)S(1)} %constant_dynamic-slice_fusion), channel_id=1, source_target_pairs={{0,1},{1,0},{2,3},{3,2},{4,5},{5,4},{6,7},{7,6},{8,9},{9,8},{10,11... | collective-permute-start | bytes 98312 | tf_op jit(solution)/shard_map/ppermute | solution.py:30
  98.3 0.0 collective-permute-done.7
  98.3 1.4 %add.28 = f32[2,256,512]{2,1,0:T(8,128)S(1)} add(f32[2,256,512]{2,1,0:T(8,128)S(1)} %bitcast.62, f32[2,256,512]{2,1,0:T(8,128)} %collective-permute-done.7) | non-fusion elementwise | flops 262144 | bytes 3145728 | tf_op jit(solution)/shard_map/add | solution.py:387
  99.7 0.0 copy-start.3
  99.7 4.3 %all-to-all-done.3.arrived_ref = bf16[16,16,128]{2,1,0:T(8,128)(2,1)S(1)} async-done(((bf16[16,16,128]{2,1,0:T(8,128)(2,1)}), bf16[16,16,128]{2,1,0:T(8,128)(2,1)S(1)}, u32[]{:S(2)}, u32[]{:S(2)}) %all-to-all-start.3) | async-done | bytes 65568 | tf_op jit(solution)/shard_map/all_to_all | solution.py:405
  104.0 0.9 mean_part.1
  104.9 5.5 %all-to-all-start.4 = ((bf16[32,16,256]{2,1,0:T(8,128)(2,1)}), bf16[32,16,256]{2,1,0:T(8,128)(2,1)S(1)}, u32[]{:S(2)}, u32[]{:S(2)}) async-start(bf16[32,16,256]{2,1,0:T(8,128)(2,1)} %mean_part.1), calls=%async_computation.4 | async-start | bytes 524288 | tf_op jit(solution)/shard_map/all_to_all | solution.py:416
  110.4 3.1 %collective-permute-start.8 = (bf16[256,512]{1,0:T(8,128)(2,1)S(1)}, bf16[256,512]{1,0:T(8,128)(2,1)S(1)}, u32[]{:S(2)}, u32[]{:S(2)}) collective-permute-start(bf16[256,512]{1,0:T(8,128)(2,1)S(1)} %fusion.8), channel_id=1, source_target_pairs={{0,16},{16,0},{1,17},{17,1},{2,18},{18,2},{3,19},{19,3},{4,20},{20... | collective-permute-start | bytes 786440 | tf_op jit(solution)/shard_map/ppermute | solution.py:30
  113.6 0.0 collective-permute-done.10
  113.6 6.9 %all-to-all-done.4 = bf16[32,16,256]{2,1,0:T(8,128)(2,1)S(1)} async-done(((bf16[32,16,256]{2,1,0:T(8,128)(2,1)}), bf16[32,16,256]{2,1,0:T(8,128)(2,1)S(1)}, u32[]{:S(2)}, u32[]{:S(2)}) %all-to-all-start.4) | async-done | bytes 262176 | tf_op jit(solution)/shard_map/all_to_all | solution.py:416
  120.5 3.5 %tail.1 = f32[16,8,128]{2,1,0:T(8,128)} custom-call(s32[1]{0:T(128)} %bitcast.18.chip_ref, bf16[512,256]{1,0:T(8,128)(2,1)S(1)} %bitcast.55), custom_call_target="tpu_custom_call" | custom-call | tf_op jit(solution)/shard_map/tail/pallas_call | solution.py:347
  124.0 6.3 %all-to-all-start.5 = ((f32[16,8,128]{2,1,0:T(8,128)}), f32[16,8,128]{2,1,0:T(8,128)S(1)}, u32[]{:S(2)}, u32[]{:S(2)}) async-start(f32[16,8,128]{2,1,0:T(8,128)} %tail.1), calls=%async_computation.5 | async-start | bytes 131072 | tf_op jit(solution)/shard_map/all_to_all | solution.py:420
  130.3 0.0 collective-permute-done.8
  130.3 0.8 fusion.7
  131.1 7.0 %all-to-all-done.5.arrived_ref = f32[16,8,128]{2,1,0:T(8,128)S(1)} async-done(((f32[16,8,128]{2,1,0:T(8,128)}), f32[16,8,128]{2,1,0:T(8,128)S(1)}, u32[]{:S(2)}, u32[]{:S(2)}) %all-to-all-start.5) | async-done | bytes 65568 | tf_op jit(solution)/shard_map/all_to_all | solution.py:420
  138.1 0.7 last_part.1
  (25 shorter events, 0.2 us)
Async XLA Ops:
  0.6 21.7 %collective-permute-start.3 = (bf16[256,512]{1,0:T(8,128)(2,1)}, bf16[256,512]{1,0:T(8,128)(2,1)S(1)}, u32[]{:S(2)}, u32[]{:S(2)}) collective-permute-start(bf16[256,512]{1,0:T(8,128)(2,1)} %bitcast.65), channel_id=1, source_target_pairs={{0,16},{16,0},{1,17},{17,1},{2,18},{18,2},{3,19},{19,3},{4,20},{20... | collective-permute-start | bytes 786440 | tf_op jit(solution)/shard_map/ppermute | solution.py:30
  4.6 15.1 %collective-permute-start = (bf16[32,512]{1,0:T(8,128)(2,1)}, bf16[32,512]{1,0:T(8,128)(2,1)S(1)}, u32[]{:S(2)}, u32[]{:S(2)}) collective-permute-start(bf16[32,512]{1,0:T(8,128)(2,1)} %param.12), channel_id=1, source_target_pairs={{0,0},{1,32},{2,2},{3,34},{4,4},{5,36},{6,6},{7,38},{8,8},{9,40},{... | collective-permute-start | bytes 98312 | tf_op jit(solution)/shard_map/ppermute | solution.py:184
  9.8 9.9 %all-to-all-start = ((bf16[4,8,512]{2,1,0:T(8,128)(2,1)}), bf16[4,8,512]{2,1,0:T(8,128)(2,1)S(1)}, u32[]{:S(2)}, u32[]{:S(2)}) async-start(bf16[4,8,512]{2,1,0:T(8,128)(2,1)} %bitcast.73), calls=%async_computation | async-start | bytes 65536 | tf_op jit(solution)/shard_map/all_to_all | solution.py:186
  15.4 4.4 %collective-permute-start.1 = (bf16[16,512]{1,0:T(8,128)(2,1)S(1)}, bf16[16,512]{1,0:T(8,128)(2,1)S(1)}, u32[]{:S(2)}, u32[]{:S(2)}) collective-permute-start(bf16[16,512]{1,0:T(8,128)(2,1)S(1)} %get-tuple-element.34), channel_id=1, source_target_pairs={{0,1},{1,2},{2,3},{3,4},{4,5},{5,6},{6,7},{7,8},{8,9},{9,10},{10,1... | collective-permute-start | bytes 49160 | tf_op jit(solution)/shard_map/ppermute | solution.py:24
  17.3 5.1 %collective-permute-start.2 = (bf16[16,512]{1,0:T(8,128)(2,1)S(1)}, bf16[16,512]{1,0:T(8,128)(2,1)S(1)}, u32[]{:S(2)}, u32[]{:S(2)}) collective-permute-start(bf16[16,512]{1,0:T(8,128)(2,1)S(1)} %get-tuple-element.33), channel_id=1, source_target_pairs={{1,0},{2,1},{3,2},{4,3},{5,4},{6,5},{7,6},{8,7},{9,8},{10,9},{11,1... | collective-permute-start | bytes 49160 | tf_op jit(solution)/shard_map/ppermute | solution.py:25
  19.8 14.7 %copy-start.1 = (bf16[1,256,512]{2,1,0:T(8,128)(2,1)S(1)}, bf16[1,256,512]{2,1,0:T(8,128)(2,1)}, u32[]{:S(2)}) copy-start(bf16[1,256,512]{2,1,0:T(8,128)(2,1)} %param.9) | copy-start | bytes 786436
  19.8 14.7 %copy-start.4 = (f32[31,512]{1,0:T(8,128)S(1)}, f32[31,512]{1,0:T(8,128)}, u32[]{:S(2)}) copy-start(f32[31,512]{1,0:T(8,128)} %taps_ref.1) | copy-start | bytes 190468
  19.8 14.7 %copy-start.5 = (f32[512]{0:T(512)S(1)}, f32[512]{0:T(512)}, u32[]{:S(2)}) copy-start(f32[512]{0:T(512)} %param.14) | copy-start | bytes 6148
  19.8 14.7 %copy-start.6 = (s32[1,256]{1,0:T(1,128)S(1)}, s32[1,256]{1,0:T(1,128)}, u32[]{:S(2)}) copy-start(s32[1,256]{1,0:T(1,128)} %mask_ref.1) | copy-start | bytes 3076
  19.8 18.6 %copy-start.10 = (bf16[1,256,512]{2,1,0:T(8,128)(2,1)S(1)}, bf16[1,256,512]{2,1,0:T(8,128)(2,1)}, u32[]{:S(2)}) copy-start(bf16[1,256,512]{2,1,0:T(8,128)(2,1)} %param.10) | copy-start | bytes 786436
  23.5 39.5 %all-to-all-start.1 = ((bf16[16,64,512]{2,1,0:T(8,128)(2,1)}), bf16[16,64,512]{2,1,0:T(8,128)(2,1)S(1)}, u32[]{:S(2)}, u32[]{:S(2)}) async-start(bf16[16,64,512]{2,1,0:T(8,128)(2,1)} %broadcast_in_dim.16), calls=%async_computation.1 | async-start | bytes 2097152 | tf_op jit(solution)/shard_map/all_to_all | solution.py:170
  36.5 15.3 %copy-start.2 = (bf16[256,512]{1,0:T(8,128)(2,1)}, bf16[256,512]{1,0:T(8,128)(2,1)S(1)}, u32[]{:S(2)}) copy-start(bf16[256,512]{1,0:T(8,128)(2,1)S(1)} %get-tuple-element.19) | copy-start | bytes 786436
  36.5 15.3 %collective-permute-start.4 = (bf16[272,512]{1,0:T(8,128)(2,1)S(1)}, bf16[272,512]{1,0:T(8,128)(2,1)S(1)}, u32[]{:S(2)}, u32[]{:S(2)}) collective-permute-start(bf16[272,512]{1,0:T(8,128)(2,1)S(1)} %get-tuple-element.20), channel_id=1, source_target_pairs={{0,16},{16,0},{1,17},{17,1},{2,18},{18,2},{3,19},{19,3},{4,20},{20... | collective-permute-start | bytes 835592 | tf_op jit(solution)/shard_map/ppermute | solution.py:30
  38.5 16.1 %collective-permute-start.6 = (bf16[2,256,512]{2,1,0:T(8,128)(2,1)S(1)}, bf16[2,256,512]{2,1,0:T(8,128)(2,1)}, u32[]{:S(2)}, u32[]{:S(2)}) collective-permute-start(bf16[2,256,512]{2,1,0:T(8,128)(2,1)S(1)} %pad_maximum_fusion.3), channel_id=1, source_target_pairs={{0,1},{1,0},{2,3},{3,2},{4,5},{5,4},{6,7},{7,6},{8,9},{9,8},{10,11... | collective-permute-start | bytes 1572872 | tf_op jit(solution)/shard_map/ppermute | solution.py:30
  51.8 0.7 copy-start.8
  52.6 4.0 %collective-permute-start.5 = (bf16[2,272,512]{2,1,0:T(8,128)(2,1)S(1)}, bf16[2,272,512]{2,1,0:T(8,128)(2,1)}, u32[]{:S(2)}, u32[]{:S(2)}) collective-permute-start(bf16[2,272,512]{2,1,0:T(8,128)(2,1)S(1)} %pad_maximum_fusion.2), channel_id=1, source_target_pairs={{0,1},{1,0},{2,3},{3,2},{4,5},{5,4},{6,7},{7,6},{8,9},{9,8},{10,11... | collective-permute-start | bytes 1671176 | tf_op jit(solution)/shard_map/ppermute | solution.py:30
  54.5 2.1 %copy-start.9 = (bf16[272,512]{1,0:T(8,128)(2,1)S(1)}, bf16[272,512]{1,0:T(8,128)(2,1)}, u32[]{:S(2)}) copy-start(bf16[272,512]{1,0:T(8,128)(2,1)} %copy-done.8) | copy-start | bytes 835588
  65.1 0.8 copy-start
  65.8 18.7 %all-to-all-start.2 = ((bf16[32,16,512]{2,1,0:T(8,128)(2,1)}), bf16[32,16,512]{2,1,0:T(8,128)(2,1)S(1)}, u32[]{:S(2)}, u32[]{:S(2)}) async-start(bf16[32,16,512]{2,1,0:T(8,128)(2,1)} %bitcast.56), calls=%async_computation.2 | async-start | bytes 1048576 | tf_op jit(solution)/shard_map/all_to_all | solution.py:402
  70.4 1.6 %copy-start.12 = (f32[1,8,2048]{2,1,0:T(8,128)S(1)}, f32[1,8,2048]{2,1,0:T(8,128)}, u32[]{:S(2)}) copy-start(f32[1,8,2048]{2,1,0:T(8,128)} %param.16) | copy-start | bytes 196612
  70.4 6.3 %copy-start.11 = (s32[2048,32]{0,1:T(8,128)S(1)}, s32[2048,32]{0,1:T(8,128)}, u32[]{:S(2)}) copy-start(s32[2048,32]{0,1:T(8,128)} %param.17) | copy-start | bytes 786436
  72.0 26.3 %copy-start.7 = (f32[512,512]{1,0:T(8,128)S(1)}, f32[512,512]{1,0:T(8,128)}, u32[]{:S(2)}) copy-start(f32[512,512]{1,0:T(8,128)} %get-tuple-element.32) | copy-start | bytes 3145732
  72.0 26.3 %collective-permute-start.7 = (f32[2,256,512]{2,1,0:T(8,128)}, f32[2,256,512]{2,1,0:T(8,128)}, u32[]{:S(2)}, u32[]{:S(2)}) collective-permute-start(f32[2,256,512]{2,1,0:T(8,128)} %bitcast.13), channel_id=1, source_target_pairs={{0,1},{1,0},{2,3},{3,2},{4,5},{5,4},{6,7},{7,6},{8,9},{9,8},{10,11... | collective-permute-start | bytes 3145736 | tf_op jit(solution)/shard_map/ppermute | solution.py:30
  74.7 3.1 %collective-permute-start.9 = (f32[8,1024]{1,0:T(8,128)S(1)}, f32[8,1024]{1,0:T(8,128)S(1)}, u32[]{:S(2)}, u32[]{:S(2)}) collective-permute-start(f32[8,1024]{1,0:T(8,128)S(1)} %dynamic-slice_bitcast_fusion), channel_id=1, source_target_pairs={{0,1},{1,0},{2,3},{3,2},{4,5},{5,4},{6,7},{7,6},{8,9},{9,8},{10,11... | collective-permute-start | bytes 98312 | tf_op jit(solution)/shard_map/ppermute | solution.py:30
  85.5 18.5 %all-to-all-start.3 = ((bf16[16,16,128]{2,1,0:T(8,128)(2,1)}), bf16[16,16,128]{2,1,0:T(8,128)(2,1)S(1)}, u32[]{:S(2)}, u32[]{:S(2)}) async-start(bf16[16,16,128]{2,1,0:T(8,128)(2,1)} %get-tuple-element.27), calls=%async_computation.3 | async-start | bytes 131072 | tf_op jit(solution)/shard_map/all_to_all | solution.py:405
  96.2 17.4 %collective-permute-start.10 = (f32[1,8,1024]{2,1,0:T(8,128)S(1)}, f32[1,8,1024]{2,1,0:T(8,128)S(1)}, u32[]{:S(2)}, u32[]{:S(2)}) collective-permute-start(f32[1,8,1024]{2,1,0:T(8,128)S(1)} %constant_dynamic-slice_fusion), channel_id=1, source_target_pairs={{0,1},{1,0},{2,3},{3,2},{4,5},{5,4},{6,7},{7,6},{8,9},{9,8},{10,11... | collective-permute-start | bytes 98312 | tf_op jit(solution)/shard_map/ppermute | solution.py:30
  99.7 30.6 %copy-start.3 = (bf16[256,512]{1,0:T(8,128)(2,1)S(1)}, bf16[256,512]{1,0:T(8,128)(2,1)}, u32[]{:S(2)}) copy-start(bf16[256,512]{1,0:T(8,128)(2,1)} %copy-done.2) | copy-start | bytes 786436
  104.9 15.6 %all-to-all-start.4 = ((bf16[32,16,256]{2,1,0:T(8,128)(2,1)}), bf16[32,16,256]{2,1,0:T(8,128)(2,1)S(1)}, u32[]{:S(2)}, u32[]{:S(2)}) async-start(bf16[32,16,256]{2,1,0:T(8,128)(2,1)} %mean_part.1), calls=%async_computation.4 | async-start | bytes 524288 | tf_op jit(solution)/shard_map/all_to_all | solution.py:416
  110.4 19.9 %collective-permute-start.8 = (bf16[256,512]{1,0:T(8,128)(2,1)S(1)}, bf16[256,512]{1,0:T(8,128)(2,1)S(1)}, u32[]{:S(2)}, u32[]{:S(2)}) collective-permute-start(bf16[256,512]{1,0:T(8,128)(2,1)S(1)} %fusion.8), channel_id=1, source_target_pairs={{0,16},{16,0},{1,17},{17,1},{2,18},{18,2},{3,19},{19,3},{4,20},{20... | collective-permute-start | bytes 786440 | tf_op jit(solution)/shard_map/ppermute | solution.py:30
  124.0 14.1 %all-to-all-start.5 = ((f32[16,8,128]{2,1,0:T(8,128)}), f32[16,8,128]{2,1,0:T(8,128)S(1)}, u32[]{:S(2)}, u32[]{:S(2)}) async-start(f32[16,8,128]{2,1,0:T(8,128)} %tail.1), calls=%async_computation.5 | async-start | bytes 131072 | tf_op jit(solution)/shard_map/all_to_all | solution.py:420
